TPU v7x, 32 devices: a whole 2x2x4 slice. The times are simulated.
32 devices in a mesh: ctx: 8 (over y, x, core), head: 4 (over z).
Axes of the slice: x: 2, y: 2, z: 4, core: 2. Of those that a mesh axis runs over, the one named last changes fastest.
Arguments:
- queries: bfloat16 [1024, 512], P('ctx', 'head'), may hold values from -6 to 6
- key_rows: bfloat16 [1024, 512], P('ctx', 'head'), may hold values from -6 to 6
- value_rows: bfloat16 [1024, 512], P('ctx', 'head'), may hold values from -6 to 6
- out_grad: bfloat16 [1024, 512], P('ctx', 'head'), may hold values from -24 to 24
- attn_out: bfloat16 [1024, 512], P('ctx', 'head'), may hold values from -6 to 6
- log_norm: float32 [1024, 4], P('ctx', 'head'), as said below
- query_weight: bfloat16 [4096, 512], P(None, 'head'), may hold values from -0.5 to 0.5
- key_weight: bfloat16 [4096, 512], P(None, 'head'), may hold values from -0.5 to 0.5
- value_weight: bfloat16 [4096, 512], P(None, 'head'), may hold values from -0.5 to 0.5
Outputs:
- input_grad: bfloat16 [1024, 4096], P('ctx', 'head')
Inputs may be any that keep to these rules, and one draw needn't show every extreme that they name: log_norm[t, h] lies between log(1 + t) and log(1 + t) + 1.5, with t the token's position.
All inputs are finite; a program needn't handle non-finite values.
Results may differ from a plain program's by a relative error of at most 0.009.
Values may be sent and summed in bfloat16 or wider, within the bound.
No kernel may reach another device: no remote copies, remote signals or barrier semaphores. Data moves between devices by JAX's collectives and lax.ppermute only.
A program may use at most 128 MiB of HBM per device.

v0:
```python
import jax
import jax.numpy as jnp
from jax import lax
from jax.sharding import PartitionSpec as P


def pair_terms(
    query_side, key_side, query_pos, key_pos, head_count, score_scale, want_query, want_keys
):
    query_rows, grad_rows, norm_rows, delta_rows = query_side
    key_block, value_block = key_side
    num_query = query_rows.shape[0]
    num_key = key_block.shape[0]
    feat_width = query_rows.shape[1]
    head_size = feat_width // head_count

    def compute():
        query_three = query_rows.reshape(num_query, head_count, head_size)
        grad_three = grad_rows.reshape(num_query, head_count, head_size)
        key_three = key_block.reshape(num_key, head_count, head_size)
        value_three = value_block.reshape(num_key, head_count, head_size)
        scores = score_scale * jnp.einsum(
            "qhd,khd->hqk", query_three, key_three, preferred_element_type=jnp.float32
        )
        visible = key_pos[None, None, :] <= query_pos[None, :, None]
        probs = jnp.where(visible, jnp.exp(scores - norm_rows.T[:, :, None]), 0.0)
        prob_grad = jnp.einsum(
            "qhd,khd->hqk", grad_three, value_three, preferred_element_type=jnp.float32
        )
        score_grad = probs * (prob_grad - delta_rows.T[:, :, None])
        score_low = score_grad.astype(jnp.bfloat16)
        results = []
        if want_query:
            query_part = score_scale * jnp.einsum(
                "hqk,khd->qhd", score_low, key_three, preferred_element_type=jnp.float32
            )
            results.append(query_part.reshape(num_query, feat_width))
        if want_keys:
            probs_low = probs.astype(jnp.bfloat16)
            key_part = score_scale * jnp.einsum(
                "hqk,qhd->khd", score_low, query_three, preferred_element_type=jnp.float32
            )
            value_part = jnp.einsum(
                "hqk,qhd->khd", probs_low, grad_three, preferred_element_type=jnp.float32
            )
            results.append(key_part.reshape(num_key, feat_width))
            results.append(value_part.reshape(num_key, feat_width))
        return tuple(results)

    def nothing():
        results = []
        if want_query:
            results.append(jnp.zeros((num_query, feat_width), jnp.float32))
        if want_keys:
            results.append(jnp.zeros((num_key, feat_width), jnp.float32))
            results.append(jnp.zeros((num_key, feat_width), jnp.float32))
        return tuple(results)

    return lax.cond(jnp.min(key_pos) <= jnp.max(query_pos), compute, nothing)


def body(
    queries,
    key_rows,
    value_rows,
    out_grad,
    attn_out,
    log_norm,
    query_weight,
    key_weight,
    value_weight,
):
    tok_rows = queries.shape[0]
    feat_width = queries.shape[1]
    head_count = log_norm.shape[1]
    head_size = feat_width // head_count
    score_scale = head_size ** (-0.5)
    ctx_index = lax.axis_index("ctx")
    delta_rows = jnp.sum(
        (out_grad.astype(jnp.float32) * attn_out.astype(jnp.float32)).reshape(
            tok_rows, head_count, head_size
        ),
        axis=2,
    )
    norm_all, delta_all = (
        lax.all_gather(log_norm, "ctx", axis=0, tiled=True),
        lax.all_gather(delta_rows, "ctx", axis=0, tiled=True),
    )
    own_pos = ctx_index * tok_rows + jnp.arange(tok_rows, dtype=jnp.int32)
    own_norm = jnp.take(norm_all, own_pos, axis=0)
    own_delta = jnp.take(delta_all, own_pos, axis=0)
    query_side = (queries, out_grad, own_norm, own_delta)
    key_side = (key_rows, value_rows)
    zero_block = jnp.zeros((tok_rows, feat_width), jnp.float32)
    shard_piece = (
        lax.all_gather(key_rows, "ctx", axis=0, tiled=True),
        lax.all_gather(value_rows, "ctx", axis=0, tiled=True),
    )
    positions = jnp.arange(shard_piece[0].shape[0], dtype=jnp.int32)
    term_list = pair_terms(
        query_side, shard_piece, own_pos, positions, head_count, score_scale, True, False
    )
    query_grad = zero_block + term_list[0]
    shard_piece = (
        lax.all_gather(queries, "ctx", axis=0, tiled=True),
        lax.all_gather(out_grad, "ctx", axis=0, tiled=True),
    )
    positions = jnp.arange(shard_piece[0].shape[0], dtype=jnp.int32)
    norm_part = jnp.take(norm_all, positions, axis=0)
    deltas = jnp.take(delta_all, positions, axis=0)
    remote_side = (shard_piece[0], shard_piece[1], norm_part, deltas)
    term_list = pair_terms(
        remote_side, key_side, positions, own_pos, head_count, score_scale, False, True
    )
    key_grad = zero_block + term_list[0]
    value_grad = zero_block + term_list[1]
    query_low = query_grad.astype(jnp.bfloat16)
    key_low = key_grad.astype(jnp.bfloat16)
    value_low = value_grad.astype(jnp.bfloat16)
    contract = (((1,), (1,)), ((), ()))
    partial_value = lax.dot_general(
        query_low, query_weight, contract, preferred_element_type=jnp.float32
    )
    partial_value = partial_value + lax.dot_general(
        key_low, key_weight, contract, preferred_element_type=jnp.float32
    )
    partial_value = partial_value + lax.dot_general(
        value_low, value_weight, contract, preferred_element_type=jnp.float32
    )
    return lax.psum_scatter(
        partial_value.astype(jnp.bfloat16), "head", scatter_dimension=1, tiled=True
    )


def solution(mesh):
    return jax.shard_map(
        body,
        mesh=mesh,
        in_specs=(
            P("ctx", "head"),
            P("ctx", "head"),
            P("ctx", "head"),
            P("ctx", "head"),
            P("ctx", "head"),
            P("ctx", "head"),
            P(None, "head"),
            P(None, "head"),
            P(None, "head"),
        ),
        out_specs=P("ctx", "head"),
        check_vma=False,
    )
```

profile of v0, /device:TPU:0, one launch (start us, length us, event | category | flops | bytes accessed | tf_op | source)
XLA Modules:
  0.0 119.9 jit_solution(11333591857317985601)
XLA Ops:
  6.5 0.0 copy-start
  6.5 0.0 reduce-scatter.2.cloned.1.call-start
  6.5 0.7 fusion.29
  7.3 0.9 multiply_reduce_fusion
  8.2 10.2 %all-gather.1 = f32[8,1,128]{2,1,0:T(1,128)S(1)} all-gather(f32[1,1,128]{2,1,0:T(1,128)S(1)} %bitcast.42), channel_id=2, replica_groups=mesh['ctx'=8,'head'=4] {'ctx'}, dimensions={0}, use_global_device_ids=true | all-gather | bytes 4608 | tf_op jit(solution)/shard_map/all_gather | solution.py:87
  18.4 1.0 gather_fusion.1
  19.4 0.0 copy-start.8
  19.4 4.5 %gather_fusion.3 = f32[1024]{0:T(1024)S(1)} fusion(f32[1024]{0:T(1024)S(1)} %bitcast.37, s32[1024]{0:T(1024)S(1)} %iota_clamp_fusion), kind=kCustom, calls=%fused_computation.3.clone | custom fusion | bytes 12288 | tf_op jit(solution)/shard_map/jit(_take)/gather | solution.py:110
  23.9 0.0 copy-done.8
  23.9 8.7 %all_gather.19 = f32[1024,1]{0,1:T(1,128)S(1)} all-gather(f32[128,1]{0,1:T(1,128)S(1)} %copy-done.8), channel_id=1, replica_groups=mesh['ctx'=8,'head'=4] {'ctx'}, dimensions={0}, use_global_device_ids=true | all-gather | bytes 4608 | tf_op jit(solution)/shard_map/all_gather | solution.py:86
  32.6 1.0 gather_fusion
  33.6 0.0 copy-start.4
  33.6 0.0 copy-start.6
  33.6 0.0 copy-start.7
  33.7 0.0 copy-start.5
  33.7 4.5 %gather_fusion.2 = f32[1024]{0:T(1024)S(1)} fusion(f32[1024]{0:T(1024)S(1)} %bitcast.35, s32[1024]{0:T(1024)S(1)} %iota_clamp_fusion), kind=kCustom, calls=%fused_computation.1.clone | custom fusion | bytes 12288 | tf_op jit(solution)/shard_map/jit(_take)/gather | solution.py:109
  38.2 0.0 copy-done.4
  38.2 8.3 %all_gather.23 = bf16[1024,128]{1,0:T(8,128)(2,1)S(1)} all-gather(bf16[128,128]{1,0:T(8,128)(2,1)S(1)} %copy-done.4), channel_id=1, replica_groups=mesh['ctx'=8,'head'=4] {'ctx'}, dimensions={0}, use_global_device_ids=true | all-gather | bytes 294912 | tf_op jit(solution)/shard_map/all_gather | solution.py:106
  47.9 0.0 copy-done.6
  47.9 10.3 %all_gather.22 = bf16[1024,128]{1,0:T(8,128)(2,1)} all-gather(bf16[128,128]{1,0:T(8,128)(2,1)S(1)} %copy-done.6), channel_id=1, replica_groups=mesh['ctx'=8,'head'=4] {'ctx'}, dimensions={0}, use_global_device_ids=true | all-gather | bytes 294912 | tf_op jit(solution)/shard_map/all_gather | solution.py:105
  58.2 0.0 copy-done.7
  58.2 8.4 %all_gather.18 = bf16[1024,128]{1,0:T(8,128)(2,1)S(1)} all-gather(bf16[128,128]{1,0:T(8,128)(2,1)S(1)} %copy-done.7), channel_id=1, replica_groups=mesh['ctx'=8,'head'=4] {'ctx'}, dimensions={0}, use_global_device_ids=true | all-gather | bytes 294912 | tf_op jit(solution)/shard_map/all_gather | solution.py:96
  66.6 0.0 copy-done.5
  66.6 9.2 %all_gather.20 = bf16[1024,128]{1,0:T(8,128)(2,1)S(1)} all-gather(bf16[128,128]{1,0:T(8,128)(2,1)S(1)} %copy-done.5), channel_id=1, replica_groups=mesh['ctx'=8,'head'=4] {'ctx'}, dimensions={0}, use_global_device_ids=true | all-gather | bytes 294912 | tf_op jit(solution)/shard_map/all_gather | solution.py:97
  75.8 0.7 conditional.2
  75.8 0.2 convolution_subtract_fusion
  76.1 0.4 fusion.7
  76.5 0.0 copy-done
  76.5 0.0 copy-start.1
  76.5 0.4 fusion.31
  77.0 0.5 copy-done.1
  77.5 4.8 %conditional.3 = (bf16[128,128]{1,0:T(8,128)(2,1)S(1)}, bf16[128,128]{1,0:T(8,128)(2,1)S(1)}) conditional(s32[]{:T(128)} %convert_element_type.55, () %tuple.29, (s32[128]{0:T(128)S(1)}, s32[1024]{0:T(1024)S(1)}, bf16[1024,128]{1,0:T(8,128)(2,1)S(1)}, bf16[128,128]{1,0:T(8,128)(2,1)S(1)}, f32[1024,1]{0,1:T(1,128)S(1)}, ...), branch_computations={%region_5.8_spmd, %region_6.9_spmd} | conditional | flops 135315456 | bytes 3813932 | solution.py:59
  77.5 0.0 copy-start.2
  77.5 0.7 copy-done.2
  78.2 1.2 fusion.18
  79.3 1.6 %fusion.23 = bf16[128,128]{1,0:T(8,128)(2,1)S(1)} fusion(bf16[1024,128]{1,0:T(8,128)(2,1)} %copy-done.2, f32[1024,128]{1,0:T(8,128)} %fusion.18, bf16[1024,128]{1,0:T(8,128)(2,1)S(1)} %get-tuple-element.58, bf16[128,128]{1,0:T(8,128)(2,1)S(1)} %get-tuple-element.59, f32[1024]{0:T(1024)S(1)} %bitcast.39), kind=kOutput, calls=%fused_computation.31 | convolution fusion | flops 67534848 | bytes 1118208 | tf_op jit(solution)/shard_map/cond/branch_1_fun/hqk,qhd->khd/dot_general | solution.py:40
  80.9 1.3 %convolution_convert_fusion = bf16[128,128]{1,0:T(8,128)(2,1)S(1)} fusion(bf16[1024,128]{1,0:T(8,128)(2,1)S(1)} %get-tuple-element.58, f32[1024,128]{1,0:T(8,128)} %fusion.18), kind=kOutput, calls=%fused_computation.32 | convolution fusion | flops 33701888 | bytes 819200 | tf_op jit(solution)/shard_map/cond/branch_1_fun/hqk,qhd->khd/dot_general | solution.py:43
  82.2 0.0 copy-start.3
  82.2 1.7 %convolution_add_fusion.1 = f32[128,4096]{1,0:T(8,128)S(1)} fusion(f32[128,4096]{1,0:T(8,128)S(1)} %fusion.31, bf16[128,128]{1,0:T(8,128)(2,1)S(1)} %get-tuple-element.63, bf16[4096,128]{1,0:T(8,128)(2,1)} %param.24), kind=kOutput, calls=%fused_computation.36 | convolution fusion | flops 134742016 | bytes 5275648 | tf_op jit(solution)/shard_map/dot_general | solution.py:124
  84.0 0.0 copy-done.3
  84.0 1.4 %fusion.26 = bf16[128,4096]{1,0:T(8,128)(2,1)} fusion(f32[128,4096]{1,0:T(8,128)S(1)} %convolution_add_fusion.1, bf16[128,128]{1,0:T(8,128)(2,1)S(1)} %get-tuple-element.64, bf16[4096,128]{1,0:T(8,128)(2,1)S(1)} %copy-done.3), kind=kOutput, calls=%fused_computation.37 | convolution fusion | flops 135266304 | bytes 4227072 | tf_op jit(solution)/shard_map/dot_general | solution.py:127
  85.4 0.0 reduce-scatter.2.cloned.1.call-update
  85.4 27.6 %reduce-scatter.2.cloned.1.call-done = bf16[128,1024]{1,0:T(8,128)(2,1)} async-done(((bf16[128,4096]{1,0:T(8,128)(2,1)}), bf16[128,1024]{1,0:T(8,128)(2,1)}) %reduce-scatter.2.cloned.1.call-update) | async-done | bytes 262160 | tf_op jit(solution)/shard_map/reduce_scatter | solution.py:130
  (9 shorter events, 0.0 us)
Async XLA Ops:
  6.5 70.0 %copy-start = (bf16[4096,128]{1,0:T(8,128)(2,1)S(1)}, bf16[4096,128]{1,0:T(8,128)(2,1)}, u32[]{:S(2)}) copy-start(bf16[4096,128]{1,0:T(8,128)(2,1)} %param.23) | copy-start | bytes 3145732
  6.5 106.5 %reduce-scatter.2.cloned.1.call-start = ((), (), s32[]{:S(2)}) async-start(), calls=%async_computation.1 | async-start | bytes 1310720 | tf_op jit(solution)/shard_map/reduce_scatter | solution.py:130
  19.4 4.6 %copy-start.8 = (f32[128,1]{0,1:T(1,128)S(1)}, f32[128,1]{0,1:T(1,128)}, u32[]{:S(2)}) copy-start(f32[128,1]{0,1:T(1,128)} %param.22) | copy-start | bytes 1540
  33.6 4.6 %copy-start.4 = (bf16[128,128]{1,0:T(8,128)(2,1)S(1)}, bf16[128,128]{1,0:T(8,128)(2,1)}, u32[]{:S(2)}) copy-start(bf16[128,128]{1,0:T(8,128)(2,1)} %param.20) | copy-start | bytes 98308
  33.6 14.3 %copy-start.6 = (bf16[128,128]{1,0:T(8,128)(2,1)S(1)}, bf16[128,128]{1,0:T(8,128)(2,1)}, u32[]{:S(2)}) copy-start(bf16[128,128]{1,0:T(8,128)(2,1)} %param.17) | copy-start | bytes 98308
  33.6 24.6 %copy-start.7 = (bf16[128,128]{1,0:T(8,128)(2,1)S(1)}, bf16[128,128]{1,0:T(8,128)(2,1)}, u32[]{:S(2)}) copy-start(bf16[128,128]{1,0:T(8,128)(2,1)} %param.18) | copy-start | bytes 98308
  33.7 32.9 %copy-start.5 = (bf16[128,128]{1,0:T(8,128)(2,1)S(1)}, bf16[128,128]{1,0:T(8,128)(2,1)}, u32[]{:S(2)}) copy-start(bf16[128,128]{1,0:T(8,128)(2,1)} %param.19) | copy-start | bytes 98308
  76.5 1.0 copy-start.1
  77.5 0.7 copy-start.2
  82.2 1.8 %copy-start.3 = (bf16[4096,128]{1,0:T(8,128)(2,1)S(1)}, bf16[4096,128]{1,0:T(8,128)(2,1)}, u32[]{:S(2)}) copy-start(bf16[4096,128]{1,0:T(8,128)(2,1)} %param.25) | copy-start | bytes 3145732
Sparse Core Ops, SparseCore 0:
  85.6 27.4 reduce-scatter.1
where the time goes:
time: 120 us
  blocking collectives  55.1 us (46%)
  waiting for transfers between devices  27.6 us (23%)
  between operations  14.9 us (12%)
  local copies, waits for them, and re-layouts  12.2 us (10%)
  matrix products  8.3 us (7%)
  other arithmetic  1.63 us (1%)
    reduce_scatter x1, waiting for transfers between devices, body(): lax.psum_scatter(partial_value.astype(jnp.bfloat16), 'head', scatter_dime...  27.6 us
    all_gather x1, blocking collectives, body(): lax.all_gather(queries, 'ctx', axis=0, tiled=True)  10.3 us
    all_gather x1, blocking collectives, body(): lax.all_gather(delta_rows, 'ctx', axis=0, tiled=True)  10.2 us
    all_gather x1, blocking collectives, body(): lax.all_gather(value_rows, 'ctx', axis=0, tiled=True)  9.21 us
    all_gather x1, blocking collectives, body(): lax.all_gather(log_norm, 'ctx', axis=0, tiled=True)  8.73 us
    all_gather x1, blocking collectives, body(): lax.all_gather(key_rows, 'ctx', axis=0, tiled=True)  8.39 us
    all_gather x1, blocking collectives, body(): lax.all_gather(out_grad, 'ctx', axis=0, tiled=True)  8.34 us
    gather x1, local copies, waits for them, and re-layouts, body(): deltas = jnp.take(delta_all, positions, axis=0)  4.53 us
  transfers between devices with their start and end apart: 1, of which 1 were waited for; matrix products, arithmetic and copies ran while one was open for 0% of the time, Pallas kernels for 0%

commit v1 on v0

v1 whole, which is shorter than its diff:
```python
import functools
import math

import jax
import jax.numpy as jnp
from jax import lax
from jax.experimental import pallas as pl
from jax.experimental.pallas import tpu as pltpu
from jax.sharding import PartitionSpec as P

NT = (((1,), (1,)), ((), ()))
PIECES = 3


def dot_nt(left, right):
    return lax.dot_general(left, right, NT, preferred_element_type=jnp.float32)


def pieces_of(column):
    out = []
    rest = column
    for _ in range(PIECES):
        low = rest.astype(jnp.bfloat16).astype(jnp.float32)
        out.append(low)
        rest = rest - low
    return out


def pack_kernel(norm_scale, k_ref, v_ref, q_ref, g_ref, a_ref, n_ref, out_ref):
    rows, width = q_ref.shape
    grad = g_ref[...]
    delta = jnp.sum(
        grad.astype(jnp.float32) * a_ref[...].astype(jnp.float32), axis=1, keepdims=True
    )
    row_at = lax.broadcasted_iota(jnp.int32, (rows, rows), 0)
    col_at = lax.broadcasted_iota(jnp.int32, (rows, rows), 1)
    norm = jnp.sum(
        jnp.where(row_at == col_at, n_ref[...] * norm_scale, 0.0), axis=1, keepdims=True
    )
    lane = lax.broadcasted_iota(jnp.int32, (rows, width), 1)
    extra = jnp.zeros((rows, width), jnp.float32)
    for at, piece in enumerate(pieces_of(norm) + pieces_of(delta)):
        extra = jnp.where(lane == at, piece, extra)
    out_ref[:, :width] = k_ref[...]
    out_ref[:, width : 2 * width] = v_ref[...]
    out_ref[:, 2 * width : 3 * width] = q_ref[...]
    out_ref[:, 3 * width : 4 * width] = extra.astype(jnp.bfloat16)
    out_ref[:, 4 * width :] = grad


def main_kernel(
    chunk, cols, scale, me_ref, all_ref, own_ref, wq_ref, wk_ref, wv_ref, out_ref, w_all, grads, sems
):
    rows = own_ref.shape[0]
    width = wq_ref.shape[1]
    copies = [
        pltpu.make_async_copy(ref, w_all.at[:, at * width : (at + 1) * width], sems.at[at])
        for at, ref in enumerate((wq_ref, wk_ref, wv_ref))
    ]
    for copy in copies:
        copy.start()
    first = me_ref[0] * rows
    exponent = scale * math.log2(math.e)
    key = own_ref[:, :width]
    value = own_ref[:, width : 2 * width]
    query = own_ref[:, 2 * width : 3 * width]
    extra = own_ref[:, 3 * width : 4 * width].astype(jnp.float32)
    grad = own_ref[:, 4 * width :]
    lane = lax.broadcasted_iota(jnp.int32, (rows, width), 1)
    in_norm = lane < PIECES
    in_delta = jnp.logical_and(lane >= PIECES, lane < 2 * PIECES)
    norm = jnp.sum(jnp.where(in_norm, extra, 0.0), axis=1, keepdims=True)
    delta = jnp.sum(jnp.where(in_delta, extra, 0.0), axis=1, keepdims=True)
    key_wide = jnp.concatenate([key, jnp.where(in_norm, -1.0, 0.0).astype(jnp.bfloat16)], axis=1)
    value_wide = jnp.concatenate(
        [jnp.where(in_delta, -1.0, 0.0).astype(jnp.bfloat16), value], axis=1
    )
    own_at = first + lax.broadcasted_iota(jnp.int32, (rows, chunk), 0)
    lane_at = lax.broadcasted_iota(jnp.int32, (rows, chunk), 1)

    def step(at, sums):
        query_sum, key_sum, value_sum = sums
        span = pl.ds(pl.multiple_of(at * chunk, chunk), chunk)
        other_at = lane_at + at * chunk
        keys = all_ref[span, :width]
        scores = dot_nt(query, keys)
        probs = jnp.where(other_at <= own_at, jnp.exp2(exponent * (scores - norm)), 0.0)
        prob_grad = dot_nt(grad, all_ref[span, width : 2 * width])
        score_low = (probs * (prob_grad - delta)).astype(jnp.bfloat16)
        query_sum += jnp.dot(score_low, keys, preferred_element_type=jnp.float32)
        scores = dot_nt(key_wide, all_ref[span, 2 * width : 4 * width])
        probs = jnp.where(own_at <= other_at, jnp.exp2(exponent * scores), 0.0)
        prob_grad = dot_nt(value_wide, all_ref[span, 3 * width :])
        score_low = (probs * prob_grad).astype(jnp.bfloat16)
        key_sum += jnp.dot(
            score_low, all_ref[span, 2 * width : 3 * width], preferred_element_type=jnp.float32
        )
        value_sum += jnp.dot(
            probs.astype(jnp.bfloat16), all_ref[span, 4 * width :], preferred_element_type=jnp.float32
        )
        return query_sum, key_sum, value_sum

    zero = jnp.zeros((rows, width), jnp.float32)
    count = all_ref.shape[0] // chunk
    if count == 1:
        sums = step(0, (zero, zero, zero))
    else:
        sums = lax.fori_loop(0, count, step, (zero, zero, zero))
    grads[:, :width] = (scale * sums[0]).astype(jnp.bfloat16)
    grads[:, width : 2 * width] = (scale * sums[1]).astype(jnp.bfloat16)
    grads[:, 2 * width :] = sums[2].astype(jnp.bfloat16)
    for copy in copies:
        copy.wait()
    for at in range(0, w_all.shape[0], cols):
        out_ref[:, at : at + cols] = dot_nt(grads[...], w_all[at : at + cols, :]).astype(jnp.bfloat16)


def body(
    queries,
    key_rows,
    value_rows,
    out_grad,
    attn_out,
    log_norm,
    query_weight,
    key_weight,
    value_weight,
):
    rows, width = queries.shape
    depth = query_weight.shape[0]
    scale = width ** (-0.5)
    vmem = pl.BlockSpec(memory_space=pltpu.VMEM)
    packed = pl.pallas_call(
        functools.partial(pack_kernel, 1.0 / scale),
        out_shape=jax.ShapeDtypeStruct((rows, 5 * width), jnp.bfloat16),
        in_specs=[vmem] * 6,
        out_specs=vmem,
    )(key_rows, value_rows, queries, out_grad, attn_out, log_norm.reshape(1, rows))
    gathered = lax.all_gather(packed, "ctx", axis=0, tiled=True)
    me = lax.axis_index("ctx").astype(jnp.int32).reshape(1)
    total = gathered.shape[0]
    chunk = math.gcd(total, 1024)
    hbm = pl.BlockSpec(memory_space=pl.ANY)
    partial_value = pl.pallas_call(
        functools.partial(main_kernel, chunk, math.gcd(depth, 512), scale),
        out_shape=jax.ShapeDtypeStruct((rows, depth), jnp.bfloat16),
        in_specs=[pl.BlockSpec(memory_space=pltpu.SMEM), vmem, vmem, hbm, hbm, hbm],
        out_specs=vmem,
        scratch_shapes=[
            pltpu.VMEM((depth, 3 * width), jnp.bfloat16),
            pltpu.VMEM((rows, 3 * width), jnp.bfloat16),
            pltpu.SemaphoreType.DMA((3,)),
        ],
        compiler_params=pltpu.CompilerParams(vmem_limit_bytes=48 * 1024 * 1024),
        cost_estimate=pl.CostEstimate(
            flops=14 * rows * total * width + 6 * rows * width * depth,
            bytes_accessed=6 * depth * width + 10 * total * width,
            transcendentals=2 * rows * total,
        ),
    )(me, gathered, packed, query_weight, key_weight, value_weight)
    return lax.psum_scatter(partial_value, "head", scatter_dimension=1, tiled=True)


def solution(mesh):
    return jax.shard_map(
        body,
        mesh=mesh,
        in_specs=(P("ctx", "head"),) * 6 + (P(None, "head"),) * 3,
        out_specs=P("ctx", "head"),
        check_vma=False,
    )
```

time: 120 us -> 80.7 us (0.67)
  blocking collectives: 55.1 us -> 0 us
  waiting for transfers between devices: 27.6 us -> 55.7 us
  matrix products: 8.3 us -> 0 us
  local copies, waits for them, and re-layouts: 12.2 us -> 5.9 us
  Pallas kernels: 0 us -> 5.29 us
  other arithmetic: 1.63 us -> 0 us
  between operations: 14.9 us -> 13.4 us
    all_gather x6 -> x0, blocking collectives: 55.1 us -> none  [the longest x1 10.3 us: body(): lax.all_gather(queries, 'ctx', axis=0, tiled=True)]
    all_gather x0 -> x1, waiting for transfers between devices: none -> 28.3 us  [body(): gathered = lax.all_gather(packed, 'ctx', axis=0, tiled=True)]
    gather x4 -> x0, local copies, waits for them, and re-layouts: 11 us -> none  [the longest x1 4.53 us: body(): deltas = jnp.take(delta_all, positions, axis=0)]
    dot_general x8 -> x0, matrix products: 8.3 us -> none  [the longest x1 1.75 us: body(): lax.dot_general(key_low, key_weight, contract, preferred_element_type=jnp...]
    unnamed x16 -> x10, local copies, waits for them, and re-layouts: 0.54 us -> 5.9 us
    pallas_call x0 -> x2, Pallas kernels: none -> 5.29 us  [the longest x1 3.68 us: body(): pl.pallas_call(functools.partial(main_kernel, chunk, math.gcd(depth, 512)...]
  transfers between devices with their start and end apart: 1 -> 2, of which waited for: 1 -> 2; matrix products, arithmetic and copies ran while one was open for 0% -> 0% of each run, Pallas kernels for 0% -> 0%
where the time goes in v1:
time: 80.7 us; the launch traced here: 80.3 us
  waiting for transfers between devices  55.7 us (69%)
  between operations  13.4 us (17%)
  local copies, waits for them, and re-layouts  5.9 us (7%)
  Pallas kernels  5.29 us (7%)
    all_gather x1, waiting for transfers between devices, body(): gathered = lax.all_gather(packed, 'ctx', axis=0, tiled=True)  28.3 us
    reduce_scatter x1, waiting for transfers between devices, body(): lax.psum_scatter(partial_value, 'head', scatter_dimension=1, tiled=True)  27.3 us
    unnamed x10, local copies, waits for them, and re-layouts  5.9 us
    pallas_call x1, Pallas kernels, body(): pl.pallas_call(functools.partial(main_kernel, chunk, math.gcd(depth, 512)...  3.68 us
    pallas_call x1, Pallas kernels, body(): pl.pallas_call(functools.partial(pack_kernel, 1.0 / scale), out_shape=jax...  1.62 us
  transfers between devices with their start and end apart: 2, of which 2 were waited for; matrix products, arithmetic and copies ran while one was open for 0% of the time, Pallas kernels for 0%

profile of v1, /device:TPU:0, one launch (start us, length us, event | category | flops | bytes accessed | tf_op | source)
XLA Modules:
  0.0 80.3 jit_solution(2102963079215138751)
XLA Ops:
  6.5 0.0 all-gather.2.cloned.1.call-start
  6.5 1.6 %shard_map.91.own_ref = bf16[128,640]{1,0:T(8,128)(2,1)} custom-call(bf16[128,128]{1,0:T(8,128)(2,1)} %k_ref.1, bf16[128,128]{1,0:T(8,128)(2,1)} %v_ref.1, bf16[128,128]{1,0:T(8,128)(2,1)} %q_ref.1, bf16[128,128]{1,0:T(8,128)(2,1)} %g_ref.1, bf16[128,128]{1,0:T(8,128)(2,1)} %a_ref.1, f32[1,128]{1,0:T(1,128)} %bitcast.2), custom_call_target="tpu_custom_call" | custom-call | tf_op jit(solution)/shard_map/pallas_call | solution.py:133
  8.2 0.0 all-gather.2.cloned.1.call-update
  8.2 0.0 reduce-scatter.2.cloned.1.call-start
  8.2 28.3 %all-gather.2.cloned.1.call-done.all_ref = bf16[1024,640]{1,0:T(8,128)(2,1)} async-done(((bf16[128,640]{1,0:T(8,128)(2,1)}), bf16[1024,640]{1,0:T(8,128)(2,1)}) %all-gather.2.cloned.1.call-update) | async-done | bytes 1310736 | tf_op jit(solution)/shard_map/all_gather | solution.py:139
  36.6 0.0 copy-start
  36.6 0.9 %copy-done = bf16[128,640]{1,0:T(8,128)(2,1)S(1)} copy-done((bf16[128,640]{1,0:T(8,128)(2,1)S(1)}, bf16[128,640]{1,0:T(8,128)(2,1)}, u32[]{:S(2)}) %copy-start) | copy-done | bytes 163864
  37.5 0.0 copy-start.1
  37.5 1.3 %copy-done.1 = bf16[1024,640]{1,0:T(8,128)(2,1)S(1)} copy-done((bf16[1024,640]{1,0:T(8,128)(2,1)S(1)}, bf16[1024,640]{1,0:T(8,128)(2,1)}, u32[]{:S(2)}) %copy-start.1) | copy-done | bytes 1310744
  38.8 0.0 copy-start.2
  38.8 1.2 %copy-done.2 = bf16[4096,128]{1,0:T(8,128)(2,1)S(1)} copy-done((bf16[4096,128]{1,0:T(8,128)(2,1)S(1)}, bf16[4096,128]{1,0:T(8,128)(2,1)}, u32[]{:S(2)}) %copy-start.2) | copy-done | bytes 1048600
  40.0 0.0 copy-start.3
  40.0 1.2 %copy-done.3 = bf16[4096,128]{1,0:T(8,128)(2,1)S(1)} copy-done((bf16[4096,128]{1,0:T(8,128)(2,1)S(1)}, bf16[4096,128]{1,0:T(8,128)(2,1)}, u32[]{:S(2)}) %copy-start.3) | copy-done | bytes 1048600
  41.3 0.0 copy-start.4
  41.3 1.2 %copy-done.4 = bf16[4096,128]{1,0:T(8,128)(2,1)S(1)} copy-done((bf16[4096,128]{1,0:T(8,128)(2,1)S(1)}, bf16[4096,128]{1,0:T(8,128)(2,1)}, u32[]{:S(2)}) %copy-start.4) | copy-done | bytes 1048600
  42.5 3.7 %shard_map.92 = bf16[128,4096]{1,0:T(8,128)(2,1)} custom-call(s32[1]{0:T(128)} %bitcast.me_ref, bf16[1024,640]{1,0:T(8,128)(2,1)S(1)} %copy-done.1, bf16[128,640]{1,0:T(8,128)(2,1)S(1)} %copy-done, bf16[4096,128]{1,0:T(8,128)(2,1)S(1)} %copy-done.2, bf16[4096,128]{1,0:T(8,128)(2,1)S(1)} %copy-done.3, bf16[4096,128]{1,0:T(8,128)(2,1)S(1)} %copy-done.4), custom_call_target="tpu_custom_call" | custom-call | flops 637534208 | bytes 4456448 | tf_op jit(solution)/shard_map/pallas_call | solution.py:144
  46.2 0.0 reduce-scatter.2.cloned.1.call-update
  46.2 27.3 %reduce-scatter.2.cloned.1.call-done = bf16[128,1024]{1,0:T(8,128)(2,1)} async-done(((bf16[128,4096]{1,0:T(8,128)(2,1)}), bf16[128,1024]{1,0:T(8,128)(2,1)}) %reduce-scatter.2.cloned.1.call-update) | async-done | bytes 262160 | tf_op jit(solution)/shard_map/reduce_scatter | solution.py:161
Async XLA Ops:
  6.5 30.0 %all-gather.2.cloned.1.call-start = ((), (), s32[]{:S(2)}) async-start(), calls=%async_computation.1 | async-start | bytes 1474560 | tf_op jit(solution)/shard_map/all_gather | solution.py:139
  8.2 65.3 %reduce-scatter.2.cloned.1.call-start = ((), (), s32[]{:S(2)}) async-start(), calls=%async_computation.2 | async-start | bytes 1310720 | tf_op jit(solution)/shard_map/reduce_scatter | solution.py:161
  36.6 0.9 %copy-start = (bf16[128,640]{1,0:T(8,128)(2,1)S(1)}, bf16[128,640]{1,0:T(8,128)(2,1)}, u32[]{:S(2)}) copy-start(bf16[128,640]{1,0:T(8,128)(2,1)} %shard_map.91.own_ref) | copy-start | bytes 491524
  37.5 1.3 %copy-start.1 = (bf16[1024,640]{1,0:T(8,128)(2,1)S(1)}, bf16[1024,640]{1,0:T(8,128)(2,1)}, u32[]{:S(2)}) copy-start(bf16[1024,640]{1,0:T(8,128)(2,1)} %all-gather.2.cloned.1.call-done.all_ref) | copy-start | bytes 3932164
  38.8 1.2 %copy-start.2 = (bf16[4096,128]{1,0:T(8,128)(2,1)S(1)}, bf16[4096,128]{1,0:T(8,128)(2,1)}, u32[]{:S(2)}) copy-start(bf16[4096,128]{1,0:T(8,128)(2,1)} %wq_ref.1) | copy-start | bytes 3145732
  40.0 1.2 %copy-start.3 = (bf16[4096,128]{1,0:T(8,128)(2,1)S(1)}, bf16[4096,128]{1,0:T(8,128)(2,1)}, u32[]{:S(2)}) copy-start(bf16[4096,128]{1,0:T(8,128)(2,1)} %wk_ref.1) | copy-start | bytes 3145732
  41.3 1.2 %copy-start.4 = (bf16[4096,128]{1,0:T(8,128)(2,1)S(1)}, bf16[4096,128]{1,0:T(8,128)(2,1)}, u32[]{:S(2)}) copy-start(bf16[4096,128]{1,0:T(8,128)(2,1)} %wv_ref.1) | copy-start | bytes 3145732
Sparse Core Ops, SparseCore 0:
  9.2 27.2 all-gather.1
  46.3 27.1 reduce-scatter.1

commit v2 on v1

v2 whole, which is shorter than its diff:
```python
import functools
import math

import jax
import jax.numpy as jnp
from jax import lax
from jax.experimental import pallas as pl
from jax.experimental.pallas import tpu as pltpu
from jax.sharding import PartitionSpec as P

NT = (((1,), (1,)), ((), ()))
TN = (((0,), (0,)), ((), ()))
PIECES = 3
EXTRA = 16
MIB = 1024 * 1024


def dot_nt(left, right):
    return lax.dot_general(left, right, NT, preferred_element_type=jnp.float32)


def dot_tn(left, right):
    return lax.dot_general(left, right, TN, preferred_element_type=jnp.float32)


def dot_nn(left, right):
    return jnp.dot(left, right, preferred_element_type=jnp.float32)


def pieces_of(value):
    out = []
    rest = value
    for _ in range(PIECES):
        low = rest.astype(jnp.bfloat16).astype(jnp.float32)
        out.append(low)
        rest = rest - low
    return out


def diagonal(rows):
    row_at = lax.broadcasted_iota(jnp.int32, (rows, rows), 0)
    col_at = lax.broadcasted_iota(jnp.int32, (rows, rows), 1)
    return row_at == col_at


def delta_of(grad, attn):
    return jnp.sum(grad.astype(jnp.float32) * attn.astype(jnp.float32), axis=1, keepdims=True)


def pack_kernel(me_ref, q_ref, k_ref, v_ref, g_ref, a_ref, n_ref, out_ref):
    rows, width = q_ref.shape
    me = me_ref[0]
    delta = delta_of(g_ref[...], a_ref[...])
    delta = jnp.sum(jnp.where(diagonal(rows), delta, 0.0), axis=0, keepdims=True)
    row = lax.broadcasted_iota(jnp.int32, (EXTRA, rows), 0)
    extra = jnp.zeros((EXTRA, rows), jnp.float32)
    for at, piece in enumerate(pieces_of(n_ref[...]) + pieces_of(delta)):
        extra = jnp.where(row == at, piece, extra)
    extra = extra.astype(jnp.bfloat16)

    def for_later(at, carry):
        out_ref[at, :rows, :width] = k_ref[...]
        out_ref[at, :rows, width:] = v_ref[...]
        out_ref[at, rows:, :] = jnp.zeros((EXTRA, 2 * width), jnp.bfloat16)
        return carry

    def for_earlier(at, carry):
        out_ref[at, :rows, :width] = q_ref[...]
        out_ref[at, :rows, width:] = g_ref[...]
        out_ref[at, rows:, :width] = extra
        out_ref[at, rows:, width:] = jnp.zeros((EXTRA, width), jnp.bfloat16)
        return carry

    lax.fori_loop(0, me + 1, for_earlier, 0)
    lax.fori_loop(me + 1, out_ref.shape[0], for_later, 0)


def main_kernel(
    group,
    scale,
    me_ref,
    got_ref,
    q_ref,
    k_ref,
    v_ref,
    g_ref,
    a_ref,
    n_ref,
    wq_ref,
    wk_ref,
    wv_ref,
    out_ref,
    w_all,
    grads,
    sems,
):
    rows, width = q_ref.shape
    copies = [
        pltpu.make_async_copy(ref, w_all.at[:, at * width : (at + 1) * width], sems.at[at])
        for at, ref in enumerate((wq_ref, wk_ref, wv_ref))
    ]
    for copy in copies:
        copy.start()
    me = me_ref[0]
    exponent = scale * math.log2(math.e)
    query, key, value, grad = q_ref[...], k_ref[...], v_ref[...], g_ref[...]
    eye = diagonal(rows)
    norm = (1.0 / scale) * jnp.sum(jnp.where(eye, n_ref[...], 0.0), axis=1, keepdims=True)
    delta = delta_of(grad, a_ref[...])

    row_at = lax.broadcasted_iota(jnp.int32, (rows, rows), 0)
    col_at = lax.broadcasted_iota(jnp.int32, (rows, rows), 1)
    probs = jnp.where(col_at <= row_at, jnp.exp2(exponent * (dot_nt(query, key) - norm)), 0.0)
    score_low = (probs * (dot_nt(grad, value) - delta)).astype(jnp.bfloat16)
    query_sum = dot_nn(score_low, key)
    key_sum = dot_tn(score_low, query)
    value_sum = dot_tn(probs.astype(jnp.bfloat16), grad)

    first_side = jnp.concatenate([query, key], axis=0)
    second_side = jnp.concatenate([grad, value], axis=0)

    def step(at, sums):
        both_sum, value_sum = sums
        blocks = [at * group + i for i in range(group)]
        first = jnp.concatenate([got_ref[b, :rows, :width] for b in blocks], axis=0)
        second = jnp.concatenate([got_ref[b, :rows, width:] for b in blocks], axis=0)
        extra = jnp.concatenate([got_ref[b, rows:, :width] for b in blocks], axis=1)
        extra = extra.astype(jnp.float32)
        norms = (1.0 / scale) * jnp.sum(extra[:PIECES], axis=0, keepdims=True)
        deltas = jnp.sum(extra[PIECES : 2 * PIECES], axis=0, keepdims=True)
        block = at * group + lax.broadcasted_iota(jnp.int32, (rows, group * rows), 1) // rows
        earlier, later = block < me, block > me
        scores = dot_nt(first_side, first)
        scores = jnp.where(earlier, scores[:rows] - norm, scores[rows:] - norms)
        probs = jnp.exp2(exponent * jnp.where(block == me, 0.0, scores))
        prob_grad = dot_nt(second_side, second)
        prob_grad = jnp.where(earlier, prob_grad[:rows] - delta, prob_grad[rows:] - deltas)
        score_grad = probs * prob_grad
        sides = jnp.concatenate(
            [jnp.where(earlier, score_grad, 0.0), jnp.where(later, score_grad, 0.0)], axis=0
        ).astype(jnp.bfloat16)
        both_sum += dot_nn(sides, first)
        value_sum += dot_nn(jnp.where(later, probs, 0.0).astype(jnp.bfloat16), second)
        return both_sum, value_sum

    sums = (jnp.concatenate([query_sum, key_sum], axis=0), value_sum)
    count = got_ref.shape[0] // group
    if count == 1:
        sums = step(0, sums)
    else:
        sums = lax.fori_loop(0, count, step, sums)
    grads[:, :width] = (scale * sums[0][:rows]).astype(jnp.bfloat16)
    grads[:, width : 2 * width] = (scale * sums[0][rows:]).astype(jnp.bfloat16)
    grads[:, 2 * width :] = sums[1].astype(jnp.bfloat16)
    for copy in copies:
        copy.wait()
    parts, _, part = out_ref.shape
    cols = math.gcd(part, 512)
    for h in range(parts):
        for at in range(0, part, cols):
            weight = w_all[h * part + at : h * part + at + cols, :]
            out_ref[h, :, at : at + cols] = dot_nt(grads[...], weight).astype(jnp.bfloat16)


def body(
    queries,
    key_rows,
    value_rows,
    out_grad,
    attn_out,
    log_norm,
    query_weight,
    key_weight,
    value_weight,
):
    rows, width = queries.shape
    depth = query_weight.shape[0]
    scale = width ** (-0.5)
    ctx = lax.axis_size("ctx")
    parts = lax.axis_size("head")
    vmem = pl.BlockSpec(memory_space=pltpu.VMEM)
    smem = pl.BlockSpec(memory_space=pltpu.SMEM)
    hbm = pl.BlockSpec(memory_space=pltpu.HBM)
    me = lax.axis_index("ctx").astype(jnp.int32).reshape(1)
    own = (queries, key_rows, value_rows, out_grad, attn_out, log_norm.reshape(1, rows))
    packed = pl.pallas_call(
        pack_kernel,
        out_shape=jax.ShapeDtypeStruct((ctx, rows + EXTRA, 2 * width), jnp.bfloat16),
        in_specs=[smem] + [vmem] * 6,
        out_specs=vmem,
        compiler_params=pltpu.CompilerParams(vmem_limit_bytes=32 * MIB),
    )(me, *own)
    got = lax.all_to_all(packed, "ctx", split_axis=0, concat_axis=0, tiled=True)
    total = ctx * rows
    group = math.gcd(ctx, 8)
    parted = pl.pallas_call(
        functools.partial(main_kernel, group, scale),
        out_shape=jax.ShapeDtypeStruct((parts, rows, depth // parts), jnp.bfloat16),
        in_specs=[smem] + [vmem] * 7 + [hbm] * 3,
        out_specs=vmem,
        scratch_shapes=[
            pltpu.VMEM((depth, 3 * width), jnp.bfloat16),
            pltpu.VMEM((rows, 3 * width), jnp.bfloat16),
            pltpu.SemaphoreType.DMA((3,)),
        ],
        compiler_params=pltpu.CompilerParams(vmem_limit_bytes=48 * MIB),
        cost_estimate=pl.CostEstimate(
            flops=14 * rows * total * width + 6 * rows * width * depth,
            bytes_accessed=6 * depth * width + 10 * total * width,
            transcendentals=2 * rows * total,
        ),
    )(me, got, *own, query_weight, key_weight, value_weight)
    swapped = lax.all_to_all(parted, "head", split_axis=0, concat_axis=0, tiled=True)
    return jnp.sum(swapped.astype(jnp.float32), axis=0).astype(jnp.bfloat16)


def solution(mesh):
    return jax.shard_map(
        body,
        mesh=mesh,
        in_specs=(P("ctx", "head"),) * 6 + (P(None, "head"),) * 3,
        out_specs=P("ctx", "head"),
        check_vma=False,
    )
```

time: 80.7 us -> 57.4 us (0.71)
  waiting for transfers between devices: 55.7 us -> 0 us
  blocking collectives: 0 us -> 45.9 us
  between operations: 13.4 us -> 0.12 us
  Pallas kernels: 5.29 us -> 2.83 us
  local copies, waits for them, and re-layouts: 5.9 us -> 7.02 us
  other arithmetic: 0 us -> 0.93 us
    all_to_all x0 -> x2, blocking collectives: none -> 45.9 us  [the longest x1 30.3 us: body(): lax.all_to_all(parted, 'head', split_axis=0, concat_axis=0, tiled=True)]
    all_gather x1 -> x0, waiting for transfers between devices: 28.3 us -> none  [body(): gathered = lax.all_gather(packed, 'ctx', axis=0, tiled=True)]
    reduce_scatter x1 -> x0, waiting for transfers between devices: 27.3 us -> none  [body(): lax.psum_scatter(partial_value, 'head', scatter_dimension=1, tiled=True)]
    pallas_call x2, Pallas kernels: 5.29 us -> 2.83 us  [the longest x1 2.6 us: body(): pl.pallas_call(functools.partial(main_kernel, group, scale), out_shape=ja...]
    unnamed x10 -> x30, local copies, waits for them, and re-layouts: 5.9 us -> 7.02 us
    reduce_sum x0 -> x1, other arithmetic: none -> 0.93 us  [body(): return jnp.sum(swapped.astype(jnp.float32), axis=0).astype(jnp.bfloat16)]
  transfers between devices with their start and end apart: 2 -> 0, of which waited for: 2 -> 0; matrix products, arithmetic and copies ran while one was open for 0% -> 0% of each run, Pallas kernels for 0% -> 0%
where the time goes in v2:
time: 57.4 us; the launch traced here: 56.8 us
  blocking collectives  45.9 us (80%)
  local copies, waits for them, and re-layouts  7.02 us (12%)
  Pallas kernels  2.83 us (5%)
  other arithmetic  0.93 us (2%)
    all_to_all x1, blocking collectives, body(): lax.all_to_all(parted, 'head', split_axis=0, concat_axis=0, tiled=True)  30.3 us
    all_to_all x1, blocking collectives, body(): got = lax.all_to_all(packed, 'ctx', split_axis=0, concat_axis=0, tiled=True)  15.6 us
    unnamed x30, local copies, waits for them, and re-layouts  7.02 us
    pallas_call x1, Pallas kernels, body(): pl.pallas_call(functools.partial(main_kernel, group, scale), out_shape=ja...  2.6 us

profile of v2, /device:TPU:0, one launch (start us, length us, event | category | flops | bytes accessed | tf_op | source)
XLA Modules:
  0.0 56.8 jit_solution(8871927892478935465)
XLA Ops:
  0.0 0.0 copy-start
  0.0 0.0 copy-start.3
  0.0 0.8 %copy-done.3 = bf16[128,128]{1,0:T(8,128)(2,1)S(1)} copy-done((bf16[128,128]{1,0:T(8,128)(2,1)S(1)}, bf16[128,128]{1,0:T(8,128)(2,1)}, u32[]{:S(2)}) %copy-start.3) | copy-done | bytes 32792
  0.8 0.0 copy-start.5
  0.9 0.8 %copy-done.5 = bf16[128,128]{1,0:T(8,128)(2,1)S(1)} copy-done((bf16[128,128]{1,0:T(8,128)(2,1)S(1)}, bf16[128,128]{1,0:T(8,128)(2,1)}, u32[]{:S(2)}) %copy-start.5) | copy-done | bytes 32792
  1.6 0.0 copy-start.7
  1.6 0.8 %copy-done.7 = bf16[128,128]{1,0:T(8,128)(2,1)S(1)} copy-done((bf16[128,128]{1,0:T(8,128)(2,1)S(1)}, bf16[128,128]{1,0:T(8,128)(2,1)}, u32[]{:S(2)}) %copy-start.7) | copy-done | bytes 32792
  2.4 0.0 copy-start.9
  2.4 0.8 %copy-done.9 = bf16[128,128]{1,0:T(8,128)(2,1)S(1)} copy-done((bf16[128,128]{1,0:T(8,128)(2,1)S(1)}, bf16[128,128]{1,0:T(8,128)(2,1)}, u32[]{:S(2)}) %copy-start.9) | copy-done | bytes 32792
  3.1 0.0 copy-start.11
  3.1 0.8 %copy-done.11 = bf16[128,128]{1,0:T(8,128)(2,1)S(1)} copy-done((bf16[128,128]{1,0:T(8,128)(2,1)S(1)}, bf16[128,128]{1,0:T(8,128)(2,1)}, u32[]{:S(2)}) %copy-start.11) | copy-done | bytes 32792
  3.9 0.0 copy-start.13
  3.9 0.7 %copy-done.13 = f32[128,1]{0,1:T(1,128)S(1)} copy-done((f32[128,1]{0,1:T(1,128)S(1)}, f32[128,1]{0,1:T(1,128)}, u32[]{:S(2)}) %copy-start.13) | copy-done | bytes 536
  4.5 0.2 shard_map.91
  4.8 0.0 copy-start.4
  4.8 0.0 copy-start.6
  4.8 0.0 copy-start.8
  4.8 0.0 copy-start.10
  4.8 0.0 copy-start.12
  4.8 0.0 copy-start.14
  4.9 15.6 %all_to_all.10.got_ref = bf16[8,144,256]{2,1,0:T(8,128)(2,1)S(1)} all-to-all(bf16[8,144,256]{2,1,0:T(8,128)(2,1)S(1)} %shard_map.91), channel_id=1, replica_groups=mesh['ctx'=8,'head'=4] {'ctx'}, dimensions={0} | all-to-all | bytes 1179648 | tf_op jit(solution)/shard_map/all_to_all | solution.py:193
  20.4 0.0 copy-done
  20.4 0.0 copy-done.4
  20.4 0.0 copy-done.6
  20.4 0.0 copy-done.8
  20.4 0.0 copy-done.10
  20.4 0.0 copy-done.12
  20.4 0.0 copy-done.14
  20.5 0.0 copy-start.1
  20.5 1.2 %copy-done.1 = bf16[4096,128]{1,0:T(8,128)(2,1)S(1)} copy-done((bf16[4096,128]{1,0:T(8,128)(2,1)S(1)}, bf16[4096,128]{1,0:T(8,128)(2,1)}, u32[]{:S(2)}) %copy-start.1) | copy-done | bytes 1048600
  21.7 0.0 copy-start.2
  21.7 1.2 %copy-done.2 = bf16[4096,128]{1,0:T(8,128)(2,1)S(1)} copy-done((bf16[4096,128]{1,0:T(8,128)(2,1)S(1)}, bf16[4096,128]{1,0:T(8,128)(2,1)}, u32[]{:S(2)}) %copy-start.2) | copy-done | bytes 1048600
  22.9 2.6 %shard_map.92 = bf16[4,128,1024]{2,1,0:T(8,128)(2,1)S(1)} custom-call(s32[1]{0:T(128)} %bitcast.me_ref, bf16[8,144,256]{2,1,0:T(8,128)(2,1)S(1)} %all_to_all.10.got_ref, bf16[128,128]{1,0:T(8,128)(2,1)S(1)} %copy-done.4, bf16[128,128]{1,0:T(8,128)(2,1)S(1)} %copy-done.6, bf16[128,128]{1,0:T(8,128)(2,1)S(1)} %copy-done.8, bf16[128,128]{1,0:T(8,128)(2,1)S(1)} %copy-done.10, ...), custom_call_target="tpu_custom_call" | custom-call | flops 637534208 | bytes 4456448 | tf_op jit(solution)/shard_map/pallas_call | solution.py:196
  25.5 30.3 %all_to_all.11 = bf16[4,128,1024]{2,1,0:T(8,128)(2,1)S(1)} all-to-all(bf16[4,128,1024]{2,1,0:T(8,128)(2,1)S(1)} %shard_map.92), channel_id=1, replica_groups=mesh['ctx'=8,'head'=4] {'head'}, dimensions={0} | all-to-all | bytes 2097152 | tf_op jit(solution)/shard_map/all_to_all | solution.py:213
  55.8 0.9 %reduce_sum.12 = bf16[128,1024]{1,0:T(8,128)(2,1)} reduce(bf16[4,128,1024]{2,1,0:T(8,128)(2,1)S(1)} %all_to_all.11, bf16[]{:T(256)} %constant.8.clone.1), dimensions={0}, to_apply=%region_0.0 | reduce | flops 393216 | bytes 1310722 | tf_op jit(solution)/shard_map/reduce_sum | solution.py:214
Async XLA Ops:
  0.0 20.4 %copy-start = (bf16[4096,128]{1,0:T(8,128)(2,1)S(1)}, bf16[4096,128]{1,0:T(8,128)(2,1)}, u32[]{:S(2)}) copy-start(bf16[4096,128]{1,0:T(8,128)(2,1)} %wq_ref.1) | copy-start | bytes 3145732
  0.0 0.8 %copy-start.3 = (bf16[128,128]{1,0:T(8,128)(2,1)S(1)}, bf16[128,128]{1,0:T(8,128)(2,1)}, u32[]{:S(2)}) copy-start(bf16[128,128]{1,0:T(8,128)(2,1)} %q_ref.3) | copy-start | bytes 98308
  0.8 0.8 %copy-start.5 = (bf16[128,128]{1,0:T(8,128)(2,1)S(1)}, bf16[128,128]{1,0:T(8,128)(2,1)}, u32[]{:S(2)}) copy-start(bf16[128,128]{1,0:T(8,128)(2,1)} %k_ref.3) | copy-start | bytes 98308
  1.6 0.8 %copy-start.7 = (bf16[128,128]{1,0:T(8,128)(2,1)S(1)}, bf16[128,128]{1,0:T(8,128)(2,1)}, u32[]{:S(2)}) copy-start(bf16[128,128]{1,0:T(8,128)(2,1)} %v_ref.3) | copy-start | bytes 98308
  2.4 0.8 %copy-start.9 = (bf16[128,128]{1,0:T(8,128)(2,1)S(1)}, bf16[128,128]{1,0:T(8,128)(2,1)}, u32[]{:S(2)}) copy-start(bf16[128,128]{1,0:T(8,128)(2,1)} %g_ref.3) | copy-start | bytes 98308
  3.1 0.8 %copy-start.11 = (bf16[128,128]{1,0:T(8,128)(2,1)S(1)}, bf16[128,128]{1,0:T(8,128)(2,1)}, u32[]{:S(2)}) copy-start(bf16[128,128]{1,0:T(8,128)(2,1)} %a_ref.3) | copy-start | bytes 98308
  3.9 0.7 %copy-start.13 = (f32[128,1]{0,1:T(1,128)S(1)}, f32[128,1]{0,1:T(1,128)}, u32[]{:S(2)}) copy-start(f32[128,1]{0,1:T(1,128)} %param.14) | copy-start | bytes 1540
  4.8 15.6 %copy-start.4 = (bf16[128,128]{1,0:T(8,128)(2,1)S(1)}, bf16[128,128]{1,0:T(8,128)(2,1)}, u32[]{:S(2)}) copy-start(bf16[128,128]{1,0:T(8,128)(2,1)} %q_ref.3) | copy-start | bytes 98308
  4.8 15.6 %copy-start.6 = (bf16[128,128]{1,0:T(8,128)(2,1)S(1)}, bf16[128,128]{1,0:T(8,128)(2,1)}, u32[]{:S(2)}) copy-start(bf16[128,128]{1,0:T(8,128)(2,1)} %k_ref.3) | copy-start | bytes 98308
  4.8 15.6 %copy-start.8 = (bf16[128,128]{1,0:T(8,128)(2,1)S(1)}, bf16[128,128]{1,0:T(8,128)(2,1)}, u32[]{:S(2)}) copy-start(bf16[128,128]{1,0:T(8,128)(2,1)} %v_ref.3) | copy-start | bytes 98308
  4.8 15.6 %copy-start.10 = (bf16[128,128]{1,0:T(8,128)(2,1)S(1)}, bf16[128,128]{1,0:T(8,128)(2,1)}, u32[]{:S(2)}) copy-start(bf16[128,128]{1,0:T(8,128)(2,1)} %g_ref.3) | copy-start | bytes 98308
  4.8 15.6 %copy-start.12 = (bf16[128,128]{1,0:T(8,128)(2,1)S(1)}, bf16[128,128]{1,0:T(8,128)(2,1)}, u32[]{:S(2)}) copy-start(bf16[128,128]{1,0:T(8,128)(2,1)} %a_ref.3) | copy-start | bytes 98308
  4.8 15.6 %copy-start.14 = (f32[128,1]{0,1:T(1,128)S(1)}, f32[128,1]{0,1:T(1,128)}, u32[]{:S(2)}) copy-start(f32[128,1]{0,1:T(1,128)} %param.14) | copy-start | bytes 1540
  20.5 1.2 %copy-start.1 = (bf16[4096,128]{1,0:T(8,128)(2,1)S(1)}, bf16[4096,128]{1,0:T(8,128)(2,1)}, u32[]{:S(2)}) copy-start(bf16[4096,128]{1,0:T(8,128)(2,1)} %wk_ref.1) | copy-start | bytes 3145732
  21.7 1.2 %copy-start.2 = (bf16[4096,128]{1,0:T(8,128)(2,1)S(1)}, bf16[4096,128]{1,0:T(8,128)(2,1)}, u32[]{:S(2)}) copy-start(bf16[4096,128]{1,0:T(8,128)(2,1)} %wv_ref.1) | copy-start | bytes 3145732

commit v3 on v2

--- a/solution.py
+++ b/solution.py
@@ -162,34 +162,203 @@
             out_ref[h, :, at : at + cols] = dot_nt(grads[...], weight).astype(jnp.bfloat16)
 
 
-def body(
-    queries,
-    key_rows,
-    value_rows,
-    out_grad,
-    attn_out,
-    log_norm,
-    query_weight,
-    key_weight,
-    value_weight,
+def send_kernel(
+    spot_ref, q_in, k_in, v_in, g_in, a_in, n_ref, wq_ref, wk_ref, wv_ref, *refs
 ):
-    rows, width = queries.shape
-    depth = query_weight.shape[0]
-    scale = width ** (-0.5)
+    q_ref, k_ref, v_ref, g_ref, a_ref, in_sems, w_sems = refs[-7:]
+    outs = refs[:-7]
+    me, head = spot_ref[0], spot_ref[1]
+    rows, width = q_ref.shape
+    hops = [ref for ref in outs if ref.shape[0] == rows + EXTRA]
+    blocks = [ref for ref in outs if ref.shape[0] != rows + EXTRA]
+    part = wq_ref.shape[0] // (len(blocks) + 1)
+    piece = blocks[0].shape[0]
+    loads = [
+        pltpu.make_async_copy(src, dst, in_sems.at[at])
+        for at, (src, dst) in enumerate(
+            ((k_in, k_ref), (v_in, v_ref), (q_in, q_ref), (g_in, g_ref), (a_in, a_ref))
+        )
+    ]
+    for load in loads:
+        load.start()
+    moves = []
+    for at, block in enumerate(blocks):
+        start = pl.multiple_of((head ^ (at + 1)) * part + me * piece, piece)
+        for col, weight in enumerate((wq_ref, wk_ref, wv_ref)):
+            moves.append(
+                pltpu.make_async_copy(
+                    weight.at[pl.ds(start, piece), :],
+                    block.at[:, col * width : (col + 1) * width],
+                    w_sems.at[3 * at + col],
+                )
+            )
+    for move in moves:
+        move.start()
+    for load in loads:
+        load.wait()
+    delta = delta_of(g_ref[...], a_ref[...])
+    delta = jnp.sum(jnp.where(diagonal(rows), delta, 0.0), axis=0, keepdims=True)
+    row = lax.broadcasted_iota(jnp.int32, (EXTRA, rows), 0)
+    extra = jnp.zeros((EXTRA, rows), jnp.float32)
+    for at, value in enumerate(pieces_of(n_ref[...]) + pieces_of(delta)):
+        extra = jnp.where(row == at, value, extra)
+    extra = extra.astype(jnp.bfloat16)
+    for at, hop in enumerate(hops):
+        later = (me ^ (at + 1)) > me
+        hop[:rows, :width] = jnp.where(later, k_ref[...], q_ref[...])
+        hop[:rows, width:] = jnp.where(later, v_ref[...], g_ref[...])
+        hop[rows:, :width] = extra
+        hop[rows:, width:] = jnp.zeros((EXTRA, width), jnp.bfloat16)
+    for move in moves:
+        move.wait()
+
+
+def grad_kernel(scale, spot_ref, q_ref, k_ref, v_ref, g_ref, a_ref, n_ref, *refs):
+    out_ref = refs[-1]
+    got = refs[:-1]
+    rows, width = q_ref.shape
+    me = spot_ref[0]
+    exponent = scale * math.log2(math.e)
+    query, key, value, grad = q_ref[...], k_ref[...], v_ref[...], g_ref[...]
+    norm = (1.0 / scale) * jnp.sum(
+        jnp.where(diagonal(rows), n_ref[...], 0.0), axis=1, keepdims=True
+    )
+    delta = delta_of(grad, a_ref[...])
+    row_at = lax.broadcasted_iota(jnp.int32, (rows, rows), 0)
+    col_at = lax.broadcasted_iota(jnp.int32, (rows, rows), 1)
+    probs = jnp.where(col_at <= row_at, jnp.exp2(exponent * (dot_nt(query, key) - norm)), 0.0)
+    score_low = (probs * (dot_nt(grad, value) - delta)).astype(jnp.bfloat16)
+    query_sum = dot_nn(score_low, key)
+    key_sum = dot_tn(score_low, query)
+    value_sum = dot_tn(probs.astype(jnp.bfloat16), grad)
+
+    first = jnp.concatenate([ref[:rows, :width] for ref in got], axis=0)
+    second = jnp.concatenate([ref[:rows, width:] for ref in got], axis=0)
+    extra = jnp.concatenate([ref[rows:, :width] for ref in got], axis=1).astype(jnp.float32)
+    norms = (1.0 / scale) * jnp.sum(extra[:PIECES], axis=0, keepdims=True)
+    deltas = jnp.sum(extra[PIECES : 2 * PIECES], axis=0, keepdims=True)
+    lanes = lax.broadcasted_iota(jnp.int32, (rows, len(got) * rows), 1)
+    earlier = ((lanes // rows + 1) ^ me) < me
+    scores = dot_nt(jnp.concatenate([query, key], axis=0), first)
+    scores = jnp.where(earlier, scores[:rows] - norm, scores[rows:] - norms)
+    probs = jnp.exp2(exponent * scores)
+    prob_grad = dot_nt(jnp.concatenate([grad, value], axis=0), second)
+    prob_grad = jnp.where(earlier, prob_grad[:rows] - delta, prob_grad[rows:] - deltas)
+    score_grad = probs * prob_grad
+    sides = jnp.concatenate(
+        [jnp.where(earlier, score_grad, 0.0), jnp.where(earlier, 0.0, score_grad)], axis=0
+    ).astype(jnp.bfloat16)
+    both_sum = dot_nn(sides, first)
+    value_sum += dot_nn(jnp.where(earlier, 0.0, probs).astype(jnp.bfloat16), second)
+    out_ref[:, :width] = (scale * (query_sum + both_sum[:rows])).astype(jnp.bfloat16)
+    out_ref[:, width : 2 * width] = (scale * (key_sum + both_sum[rows:])).astype(jnp.bfloat16)
+    out_ref[:, 2 * width :] = value_sum.astype(jnp.bfloat16)
+
+
+def project_kernel(count, order, spot_ref, wq_ref, wk_ref, wv_ref, *refs):
+    grads = refs[:count]
+    shares = refs[count:-3]
+    out_ref, w_own, sems = refs[-3:]
+    width = wq_ref.shape[1]
+    part = out_ref.shape[1]
+    me, head = spot_ref[0], spot_ref[1]
+    start = pl.multiple_of(head * part, part)
+    loads = [
+        pltpu.make_async_copy(
+            ref.at[pl.ds(start, part), :], w_own.at[:, at * width : (at + 1) * width], sems.at[at]
+        )
+        for at, ref in enumerate((wq_ref, wk_ref, wv_ref))
+    ]
+    for load in loads:
+        load.start()
+    for load in loads:
+        load.wait()
+    piece = shares[0].shape[1]
+    for offset, share in zip(order, shares):
+        at = pl.multiple_of((me ^ offset) * piece, piece)
+        total = dot_nt(grads[0][...], w_own[pl.ds(at, piece), :])
+        for other in range(count - 1):
+            total += dot_nt(grads[other + 1][...], share[other])
+        out_ref[:, pl.ds(at, piece)] = total.astype(jnp.bfloat16)
+
+
+def swap(value, axis, offset):
+    size = lax.axis_size(axis)
+    return lax.ppermute(value, axis, [(at, at ^ offset) for at in range(size)])
+
+
+def near_body(own, weights, spot, scale):
+    rows, width = own[0].shape
+    depth = weights[0].shape[0]
+    ctx = lax.axis_size("ctx")
+    parts = lax.axis_size("head")
+    part = depth // parts
+    piece = part // ctx
+    vmem = pl.BlockSpec(memory_space=pltpu.VMEM)
+    smem = pl.BlockSpec(memory_space=pltpu.SMEM)
+    hbm = pl.BlockSpec(memory_space=pl.ANY)
+    params = pltpu.CompilerParams(vmem_limit_bytes=58 * MIB)
+    hop = jax.ShapeDtypeStruct((rows + EXTRA, 2 * width), jnp.bfloat16)
+    block = jax.ShapeDtypeStruct((piece, 3 * width), jnp.bfloat16)
+    sent = pl.pallas_call(
+        send_kernel,
+        out_shape=[hop] * (ctx - 1) + [block] * (parts - 1),
+        in_specs=[smem] + [hbm] * 5 + [vmem] + [hbm] * 3,
+        out_specs=[vmem] * (ctx + parts - 2),
+        scratch_shapes=[pltpu.VMEM((rows, width), jnp.bfloat16)] * 5
+        + [pltpu.SemaphoreType.DMA((5,)), pltpu.SemaphoreType.DMA((3 * (parts - 1),))],
+        compiler_params=params,
+    )(spot, *own, *weights)
+    got = [swap(sent[at], "ctx", at + 1) for at in range(ctx - 1)]
+    shares = {0: jnp.stack([swap(sent[ctx - 1 + at], "head", at + 1) for at in range(parts - 1)])}
+    for offset in range(2, ctx, 2):
+        shares[offset] = swap(shares[0], "ctx", offset)
+    for offset in range(0, ctx, 2):
+        shares[offset + 1] = swap(shares[offset], "ctx", 1)
+    grads = pl.pallas_call(
+        functools.partial(grad_kernel, scale),
+        out_shape=jax.ShapeDtypeStruct((rows, 3 * width), jnp.bfloat16),
+        in_specs=[smem] + [vmem] * (ctx + 5),
+        out_specs=vmem,
+        compiler_params=pltpu.CompilerParams(vmem_limit_bytes=32 * MIB),
+        cost_estimate=pl.CostEstimate(
+            flops=14 * rows * rows * ctx * width,
+            bytes_accessed=4 * rows * ctx * width,
+            transcendentals=rows * rows * ctx,
+        ),
+    )(spot, *own, *got)
+    all_grads = [grads] + [swap(grads, "head", at) for at in range(1, parts)]
+    return pl.pallas_call(
+        functools.partial(project_kernel, parts, tuple(shares)),
+        out_shape=jax.ShapeDtypeStruct((rows, part), jnp.bfloat16),
+        in_specs=[smem] + [hbm] * 3 + [vmem] * (parts + ctx),
+        out_specs=vmem,
+        scratch_shapes=[
+            pltpu.VMEM((part, 3 * width), jnp.bfloat16),
+            pltpu.SemaphoreType.DMA((3,)),
+        ],
+        compiler_params=params,
+        cost_estimate=pl.CostEstimate(
+            flops=6 * rows * width * depth, bytes_accessed=6 * depth * width, transcendentals=0
+        ),
+    )(spot, *weights, *all_grads, *shares.values())
+
+
+def far_body(own, weights, spot, scale):
+    rows, width = own[0].shape
+    depth = weights[0].shape[0]
     ctx = lax.axis_size("ctx")
     parts = lax.axis_size("head")
     vmem = pl.BlockSpec(memory_space=pltpu.VMEM)
     smem = pl.BlockSpec(memory_space=pltpu.SMEM)
-    hbm = pl.BlockSpec(memory_space=pltpu.HBM)
-    me = lax.axis_index("ctx").astype(jnp.int32).reshape(1)
-    own = (queries, key_rows, value_rows, out_grad, attn_out, log_norm.reshape(1, rows))
+    hbm = pl.BlockSpec(memory_space=pl.ANY)
     packed = pl.pallas_call(
         pack_kernel,
         out_shape=jax.ShapeDtypeStruct((ctx, rows + EXTRA, 2 * width), jnp.bfloat16),
         in_specs=[smem] + [vmem] * 6,
         out_specs=vmem,
         compiler_params=pltpu.CompilerParams(vmem_limit_bytes=32 * MIB),
-    )(me, *own)
+    )(spot, *own)
     got = lax.all_to_all(packed, "ctx", split_axis=0, concat_axis=0, tiled=True)
     total = ctx * rows
     group = math.gcd(ctx, 8)
@@ -209,9 +378,29 @@
             bytes_accessed=6 * depth * width + 10 * total * width,
             transcendentals=2 * rows * total,
         ),
-    )(me, got, *own, query_weight, key_weight, value_weight)
+    )(spot, got, *own, *weights)
     swapped = lax.all_to_all(parted, "head", split_axis=0, concat_axis=0, tiled=True)
     return jnp.sum(swapped.astype(jnp.float32), axis=0).astype(jnp.bfloat16)
+
+
+def body(
+    queries,
+    key_rows,
+    value_rows,
+    out_grad,
+    attn_out,
+    log_norm,
+    query_weight,
+    key_weight,
+    value_weight,
+):
+    rows, width = queries.shape
+    ctx, parts = lax.axis_size("ctx"), lax.axis_size("head")
+    spot = jnp.stack([lax.axis_index("ctx"), lax.axis_index("head")]).astype(jnp.int32)
+    own = (queries, key_rows, value_rows, out_grad, attn_out, log_norm.reshape(1, rows))
+    weights = (query_weight, key_weight, value_weight)
+    near = ctx <= 8 and parts <= 4 and ctx & (ctx - 1) == 0 and parts & (parts - 1) == 0
+    return (near_body if near else far_body)(own, weights, spot, width ** (-0.5))
 
 
 def solution(mesh):

time: 57.4 us -> 73.1 us (1.27)
  blocking collectives: 45.9 us -> 0 us
  waiting for transfers between devices: 0 us -> 43.2 us
  starting transfers between devices: 0 us -> 17.8 us
  Pallas kernels: 2.83 us -> 9.28 us
  local copies, waits for them, and re-layouts: 7.02 us -> 1.64 us
    all_to_all x2 -> x0, blocking collectives: 45.9 us -> none  [the longest x1 30.3 us: body(): lax.all_to_all(parted, 'head', split_axis=0, concat_axis=0, tiled=True)]
    ppermute x0 -> x20, waiting for transfers between devices: none -> 43.2 us  [swap(): return lax.ppermute(value, axis, [(at, at ^ offset) for at in range(size)])]
    ppermute x0 -> x20, starting transfers between devices: none -> 17.8 us  [swap(): return lax.ppermute(value, axis, [(at, at ^ offset) for at in range(size)])]
    pallas_call x2 -> x3, Pallas kernels: 2.83 us -> 9.28 us  [the longest x1 5.02 us: near_body(): pl.pallas_call(functools.partial(project_kernel, parts, tuple(shares)), o...]
    unnamed x30 -> x48, local copies, waits for them, and re-layouts: 7.02 us -> 1.64 us
    reduce_sum x1 -> x0, other arithmetic: 0.93 us -> none  [body(): return jnp.sum(swapped.astype(jnp.float32), axis=0).astype(jnp.bfloat16)]
  transfers between devices with their start and end apart: 0 -> 20, of which waited for: 0 -> 9; matrix products, arithmetic and copies ran while one was open for 0% -> 0% of each run, Pallas kernels for 0% -> 2%
where the time goes in v3:
time: 73.1 us; the launch traced here: 72.8 us
  waiting for transfers between devices  43.2 us (59%)
  starting transfers between devices  17.8 us (24%)
  Pallas kernels  9.28 us (13%)
  local copies, waits for them, and re-layouts  1.64 us (2%)
    ppermute x20, waiting for transfers between devices, swap(): return lax.ppermute(value, axis, [(at, at ^ offset) for at in range(size)])  43.2 us
    ppermute x20, starting transfers between devices, swap(): return lax.ppermute(value, axis, [(at, at ^ offset) for at in range(size)])  17.8 us
    pallas_call x1, Pallas kernels, near_body(): pl.pallas_call(functools.partial(project_kernel, parts, tuple(shares)), o...  5.02 us
    pallas_call x1, Pallas kernels, near_body(): pl.pallas_call(send_kernel, out_shape=[hop] * (ctx - 1) + [block] * (part...  2.96 us
    unnamed x48, local copies, waits for them, and re-layouts  1.64 us
  transfers between devices with their start and end apart: 20, of which 9 were waited for; matrix products, arithmetic and copies ran while one was open for 0% of the time, Pallas kernels for 2%

profile of v3, /device:TPU:0, one launch (start us, length us, event | category | flops | bytes accessed | tf_op | source)
XLA Modules:
  0.0 72.8 jit_solution(15167548276132188488)
XLA Ops:
  0.0 0.7 pad_add_fusion.spot_ref
  0.7 3.0 %shard_map.91 = (bf16[144,256]{1,0:T(8,128)(2,1)}, bf16[144,256]{1,0:T(8,128)(2,1)}, bf16[144,256]{1,0:T(8,128)(2,1)}, bf16[144,256]{1,0:T(8,128)(2,1)}, bf16[14...) custom-call(s32[2]{0:T(128)} %pad_add_fusion.spot_ref, ...), custom_call_target="tpu_custom_call" | custom-call | tf_op jit(solution)/shard_map/pallas_call | solution.py:303
  3.6 3.1 %collective-permute-start.10 = (bf16[128,384]{1,0:T(8,128)(2,1)}, bf16[128,384]{1,0:T(8,128)(2,1)S(1)}, u32[]{:S(2)}, u32[]{:S(2)}) collective-permute-start(bf16[128,384]{1,0:T(8,128)(2,1)} %get-tuple-element.22), channel_id=1, source_target_pairs={{0,1},{1,0},{2,3},{3,2},{4,5},{5,4},{6,7},{7,6},{8,9},{9,8},{10,11... | collective-permute-start | bytes 294920 | tf_op jit(solution)/shard_map/ppermute | solution.py:287
  6.7 2.6 %collective-permute-start.11 = (bf16[128,384]{1,0:T(8,128)(2,1)}, bf16[128,384]{1,0:T(8,128)(2,1)S(1)}, u32[]{:S(2)}, u32[]{:S(2)}) collective-permute-start(bf16[128,384]{1,0:T(8,128)(2,1)} %get-tuple-element.23), channel_id=1, source_target_pairs={{0,2},{1,3},{2,0},{3,1},{4,6},{5,7},{6,4},{7,5},{8,10},{9,11},{10,... | collective-permute-start | bytes 294920 | tf_op jit(solution)/shard_map/ppermute | solution.py:287
  9.3 0.0 collective-permute-start.12
  9.3 0.0 collective-permute-start
  9.3 0.4 collective-permute-done.10
  9.7 7.6 %collective-permute-done.11 = bf16[128,384]{1,0:T(8,128)(2,1)S(1)} collective-permute-done((bf16[128,384]{1,0:T(8,128)(2,1)}, bf16[128,384]{1,0:T(8,128)(2,1)S(1)}, u32[]{:S(2)}, u32[]{:S(2)}) %collective-permute-start.11) | collective-permute-done | bytes 98336 | tf_op jit(solution)/shard_map/ppermute | solution.py:287
  17.4 0.0 collective-permute-done.12
  17.4 0.0 copy-start.20
  17.4 0.0 copy-start.19
  17.4 0.0 copy-start.1
  17.4 0.0 copy-start.2
  17.4 0.0 copy-start.3
  17.4 0.0 copy-start.4
  17.4 0.0 copy-start.5
  17.5 0.0 copy-start.8
  17.5 2.5 %collective-permute-start.15 = (bf16[3,128,384]{2,1,0:T(8,128)(2,1)S(1)}, bf16[3,128,384]{2,1,0:T(8,128)(2,1)S(1)}, u32[]{:S(2)}, u32[]{:S(2)}) collective-permute-start(bf16[3,128,384]{2,1,0:T(8,128)(2,1)S(1)} %pad_maximum_fusion.refs_4_), channel_id=1, source_target_pairs={{0,24},{4,28},{8,16},{12,20},{16,8},{20,12},{24,0},{28,4},{1,25},{... | collective-permute-start | bytes 884744 | tf_op jit(solution)/shard_map/ppermute | solution.py:287
  20.0 0.5 collective-permute-start.14
  20.5 0.5 collective-permute-start.13
  21.1 1.5 %collective-permute-start.1 = (bf16[144,256]{1,0:T(8,128)(2,1)}, bf16[144,256]{1,0:T(8,128)(2,1)S(1)}, u32[]{:S(2)}, u32[]{:S(2)}) collective-permute-start(bf16[144,256]{1,0:T(8,128)(2,1)} %get-tuple-element.16), channel_id=1, source_target_pairs={{0,8},{4,12},{8,0},{12,4},{16,24},{20,28},{24,16},{28,20},{1,9},{5... | collective-permute-start | bytes 221192 | tf_op jit(solution)/shard_map/ppermute | solution.py:287
  22.6 0.0 collective-permute-done.refs_0_
  22.6 0.0 copy-done.23
  22.6 0.0 collective-permute-start.2
  22.6 11.6 %collective-permute-done.1.refs_1_ = bf16[144,256]{1,0:T(8,128)(2,1)S(1)} collective-permute-done((bf16[144,256]{1,0:T(8,128)(2,1)}, bf16[144,256]{1,0:T(8,128)(2,1)S(1)}, u32[]{:S(2)}, u32[]{:S(2)}) %collective-permute-start.1) | collective-permute-done | bytes 73760 | tf_op jit(solution)/shard_map/ppermute | solution.py:287
  34.1 0.0 copy-done.22
  34.1 0.5 collective-permute-start.3
  34.6 0.0 collective-permute-done.2.refs_2_
  34.6 0.0 copy-done.21
  34.6 0.2 collective-permute-start.4
  34.9 4.4 %collective-permute-done.3.refs_3_ = bf16[144,256]{1,0:T(8,128)(2,1)S(1)} collective-permute-done((bf16[144,256]{1,0:T(8,128)(2,1)S(1)}, bf16[144,256]{1,0:T(8,128)(2,1)S(1)}, u32[]{:S(2)}, u32[]{:S(2)}) %collective-permute-start.3) | collective-permute-done | bytes 73760 | tf_op jit(solution)/shard_map/ppermute | solution.py:287
  39.2 0.0 copy-done.20
  39.2 0.7 collective-permute-start.5
  39.9 0.0 collective-permute-done.4.refs_4_
  39.9 0.0 copy-done.19
  39.9 1.1 %collective-permute-start.6 = (bf16[144,256]{1,0:T(8,128)(2,1)S(1)}, bf16[144,256]{1,0:T(8,128)(2,1)S(1)}, u32[]{:S(2)}, u32[]{:S(2)}) collective-permute-start(bf16[144,256]{1,0:T(8,128)(2,1)S(1)} %copy-done.19), channel_id=1, source_target_pairs={{0,28},{4,24},{8,20},{12,16},{16,12},{20,8},{24,4},{28,0},{1,29},{... | collective-permute-start | bytes 221192 | tf_op jit(solution)/shard_map/ppermute | solution.py:287
  41.1 4.0 %collective-permute-done.5.refs_5_ = bf16[144,256]{1,0:T(8,128)(2,1)S(1)} collective-permute-done((bf16[144,256]{1,0:T(8,128)(2,1)S(1)}, bf16[144,256]{1,0:T(8,128)(2,1)S(1)}, u32[]{:S(2)}, u32[]{:S(2)}) %collective-permute-start.5) | collective-permute-done | bytes 73760 | tf_op jit(solution)/shard_map/ppermute | solution.py:287
  45.1 0.3 collective-permute-done.6.refs_6_
  45.4 0.0 copy-done.2
  45.4 1.3 %shard_map.92.refs_0_ = bf16[128,384]{1,0:T(8,128)(2,1)S(1)} custom-call(s32[2]{0:T(128)S(1)} %copy-done.6, bf16[128,128]{1,0:T(8,128)(2,1)S(1)} %copy-done.1, bf16[128,128]{1,0:T(8,128)(2,1)S(1)} %copy-done.2, bf16[128,128]{1,0:T(8,128)(2,1)S(1)} %copy-done.3, bf16[128,128]{1,0:T(8,128)(2,1)S(1)} %copy-done.4, bf16[128,128]{1,0:T(8,128)(2,1)S(1)} %copy-done.5, ...), custom_call_target="tpu_custom_call" | custom-call | flops 234881024 | bytes 524288 | tf_op jit(solution)/shard_map/pallas_call | solution.py:318
  46.8 0.9 %collective-permute-start.9 = (bf16[128,384]{1,0:T(8,128)(2,1)S(1)}, bf16[128,384]{1,0:T(8,128)(2,1)S(1)}, u32[]{:S(2)}, u32[]{:S(2)}) collective-permute-start(bf16[128,384]{1,0:T(8,128)(2,1)S(1)} %shard_map.92.refs_0_), channel_id=1, source_target_pairs={{0,3},{1,2},{2,1},{3,0},{4,7},{5,6},{6,5},{7,4},{8,11},{9,10},{10,... | collective-permute-start | bytes 294920 | tf_op jit(solution)/shard_map/ppermute | solution.py:287
  47.7 0.2 collective-permute-start.16
  47.9 0.0 collective-permute-done.15.refs_7_
  47.9 0.3 collective-permute-start.19
  48.2 0.0 collective-permute-done.14.refs_6_
  48.2 0.2 collective-permute-start.18
  48.4 0.0 collective-permute-done.13.refs_5_
  48.4 0.3 collective-permute-start.17
  48.7 5.2 %collective-permute-done.9.refs_3_ = bf16[128,384]{1,0:T(8,128)(2,1)S(1)} collective-permute-done((bf16[128,384]{1,0:T(8,128)(2,1)S(1)}, bf16[128,384]{1,0:T(8,128)(2,1)S(1)}, u32[]{:S(2)}, u32[]{:S(2)}) %collective-permute-start.9) | collective-permute-done | bytes 98336 | tf_op jit(solution)/shard_map/ppermute | solution.py:287
  53.9 2.0 %collective-permute-start.8 = (bf16[128,384]{1,0:T(8,128)(2,1)S(1)}, bf16[128,384]{1,0:T(8,128)(2,1)S(1)}, u32[]{:S(2)}, u32[]{:S(2)}) collective-permute-start(bf16[128,384]{1,0:T(8,128)(2,1)S(1)} %shard_map.92.refs_0_), channel_id=1, source_target_pairs={{0,2},{1,3},{2,0},{3,1},{4,6},{5,7},{6,4},{7,5},{8,10},{9,11},{10,... | collective-permute-start | bytes 294920 | tf_op jit(solution)/shard_map/ppermute | solution.py:287
  55.9 5.7 %collective-permute-done.8.refs_2_ = bf16[128,384]{1,0:T(8,128)(2,1)S(1)} collective-permute-done((bf16[128,384]{1,0:T(8,128)(2,1)S(1)}, bf16[128,384]{1,0:T(8,128)(2,1)S(1)}, u32[]{:S(2)}, u32[]{:S(2)}) %collective-permute-start.8) | collective-permute-done | bytes 98336 | tf_op jit(solution)/shard_map/ppermute | solution.py:287
  61.5 0.6 collective-permute-start.7
  62.1 4.1 %collective-permute-done.7.refs_1_ = bf16[128,384]{1,0:T(8,128)(2,1)S(1)} collective-permute-done((bf16[128,384]{1,0:T(8,128)(2,1)S(1)}, bf16[128,384]{1,0:T(8,128)(2,1)S(1)}, u32[]{:S(2)}, u32[]{:S(2)}) %collective-permute-start.7) | collective-permute-done | bytes 98336 | tf_op jit(solution)/shard_map/ppermute | solution.py:287
  66.2 0.0 collective-permute-done.16.refs_8_
  66.2 0.0 collective-permute-done.19.refs_11_
  66.2 0.0 copy-start.13
  66.2 0.0 collective-permute-done.18.refs_10_
  66.2 0.0 collective-permute-done.17.refs_9_
  66.3 0.5 copy-done.18
  66.8 0.1 copy-done.12
  66.9 0.1 copy-done.13
  67.0 0.1 copy-done.14
  67.1 0.7 copy-done.15
  67.8 5.0 %shard_map.93 = bf16[128,1024]{1,0:T(8,128)(2,1)} custom-call(s32[2]{0:T(128)} %pad_add_fusion.spot_ref, bf16[4096,128]{1,0:T(8,128)(2,1)} %wq_ref.3, bf16[4096,128]{1,0:T(8,128)(2,1)} %wk_ref.3, bf16[4096,128]{1,0:T(8,128)(2,1)} %wv_ref.3, bf16[128,384]{1,0:T(8,128)(2,1)} %copy-done, bf16[128,384]{1,0:T(8,128)(2,1)} %copy-done.18, ...), custom_call_target="tpu_custom_call" | custom-call | flops 402653184 | bytes 3145728 | tf_op jit(solution)/shard_map/pallas_call | solution.py:331
  (29 shorter events, 0.1 us)
Async XLA Ops:
  3.6 6.1 %collective-permute-start.10 = (bf16[128,384]{1,0:T(8,128)(2,1)}, bf16[128,384]{1,0:T(8,128)(2,1)S(1)}, u32[]{:S(2)}, u32[]{:S(2)}) collective-permute-start(bf16[128,384]{1,0:T(8,128)(2,1)} %get-tuple-element.22), channel_id=1, source_target_pairs={{0,1},{1,0},{2,3},{3,2},{4,5},{5,4},{6,7},{7,6},{8,9},{9,8},{10,11... | collective-permute-start | bytes 294920 | tf_op jit(solution)/shard_map/ppermute | solution.py:287
  6.7 10.6 %collective-permute-start.11 = (bf16[128,384]{1,0:T(8,128)(2,1)}, bf16[128,384]{1,0:T(8,128)(2,1)S(1)}, u32[]{:S(2)}, u32[]{:S(2)}) collective-permute-start(bf16[128,384]{1,0:T(8,128)(2,1)} %get-tuple-element.23), channel_id=1, source_target_pairs={{0,2},{1,3},{2,0},{3,1},{4,6},{5,7},{6,4},{7,5},{8,10},{9,11},{10,... | collective-permute-start | bytes 294920 | tf_op jit(solution)/shard_map/ppermute | solution.py:287
  9.3 8.0 %collective-permute-start.12 = (bf16[128,384]{1,0:T(8,128)(2,1)}, bf16[128,384]{1,0:T(8,128)(2,1)S(1)}, u32[]{:S(2)}, u32[]{:S(2)}) collective-permute-start(bf16[128,384]{1,0:T(8,128)(2,1)} %get-tuple-element.24), channel_id=1, source_target_pairs={{0,3},{1,2},{2,1},{3,0},{4,7},{5,6},{6,5},{7,4},{8,11},{9,10},{10,... | collective-permute-start | bytes 294920 | tf_op jit(solution)/shard_map/ppermute | solution.py:287
  9.3 13.2 %collective-permute-start = (bf16[144,256]{1,0:T(8,128)(2,1)}, bf16[144,256]{1,0:T(8,128)(2,1)S(1)}, u32[]{:S(2)}, u32[]{:S(2)}) collective-permute-start(bf16[144,256]{1,0:T(8,128)(2,1)} %get-tuple-element.15), channel_id=1, source_target_pairs={{0,4},{4,0},{8,12},{12,8},{16,20},{20,16},{24,28},{28,24},{1,5},{5... | collective-permute-start | bytes 221192 | tf_op jit(solution)/shard_map/ppermute | solution.py:287
  17.4 5.2 %copy-start.23 = (bf16[144,256]{1,0:T(8,128)(2,1)S(1)}, bf16[144,256]{1,0:T(8,128)(2,1)}, u32[]{:S(2)}) copy-start(bf16[144,256]{1,0:T(8,128)(2,1)} %get-tuple-element.17) | copy-start | bytes 221188
  17.4 16.8 %copy-start.22 = (bf16[144,256]{1,0:T(8,128)(2,1)S(1)}, bf16[144,256]{1,0:T(8,128)(2,1)}, u32[]{:S(2)}) copy-start(bf16[144,256]{1,0:T(8,128)(2,1)} %get-tuple-element.18) | copy-start | bytes 221188
  17.4 17.3 %copy-start.21 = (bf16[144,256]{1,0:T(8,128)(2,1)S(1)}, bf16[144,256]{1,0:T(8,128)(2,1)}, u32[]{:S(2)}) copy-start(bf16[144,256]{1,0:T(8,128)(2,1)} %get-tuple-element.19) | copy-start | bytes 221188
  17.4 21.9 %copy-start.20 = (bf16[144,256]{1,0:T(8,128)(2,1)S(1)}, bf16[144,256]{1,0:T(8,128)(2,1)}, u32[]{:S(2)}) copy-start(bf16[144,256]{1,0:T(8,128)(2,1)} %get-tuple-element.20) | copy-start | bytes 221188
  17.4 22.6 %copy-start.19 = (bf16[144,256]{1,0:T(8,128)(2,1)S(1)}, bf16[144,256]{1,0:T(8,128)(2,1)}, u32[]{:S(2)}) copy-start(bf16[144,256]{1,0:T(8,128)(2,1)} %get-tuple-element.21) | copy-start | bytes 221188
  17.4 28.0 %copy-start.1 = (bf16[128,128]{1,0:T(8,128)(2,1)S(1)}, bf16[128,128]{1,0:T(8,128)(2,1)}, u32[]{:S(2)}) copy-start(bf16[128,128]{1,0:T(8,128)(2,1)} %q_ref.1) | copy-start | bytes 98308
  17.4 28.0 %copy-start.2 = (bf16[128,128]{1,0:T(8,128)(2,1)S(1)}, bf16[128,128]{1,0:T(8,128)(2,1)}, u32[]{:S(2)}) copy-start(bf16[128,128]{1,0:T(8,128)(2,1)} %k_ref.1) | copy-start | bytes 98308
  17.4 28.0 %copy-start.3 = (bf16[128,128]{1,0:T(8,128)(2,1)S(1)}, bf16[128,128]{1,0:T(8,128)(2,1)}, u32[]{:S(2)}) copy-start(bf16[128,128]{1,0:T(8,128)(2,1)} %v_ref.1) | copy-start | bytes 98308
  17.4 28.0 %copy-start.4 = (bf16[128,128]{1,0:T(8,128)(2,1)S(1)}, bf16[128,128]{1,0:T(8,128)(2,1)}, u32[]{:S(2)}) copy-start(bf16[128,128]{1,0:T(8,128)(2,1)} %g_ref.1) | copy-start | bytes 98308
  17.4 28.0 %copy-start.5 = (bf16[128,128]{1,0:T(8,128)(2,1)S(1)}, bf16[128,128]{1,0:T(8,128)(2,1)}, u32[]{:S(2)}) copy-start(bf16[128,128]{1,0:T(8,128)(2,1)} %a_ref.1) | copy-start | bytes 98308
  17.5 30.2 %copy-start.8 = (bf16[3,128,384]{2,1,0:T(8,128)(2,1)}, bf16[3,128,384]{2,1,0:T(8,128)(2,1)S(1)}, u32[]{:S(2)}) copy-start(bf16[3,128,384]{2,1,0:T(8,128)(2,1)S(1)} %pad_maximum_fusion.refs_4_) | copy-start | bytes 884740
  17.5 30.4 %collective-permute-start.15 = (bf16[3,128,384]{2,1,0:T(8,128)(2,1)S(1)}, bf16[3,128,384]{2,1,0:T(8,128)(2,1)S(1)}, u32[]{:S(2)}, u32[]{:S(2)}) collective-permute-start(bf16[3,128,384]{2,1,0:T(8,128)(2,1)S(1)} %pad_maximum_fusion.refs_4_), channel_id=1, source_target_pairs={{0,24},{4,28},{8,16},{12,20},{16,8},{20,12},{24,0},{28,4},{1,25},{... | collective-permute-start | bytes 884744 | tf_op jit(solution)/shard_map/ppermute | solution.py:287
  20.0 28.2 %collective-permute-start.14 = (bf16[3,128,384]{2,1,0:T(8,128)(2,1)S(1)}, bf16[3,128,384]{2,1,0:T(8,128)(2,1)S(1)}, u32[]{:S(2)}, u32[]{:S(2)}) collective-permute-start(bf16[3,128,384]{2,1,0:T(8,128)(2,1)S(1)} %pad_maximum_fusion.refs_4_), channel_id=1, source_target_pairs={{0,16},{4,20},{8,24},{12,28},{16,0},{20,4},{24,8},{28,12},{1,17},{... | collective-permute-start | bytes 884744 | tf_op jit(solution)/shard_map/ppermute | solution.py:287
  20.5 27.9 %collective-permute-start.13 = (bf16[3,128,384]{2,1,0:T(8,128)(2,1)S(1)}, bf16[3,128,384]{2,1,0:T(8,128)(2,1)S(1)}, u32[]{:S(2)}, u32[]{:S(2)}) collective-permute-start(bf16[3,128,384]{2,1,0:T(8,128)(2,1)S(1)} %pad_maximum_fusion.refs_4_), channel_id=1, source_target_pairs={{0,8},{4,12},{8,0},{12,4},{16,24},{20,28},{24,16},{28,20},{1,9},{5... | collective-permute-start | bytes 884744 | tf_op jit(solution)/shard_map/ppermute | solution.py:287
  21.1 13.1 %collective-permute-start.1 = (bf16[144,256]{1,0:T(8,128)(2,1)}, bf16[144,256]{1,0:T(8,128)(2,1)S(1)}, u32[]{:S(2)}, u32[]{:S(2)}) collective-permute-start(bf16[144,256]{1,0:T(8,128)(2,1)} %get-tuple-element.16), channel_id=1, source_target_pairs={{0,8},{4,12},{8,0},{12,4},{16,24},{20,28},{24,16},{28,20},{1,9},{5... | collective-permute-start | bytes 221192 | tf_op jit(solution)/shard_map/ppermute | solution.py:287
  22.6 12.1 %collective-permute-start.2 = (bf16[144,256]{1,0:T(8,128)(2,1)S(1)}, bf16[144,256]{1,0:T(8,128)(2,1)S(1)}, u32[]{:S(2)}, u32[]{:S(2)}) collective-permute-start(bf16[144,256]{1,0:T(8,128)(2,1)S(1)} %copy-done.23), channel_id=1, source_target_pairs={{0,12},{4,8},{8,4},{12,0},{16,28},{20,24},{24,20},{28,16},{1,13},{... | collective-permute-start | bytes 221192 | tf_op jit(solution)/shard_map/ppermute | solution.py:287
  34.1 5.1 %collective-permute-start.3 = (bf16[144,256]{1,0:T(8,128)(2,1)S(1)}, bf16[144,256]{1,0:T(8,128)(2,1)S(1)}, u32[]{:S(2)}, u32[]{:S(2)}) collective-permute-start(bf16[144,256]{1,0:T(8,128)(2,1)S(1)} %copy-done.22), channel_id=1, source_target_pairs={{0,16},{4,20},{8,24},{12,28},{16,0},{20,4},{24,8},{28,12},{1,17},{... | collective-permute-start | bytes 221192 | tf_op jit(solution)/shard_map/ppermute | solution.py:287
  34.6 5.3 %collective-permute-start.4 = (bf16[144,256]{1,0:T(8,128)(2,1)S(1)}, bf16[144,256]{1,0:T(8,128)(2,1)S(1)}, u32[]{:S(2)}, u32[]{:S(2)}) collective-permute-start(bf16[144,256]{1,0:T(8,128)(2,1)S(1)} %copy-done.21), channel_id=1, source_target_pairs={{0,20},{4,16},{8,28},{12,24},{16,4},{20,0},{24,12},{28,8},{1,21},{... | collective-permute-start | bytes 221192 | tf_op jit(solution)/shard_map/ppermute | solution.py:287
  39.2 6.2 %copy-start.6 = (s32[2]{0:T(128)S(1)}, s32[2]{0:T(128)}, u32[]{:S(2)}) copy-start(s32[2]{0:T(128)} %pad_add_fusion.spot_ref) | copy-start | bytes 28
  39.2 6.2 %copy-start.7 = (f32[128,1]{0,1:T(1,128)S(1)}, f32[128,1]{0,1:T(1,128)}, u32[]{:S(2)}) copy-start(f32[128,1]{0,1:T(1,128)} %param.14) | copy-start | bytes 1540
  39.2 5.9 %collective-permute-start.5 = (bf16[144,256]{1,0:T(8,128)(2,1)S(1)}, bf16[144,256]{1,0:T(8,128)(2,1)S(1)}, u32[]{:S(2)}, u32[]{:S(2)}) collective-permute-start(bf16[144,256]{1,0:T(8,128)(2,1)S(1)} %copy-done.20), channel_id=1, source_target_pairs={{0,24},{4,28},{8,16},{12,20},{16,8},{20,12},{24,0},{28,4},{1,25},{... | collective-permute-start | bytes 221192 | tf_op jit(solution)/shard_map/ppermute | solution.py:287
  39.9 5.5 %collective-permute-start.6 = (bf16[144,256]{1,0:T(8,128)(2,1)S(1)}, bf16[144,256]{1,0:T(8,128)(2,1)S(1)}, u32[]{:S(2)}, u32[]{:S(2)}) collective-permute-start(bf16[144,256]{1,0:T(8,128)(2,1)S(1)} %copy-done.19), channel_id=1, source_target_pairs={{0,28},{4,24},{8,20},{12,16},{16,12},{20,8},{24,4},{28,0},{1,29},{... | collective-permute-start | bytes 221192 | tf_op jit(solution)/shard_map/ppermute | solution.py:287
  46.8 19.5 %copy-start = (bf16[128,384]{1,0:T(8,128)(2,1)}, bf16[128,384]{1,0:T(8,128)(2,1)S(1)}, u32[]{:S(2)}) copy-start(bf16[128,384]{1,0:T(8,128)(2,1)S(1)} %shard_map.92.refs_0_) | copy-start | bytes 294916
  46.8 7.1 %collective-permute-start.9 = (bf16[128,384]{1,0:T(8,128)(2,1)S(1)}, bf16[128,384]{1,0:T(8,128)(2,1)S(1)}, u32[]{:S(2)}, u32[]{:S(2)}) collective-permute-start(bf16[128,384]{1,0:T(8,128)(2,1)S(1)} %shard_map.92.refs_0_), channel_id=1, source_target_pairs={{0,3},{1,2},{2,1},{3,0},{4,7},{5,6},{6,5},{7,4},{8,11},{9,10},{10,... | collective-permute-start | bytes 294920 | tf_op jit(solution)/shard_map/ppermute | solution.py:287
  47.7 18.5 %collective-permute-start.16 = (bf16[3,128,384]{2,1,0:T(8,128)(2,1)S(1)}, bf16[3,128,384]{2,1,0:T(8,128)(2,1)S(1)}, u32[]{:S(2)}, u32[]{:S(2)}) collective-permute-start(bf16[3,128,384]{2,1,0:T(8,128)(2,1)S(1)} %pad_maximum_fusion.refs_4_), channel_id=1, source_target_pairs={{0,4},{4,0},{8,12},{12,8},{16,20},{20,16},{24,28},{28,24},{1,5},{5... | collective-permute-start | bytes 884744 | tf_op jit(solution)/shard_map/ppermute | solution.py:287
  47.9 18.3 %copy-start.9 = (bf16[3,128,384]{2,1,0:T(8,128)(2,1)}, bf16[3,128,384]{2,1,0:T(8,128)(2,1)S(1)}, u32[]{:S(2)}) copy-start(bf16[3,128,384]{2,1,0:T(8,128)(2,1)S(1)} %collective-permute-done.15.refs_7_) | copy-start | bytes 884740
  47.9 18.3 %collective-permute-start.19 = (bf16[3,128,384]{2,1,0:T(8,128)(2,1)S(1)}, bf16[3,128,384]{2,1,0:T(8,128)(2,1)S(1)}, u32[]{:S(2)}, u32[]{:S(2)}) collective-permute-start(bf16[3,128,384]{2,1,0:T(8,128)(2,1)S(1)} %collective-permute-done.15.refs_7_), channel_id=1, source_target_pairs={{0,4},{4,0},{8,12},{12,8},{16,20},{20,16},{24,28},{28,24},{1,5},{5... | collective-permute-start | bytes 884744 | tf_op jit(solution)/shard_map/ppermute | solution.py:287
  48.2 18.0 %copy-start.10 = (bf16[3,128,384]{2,1,0:T(8,128)(2,1)}, bf16[3,128,384]{2,1,0:T(8,128)(2,1)S(1)}, u32[]{:S(2)}) copy-start(bf16[3,128,384]{2,1,0:T(8,128)(2,1)S(1)} %collective-permute-done.14.refs_6_) | copy-start | bytes 884740
  48.2 18.0 %collective-permute-start.18 = (bf16[3,128,384]{2,1,0:T(8,128)(2,1)S(1)}, bf16[3,128,384]{2,1,0:T(8,128)(2,1)S(1)}, u32[]{:S(2)}, u32[]{:S(2)}) collective-permute-start(bf16[3,128,384]{2,1,0:T(8,128)(2,1)S(1)} %collective-permute-done.14.refs_6_), channel_id=1, source_target_pairs={{0,4},{4,0},{8,12},{12,8},{16,20},{20,16},{24,28},{28,24},{1,5},{5... | collective-permute-start | bytes 884744 | tf_op jit(solution)/shard_map/ppermute | solution.py:287
  48.4 17.8 %copy-start.11 = (bf16[3,128,384]{2,1,0:T(8,128)(2,1)}, bf16[3,128,384]{2,1,0:T(8,128)(2,1)S(1)}, u32[]{:S(2)}) copy-start(bf16[3,128,384]{2,1,0:T(8,128)(2,1)S(1)} %collective-permute-done.13.refs_5_) | copy-start | bytes 884740
  48.4 17.8 %collective-permute-start.17 = (bf16[3,128,384]{2,1,0:T(8,128)(2,1)S(1)}, bf16[3,128,384]{2,1,0:T(8,128)(2,1)S(1)}, u32[]{:S(2)}, u32[]{:S(2)}) collective-permute-start(bf16[3,128,384]{2,1,0:T(8,128)(2,1)S(1)} %collective-permute-done.13.refs_5_), channel_id=1, source_target_pairs={{0,4},{4,0},{8,12},{12,8},{16,20},{20,16},{24,28},{28,24},{1,5},{5... | collective-permute-start | bytes 884744 | tf_op jit(solution)/shard_map/ppermute | solution.py:287
  53.9 12.3 %copy-start.16 = (bf16[128,384]{1,0:T(8,128)(2,1)}, bf16[128,384]{1,0:T(8,128)(2,1)S(1)}, u32[]{:S(2)}) copy-start(bf16[128,384]{1,0:T(8,128)(2,1)S(1)} %collective-permute-done.9.refs_3_) | copy-start | bytes 294916
  53.9 7.6 %collective-permute-start.8 = (bf16[128,384]{1,0:T(8,128)(2,1)S(1)}, bf16[128,384]{1,0:T(8,128)(2,1)S(1)}, u32[]{:S(2)}, u32[]{:S(2)}) collective-permute-start(bf16[128,384]{1,0:T(8,128)(2,1)S(1)} %shard_map.92.refs_0_), channel_id=1, source_target_pairs={{0,2},{1,3},{2,0},{3,1},{4,6},{5,7},{6,4},{7,5},{8,10},{9,11},{10,... | collective-permute-start | bytes 294920 | tf_op jit(solution)/shard_map/ppermute | solution.py:287
  61.5 4.7 %copy-start.17 = (bf16[128,384]{1,0:T(8,128)(2,1)}, bf16[128,384]{1,0:T(8,128)(2,1)S(1)}, u32[]{:S(2)}) copy-start(bf16[128,384]{1,0:T(8,128)(2,1)S(1)} %collective-permute-done.8.refs_2_) | copy-start | bytes 294916
  61.5 4.6 %collective-permute-start.7 = (bf16[128,384]{1,0:T(8,128)(2,1)S(1)}, bf16[128,384]{1,0:T(8,128)(2,1)S(1)}, u32[]{:S(2)}, u32[]{:S(2)}) collective-permute-start(bf16[128,384]{1,0:T(8,128)(2,1)S(1)} %shard_map.92.refs_0_), channel_id=1, source_target_pairs={{0,1},{1,0},{2,3},{3,2},{4,5},{5,4},{6,7},{7,6},{8,9},{9,8},{10,11... | collective-permute-start | bytes 294920 | tf_op jit(solution)/shard_map/ppermute | solution.py:287
  66.2 0.6 copy-start.18
  66.2 0.7 %copy-start.12 = (bf16[3,128,384]{2,1,0:T(8,128)(2,1)}, bf16[3,128,384]{2,1,0:T(8,128)(2,1)S(1)}, u32[]{:S(2)}) copy-start(bf16[3,128,384]{2,1,0:T(8,128)(2,1)S(1)} %collective-permute-done.16.refs_8_) | copy-start | bytes 884740
  66.2 0.9 %copy-start.13 = (bf16[3,128,384]{2,1,0:T(8,128)(2,1)}, bf16[3,128,384]{2,1,0:T(8,128)(2,1)S(1)}, u32[]{:S(2)}) copy-start(bf16[3,128,384]{2,1,0:T(8,128)(2,1)S(1)} %collective-permute-done.19.refs_11_) | copy-start | bytes 884740
  66.2 0.9 %copy-start.14 = (bf16[3,128,384]{2,1,0:T(8,128)(2,1)}, bf16[3,128,384]{2,1,0:T(8,128)(2,1)S(1)}, u32[]{:S(2)}) copy-start(bf16[3,128,384]{2,1,0:T(8,128)(2,1)S(1)} %collective-permute-done.18.refs_10_) | copy-start | bytes 884740
  67.1 0.7 copy-start.15

commit v4 on v3

--- a/solution.py
+++ b/solution.py
@@ -162,38 +162,19 @@
             out_ref[h, :, at : at + cols] = dot_nt(grads[...], weight).astype(jnp.bfloat16)
 
 
-def send_kernel(
-    spot_ref, q_in, k_in, v_in, g_in, a_in, n_ref, wq_ref, wk_ref, wv_ref, *refs
-):
-    q_ref, k_ref, v_ref, g_ref, a_ref, in_sems, w_sems = refs[-7:]
-    outs = refs[:-7]
-    me, head = spot_ref[0], spot_ref[1]
+def send_kernel(q_in, k_in, v_in, g_in, a_in, n_ref, *refs):
+    q_ref, k_ref, v_ref, g_ref, a_ref, sems = refs[-6:]
+    hops = refs[:-6]
+    me = lax.axis_index("ctx")
     rows, width = q_ref.shape
-    hops = [ref for ref in outs if ref.shape[0] == rows + EXTRA]
-    blocks = [ref for ref in outs if ref.shape[0] != rows + EXTRA]
-    part = wq_ref.shape[0] // (len(blocks) + 1)
-    piece = blocks[0].shape[0]
     loads = [
-        pltpu.make_async_copy(src, dst, in_sems.at[at])
+        pltpu.make_async_copy(src, dst, sems.at[at])
         for at, (src, dst) in enumerate(
             ((k_in, k_ref), (v_in, v_ref), (q_in, q_ref), (g_in, g_ref), (a_in, a_ref))
         )
     ]
     for load in loads:
         load.start()
-    moves = []
-    for at, block in enumerate(blocks):
-        start = pl.multiple_of((head ^ (at + 1)) * part + me * piece, piece)
-        for col, weight in enumerate((wq_ref, wk_ref, wv_ref)):
-            moves.append(
-                pltpu.make_async_copy(
-                    weight.at[pl.ds(start, piece), :],
-                    block.at[:, col * width : (col + 1) * width],
-                    w_sems.at[3 * at + col],
-                )
-            )
-    for move in moves:
-        move.start()
     for load in loads:
         load.wait()
     delta = delta_of(g_ref[...], a_ref[...])
@@ -205,19 +186,35 @@
     extra = extra.astype(jnp.bfloat16)
     for at, hop in enumerate(hops):
         later = (me ^ (at + 1)) > me
-        hop[:rows, :width] = jnp.where(later, k_ref[...], q_ref[...])
-        hop[:rows, width:] = jnp.where(later, v_ref[...], g_ref[...])
+
+        @pl.when(later)
+        def _():
+            hop[:rows, :width] = k_ref[...]
+            hop[:rows, width:] = v_ref[...]
+
+        @pl.when(jnp.logical_not(later))
+        def _():
+            hop[:rows, :width] = q_ref[...]
+            hop[:rows, width:] = g_ref[...]
+
         hop[rows:, :width] = extra
         hop[rows:, width:] = jnp.zeros((EXTRA, width), jnp.bfloat16)
-    for move in moves:
-        move.wait()
-
-
-def grad_kernel(scale, spot_ref, q_ref, k_ref, v_ref, g_ref, a_ref, n_ref, *refs):
-    out_ref = refs[-1]
-    got = refs[:-1]
+
+
+def near_kernel(
+    scale, parts, q_ref, k_ref, v_ref, g_ref, a_ref, n_ref, wq_ref, wk_ref, wv_ref, *refs
+):
+    w_all, grads, sems = refs[-3:]
+    outs = refs[-3 - parts : -3]
+    got = refs[: -3 - parts]
     rows, width = q_ref.shape
-    me = spot_ref[0]
+    copies = [
+        pltpu.make_async_copy(ref, w_all.at[:, at * width : (at + 1) * width], sems.at[at])
+        for at, ref in enumerate((wq_ref, wk_ref, wv_ref))
+    ]
+    for copy in copies:
+        copy.start()
+    me, head = lax.axis_index("ctx"), lax.axis_index("head")
     exponent = scale * math.log2(math.e)
     query, key, value, grad = q_ref[...], k_ref[...], v_ref[...], g_ref[...]
     norm = (1.0 / scale) * jnp.sum(
@@ -250,36 +247,18 @@
     ).astype(jnp.bfloat16)
     both_sum = dot_nn(sides, first)
     value_sum += dot_nn(jnp.where(earlier, 0.0, probs).astype(jnp.bfloat16), second)
-    out_ref[:, :width] = (scale * (query_sum + both_sum[:rows])).astype(jnp.bfloat16)
-    out_ref[:, width : 2 * width] = (scale * (key_sum + both_sum[rows:])).astype(jnp.bfloat16)
-    out_ref[:, 2 * width :] = value_sum.astype(jnp.bfloat16)
-
-
-def project_kernel(count, order, spot_ref, wq_ref, wk_ref, wv_ref, *refs):
-    grads = refs[:count]
-    shares = refs[count:-3]
-    out_ref, w_own, sems = refs[-3:]
-    width = wq_ref.shape[1]
-    part = out_ref.shape[1]
-    me, head = spot_ref[0], spot_ref[1]
-    start = pl.multiple_of(head * part, part)
-    loads = [
-        pltpu.make_async_copy(
-            ref.at[pl.ds(start, part), :], w_own.at[:, at * width : (at + 1) * width], sems.at[at]
-        )
-        for at, ref in enumerate((wq_ref, wk_ref, wv_ref))
-    ]
-    for load in loads:
-        load.start()
-    for load in loads:
-        load.wait()
-    piece = shares[0].shape[1]
-    for offset, share in zip(order, shares):
-        at = pl.multiple_of((me ^ offset) * piece, piece)
-        total = dot_nt(grads[0][...], w_own[pl.ds(at, piece), :])
-        for other in range(count - 1):
-            total += dot_nt(grads[other + 1][...], share[other])
-        out_ref[:, pl.ds(at, piece)] = total.astype(jnp.bfloat16)
+    grads[:, :width] = (scale * (query_sum + both_sum[:rows])).astype(jnp.bfloat16)
+    grads[:, width : 2 * width] = (scale * (key_sum + both_sum[rows:])).astype(jnp.bfloat16)
+    grads[:, 2 * width :] = value_sum.astype(jnp.bfloat16)
+    for copy in copies:
+        copy.wait()
+    part = outs[0].shape[1]
+    cols = math.gcd(part, 512)
+    for offset in range(parts - 1, -1, -1):
+        start = (head ^ offset) * part
+        for at in range(0, part, cols):
+            weight = w_all[pl.ds(pl.multiple_of(start + at, cols), cols), :]
+            outs[offset][:, at : at + cols] = dot_nt(grads[...], weight).astype(jnp.bfloat16)
 
 
 def swap(value, axis, offset):
@@ -287,68 +266,55 @@
     return lax.ppermute(value, axis, [(at, at ^ offset) for at in range(size)])
 
 
-def near_body(own, weights, spot, scale):
+def near_body(own, weights, scale):
     rows, width = own[0].shape
     depth = weights[0].shape[0]
     ctx = lax.axis_size("ctx")
     parts = lax.axis_size("head")
-    part = depth // parts
-    piece = part // ctx
     vmem = pl.BlockSpec(memory_space=pltpu.VMEM)
-    smem = pl.BlockSpec(memory_space=pltpu.SMEM)
     hbm = pl.BlockSpec(memory_space=pl.ANY)
-    params = pltpu.CompilerParams(vmem_limit_bytes=58 * MIB)
+    params = pltpu.CompilerParams(vmem_limit_bytes=60 * MIB)
     hop = jax.ShapeDtypeStruct((rows + EXTRA, 2 * width), jnp.bfloat16)
-    block = jax.ShapeDtypeStruct((piece, 3 * width), jnp.bfloat16)
     sent = pl.pallas_call(
         send_kernel,
-        out_shape=[hop] * (ctx - 1) + [block] * (parts - 1),
-        in_specs=[smem] + [hbm] * 5 + [vmem] + [hbm] * 3,
-        out_specs=[vmem] * (ctx + parts - 2),
+        out_shape=[hop] * (ctx - 1),
+        in_specs=[hbm] * 5 + [vmem],
+        out_specs=[vmem] * (ctx - 1),
         scratch_shapes=[pltpu.VMEM((rows, width), jnp.bfloat16)] * 5
-        + [pltpu.SemaphoreType.DMA((5,)), pltpu.SemaphoreType.DMA((3 * (parts - 1),))],
+        + [pltpu.SemaphoreType.DMA((5,))],
         compiler_params=params,
-    )(spot, *own, *weights)
-    got = [swap(sent[at], "ctx", at + 1) for at in range(ctx - 1)]
-    shares = {0: jnp.stack([swap(sent[ctx - 1 + at], "head", at + 1) for at in range(parts - 1)])}
-    for offset in range(2, ctx, 2):
-        shares[offset] = swap(shares[0], "ctx", offset)
-    for offset in range(0, ctx, 2):
-        shares[offset + 1] = swap(shares[offset], "ctx", 1)
-    grads = pl.pallas_call(
-        functools.partial(grad_kernel, scale),
-        out_shape=jax.ShapeDtypeStruct((rows, 3 * width), jnp.bfloat16),
-        in_specs=[smem] + [vmem] * (ctx + 5),
-        out_specs=vmem,
-        compiler_params=pltpu.CompilerParams(vmem_limit_bytes=32 * MIB),
-        cost_estimate=pl.CostEstimate(
-            flops=14 * rows * rows * ctx * width,
-            bytes_accessed=4 * rows * ctx * width,
-            transcendentals=rows * rows * ctx,
-        ),
-    )(spot, *own, *got)
-    all_grads = [grads] + [swap(grads, "head", at) for at in range(1, parts)]
-    return pl.pallas_call(
-        functools.partial(project_kernel, parts, tuple(shares)),
-        out_shape=jax.ShapeDtypeStruct((rows, part), jnp.bfloat16),
-        in_specs=[smem] + [hbm] * 3 + [vmem] * (parts + ctx),
-        out_specs=vmem,
+    )(*own)
+    got = [swap(value, "ctx", at + 1) for at, value in enumerate(sent)]
+    block = jax.ShapeDtypeStruct((rows, depth // parts), jnp.bfloat16)
+    blocks = pl.pallas_call(
+        functools.partial(near_kernel, scale, parts),
+        out_shape=[block] * parts,
+        in_specs=[vmem] * 6 + [hbm] * 3 + [vmem] * (ctx - 1),
+        out_specs=[vmem] * parts,
         scratch_shapes=[
-            pltpu.VMEM((part, 3 * width), jnp.bfloat16),
+            pltpu.VMEM((depth, 3 * width), jnp.bfloat16),
+            pltpu.VMEM((rows, 3 * width), jnp.bfloat16),
             pltpu.SemaphoreType.DMA((3,)),
         ],
         compiler_params=params,
         cost_estimate=pl.CostEstimate(
-            flops=6 * rows * width * depth, bytes_accessed=6 * depth * width, transcendentals=0
+            flops=14 * rows * rows * ctx * width + 6 * rows * width * depth,
+            bytes_accessed=4 * rows * ctx * width + 6 * depth * width,
+            transcendentals=rows * rows * ctx,
         ),
-    )(spot, *weights, *all_grads, *shares.values())
-
-
-def far_body(own, weights, spot, scale):
+    )(*own, *weights, *got)
+    total = blocks[0].astype(jnp.float32)
+    for at in range(1, parts):
+        total = total + swap(blocks[at], "head", at).astype(jnp.float32)
+    return total.astype(jnp.bfloat16)
+
+
+def far_body(own, weights, scale):
     rows, width = own[0].shape
     depth = weights[0].shape[0]
     ctx = lax.axis_size("ctx")
     parts = lax.axis_size("head")
+    spot = lax.axis_index("ctx").astype(jnp.int32).reshape(1)
     vmem = pl.BlockSpec(memory_space=pltpu.VMEM)
     smem = pl.BlockSpec(memory_space=pltpu.SMEM)
     hbm = pl.BlockSpec(memory_space=pl.ANY)
@@ -396,11 +362,10 @@
 ):
     rows, width = queries.shape
     ctx, parts = lax.axis_size("ctx"), lax.axis_size("head")
-    spot = jnp.stack([lax.axis_index("ctx"), lax.axis_index("head")]).astype(jnp.int32)
     own = (queries, key_rows, value_rows, out_grad, attn_out, log_norm.reshape(1, rows))
     weights = (query_weight, key_weight, value_weight)
     near = ctx <= 8 and parts <= 4 and ctx & (ctx - 1) == 0 and parts & (parts - 1) == 0
-    return (near_body if near else far_body)(own, weights, spot, width ** (-0.5))
+    return (near_body if near else far_body)(own, weights, width ** (-0.5))
 
 
 def solution(mesh):

time: 73.1 us -> 48.7 us (0.67)
  the two profiles are of different devices: /device:TPU:0 before, /device:TPU:18 now
where the time goes in v4:
time: 48.7 us; the launch traced here: 48.4 us
  waiting for transfers between devices  28.2 us (58%)
  starting transfers between devices  9.59 us (20%)
  Pallas kernels  7.42 us (15%)
  other arithmetic  1.82 us (4%)
  local copies, waits for them, and re-layouts  1.25 us (3%)
    ppermute x10, waiting for transfers between devices, swap(): return lax.ppermute(value, axis, [(at, at ^ offset) for at in range(size)])  28.2 us
    ppermute x10, starting transfers between devices, swap(): return lax.ppermute(value, axis, [(at, at ^ offset) for at in range(size)])  9.59 us
    pallas_call x1, Pallas kernels, near_body(): pl.pallas_call(functools.partial(near_kernel, scale, parts), out_shape=[b...  4.89 us
    pallas_call x1, Pallas kernels, near_body(): pl.pallas_call(send_kernel, out_shape=[hop] * (ctx - 1), in_specs=[hbm] *...  2.52 us
    convert_element_type x1, other arithmetic, near_body(): return total.astype(jnp.bfloat16)  1.82 us
    unnamed x14, local copies, waits for them, and re-layouts  1.25 us
  transfers between devices with their start and end apart: 10, of which 6 were waited for; matrix products, arithmetic and copies ran while one was open for 0% of the time, Pallas kernels for 0%

profile of v4, /device:TPU:18, one launch (start us, length us, event | category | flops | bytes accessed | tf_op | source)
XLA Modules:
  0.0 48.4 jit_solution(16707155495715015718)
XLA Ops:
  0.0 2.5 %shard_map.91 = (bf16[144,256]{1,0:T(8,128)(2,1)}, bf16[144,256]{1,0:T(8,128)(2,1)}, bf16[144,256]{1,0:T(8,128)(2,1)}, bf16[144,256]{1,0:T(8,128)(2,1)}, bf16[14...) custom-call(bf16[128,128]{1,0:T(8,128)(2,1)} %q_ref.1, bf16[128,128]{1,0:T(8,128)(2,1)} %k_ref.1, ...), custom_call_target="tpu_custom_call" | custom-call | tf_op jit(solution)/shard_map/pallas_call | solution.py:278
  2.5 0.1 collective-permute-start
  2.6 0.6 %collective-permute-start.1 = (bf16[144,256]{1,0:T(8,128)(2,1)}, bf16[144,256]{1,0:T(8,128)(2,1)S(1)}, u32[]{:S(2)}, u32[]{:S(2)}) collective-permute-start(bf16[144,256]{1,0:T(8,128)(2,1)} %get-tuple-element.17), channel_id=1, source_target_pairs={{0,8},{4,12},{8,0},{12,4},{16,24},{20,28},{24,16},{28,20},{1,9},{5... | collective-permute-start | bytes 221192 | tf_op jit(solution)/shard_map/ppermute | solution.py:266
  3.2 1.3 %collective-permute-start.2 = (bf16[144,256]{1,0:T(8,128)(2,1)}, bf16[144,256]{1,0:T(8,128)(2,1)S(1)}, u32[]{:S(2)}, u32[]{:S(2)}) collective-permute-start(bf16[144,256]{1,0:T(8,128)(2,1)} %get-tuple-element.18), channel_id=1, source_target_pairs={{0,12},{4,8},{8,4},{12,0},{16,28},{20,24},{24,20},{28,16},{1,13},{... | collective-permute-start | bytes 221192 | tf_op jit(solution)/shard_map/ppermute | solution.py:266
  4.5 1.5 %collective-permute-start.3 = (bf16[144,256]{1,0:T(8,128)(2,1)}, bf16[144,256]{1,0:T(8,128)(2,1)S(1)}, u32[]{:S(2)}, u32[]{:S(2)}) collective-permute-start(bf16[144,256]{1,0:T(8,128)(2,1)} %get-tuple-element.19), channel_id=1, source_target_pairs={{0,16},{4,20},{8,24},{12,28},{16,0},{20,4},{24,8},{28,12},{1,17},{... | collective-permute-start | bytes 221192 | tf_op jit(solution)/shard_map/ppermute | solution.py:266
  6.0 0.2 collective-permute-start.4
  6.2 0.0 collective-permute-done.refs_0_
  6.2 0.0 copy-start
  6.2 1.5 %collective-permute-start.5 = (bf16[144,256]{1,0:T(8,128)(2,1)}, bf16[144,256]{1,0:T(8,128)(2,1)S(1)}, u32[]{:S(2)}, u32[]{:S(2)}) collective-permute-start(bf16[144,256]{1,0:T(8,128)(2,1)} %get-tuple-element.21), channel_id=1, source_target_pairs={{0,24},{4,28},{8,16},{12,20},{16,8},{20,12},{24,0},{28,4},{1,25},{... | collective-permute-start | bytes 221192 | tf_op jit(solution)/shard_map/ppermute | solution.py:266
  7.7 0.3 collective-permute-done.1.refs_1_
  8.0 0.0 copy-start.1
  8.0 0.9 %collective-permute-start.6 = (bf16[144,256]{1,0:T(8,128)(2,1)}, bf16[144,256]{1,0:T(8,128)(2,1)S(1)}, u32[]{:S(2)}, u32[]{:S(2)}) collective-permute-start(bf16[144,256]{1,0:T(8,128)(2,1)} %get-tuple-element.22), channel_id=1, source_target_pairs={{0,28},{4,24},{8,20},{12,16},{16,12},{20,8},{24,4},{28,0},{1,29},{... | collective-permute-start | bytes 221192 | tf_op jit(solution)/shard_map/ppermute | solution.py:266
  8.9 0.0 collective-permute-done.2.refs_2_
  8.9 0.0 copy-start.2
  8.9 0.3 collective-permute-done.3.refs_3_
  9.2 0.0 copy-start.3
  9.2 4.5 %collective-permute-done.4.refs_4_ = bf16[144,256]{1,0:T(8,128)(2,1)S(1)} collective-permute-done((bf16[144,256]{1,0:T(8,128)(2,1)}, bf16[144,256]{1,0:T(8,128)(2,1)S(1)}, u32[]{:S(2)}, u32[]{:S(2)}) %collective-permute-start.4) | collective-permute-done | bytes 73760 | tf_op jit(solution)/shard_map/ppermute | solution.py:266
  13.7 0.0 copy-start.4
  13.7 0.0 collective-permute-done.5.refs_5_
  13.7 0.0 copy-start.5
  13.7 0.0 collective-permute-done.6.refs_6_
  13.7 0.0 copy-done
  13.7 0.0 copy-done.1
  13.7 0.0 copy-done.2
  13.7 0.0 copy-done.3
  13.8 0.6 %copy-done.4 = bf16[144,256]{1,0:T(8,128)(2,1)} copy-done((bf16[144,256]{1,0:T(8,128)(2,1)}, bf16[144,256]{1,0:T(8,128)(2,1)S(1)}, u32[]{:S(2)}) %copy-start.4) | copy-done | bytes 73752
  14.3 0.0 copy-done.5
  14.4 0.0 copy-start.6
  14.4 0.6 %copy-done.6 = bf16[144,256]{1,0:T(8,128)(2,1)} copy-done((bf16[144,256]{1,0:T(8,128)(2,1)}, bf16[144,256]{1,0:T(8,128)(2,1)S(1)}, u32[]{:S(2)}) %copy-start.6) | copy-done | bytes 73752
  15.0 4.9 %shard_map.92 = (bf16[128,1024]{1,0:T(8,128)(2,1)}, bf16[128,1024]{1,0:T(8,128)(2,1)}, bf16[128,1024]{1,0:T(8,128)(2,1)}, bf16[128,1024]{1,0:T(8,128)(2,1)}) custom-call(bf16[128,128]{1,0:T(8,128)(2,1)} %q_ref.1, bf16[128,128]{1,0:T(8,128)(2,1)} %k_ref.1, bf16[128,128]{1,0:T(8,128)(2,1)} %v_ref.1, bf16[128,128]{1,0:T(8,128)(2,1)} %g_ref.1, ...), custom_call_target="tpu_custom_call" | custom-call | flops 637534208 | bytes 3670016 | tf_op jit(solution)/shard_map/pallas_call | solution.py:289
  19.9 1.6 %collective-permute-start.7 = (bf16[128,1024]{1,0:T(8,128)(2,1)}, bf16[128,1024]{1,0:T(8,128)(2,1)S(1)}, u32[]{:S(2)}, u32[]{:S(2)}) collective-permute-start(bf16[128,1024]{1,0:T(8,128)(2,1)} %get-tuple-element.24), channel_id=1, source_target_pairs={{0,1},{1,0},{2,3},{3,2},{4,5},{5,4},{6,7},{7,6},{8,9},{9,8},{10,11... | collective-permute-start | bytes 786440 | tf_op jit(solution)/shard_map/ppermute | solution.py:266
  21.5 0.3 collective-permute-start.8
  21.9 1.6 %collective-permute-start.9 = (bf16[128,1024]{1,0:T(8,128)(2,1)}, bf16[128,1024]{1,0:T(8,128)(2,1)S(1)}, u32[]{:S(2)}, u32[]{:S(2)}) collective-permute-start(bf16[128,1024]{1,0:T(8,128)(2,1)} %get-tuple-element.26), channel_id=1, source_target_pairs={{0,3},{1,2},{2,1},{3,0},{4,7},{5,6},{6,5},{7,4},{8,11},{9,10},{10,... | collective-permute-start | bytes 786440 | tf_op jit(solution)/shard_map/ppermute | solution.py:266
  23.4 8.6 %collective-permute-done.7 = bf16[128,1024]{1,0:T(8,128)(2,1)S(1)} collective-permute-done((bf16[128,1024]{1,0:T(8,128)(2,1)}, bf16[128,1024]{1,0:T(8,128)(2,1)S(1)}, u32[]{:S(2)}, u32[]{:S(2)}) %collective-permute-start.7) | collective-permute-done | bytes 262176 | tf_op jit(solution)/shard_map/ppermute | solution.py:266
  32.1 8.1 %collective-permute-done.8 = bf16[128,1024]{1,0:T(8,128)(2,1)S(1)} collective-permute-done((bf16[128,1024]{1,0:T(8,128)(2,1)}, bf16[128,1024]{1,0:T(8,128)(2,1)S(1)}, u32[]{:S(2)}, u32[]{:S(2)}) %collective-permute-start.8) | collective-permute-done | bytes 262176 | tf_op jit(solution)/shard_map/ppermute | solution.py:266
  40.1 6.4 %collective-permute-done.9 = bf16[128,1024]{1,0:T(8,128)(2,1)S(1)} collective-permute-done((bf16[128,1024]{1,0:T(8,128)(2,1)}, bf16[128,1024]{1,0:T(8,128)(2,1)S(1)}, u32[]{:S(2)}, u32[]{:S(2)}) %collective-permute-start.9) | collective-permute-done | bytes 262176 | tf_op jit(solution)/shard_map/ppermute | solution.py:266
  46.6 1.8 %add_convert_fusion = bf16[128,1024]{1,0:T(8,128)(2,1)} fusion(bf16[128,1024]{1,0:T(8,128)(2,1)S(1)} %collective-permute-done.9, bf16[128,1024]{1,0:T(8,128)(2,1)S(1)} %collective-permute-done.8, bf16[128,1024]{1,0:T(8,128)(2,1)S(1)} %collective-permute-done.7, bf16[128,1024]{1,0:T(8,128)(2,1)} %get-tuple-element.23), kind=kLoop, calls=%fused_computation | loop fusion | flops 1048576 | bytes 1310720 | tf_op jit(solution)/shard_map/convert_element_type | solution.py:309
Async XLA Ops:
  2.5 3.6 %collective-permute-start = (bf16[144,256]{1,0:T(8,128)(2,1)}, bf16[144,256]{1,0:T(8,128)(2,1)S(1)}, u32[]{:S(2)}, u32[]{:S(2)}) collective-permute-start(bf16[144,256]{1,0:T(8,128)(2,1)} %get-tuple-element.16), channel_id=1, source_target_pairs={{0,4},{4,0},{8,12},{12,8},{16,20},{20,16},{24,28},{28,24},{1,5},{5... | collective-permute-start | bytes 221192 | tf_op jit(solution)/shard_map/ppermute | solution.py:266
  2.6 5.3 %collective-permute-start.1 = (bf16[144,256]{1,0:T(8,128)(2,1)}, bf16[144,256]{1,0:T(8,128)(2,1)S(1)}, u32[]{:S(2)}, u32[]{:S(2)}) collective-permute-start(bf16[144,256]{1,0:T(8,128)(2,1)} %get-tuple-element.17), channel_id=1, source_target_pairs={{0,8},{4,12},{8,0},{12,4},{16,24},{20,28},{24,16},{28,20},{1,9},{5... | collective-permute-start | bytes 221192 | tf_op jit(solution)/shard_map/ppermute | solution.py:266
  3.2 5.7 %collective-permute-start.2 = (bf16[144,256]{1,0:T(8,128)(2,1)}, bf16[144,256]{1,0:T(8,128)(2,1)S(1)}, u32[]{:S(2)}, u32[]{:S(2)}) collective-permute-start(bf16[144,256]{1,0:T(8,128)(2,1)} %get-tuple-element.18), channel_id=1, source_target_pairs={{0,12},{4,8},{8,4},{12,0},{16,28},{20,24},{24,20},{28,16},{1,13},{... | collective-permute-start | bytes 221192 | tf_op jit(solution)/shard_map/ppermute | solution.py:266
  4.5 4.7 %collective-permute-start.3 = (bf16[144,256]{1,0:T(8,128)(2,1)}, bf16[144,256]{1,0:T(8,128)(2,1)S(1)}, u32[]{:S(2)}, u32[]{:S(2)}) collective-permute-start(bf16[144,256]{1,0:T(8,128)(2,1)} %get-tuple-element.19), channel_id=1, source_target_pairs={{0,16},{4,20},{8,24},{12,28},{16,0},{20,4},{24,8},{28,12},{1,17},{... | collective-permute-start | bytes 221192 | tf_op jit(solution)/shard_map/ppermute | solution.py:266
  6.0 7.7 %collective-permute-start.4 = (bf16[144,256]{1,0:T(8,128)(2,1)}, bf16[144,256]{1,0:T(8,128)(2,1)S(1)}, u32[]{:S(2)}, u32[]{:S(2)}) collective-permute-start(bf16[144,256]{1,0:T(8,128)(2,1)} %get-tuple-element.20), channel_id=1, source_target_pairs={{0,20},{4,16},{8,28},{12,24},{16,4},{20,0},{24,12},{28,8},{1,21},{... | collective-permute-start | bytes 221192 | tf_op jit(solution)/shard_map/ppermute | solution.py:266
  6.2 7.5 %copy-start = (bf16[144,256]{1,0:T(8,128)(2,1)}, bf16[144,256]{1,0:T(8,128)(2,1)S(1)}, u32[]{:S(2)}) copy-start(bf16[144,256]{1,0:T(8,128)(2,1)S(1)} %collective-permute-done.refs_0_) | copy-start | bytes 221188
  6.2 7.5 %collective-permute-start.5 = (bf16[144,256]{1,0:T(8,128)(2,1)}, bf16[144,256]{1,0:T(8,128)(2,1)S(1)}, u32[]{:S(2)}, u32[]{:S(2)}) collective-permute-start(bf16[144,256]{1,0:T(8,128)(2,1)} %get-tuple-element.21), channel_id=1, source_target_pairs={{0,24},{4,28},{8,16},{12,20},{16,8},{20,12},{24,0},{28,4},{1,25},{... | collective-permute-start | bytes 221192 | tf_op jit(solution)/shard_map/ppermute | solution.py:266
  8.0 5.8 %copy-start.1 = (bf16[144,256]{1,0:T(8,128)(2,1)}, bf16[144,256]{1,0:T(8,128)(2,1)S(1)}, u32[]{:S(2)}) copy-start(bf16[144,256]{1,0:T(8,128)(2,1)S(1)} %collective-permute-done.1.refs_1_) | copy-start | bytes 221188
  8.0 5.8 %collective-permute-start.6 = (bf16[144,256]{1,0:T(8,128)(2,1)}, bf16[144,256]{1,0:T(8,128)(2,1)S(1)}, u32[]{:S(2)}, u32[]{:S(2)}) collective-permute-start(bf16[144,256]{1,0:T(8,128)(2,1)} %get-tuple-element.22), channel_id=1, source_target_pairs={{0,28},{4,24},{8,20},{12,16},{16,12},{20,8},{24,4},{28,0},{1,29},{... | collective-permute-start | bytes 221192 | tf_op jit(solution)/shard_map/ppermute | solution.py:266
  8.9 4.9 %copy-start.2 = (bf16[144,256]{1,0:T(8,128)(2,1)}, bf16[144,256]{1,0:T(8,128)(2,1)S(1)}, u32[]{:S(2)}) copy-start(bf16[144,256]{1,0:T(8,128)(2,1)S(1)} %collective-permute-done.2.refs_2_) | copy-start | bytes 221188
  9.2 4.5 %copy-start.3 = (bf16[144,256]{1,0:T(8,128)(2,1)}, bf16[144,256]{1,0:T(8,128)(2,1)S(1)}, u32[]{:S(2)}) copy-start(bf16[144,256]{1,0:T(8,128)(2,1)S(1)} %collective-permute-done.3.refs_3_) | copy-start | bytes 221188
  13.7 0.6 %copy-start.4 = (bf16[144,256]{1,0:T(8,128)(2,1)}, bf16[144,256]{1,0:T(8,128)(2,1)S(1)}, u32[]{:S(2)}) copy-start(bf16[144,256]{1,0:T(8,128)(2,1)S(1)} %collective-permute-done.4.refs_4_) | copy-start | bytes 221188
  13.7 0.7 %copy-start.5 = (bf16[144,256]{1,0:T(8,128)(2,1)}, bf16[144,256]{1,0:T(8,128)(2,1)S(1)}, u32[]{:S(2)}) copy-start(bf16[144,256]{1,0:T(8,128)(2,1)S(1)} %collective-permute-done.5.refs_5_) | copy-start | bytes 221188
  14.4 0.6 %copy-start.6 = (bf16[144,256]{1,0:T(8,128)(2,1)}, bf16[144,256]{1,0:T(8,128)(2,1)S(1)}, u32[]{:S(2)}) copy-start(bf16[144,256]{1,0:T(8,128)(2,1)S(1)} %collective-permute-done.6.refs_6_) | copy-start | bytes 221188
  19.9 12.2 %collective-permute-start.7 = (bf16[128,1024]{1,0:T(8,128)(2,1)}, bf16[128,1024]{1,0:T(8,128)(2,1)S(1)}, u32[]{:S(2)}, u32[]{:S(2)}) collective-permute-start(bf16[128,1024]{1,0:T(8,128)(2,1)} %get-tuple-element.24), channel_id=1, source_target_pairs={{0,1},{1,0},{2,3},{3,2},{4,5},{5,4},{6,7},{7,6},{8,9},{9,8},{10,11... | collective-permute-start | bytes 786440 | tf_op jit(solution)/shard_map/ppermute | solution.py:266
  21.5 18.6 %collective-permute-start.8 = (bf16[128,1024]{1,0:T(8,128)(2,1)}, bf16[128,1024]{1,0:T(8,128)(2,1)S(1)}, u32[]{:S(2)}, u32[]{:S(2)}) collective-permute-start(bf16[128,1024]{1,0:T(8,128)(2,1)} %get-tuple-element.25), channel_id=1, source_target_pairs={{0,2},{1,3},{2,0},{3,1},{4,6},{5,7},{6,4},{7,5},{8,10},{9,11},{10,... | collective-permute-start | bytes 786440 | tf_op jit(solution)/shard_map/ppermute | solution.py:266
  21.9 24.7 %collective-permute-start.9 = (bf16[128,1024]{1,0:T(8,128)(2,1)}, bf16[128,1024]{1,0:T(8,128)(2,1)S(1)}, u32[]{:S(2)}, u32[]{:S(2)}) collective-permute-start(bf16[128,1024]{1,0:T(8,128)(2,1)} %get-tuple-element.26), channel_id=1, source_target_pairs={{0,3},{1,2},{2,1},{3,0},{4,7},{5,6},{6,5},{7,4},{8,11},{9,10},{10,... | collective-permute-start | bytes 786440 | tf_op jit(solution)/shard_map/ppermute | solution.py:266

commit v5 on v4

--- a/solution.py
+++ b/solution.py
@@ -162,65 +162,57 @@
             out_ref[h, :, at : at + cols] = dot_nt(grads[...], weight).astype(jnp.bfloat16)
 
 
-def send_kernel(q_in, k_in, v_in, g_in, a_in, n_ref, *refs):
-    q_ref, k_ref, v_ref, g_ref, a_ref, sems = refs[-6:]
-    hops = refs[:-6]
+def split_rows(own_ref, rows):
+    return [own_ref[at * rows : (at + 1) * rows, :] for at in range(5)]
+
+
+def send_kernel(own_ref, n_ref, *hops):
     me = lax.axis_index("ctx")
-    rows, width = q_ref.shape
-    loads = [
-        pltpu.make_async_copy(src, dst, sems.at[at])
-        for at, (src, dst) in enumerate(
-            ((k_in, k_ref), (v_in, v_ref), (q_in, q_ref), (g_in, g_ref), (a_in, a_ref))
-        )
-    ]
-    for load in loads:
-        load.start()
-    for load in loads:
-        load.wait()
-    delta = delta_of(g_ref[...], a_ref[...])
+    rows, width = n_ref.shape[1], own_ref.shape[1]
+    query, key, value, grad, attn = split_rows(own_ref, rows)
+    delta = delta_of(grad, attn)
     delta = jnp.sum(jnp.where(diagonal(rows), delta, 0.0), axis=0, keepdims=True)
     row = lax.broadcasted_iota(jnp.int32, (EXTRA, rows), 0)
     extra = jnp.zeros((EXTRA, rows), jnp.float32)
-    for at, value in enumerate(pieces_of(n_ref[...]) + pieces_of(delta)):
-        extra = jnp.where(row == at, value, extra)
+    for at, part in enumerate(pieces_of(n_ref[...]) + pieces_of(delta)):
+        extra = jnp.where(row == at, part, extra)
     extra = extra.astype(jnp.bfloat16)
     for at, hop in enumerate(hops):
         later = (me ^ (at + 1)) > me
 
         @pl.when(later)
         def _():
-            hop[:rows, :width] = k_ref[...]
-            hop[:rows, width:] = v_ref[...]
+            hop[:rows, :width] = key
+            hop[:rows, width:] = value
 
         @pl.when(jnp.logical_not(later))
         def _():
-            hop[:rows, :width] = q_ref[...]
-            hop[:rows, width:] = g_ref[...]
+            hop[:rows, :width] = query
+            hop[:rows, width:] = grad
 
         hop[rows:, :width] = extra
         hop[rows:, width:] = jnp.zeros((EXTRA, width), jnp.bfloat16)
 
 
-def near_kernel(
-    scale, parts, q_ref, k_ref, v_ref, g_ref, a_ref, n_ref, wq_ref, wk_ref, wv_ref, *refs
-):
-    w_all, grads, sems = refs[-3:]
-    outs = refs[-3 - parts : -3]
-    got = refs[: -3 - parts]
-    rows, width = q_ref.shape
-    copies = [
-        pltpu.make_async_copy(ref, w_all.at[:, at * width : (at + 1) * width], sems.at[at])
-        for at, ref in enumerate((wq_ref, wk_ref, wv_ref))
-    ]
-    for copy in copies:
-        copy.start()
+def project(grads, w_ref, start, out_ref):
+    part = out_ref.shape[1]
+    cols = math.gcd(part, 512)
+    for at in range(0, part, cols):
+        weight = w_ref[pl.ds(pl.multiple_of(start + at, cols), cols), :]
+        out_ref[:, at : at + cols] = dot_nt(grads[...], weight).astype(out_ref.dtype)
+
+
+def near_kernel(scale, part, own_ref, n_ref, w_ref, *refs):
+    grads, front, back = refs[-3:]
+    got = refs[:-3]
+    rows, width = n_ref.shape[1], own_ref.shape[1]
     me, head = lax.axis_index("ctx"), lax.axis_index("head")
     exponent = scale * math.log2(math.e)
-    query, key, value, grad = q_ref[...], k_ref[...], v_ref[...], g_ref[...]
+    query, key, value, grad, attn = split_rows(own_ref, rows)
     norm = (1.0 / scale) * jnp.sum(
         jnp.where(diagonal(rows), n_ref[...], 0.0), axis=1, keepdims=True
     )
-    delta = delta_of(grad, a_ref[...])
+    delta = delta_of(grad, attn)
     row_at = lax.broadcasted_iota(jnp.int32, (rows, rows), 0)
     col_at = lax.broadcasted_iota(jnp.int32, (rows, rows), 1)
     probs = jnp.where(col_at <= row_at, jnp.exp2(exponent * (dot_nt(query, key) - norm)), 0.0)
@@ -250,15 +242,17 @@
     grads[:, :width] = (scale * (query_sum + both_sum[:rows])).astype(jnp.bfloat16)
     grads[:, width : 2 * width] = (scale * (key_sum + both_sum[rows:])).astype(jnp.bfloat16)
     grads[:, 2 * width :] = value_sum.astype(jnp.bfloat16)
-    for copy in copies:
-        copy.wait()
-    part = outs[0].shape[1]
-    cols = math.gcd(part, 512)
-    for offset in range(parts - 1, -1, -1):
-        start = (head ^ offset) * part
-        for at in range(0, part, cols):
-            weight = w_all[pl.ds(pl.multiple_of(start + at, cols), cols), :]
-            outs[offset][:, at : at + cols] = dot_nt(grads[...], weight).astype(jnp.bfloat16)
+    start = (head ^ 3) * part
+    project(grads, w_ref, start, front)
+    project(grads, w_ref, start + part // 2, back)
+
+
+def rest_kernel(part, grads, w_ref, front, back, near, mine):
+    head = lax.axis_index("head")
+    project(grads, w_ref, (head ^ 2) * part, front)
+    project(grads, w_ref, (head ^ 2) * part + part // 2, back)
+    project(grads, w_ref, (head ^ 1) * part, near)
+    project(grads, w_ref, head * part, mine)
 
 
 def swap(value, axis, offset):
@@ -270,43 +264,54 @@
     rows, width = own[0].shape
     depth = weights[0].shape[0]
     ctx = lax.axis_size("ctx")
-    parts = lax.axis_size("head")
+    part = depth // lax.axis_size("head")
     vmem = pl.BlockSpec(memory_space=pltpu.VMEM)
-    hbm = pl.BlockSpec(memory_space=pl.ANY)
-    params = pltpu.CompilerParams(vmem_limit_bytes=60 * MIB)
+    params = pltpu.CompilerParams(vmem_limit_bytes=32 * MIB)
     hop = jax.ShapeDtypeStruct((rows + EXTRA, 2 * width), jnp.bfloat16)
+    norm = own[-1]
+    mine = jnp.concatenate(own[:-1], axis=0)
+    weight = jnp.concatenate(weights, axis=1)
     sent = pl.pallas_call(
         send_kernel,
         out_shape=[hop] * (ctx - 1),
-        in_specs=[hbm] * 5 + [vmem],
+        in_specs=[vmem] * 2,
         out_specs=[vmem] * (ctx - 1),
-        scratch_shapes=[pltpu.VMEM((rows, width), jnp.bfloat16)] * 5
-        + [pltpu.SemaphoreType.DMA((5,))],
         compiler_params=params,
-    )(*own)
-    got = [swap(value, "ctx", at + 1) for at, value in enumerate(sent)]
-    block = jax.ShapeDtypeStruct((rows, depth // parts), jnp.bfloat16)
-    blocks = pl.pallas_call(
-        functools.partial(near_kernel, scale, parts),
-        out_shape=[block] * parts,
-        in_specs=[vmem] * 6 + [hbm] * 3 + [vmem] * (ctx - 1),
-        out_specs=[vmem] * parts,
-        scratch_shapes=[
-            pltpu.VMEM((depth, 3 * width), jnp.bfloat16),
-            pltpu.VMEM((rows, 3 * width), jnp.bfloat16),
-            pltpu.SemaphoreType.DMA((3,)),
-        ],
+    )(mine, norm)
+    got = {at: swap(sent[at - 1], "ctx", at) for at in range(ctx - 1, 0, -1)}
+    got = [got[at] for at in range(1, ctx)]
+    half_low = jax.ShapeDtypeStruct((rows, part // 2), jnp.bfloat16)
+    half = jax.ShapeDtypeStruct((rows, part // 2), jnp.float32)
+    low = jax.ShapeDtypeStruct((rows, part), jnp.bfloat16)
+    full = jax.ShapeDtypeStruct((rows, part), jnp.float32)
+    grads, front, back = pl.pallas_call(
+        functools.partial(near_kernel, scale, part),
+        out_shape=[jax.ShapeDtypeStruct((rows, 3 * width), jnp.bfloat16), half_low, half_low],
+        in_specs=[vmem] * (ctx + 2),
+        out_specs=[vmem] * 3,
         compiler_params=params,
         cost_estimate=pl.CostEstimate(
-            flops=14 * rows * rows * ctx * width + 6 * rows * width * depth,
-            bytes_accessed=4 * rows * ctx * width + 6 * depth * width,
+            flops=14 * rows * rows * ctx * width + 6 * rows * width * part,
+            bytes_accessed=4 * rows * ctx * width + 6 * part * width,
             transcendentals=rows * rows * ctx,
         ),
-    )(*own, *weights, *got)
-    total = blocks[0].astype(jnp.float32)
-    for at in range(1, parts):
-        total = total + swap(blocks[at], "head", at).astype(jnp.float32)
-    return total.astype(jnp.bfloat16)
+    )(mine, norm, weight, *got)
+    front, back = swap(front, "head", 1), swap(back, "head", 1)
+    two_front, two_back, near, total = pl.pallas_call(
+        functools.partial(rest_kernel, part),
+        out_shape=[half, half, low, full],
+        in_specs=[vmem] * 2,
+        out_specs=[vmem] * 4,
+        compiler_params=params,
+        cost_estimate=pl.CostEstimate(
+            flops=18 * rows * width * part, bytes_accessed=18 * part * width, transcendentals=0
+        ),
+    )(grads, weight)
+    front = swap((two_front + front.astype(jnp.float32)).astype(jnp.bfloat16), "head", 2)
+    back = swap((two_back + back.astype(jnp.float32)).astype(jnp.bfloat16), "head", 2)
+    near = swap(near, "head", 1)
+    far_sum = jnp.concatenate([front, back], axis=1).astype(jnp.float32)
+    return (total + near.astype(jnp.float32) + far_sum).astype(jnp.bfloat16)
 
 
 def far_body(own, weights, scale):
@@ -364,7 +369,7 @@
     ctx, parts = lax.axis_size("ctx"), lax.axis_size("head")
     own = (queries, key_rows, value_rows, out_grad, attn_out, log_norm.reshape(1, rows))
     weights = (query_weight, key_weight, value_weight)
-    near = ctx <= 8 and parts <= 4 and ctx & (ctx - 1) == 0 and parts & (parts - 1) == 0
+    near = ctx <= 8 and parts == 4 and ctx & (ctx - 1) == 0
     return (near_body if near else far_body)(own, weights, width ** (-0.5))
 
 

time: 48.7 us -> 48.4 us (level)
  the two profiles are of different devices: /device:TPU:18 before, /device:TPU:0 now
where the time goes in v5:
time: 48.4 us; the launch traced here: 47.8 us
  waiting for transfers between devices  21.3 us (44%)
  starting transfers between devices  15.9 us (33%)
  local copies, waits for them, and re-layouts  7.62 us (16%)
  Pallas kernels  2.1 us (4%)
  other arithmetic  0.87 us (2%)
    ppermute x12, waiting for transfers between devices, swap(): return lax.ppermute(value, axis, [(at, at ^ offset) for at in range(size)])  21.3 us
    ppermute x12, starting transfers between devices, swap(): return lax.ppermute(value, axis, [(at, at ^ offset) for at in range(size)])  15.9 us
    unnamed x12, local copies, waits for them, and re-layouts  6.61 us
    pallas_call x1, Pallas kernels, near_body(): pl.pallas_call(functools.partial(near_kernel, scale, part), out_shape=[ja...  1.05 us
  transfers between devices with their start and end apart: 12, of which 5 were waited for; matrix products, arithmetic and copies ran while one was open for 7% of the time, Pallas kernels for 2%

profile of v5, /device:TPU:0, one launch (start us, length us, event | category | flops | bytes accessed | tf_op | source)
XLA Modules:
  0.0 47.8 jit_solution(2622458277492432938)
XLA Ops:
  0.0 0.8 %constant_dynamic-update-slice_fusion.4 = bf16[640,128]{1,0:T(8,128)(2,1)S(1)} fusion(bf16[128,128]{1,0:T(8,128)(2,1)} %param.9), kind=kLoop, calls=%fused_computation.7 | loop fusion | bytes 65536
  0.8 0.8 %constant_dynamic-update-slice_fusion.3 = bf16[640,128]{1,0:T(8,128)(2,1)S(1)} fusion(bf16[640,128]{1,0:T(8,128)(2,1)S(1)} %constant_dynamic-update-slice_fusion.4, bf16[128,128]{1,0:T(8,128)(2,1)} %param.10), kind=kLoop, calls=%fused_computation.6 | loop fusion | bytes 65536
  1.5 0.8 %constant_dynamic-update-slice_fusion.2 = bf16[640,128]{1,0:T(8,128)(2,1)S(1)} fusion(bf16[640,128]{1,0:T(8,128)(2,1)S(1)} %constant_dynamic-update-slice_fusion.3, bf16[128,128]{1,0:T(8,128)(2,1)} %param.11), kind=kLoop, calls=%fused_computation.5 | loop fusion | bytes 65536
  2.3 0.8 %constant_dynamic-update-slice_fusion.1 = bf16[640,128]{1,0:T(8,128)(2,1)S(1)} fusion(bf16[640,128]{1,0:T(8,128)(2,1)S(1)} %constant_dynamic-update-slice_fusion.2, bf16[128,128]{1,0:T(8,128)(2,1)} %param.12), kind=kLoop, calls=%fused_computation.4 | loop fusion | bytes 65536
  3.1 0.8 %constant_dynamic-update-slice_fusion.own_ref = bf16[640,128]{1,0:T(8,128)(2,1)S(1)} fusion(bf16[640,128]{1,0:T(8,128)(2,1)S(1)} %constant_dynamic-update-slice_fusion.1, bf16[128,128]{1,0:T(8,128)(2,1)} %param.13), kind=kLoop, calls=%fused_computation.3 | loop fusion | bytes 65536 | tf_op jit(solution)/shard_map/concatenate | solution.py:272
  3.8 0.0 copy-start
  3.8 0.7 %copy-done = f32[128,1]{0,1:T(1,128)S(1)} copy-done((f32[128,1]{0,1:T(1,128)S(1)}, f32[128,1]{0,1:T(1,128)}, u32[]{:S(2)}) %copy-start) | copy-done | bytes 536
  4.5 0.0 copy-start.2
  4.5 0.2 shard_map.91
  4.7 0.5 %collective-permute-start = (bf16[144,256]{1,0:T(8,128)(2,1)S(1)}, bf16[144,256]{1,0:T(8,128)(2,1)S(1)}, u32[]{:S(2)}, u32[]{:S(2)}) collective-permute-start(bf16[144,256]{1,0:T(8,128)(2,1)S(1)} %get-tuple-element.19), channel_id=1, source_target_pairs={{0,4},{4,0},{8,12},{12,8},{16,20},{20,16},{24,28},{28,24},{1,5},{5... | collective-permute-start | bytes 221192 | tf_op jit(solution)/shard_map/ppermute | solution.py:260
  5.2 2.6 %collective-permute-start.1 = (bf16[144,256]{1,0:T(8,128)(2,1)S(1)}, bf16[144,256]{1,0:T(8,128)(2,1)S(1)}, u32[]{:S(2)}, u32[]{:S(2)}) collective-permute-start(bf16[144,256]{1,0:T(8,128)(2,1)S(1)} %get-tuple-element.20), channel_id=1, source_target_pairs={{0,8},{4,12},{8,0},{12,4},{16,24},{20,28},{24,16},{28,20},{1,9},{5... | collective-permute-start | bytes 221192 | tf_op jit(solution)/shard_map/ppermute | solution.py:260
  7.8 0.1 collective-permute-start.2
  7.8 1.8 %collective-permute-start.3 = (bf16[144,256]{1,0:T(8,128)(2,1)S(1)}, bf16[144,256]{1,0:T(8,128)(2,1)S(1)}, u32[]{:S(2)}, u32[]{:S(2)}) collective-permute-start(bf16[144,256]{1,0:T(8,128)(2,1)S(1)} %get-tuple-element.22), channel_id=1, source_target_pairs={{0,16},{4,20},{8,24},{12,28},{16,0},{20,4},{24,8},{28,12},{1,17},{... | collective-permute-start | bytes 221192 | tf_op jit(solution)/shard_map/ppermute | solution.py:260
  9.6 0.0 copy-start.1
  9.6 0.0 collective-permute-start.4
  9.6 1.4 %constant_dynamic-update-slice_fusion.7 = bf16[4096,384]{1,0:T(8,128)(2,1)S(1)} fusion(bf16[4096,128]{1,0:T(8,128)(2,1)} %param.15), kind=kLoop, calls=%fused_computation.10 | loop fusion | bytes 2097152
  11.0 1.5 %constant_dynamic-update-slice_fusion.6 = bf16[4096,384]{1,0:T(8,128)(2,1)S(1)} fusion(bf16[4096,384]{1,0:T(8,128)(2,1)S(1)} %constant_dynamic-update-slice_fusion.7, bf16[4096,128]{1,0:T(8,128)(2,1)} %param.16), kind=kLoop, calls=%fused_computation.9 | loop fusion | bytes 2097152
  12.5 0.0 collective-permute-done.refs_0_
  12.5 2.7 %collective-permute-start.5 = (bf16[144,256]{1,0:T(8,128)(2,1)S(1)}, bf16[144,256]{1,0:T(8,128)(2,1)S(1)}, u32[]{:S(2)}, u32[]{:S(2)}) collective-permute-start(bf16[144,256]{1,0:T(8,128)(2,1)S(1)} %get-tuple-element.24), channel_id=1, source_target_pairs={{0,24},{4,28},{8,16},{12,20},{16,8},{20,12},{24,0},{28,4},{1,25},{... | collective-permute-start | bytes 221192 | tf_op jit(solution)/shard_map/ppermute | solution.py:260
  15.2 0.0 collective-permute-done.1.refs_1_
  15.2 0.1 collective-permute-start.6
  15.3 0.0 copy-done.2
  15.3 0.2 constant_dynamic-update-slice_fusion.5.w_ref
  15.6 0.0 collective-permute-done.2.refs_2_
  15.6 0.0 collective-permute-done.3.refs_3_
  15.6 0.0 collective-permute-done.4.refs_4_
  15.6 2.5 %collective-permute-done.5.refs_5_ = bf16[144,256]{1,0:T(8,128)(2,1)S(1)} collective-permute-done((bf16[144,256]{1,0:T(8,128)(2,1)S(1)}, bf16[144,256]{1,0:T(8,128)(2,1)S(1)}, u32[]{:S(2)}, u32[]{:S(2)}) %collective-permute-start.5) | collective-permute-done | bytes 73760 | tf_op jit(solution)/shard_map/ppermute | solution.py:260
  18.1 2.2 %collective-permute-done.6.refs_6_ = bf16[144,256]{1,0:T(8,128)(2,1)S(1)} collective-permute-done((bf16[144,256]{1,0:T(8,128)(2,1)S(1)}, bf16[144,256]{1,0:T(8,128)(2,1)S(1)}, u32[]{:S(2)}, u32[]{:S(2)}) %collective-permute-start.6) | collective-permute-done | bytes 73760 | tf_op jit(solution)/shard_map/ppermute | solution.py:260
  20.3 0.0 copy-done.1
  20.3 1.1 %shard_map.92 = (bf16[128,384]{1,0:T(8,128)(2,1)S(1)}, bf16[128,512]{1,0:T(8,128)(2,1)S(1)}, bf16[128,512]{1,0:T(8,128)(2,1)S(1)}) custom-call(bf16[640,128]{1,0:T(8,128)(2,1)S(1)} %constant_dynamic-update-slice_fusion.own_ref, f32[1,128]{1,0:T(1,128)S(1)} %bitcast.2, bf16[4096,384]{1,0:T(8,128)(2,1)S(1)} %constant_dynamic-update-slice_fusion.5.w_ref, ...), custom_call_target="tpu_custom_call" | custom-call | flops 335544320 | bytes 1310720 | tf_op jit(solution)/shard_map/pallas_call | solution.py:287
  21.4 1.6 %collective-permute-start.10 = (bf16[128,512]{1,0:T(8,128)(2,1)S(1)}, bf16[128,512]{1,0:T(8,128)(2,1)S(1)}, u32[]{:S(2)}, u32[]{:S(2)}) collective-permute-start(bf16[128,512]{1,0:T(8,128)(2,1)S(1)} %get-tuple-element.32), channel_id=1, source_target_pairs={{0,1},{1,0},{2,3},{3,2},{4,5},{5,4},{6,7},{7,6},{8,9},{9,8},{10,11... | collective-permute-start | bytes 393224 | tf_op jit(solution)/shard_map/ppermute | solution.py:260
  23.0 0.9 %shard_map.93 = (f32[128,512]{1,0:T(8,128)S(1)}, f32[128,512]{1,0:T(8,128)S(1)}, bf16[128,1024]{1,0:T(8,128)(2,1)S(1)}, f32[128,1024]{1,0:T(8,128)S(1)}) custom-call(bf16[128,384]{1,0:T(8,128)(2,1)S(1)} %get-tuple-element.26.grads, bf16[4096,384]{1,0:T(8,128)(2,1)S(1)} %constant_dynamic-update-slice_fusion.5.w_ref), custom_call_target="tpu_custom_call" | custom-call | flops 301989888 | bytes 2359296 | tf_op jit(solution)/shard_map/pallas_call | solution.py:300
  23.9 0.5 %collective-permute-start.7 = (bf16[128,1024]{1,0:T(8,128)(2,1)S(1)}, bf16[128,1024]{1,0:T(8,128)(2,1)S(1)}, u32[]{:S(2)}, u32[]{:S(2)}) collective-permute-start(bf16[128,1024]{1,0:T(8,128)(2,1)S(1)} %get-tuple-element.28), channel_id=1, source_target_pairs={{0,1},{1,0},{2,3},{3,2},{4,5},{5,4},{6,7},{7,6},{8,9},{9,8},{10,11... | collective-permute-start | bytes 786440 | tf_op jit(solution)/shard_map/ppermute | solution.py:260
  24.4 1.6 %collective-permute-start.8 = (bf16[128,512]{1,0:T(8,128)(2,1)S(1)}, bf16[128,512]{1,0:T(8,128)(2,1)S(1)}, u32[]{:S(2)}, u32[]{:S(2)}) collective-permute-start(bf16[128,512]{1,0:T(8,128)(2,1)S(1)} %get-tuple-element.30), channel_id=1, source_target_pairs={{0,1},{1,0},{2,3},{3,2},{4,5},{5,4},{6,7},{7,6},{8,9},{9,8},{10,11... | collective-permute-start | bytes 393224 | tf_op jit(solution)/shard_map/ppermute | solution.py:260
  26.0 1.6 %collective-permute-done.10 = bf16[128,512]{1,0:T(8,128)(2,1)S(1)} collective-permute-done((bf16[128,512]{1,0:T(8,128)(2,1)S(1)}, bf16[128,512]{1,0:T(8,128)(2,1)S(1)}, u32[]{:S(2)}, u32[]{:S(2)}) %collective-permute-start.10) | collective-permute-done | bytes 131104 | tf_op jit(solution)/shard_map/ppermute | solution.py:260
  27.6 2.7 %collective-permute-start.11 = (bf16[128,512]{1,0:T(8,128)(2,1)S(1)}, bf16[128,512]{1,0:T(8,128)(2,1)S(1)}, u32[]{:S(2)}, u32[]{:S(2)}) collective-permute-start(bf16[128,512]{1,0:T(8,128)(2,1)S(1)} %add_convert_fusion.1), channel_id=1, source_target_pairs={{0,2},{1,3},{2,0},{3,1},{4,6},{5,7},{6,4},{7,5},{8,10},{9,11},{10,... | collective-permute-start | bytes 393224 | tf_op jit(solution)/shard_map/ppermute | solution.py:260
  30.2 8.0 %collective-permute-done.8 = bf16[128,512]{1,0:T(8,128)(2,1)S(1)} collective-permute-done((bf16[128,512]{1,0:T(8,128)(2,1)S(1)}, bf16[128,512]{1,0:T(8,128)(2,1)S(1)}, u32[]{:S(2)}, u32[]{:S(2)}) %collective-permute-start.8) | collective-permute-done | bytes 131104 | tf_op jit(solution)/shard_map/ppermute | solution.py:260
  38.3 1.8 %collective-permute-start.9 = (bf16[128,512]{1,0:T(8,128)(2,1)S(1)}, bf16[128,512]{1,0:T(8,128)(2,1)S(1)}, u32[]{:S(2)}, u32[]{:S(2)}) collective-permute-start(bf16[128,512]{1,0:T(8,128)(2,1)S(1)} %add_convert_fusion.2), channel_id=1, source_target_pairs={{0,2},{1,3},{2,0},{3,1},{4,6},{5,7},{6,4},{7,5},{8,10},{9,11},{10,... | collective-permute-start | bytes 393224 | tf_op jit(solution)/shard_map/ppermute | solution.py:260
  40.0 0.0 collective-permute-done.7
  40.0 0.0 collective-permute-done.11
  40.0 7.0 %collective-permute-done.9 = bf16[128,512]{1,0:T(8,128)(2,1)S(1)} collective-permute-done((bf16[128,512]{1,0:T(8,128)(2,1)S(1)}, bf16[128,512]{1,0:T(8,128)(2,1)S(1)}, u32[]{:S(2)}, u32[]{:S(2)}) %collective-permute-start.9) | collective-permute-done | bytes 131104 | tf_op jit(solution)/shard_map/ppermute | solution.py:260
  47.0 0.8 %add_convert_fusion = bf16[128,1024]{1,0:T(8,128)(2,1)} fusion(f32[128,1024]{1,0:T(8,128)S(1)} %get-tuple-element.27, bf16[128,1024]{1,0:T(8,128)(2,1)S(1)} %collective-permute-done.7, bf16[128,512]{1,0:T(8,128)(2,1)S(1)} %collective-permute-done.11, bf16[128,512]{1,0:T(8,128)(2,1)S(1)} %collective-permute-done.9), kind=kLoop, calls=%fused_computation | loop fusion | flops 1048576 | bytes 1310720 | tf_op jit(solution)/shard_map/convert_element_type | solution.py:314
  (2 shorter events, 0.1 us)
Async XLA Ops:
  3.8 0.7 %copy-start = (f32[128,1]{0,1:T(1,128)S(1)}, f32[128,1]{0,1:T(1,128)}, u32[]{:S(2)}) copy-start(f32[128,1]{0,1:T(1,128)} %param.14) | copy-start | bytes 1540
  4.5 10.8 %copy-start.2 = (bf16[4096,128]{1,0:T(8,128)(2,1)S(1)}, bf16[4096,128]{1,0:T(8,128)(2,1)}, u32[]{:S(2)}) copy-start(bf16[4096,128]{1,0:T(8,128)(2,1)} %param.17) | copy-start | bytes 3145732
  4.7 7.8 %collective-permute-start = (bf16[144,256]{1,0:T(8,128)(2,1)S(1)}, bf16[144,256]{1,0:T(8,128)(2,1)S(1)}, u32[]{:S(2)}, u32[]{:S(2)}) collective-permute-start(bf16[144,256]{1,0:T(8,128)(2,1)S(1)} %get-tuple-element.19), channel_id=1, source_target_pairs={{0,4},{4,0},{8,12},{12,8},{16,20},{20,16},{24,28},{28,24},{1,5},{5... | collective-permute-start | bytes 221192 | tf_op jit(solution)/shard_map/ppermute | solution.py:260
  5.2 10.0 %collective-permute-start.1 = (bf16[144,256]{1,0:T(8,128)(2,1)S(1)}, bf16[144,256]{1,0:T(8,128)(2,1)S(1)}, u32[]{:S(2)}, u32[]{:S(2)}) collective-permute-start(bf16[144,256]{1,0:T(8,128)(2,1)S(1)} %get-tuple-element.20), channel_id=1, source_target_pairs={{0,8},{4,12},{8,0},{12,4},{16,24},{20,28},{24,16},{28,20},{1,9},{5... | collective-permute-start | bytes 221192 | tf_op jit(solution)/shard_map/ppermute | solution.py:260
  7.8 7.8 %collective-permute-start.2 = (bf16[144,256]{1,0:T(8,128)(2,1)S(1)}, bf16[144,256]{1,0:T(8,128)(2,1)S(1)}, u32[]{:S(2)}, u32[]{:S(2)}) collective-permute-start(bf16[144,256]{1,0:T(8,128)(2,1)S(1)} %get-tuple-element.21), channel_id=1, source_target_pairs={{0,12},{4,8},{8,4},{12,0},{16,28},{20,24},{24,20},{28,16},{1,13},{... | collective-permute-start | bytes 221192 | tf_op jit(solution)/shard_map/ppermute | solution.py:260
  7.8 7.8 %collective-permute-start.3 = (bf16[144,256]{1,0:T(8,128)(2,1)S(1)}, bf16[144,256]{1,0:T(8,128)(2,1)S(1)}, u32[]{:S(2)}, u32[]{:S(2)}) collective-permute-start(bf16[144,256]{1,0:T(8,128)(2,1)S(1)} %get-tuple-element.22), channel_id=1, source_target_pairs={{0,16},{4,20},{8,24},{12,28},{16,0},{20,4},{24,8},{28,12},{1,17},{... | collective-permute-start | bytes 221192 | tf_op jit(solution)/shard_map/ppermute | solution.py:260
  9.6 10.7 %copy-start.1 = (f32[128,1]{0,1:T(1,128)S(1)}, f32[128,1]{0,1:T(1,128)}, u32[]{:S(2)}) copy-start(f32[128,1]{0,1:T(1,128)} %param.14) | copy-start | bytes 1540
  9.6 6.0 %collective-permute-start.4 = (bf16[144,256]{1,0:T(8,128)(2,1)S(1)}, bf16[144,256]{1,0:T(8,128)(2,1)S(1)}, u32[]{:S(2)}, u32[]{:S(2)}) collective-permute-start(bf16[144,256]{1,0:T(8,128)(2,1)S(1)} %get-tuple-element.23), channel_id=1, source_target_pairs={{0,20},{4,16},{8,28},{12,24},{16,4},{20,0},{24,12},{28,8},{1,21},{... | collective-permute-start | bytes 221192 | tf_op jit(solution)/shard_map/ppermute | solution.py:260
  12.5 5.5 %collective-permute-start.5 = (bf16[144,256]{1,0:T(8,128)(2,1)S(1)}, bf16[144,256]{1,0:T(8,128)(2,1)S(1)}, u32[]{:S(2)}, u32[]{:S(2)}) collective-permute-start(bf16[144,256]{1,0:T(8,128)(2,1)S(1)} %get-tuple-element.24), channel_id=1, source_target_pairs={{0,24},{4,28},{8,16},{12,20},{16,8},{20,12},{24,0},{28,4},{1,25},{... | collective-permute-start | bytes 221192 | tf_op jit(solution)/shard_map/ppermute | solution.py:260
  15.2 5.1 %collective-permute-start.6 = (bf16[144,256]{1,0:T(8,128)(2,1)S(1)}, bf16[144,256]{1,0:T(8,128)(2,1)S(1)}, u32[]{:S(2)}, u32[]{:S(2)}) collective-permute-start(bf16[144,256]{1,0:T(8,128)(2,1)S(1)} %get-tuple-element.25), channel_id=1, source_target_pairs={{0,28},{4,24},{8,20},{12,16},{16,12},{20,8},{24,4},{28,0},{1,29},{... | collective-permute-start | bytes 221192 | tf_op jit(solution)/shard_map/ppermute | solution.py:260
  21.4 6.2 %collective-permute-start.10 = (bf16[128,512]{1,0:T(8,128)(2,1)S(1)}, bf16[128,512]{1,0:T(8,128)(2,1)S(1)}, u32[]{:S(2)}, u32[]{:S(2)}) collective-permute-start(bf16[128,512]{1,0:T(8,128)(2,1)S(1)} %get-tuple-element.32), channel_id=1, source_target_pairs={{0,1},{1,0},{2,3},{3,2},{4,5},{5,4},{6,7},{7,6},{8,9},{9,8},{10,11... | collective-permute-start | bytes 393224 | tf_op jit(solution)/shard_map/ppermute | solution.py:260
  23.9 16.2 %collective-permute-start.7 = (bf16[128,1024]{1,0:T(8,128)(2,1)S(1)}, bf16[128,1024]{1,0:T(8,128)(2,1)S(1)}, u32[]{:S(2)}, u32[]{:S(2)}) collective-permute-start(bf16[128,1024]{1,0:T(8,128)(2,1)S(1)} %get-tuple-element.28), channel_id=1, source_target_pairs={{0,1},{1,0},{2,3},{3,2},{4,5},{5,4},{6,7},{7,6},{8,9},{9,8},{10,11... | collective-permute-start | bytes 786440 | tf_op jit(solution)/shard_map/ppermute | solution.py:260
  24.4 13.9 %collective-permute-start.8 = (bf16[128,512]{1,0:T(8,128)(2,1)S(1)}, bf16[128,512]{1,0:T(8,128)(2,1)S(1)}, u32[]{:S(2)}, u32[]{:S(2)}) collective-permute-start(bf16[128,512]{1,0:T(8,128)(2,1)S(1)} %get-tuple-element.30), channel_id=1, source_target_pairs={{0,1},{1,0},{2,3},{3,2},{4,5},{5,4},{6,7},{7,6},{8,9},{9,8},{10,11... | collective-permute-start | bytes 393224 | tf_op jit(solution)/shard_map/ppermute | solution.py:260
  27.6 12.5 %collective-permute-start.11 = (bf16[128,512]{1,0:T(8,128)(2,1)S(1)}, bf16[128,512]{1,0:T(8,128)(2,1)S(1)}, u32[]{:S(2)}, u32[]{:S(2)}) collective-permute-start(bf16[128,512]{1,0:T(8,128)(2,1)S(1)} %add_convert_fusion.1), channel_id=1, source_target_pairs={{0,2},{1,3},{2,0},{3,1},{4,6},{5,7},{6,4},{7,5},{8,10},{9,11},{10,... | collective-permute-start | bytes 393224 | tf_op jit(solution)/shard_map/ppermute | solution.py:260
  38.3 8.8 %collective-permute-start.9 = (bf16[128,512]{1,0:T(8,128)(2,1)S(1)}, bf16[128,512]{1,0:T(8,128)(2,1)S(1)}, u32[]{:S(2)}, u32[]{:S(2)}) collective-permute-start(bf16[128,512]{1,0:T(8,128)(2,1)S(1)} %add_convert_fusion.2), channel_id=1, source_target_pairs={{0,2},{1,3},{2,0},{3,1},{4,6},{5,7},{6,4},{7,5},{8,10},{9,11},{10,... | collective-permute-start | bytes 393224 | tf_op jit(solution)/shard_map/ppermute | solution.py:260

commit v6 on v5

--- a/solution.py
+++ b/solution.py
@@ -162,33 +162,40 @@
             out_ref[h, :, at : at + cols] = dot_nt(grads[...], weight).astype(jnp.bfloat16)
 
 
-def split_rows(own_ref, rows):
-    return [own_ref[at * rows : (at + 1) * rows, :] for at in range(5)]
-
-
-def send_kernel(own_ref, n_ref, *hops):
+def send_kernel(q_in, k_in, v_in, g_in, a_in, n_ref, *refs):
+    q_ref, k_ref, v_ref, g_ref, a_ref, sems = refs[-6:]
+    hops = refs[:-6]
     me = lax.axis_index("ctx")
-    rows, width = n_ref.shape[1], own_ref.shape[1]
-    query, key, value, grad, attn = split_rows(own_ref, rows)
-    delta = delta_of(grad, attn)
+    rows, width = q_ref.shape
+    loads = [
+        pltpu.make_async_copy(src, dst, sems.at[at])
+        for at, (src, dst) in enumerate(
+            ((g_in, g_ref), (a_in, a_ref), (k_in, k_ref), (v_in, v_ref), (q_in, q_ref))
+        )
+    ]
+    for load in loads:
+        load.start()
+    for load in loads:
+        load.wait()
+    delta = delta_of(g_ref[...], a_ref[...])
     delta = jnp.sum(jnp.where(diagonal(rows), delta, 0.0), axis=0, keepdims=True)
     row = lax.broadcasted_iota(jnp.int32, (EXTRA, rows), 0)
     extra = jnp.zeros((EXTRA, rows), jnp.float32)
     for at, part in enumerate(pieces_of(n_ref[...]) + pieces_of(delta)):
         extra = jnp.where(row == at, part, extra)
     extra = extra.astype(jnp.bfloat16)
-    for at, hop in enumerate(hops):
-        later = (me ^ (at + 1)) > me
+    for bit, hop in enumerate(hops):
+        later = (me & (1 << bit)) == 0
 
         @pl.when(later)
         def _():
-            hop[:rows, :width] = key
-            hop[:rows, width:] = value
+            hop[:rows, :width] = k_ref[...]
+            hop[:rows, width:] = v_ref[...]
 
         @pl.when(jnp.logical_not(later))
         def _():
-            hop[:rows, :width] = query
-            hop[:rows, width:] = grad
+            hop[:rows, :width] = q_ref[...]
+            hop[:rows, width:] = g_ref[...]
 
         hop[rows:, :width] = extra
         hop[rows:, width:] = jnp.zeros((EXTRA, width), jnp.bfloat16)
@@ -202,17 +209,17 @@
         out_ref[:, at : at + cols] = dot_nt(grads[...], weight).astype(out_ref.dtype)
 
 
-def near_kernel(scale, part, own_ref, n_ref, w_ref, *refs):
+def near_kernel(scale, part, q_ref, k_ref, v_ref, g_ref, a_ref, n_ref, w_ref, *refs):
     grads, front, back = refs[-3:]
     got = refs[:-3]
-    rows, width = n_ref.shape[1], own_ref.shape[1]
+    rows, width = q_ref.shape
     me, head = lax.axis_index("ctx"), lax.axis_index("head")
     exponent = scale * math.log2(math.e)
-    query, key, value, grad, attn = split_rows(own_ref, rows)
+    query, key, value, grad = q_ref[...], k_ref[...], v_ref[...], g_ref[...]
     norm = (1.0 / scale) * jnp.sum(
         jnp.where(diagonal(rows), n_ref[...], 0.0), axis=1, keepdims=True
     )
-    delta = delta_of(grad, attn)
+    delta = delta_of(grad, a_ref[...])
     row_at = lax.broadcasted_iota(jnp.int32, (rows, rows), 0)
     col_at = lax.broadcasted_iota(jnp.int32, (rows, rows), 1)
     probs = jnp.where(col_at <= row_at, jnp.exp2(exponent * (dot_nt(query, key) - norm)), 0.0)
@@ -247,10 +254,14 @@
     project(grads, w_ref, start + part // 2, back)
 
 
-def rest_kernel(part, grads, w_ref, front, back, near, mine):
+def far_kernel(part, grads, w_ref, front, back):
+    start = (lax.axis_index("head") ^ 2) * part
+    project(grads, w_ref, start, front)
+    project(grads, w_ref, start + part // 2, back)
+
+
+def close_kernel(part, grads, w_ref, near, mine):
     head = lax.axis_index("head")
-    project(grads, w_ref, (head ^ 2) * part, front)
-    project(grads, w_ref, (head ^ 2) * part + part // 2, back)
     project(grads, w_ref, (head ^ 1) * part, near)
     project(grads, w_ref, head * part, mine)
 
@@ -266,19 +277,26 @@
     ctx = lax.axis_size("ctx")
     part = depth // lax.axis_size("head")
     vmem = pl.BlockSpec(memory_space=pltpu.VMEM)
+    hbm = pl.BlockSpec(memory_space=pl.ANY)
     params = pltpu.CompilerParams(vmem_limit_bytes=32 * MIB)
     hop = jax.ShapeDtypeStruct((rows + EXTRA, 2 * width), jnp.bfloat16)
-    norm = own[-1]
-    mine = jnp.concatenate(own[:-1], axis=0)
-    weight = jnp.concatenate(weights, axis=1)
+    bits = (ctx - 1).bit_length()
     sent = pl.pallas_call(
         send_kernel,
-        out_shape=[hop] * (ctx - 1),
-        in_specs=[vmem] * 2,
-        out_specs=[vmem] * (ctx - 1),
-        compiler_params=params,
-    )(mine, norm)
-    got = {at: swap(sent[at - 1], "ctx", at) for at in range(ctx - 1, 0, -1)}
+        out_shape=[hop] * bits,
+        in_specs=[hbm] * 5 + [vmem],
+        out_specs=[vmem] * bits,
+        scratch_shapes=[pltpu.VMEM((rows, width), jnp.bfloat16)] * 5
+        + [pltpu.SemaphoreType.DMA((5,))],
+        compiler_params=pltpu.CompilerParams(vmem_limit_bytes=60 * MIB),
+    )(*own)
+    got = {}
+    for at in range(ctx - 1, 0, -1):
+        got[at] = swap(sent[at.bit_length() - 1], "ctx", at)
+    early = tuple(got[at] for at in range(ctx - 1, ctx // 2, -1))
+    early, weights = lax.optimization_barrier((early, weights))
+    got.update(zip(range(ctx - 1, ctx // 2, -1), early))
+    weight = jnp.concatenate(weights, axis=1)
     got = [got[at] for at in range(1, ctx)]
     half_low = jax.ShapeDtypeStruct((rows, part // 2), jnp.bfloat16)
     half = jax.ShapeDtypeStruct((rows, part // 2), jnp.float32)
@@ -287,7 +305,7 @@
     grads, front, back = pl.pallas_call(
         functools.partial(near_kernel, scale, part),
         out_shape=[jax.ShapeDtypeStruct((rows, 3 * width), jnp.bfloat16), half_low, half_low],
-        in_specs=[vmem] * (ctx + 2),
+        in_specs=[vmem] * (ctx + 6),
         out_specs=[vmem] * 3,
         compiler_params=params,
         cost_estimate=pl.CostEstimate(
@@ -295,18 +313,24 @@
             bytes_accessed=4 * rows * ctx * width + 6 * part * width,
             transcendentals=rows * rows * ctx,
         ),
-    )(mine, norm, weight, *got)
+    )(*own, weight, *got)
     front, back = swap(front, "head", 1), swap(back, "head", 1)
-    two_front, two_back, near, total = pl.pallas_call(
-        functools.partial(rest_kernel, part),
-        out_shape=[half, half, low, full],
-        in_specs=[vmem] * 2,
-        out_specs=[vmem] * 4,
-        compiler_params=params,
-        cost_estimate=pl.CostEstimate(
-            flops=18 * rows * width * part, bytes_accessed=18 * part * width, transcendentals=0
-        ),
-    )(grads, weight)
+    def projected(kernel, outs, operands):
+        count = sum(out.shape[1] for out in outs)
+        return pl.pallas_call(
+            functools.partial(kernel, part),
+            out_shape=outs,
+            in_specs=[vmem] * 2,
+            out_specs=[vmem] * 2,
+            compiler_params=params,
+            cost_estimate=pl.CostEstimate(
+                flops=6 * rows * width * count, bytes_accessed=6 * count * width, transcendentals=0
+            ),
+        )(*operands)
+
+    two_front, two_back = projected(far_kernel, [half, half], (grads, weight))
+    near, total = projected(close_kernel, [low, full], (grads, weight))
+    near, back = lax.optimization_barrier((near, back))
     front = swap((two_front + front.astype(jnp.float32)).astype(jnp.bfloat16), "head", 2)
     back = swap((two_back + back.astype(jnp.float32)).astype(jnp.bfloat16), "head", 2)
     near = swap(near, "head", 1)

time: 48.4 us -> 39.1 us (0.81)
  waiting for transfers between devices: 21.3 us -> 12.8 us
  local copies, waits for them, and re-layouts: 7.62 us -> 3.16 us
  Pallas kernels: 2.1 us -> 4.49 us
  starting transfers between devices: 15.9 us -> 17.3 us
    ppermute x12, waiting for transfers between devices: 21.3 us -> 12.8 us  [swap(): return lax.ppermute(value, axis, [(at, at ^ offset) for at in range(size)])]
    unnamed x12 -> x16, local copies, waits for them, and re-layouts: 6.61 us -> 2.91 us
    pallas_call x2 -> x3, Pallas kernels: 1.05 us -> 3.43 us  [the longest x1 2.42 us: near_body(): pl.pallas_call(send_kernel, out_shape=[hop] * bits, in_specs=[hbm] * 5 +...]
    ppermute x12, starting transfers between devices: 15.9 us -> 17.3 us  [swap(): return lax.ppermute(value, axis, [(at, at ^ offset) for at in range(size)])]
    concatenate x1 -> x0, local copies, waits for them, and re-layouts: 0.77 us -> none  [near_body(): mine = jnp.concatenate(own[:-1], axis=0)]
  transfers between devices with their start and end apart: 12 -> 12, of which waited for: 5 -> 6; matrix products, arithmetic and copies ran while one was open for 7% -> 8% of each run, Pallas kernels for 2% -> 3%
where the time goes in v6:
time: 39.1 us; the launch traced here: 38.8 us
  starting transfers between devices  17.3 us (44%)
  waiting for transfers between devices  12.8 us (33%)
  Pallas kernels  4.49 us (11%)
  local copies, waits for them, and re-layouts  3.16 us (8%)
  other arithmetic  0.86 us (2%)
    ppermute x12, starting transfers between devices, swap(): return lax.ppermute(value, axis, [(at, at ^ offset) for at in range(size)])  17.3 us
    ppermute x12, waiting for transfers between devices, swap(): return lax.ppermute(value, axis, [(at, at ^ offset) for at in range(size)])  12.8 us
    unnamed x16, local copies, waits for them, and re-layouts  2.91 us
    pallas_call x1, Pallas kernels, near_body(): pl.pallas_call(send_kernel, out_shape=[hop] * bits, in_specs=[hbm] * 5 +...  2.42 us
    pallas_call x1, Pallas kernels, near_body(): pl.pallas_call(functools.partial(near_kernel, scale, part), out_shape=[ja...  1.06 us
    pallas_call x2, Pallas kernels, projected(): pl.pallas_call(functools.partial(kernel, part), out_shape=outs, in_specs=...  1.01 us
    convert_element_type x1, other arithmetic, near_body(): return (total + near.astype(jnp.float32) + far_sum).astype(jnp.bfloat16)  0.8 us
  transfers between devices with their start and end apart: 12, of which 6 were waited for; matrix products, arithmetic and copies ran while one was open for 8% of the time, Pallas kernels for 3%

profile of v6, /device:TPU:0, one launch (start us, length us, event | category | flops | bytes accessed | tf_op | source)
XLA Modules:
  0.0 38.8 jit_solution(7046337202577018026)
XLA Ops:
  0.0 0.0 copy-start.6
  0.0 2.4 %shard_map.91 = (bf16[144,256]{1,0:T(8,128)(2,1)}, bf16[144,256]{1,0:T(8,128)(2,1)}, bf16[144,256]{1,0:T(8,128)(2,1)}) custom-call(bf16[128,128]{1,0:T(8,128)(2,1)} %q_ref.1, bf16[128,128]{1,0:T(8,128)(2,1)} %k_ref.1, bf16[128,128]{1,0:T(8,128)(2,1)} %v_ref.1, bf16[128,128]{1,0:T(8,128)(2,1)} %g_ref.1, bf16[128,128]{1,0:T(8,128)(2,1)} %a_ref.1, f32[1,128]{1,0:T(1,128)} %bitcast.1), custom_call_target="tpu_custom_call" | custom-call | tf_op jit(solution)/shard_map/pallas_call | solution.py:284
  2.4 3.4 %collective-permute-start = (bf16[144,256]{1,0:T(8,128)(2,1)}, bf16[144,256]{1,0:T(8,128)(2,1)S(1)}, u32[]{:S(2)}, u32[]{:S(2)}) collective-permute-start(bf16[144,256]{1,0:T(8,128)(2,1)} %get-tuple-element.23), channel_id=1, source_target_pairs={{0,28},{4,24},{8,20},{12,16},{16,12},{20,8},{24,4},{28,0},{1,29},{... | collective-permute-start | bytes 221192 | tf_op jit(solution)/shard_map/ppermute | solution.py:271
  5.8 0.6 %collective-permute-start.1 = (bf16[144,256]{1,0:T(8,128)(2,1)}, bf16[144,256]{1,0:T(8,128)(2,1)S(1)}, u32[]{:S(2)}, u32[]{:S(2)}) collective-permute-start(bf16[144,256]{1,0:T(8,128)(2,1)} %get-tuple-element.23), channel_id=1, source_target_pairs={{0,24},{4,28},{8,16},{12,20},{16,8},{20,12},{24,0},{28,4},{1,25},{... | collective-permute-start | bytes 221192 | tf_op jit(solution)/shard_map/ppermute | solution.py:271
  6.5 1.4 %collective-permute-start.2 = (bf16[144,256]{1,0:T(8,128)(2,1)}, bf16[144,256]{1,0:T(8,128)(2,1)S(1)}, u32[]{:S(2)}, u32[]{:S(2)}) collective-permute-start(bf16[144,256]{1,0:T(8,128)(2,1)} %get-tuple-element.23), channel_id=1, source_target_pairs={{0,20},{4,16},{8,28},{12,24},{16,4},{20,0},{24,12},{28,8},{1,21},{... | collective-permute-start | bytes 221192 | tf_op jit(solution)/shard_map/ppermute | solution.py:271
  7.8 0.3 collective-permute-start.6
  8.1 1.7 %collective-permute-start.4 = (bf16[144,256]{1,0:T(8,128)(2,1)}, bf16[144,256]{1,0:T(8,128)(2,1)S(1)}, u32[]{:S(2)}, u32[]{:S(2)}) collective-permute-start(bf16[144,256]{1,0:T(8,128)(2,1)} %get-tuple-element.28), channel_id=1, source_target_pairs={{0,8},{4,12},{8,0},{12,4},{16,24},{20,28},{24,16},{28,20},{1,9},{5... | collective-permute-start | bytes 221192 | tf_op jit(solution)/shard_map/ppermute | solution.py:271
  9.8 0.0 collective-permute-done.refs_6_
  9.8 1.0 %collective-permute-start.5 = (bf16[144,256]{1,0:T(8,128)(2,1)}, bf16[144,256]{1,0:T(8,128)(2,1)S(1)}, u32[]{:S(2)}, u32[]{:S(2)}) collective-permute-start(bf16[144,256]{1,0:T(8,128)(2,1)} %get-tuple-element.28), channel_id=1, source_target_pairs={{0,12},{4,8},{8,4},{12,0},{16,28},{20,24},{24,20},{28,16},{1,13},{... | collective-permute-start | bytes 221192 | tf_op jit(solution)/shard_map/ppermute | solution.py:271
  10.8 1.1 %collective-permute-done.1.refs_5_ = bf16[144,256]{1,0:T(8,128)(2,1)S(1)} collective-permute-done((bf16[144,256]{1,0:T(8,128)(2,1)}, bf16[144,256]{1,0:T(8,128)(2,1)S(1)}, u32[]{:S(2)}, u32[]{:S(2)}) %collective-permute-start.1) | collective-permute-done | bytes 73760 | tf_op jit(solution)/shard_map/ppermute | solution.py:271
  11.9 0.0 copy-start
  11.9 0.0 copy-start.1
  11.9 0.0 copy-start.2
  11.9 0.0 copy-start.3
  11.9 0.0 copy-start.4
  11.9 0.0 copy-start.5
  11.9 0.1 collective-permute-start.3
  12.0 0.6 %collective-permute-done.2.refs_4_ = bf16[144,256]{1,0:T(8,128)(2,1)S(1)} collective-permute-done((bf16[144,256]{1,0:T(8,128)(2,1)}, bf16[144,256]{1,0:T(8,128)(2,1)S(1)}, u32[]{:S(2)}, u32[]{:S(2)}) %collective-permute-start.2) | collective-permute-done | bytes 73760 | tf_op jit(solution)/shard_map/ppermute | solution.py:271
  12.6 1.4 %constant_dynamic-update-slice_fusion.2 = bf16[4096,384]{1,0:T(8,128)(2,1)S(1)} fusion(bf16[4096,128]{1,0:T(8,128)(2,1)} %param.15), kind=kLoop, calls=%fused_computation.5 | loop fusion | bytes 2097152
  14.0 1.5 %constant_dynamic-update-slice_fusion.1 = bf16[4096,384]{1,0:T(8,128)(2,1)S(1)} fusion(bf16[4096,384]{1,0:T(8,128)(2,1)S(1)} %constant_dynamic-update-slice_fusion.2, bf16[4096,128]{1,0:T(8,128)(2,1)} %param.16), kind=kLoop, calls=%fused_computation.4 | loop fusion | bytes 2097152
  15.5 0.0 copy-done.6
  15.5 0.2 constant_dynamic-update-slice_fusion.w_ref
  15.8 0.0 collective-permute-done.6.refs_3_
  15.8 0.0 collective-permute-done.4.refs_1_
  15.8 0.0 collective-permute-done.5.refs_2_
  15.8 0.0 collective-permute-done.3.refs_0_
  15.8 0.0 copy-done
  15.8 0.0 copy-done.1
  15.8 0.0 copy-done.2
  15.8 0.0 copy-done.3
  15.8 0.0 copy-done.4
  15.8 0.0 copy-done.5
  15.9 1.1 %shard_map.92 = (bf16[128,384]{1,0:T(8,128)(2,1)S(1)}, bf16[128,512]{1,0:T(8,128)(2,1)S(1)}, bf16[128,512]{1,0:T(8,128)(2,1)S(1)}) custom-call(bf16[128,128]{1,0:T(8,128)(2,1)S(1)} %copy-done, bf16[128,128]{1,0:T(8,128)(2,1)S(1)} %copy-done.1, bf16[128,128]{1,0:T(8,128)(2,1)S(1)} %copy-done.2, bf16[128,128]{1,0:T(8,128)(2,1)S(1)} %copy-done.3, ...), custom_call_target="tpu_custom_call" | custom-call | flops 335544320 | bytes 1310720 | tf_op jit(solution)/shard_map/pallas_call | solution.py:305
  16.9 1.5 %collective-permute-start.9 = (bf16[128,512]{1,0:T(8,128)(2,1)S(1)}, bf16[128,512]{1,0:T(8,128)(2,1)S(1)}, u32[]{:S(2)}, u32[]{:S(2)}) collective-permute-start(bf16[128,512]{1,0:T(8,128)(2,1)S(1)} %get-tuple-element.38), channel_id=1, source_target_pairs={{0,1},{1,0},{2,3},{3,2},{4,5},{5,4},{6,7},{7,6},{8,9},{9,8},{10,11... | collective-permute-start | bytes 393224 | tf_op jit(solution)/shard_map/ppermute | solution.py:271
  18.5 0.6 %collective-permute-start.7 = (bf16[128,512]{1,0:T(8,128)(2,1)S(1)}, bf16[128,512]{1,0:T(8,128)(2,1)S(1)}, u32[]{:S(2)}, u32[]{:S(2)}) collective-permute-start(bf16[128,512]{1,0:T(8,128)(2,1)S(1)} %get-tuple-element.35), channel_id=1, source_target_pairs={{0,1},{1,0},{2,3},{3,2},{4,5},{5,4},{6,7},{7,6},{8,9},{9,8},{10,11... | collective-permute-start | bytes 393224 | tf_op jit(solution)/shard_map/ppermute | solution.py:271
  19.0 0.4 shard_map.94
  19.4 0.6 %shard_map.93 = (bf16[128,1024]{1,0:T(8,128)(2,1)S(1)}, f32[128,1024]{1,0:T(8,128)S(1)}) custom-call(bf16[128,384]{1,0:T(8,128)(2,1)S(1)} %get-tuple-element.32.grads, bf16[4096,384]{1,0:T(8,128)(2,1)S(1)} %constant_dynamic-update-slice_fusion.w_ref), custom_call_target="tpu_custom_call" | custom-call | flops 201326592 | bytes 1572864 | tf_op jit(solution)/shard_map/pallas_call | solution.py:320
  20.1 3.2 %collective-permute-done.9 = bf16[128,512]{1,0:T(8,128)(2,1)S(1)} collective-permute-done((bf16[128,512]{1,0:T(8,128)(2,1)S(1)}, bf16[128,512]{1,0:T(8,128)(2,1)S(1)}, u32[]{:S(2)}, u32[]{:S(2)}) %collective-permute-start.9) | collective-permute-done | bytes 131104 | tf_op jit(solution)/shard_map/ppermute | solution.py:271
  23.3 2.6 %collective-permute-start.10 = (bf16[128,512]{1,0:T(8,128)(2,1)S(1)}, bf16[128,512]{1,0:T(8,128)(2,1)S(1)}, u32[]{:S(2)}, u32[]{:S(2)}) collective-permute-start(bf16[128,512]{1,0:T(8,128)(2,1)S(1)} %add_convert_fusion.2), channel_id=1, source_target_pairs={{0,2},{1,3},{2,0},{3,1},{4,6},{5,7},{6,4},{7,5},{8,10},{9,11},{10,... | collective-permute-start | bytes 393224 | tf_op jit(solution)/shard_map/ppermute | solution.py:271
  25.9 0.0 collective-permute-done.7
  25.9 1.6 %collective-permute-start.8 = (bf16[128,1024]{1,0:T(8,128)(2,1)S(1)}, bf16[128,1024]{1,0:T(8,128)(2,1)S(1)}, u32[]{:S(2)}, u32[]{:S(2)}) collective-permute-start(bf16[128,1024]{1,0:T(8,128)(2,1)S(1)} %get-tuple-element.36), channel_id=1, source_target_pairs={{0,1},{1,0},{2,3},{3,2},{4,5},{5,4},{6,7},{7,6},{8,9},{9,8},{10,11... | collective-permute-start | bytes 786440 | tf_op jit(solution)/shard_map/ppermute | solution.py:271
  27.5 2.6 %collective-permute-start.11 = (bf16[128,512]{1,0:T(8,128)(2,1)S(1)}, bf16[128,512]{1,0:T(8,128)(2,1)S(1)}, u32[]{:S(2)}, u32[]{:S(2)}) collective-permute-start(bf16[128,512]{1,0:T(8,128)(2,1)S(1)} %add_convert_fusion.1), channel_id=1, source_target_pairs={{0,2},{1,3},{2,0},{3,1},{4,6},{5,7},{6,4},{7,5},{8,10},{9,11},{10,... | collective-permute-start | bytes 393224 | tf_op jit(solution)/shard_map/ppermute | solution.py:271
  30.1 3.4 %collective-permute-done.10 = bf16[128,512]{1,0:T(8,128)(2,1)S(1)} collective-permute-done((bf16[128,512]{1,0:T(8,128)(2,1)S(1)}, bf16[128,512]{1,0:T(8,128)(2,1)S(1)}, u32[]{:S(2)}, u32[]{:S(2)}) %collective-permute-start.10) | collective-permute-done | bytes 131104 | tf_op jit(solution)/shard_map/ppermute | solution.py:271
  33.5 3.5 %collective-permute-done.11 = bf16[128,512]{1,0:T(8,128)(2,1)S(1)} collective-permute-done((bf16[128,512]{1,0:T(8,128)(2,1)S(1)}, bf16[128,512]{1,0:T(8,128)(2,1)S(1)}, u32[]{:S(2)}, u32[]{:S(2)}) %collective-permute-start.11) | collective-permute-done | bytes 131104 | tf_op jit(solution)/shard_map/ppermute | solution.py:271
  37.0 1.0 %collective-permute-done.8 = bf16[128,1024]{1,0:T(8,128)(2,1)S(1)} collective-permute-done((bf16[128,1024]{1,0:T(8,128)(2,1)S(1)}, bf16[128,1024]{1,0:T(8,128)(2,1)S(1)}, u32[]{:S(2)}, u32[]{:S(2)}) %collective-permute-start.8) | collective-permute-done | bytes 262176 | tf_op jit(solution)/shard_map/ppermute | solution.py:271
  38.0 0.8 %add_convert_fusion = bf16[128,1024]{1,0:T(8,128)(2,1)} fusion(f32[128,1024]{1,0:T(8,128)S(1)} %get-tuple-element.33, bf16[128,1024]{1,0:T(8,128)(2,1)S(1)} %collective-permute-done.8, bf16[128,512]{1,0:T(8,128)(2,1)S(1)} %collective-permute-done.11, bf16[128,512]{1,0:T(8,128)(2,1)S(1)} %collective-permute-done.10), kind=kLoop, calls=%fused_computation | loop fusion | flops 1048576 | bytes 1310720 | tf_op jit(solution)/shard_map/convert_element_type | solution.py:338
  (2 shorter events, 0.1 us)
Async XLA Ops:
  0.0 15.5 %copy-start.6 = (bf16[4096,128]{1,0:T(8,128)(2,1)S(1)}, bf16[4096,128]{1,0:T(8,128)(2,1)}, u32[]{:S(2)}) copy-start(bf16[4096,128]{1,0:T(8,128)(2,1)} %param.17) | copy-start | bytes 3145732
  2.4 7.4 %collective-permute-start = (bf16[144,256]{1,0:T(8,128)(2,1)}, bf16[144,256]{1,0:T(8,128)(2,1)S(1)}, u32[]{:S(2)}, u32[]{:S(2)}) collective-permute-start(bf16[144,256]{1,0:T(8,128)(2,1)} %get-tuple-element.23), channel_id=1, source_target_pairs={{0,28},{4,24},{8,20},{12,16},{16,12},{20,8},{24,4},{28,0},{1,29},{... | collective-permute-start | bytes 221192 | tf_op jit(solution)/shard_map/ppermute | solution.py:271
  5.8 6.1 %collective-permute-start.1 = (bf16[144,256]{1,0:T(8,128)(2,1)}, bf16[144,256]{1,0:T(8,128)(2,1)S(1)}, u32[]{:S(2)}, u32[]{:S(2)}) collective-permute-start(bf16[144,256]{1,0:T(8,128)(2,1)} %get-tuple-element.23), channel_id=1, source_target_pairs={{0,24},{4,28},{8,16},{12,20},{16,8},{20,12},{24,0},{28,4},{1,25},{... | collective-permute-start | bytes 221192 | tf_op jit(solution)/shard_map/ppermute | solution.py:271
  6.5 6.1 %collective-permute-start.2 = (bf16[144,256]{1,0:T(8,128)(2,1)}, bf16[144,256]{1,0:T(8,128)(2,1)S(1)}, u32[]{:S(2)}, u32[]{:S(2)}) collective-permute-start(bf16[144,256]{1,0:T(8,128)(2,1)} %get-tuple-element.23), channel_id=1, source_target_pairs={{0,20},{4,16},{8,28},{12,24},{16,4},{20,0},{24,12},{28,8},{1,21},{... | collective-permute-start | bytes 221192 | tf_op jit(solution)/shard_map/ppermute | solution.py:271
  7.8 7.9 %collective-permute-start.6 = (bf16[144,256]{1,0:T(8,128)(2,1)}, bf16[144,256]{1,0:T(8,128)(2,1)S(1)}, u32[]{:S(2)}, u32[]{:S(2)}) collective-permute-start(bf16[144,256]{1,0:T(8,128)(2,1)} %get-tuple-element.23), channel_id=1, source_target_pairs={{0,16},{4,20},{8,24},{12,28},{16,0},{20,4},{24,8},{28,12},{1,17},{... | collective-permute-start | bytes 221192 | tf_op jit(solution)/shard_map/ppermute | solution.py:271
  8.1 7.6 %collective-permute-start.4 = (bf16[144,256]{1,0:T(8,128)(2,1)}, bf16[144,256]{1,0:T(8,128)(2,1)S(1)}, u32[]{:S(2)}, u32[]{:S(2)}) collective-permute-start(bf16[144,256]{1,0:T(8,128)(2,1)} %get-tuple-element.28), channel_id=1, source_target_pairs={{0,8},{4,12},{8,0},{12,4},{16,24},{20,28},{24,16},{28,20},{1,9},{5... | collective-permute-start | bytes 221192 | tf_op jit(solution)/shard_map/ppermute | solution.py:271
  9.8 6.0 %collective-permute-start.5 = (bf16[144,256]{1,0:T(8,128)(2,1)}, bf16[144,256]{1,0:T(8,128)(2,1)S(1)}, u32[]{:S(2)}, u32[]{:S(2)}) collective-permute-start(bf16[144,256]{1,0:T(8,128)(2,1)} %get-tuple-element.28), channel_id=1, source_target_pairs={{0,12},{4,8},{8,4},{12,0},{16,28},{20,24},{24,20},{28,16},{1,13},{... | collective-permute-start | bytes 221192 | tf_op jit(solution)/shard_map/ppermute | solution.py:271
  11.9 3.9 %copy-start = (bf16[128,128]{1,0:T(8,128)(2,1)S(1)}, bf16[128,128]{1,0:T(8,128)(2,1)}, u32[]{:S(2)}) copy-start(bf16[128,128]{1,0:T(8,128)(2,1)} %q_ref.1) | copy-start | bytes 98308
  11.9 3.9 %copy-start.1 = (bf16[128,128]{1,0:T(8,128)(2,1)S(1)}, bf16[128,128]{1,0:T(8,128)(2,1)}, u32[]{:S(2)}) copy-start(bf16[128,128]{1,0:T(8,128)(2,1)} %k_ref.1) | copy-start | bytes 98308
  11.9 3.9 %copy-start.2 = (bf16[128,128]{1,0:T(8,128)(2,1)S(1)}, bf16[128,128]{1,0:T(8,128)(2,1)}, u32[]{:S(2)}) copy-start(bf16[128,128]{1,0:T(8,128)(2,1)} %v_ref.1) | copy-start | bytes 98308
  11.9 3.9 %copy-start.3 = (bf16[128,128]{1,0:T(8,128)(2,1)S(1)}, bf16[128,128]{1,0:T(8,128)(2,1)}, u32[]{:S(2)}) copy-start(bf16[128,128]{1,0:T(8,128)(2,1)} %g_ref.1) | copy-start | bytes 98308
  11.9 3.9 %copy-start.4 = (bf16[128,128]{1,0:T(8,128)(2,1)S(1)}, bf16[128,128]{1,0:T(8,128)(2,1)}, u32[]{:S(2)}) copy-start(bf16[128,128]{1,0:T(8,128)(2,1)} %a_ref.1) | copy-start | bytes 98308
  11.9 3.9 %copy-start.5 = (f32[128,1]{0,1:T(1,128)S(1)}, f32[128,1]{0,1:T(1,128)}, u32[]{:S(2)}) copy-start(f32[128,1]{0,1:T(1,128)} %param.14) | copy-start | bytes 1540
  11.9 3.9 %collective-permute-start.3 = (bf16[144,256]{1,0:T(8,128)(2,1)}, bf16[144,256]{1,0:T(8,128)(2,1)S(1)}, u32[]{:S(2)}, u32[]{:S(2)}) collective-permute-start(bf16[144,256]{1,0:T(8,128)(2,1)} %get-tuple-element.27), channel_id=1, source_target_pairs={{0,4},{4,0},{8,12},{12,8},{16,20},{20,16},{24,28},{28,24},{1,5},{5... | collective-permute-start | bytes 221192 | tf_op jit(solution)/shard_map/ppermute | solution.py:271
  16.9 6.4 %collective-permute-start.9 = (bf16[128,512]{1,0:T(8,128)(2,1)S(1)}, bf16[128,512]{1,0:T(8,128)(2,1)S(1)}, u32[]{:S(2)}, u32[]{:S(2)}) collective-permute-start(bf16[128,512]{1,0:T(8,128)(2,1)S(1)} %get-tuple-element.38), channel_id=1, source_target_pairs={{0,1},{1,0},{2,3},{3,2},{4,5},{5,4},{6,7},{7,6},{8,9},{9,8},{10,11... | collective-permute-start | bytes 393224 | tf_op jit(solution)/shard_map/ppermute | solution.py:271
  18.5 7.5 %collective-permute-start.7 = (bf16[128,512]{1,0:T(8,128)(2,1)S(1)}, bf16[128,512]{1,0:T(8,128)(2,1)S(1)}, u32[]{:S(2)}, u32[]{:S(2)}) collective-permute-start(bf16[128,512]{1,0:T(8,128)(2,1)S(1)} %get-tuple-element.35), channel_id=1, source_target_pairs={{0,1},{1,0},{2,3},{3,2},{4,5},{5,4},{6,7},{7,6},{8,9},{9,8},{10,11... | collective-permute-start | bytes 393224 | tf_op jit(solution)/shard_map/ppermute | solution.py:271
  23.3 10.2 %collective-permute-start.10 = (bf16[128,512]{1,0:T(8,128)(2,1)S(1)}, bf16[128,512]{1,0:T(8,128)(2,1)S(1)}, u32[]{:S(2)}, u32[]{:S(2)}) collective-permute-start(bf16[128,512]{1,0:T(8,128)(2,1)S(1)} %add_convert_fusion.2), channel_id=1, source_target_pairs={{0,2},{1,3},{2,0},{3,1},{4,6},{5,7},{6,4},{7,5},{8,10},{9,11},{10,... | collective-permute-start | bytes 393224 | tf_op jit(solution)/shard_map/ppermute | solution.py:271
  25.9 12.0 %collective-permute-start.8 = (bf16[128,1024]{1,0:T(8,128)(2,1)S(1)}, bf16[128,1024]{1,0:T(8,128)(2,1)S(1)}, u32[]{:S(2)}, u32[]{:S(2)}) collective-permute-start(bf16[128,1024]{1,0:T(8,128)(2,1)S(1)} %get-tuple-element.36), channel_id=1, source_target_pairs={{0,1},{1,0},{2,3},{3,2},{4,5},{5,4},{6,7},{7,6},{8,9},{9,8},{10,11... | collective-permute-start | bytes 786440 | tf_op jit(solution)/shard_map/ppermute | solution.py:271
  27.5 9.5 %collective-permute-start.11 = (bf16[128,512]{1,0:T(8,128)(2,1)S(1)}, bf16[128,512]{1,0:T(8,128)(2,1)S(1)}, u32[]{:S(2)}, u32[]{:S(2)}) collective-permute-start(bf16[128,512]{1,0:T(8,128)(2,1)S(1)} %add_convert_fusion.1), channel_id=1, source_target_pairs={{0,2},{1,3},{2,0},{3,1},{4,6},{5,7},{6,4},{7,5},{8,10},{9,11},{10,... | collective-permute-start | bytes 393224 | tf_op jit(solution)/shard_map/ppermute | solution.py:271

commit v7 on v6

--- a/solution.py
+++ b/solution.py
@@ -162,19 +162,39 @@
             out_ref[h, :, at : at + cols] = dot_nt(grads[...], weight).astype(jnp.bfloat16)
 
 
-def send_kernel(q_in, k_in, v_in, g_in, a_in, n_ref, *refs):
-    q_ref, k_ref, v_ref, g_ref, a_ref, sems = refs[-6:]
-    hops = refs[:-6]
+def send_kernel(q_in, k_in, v_in, g_in, a_in, n_in, *refs):
+    g_ref, a_ref, n_ref, extra_ref, in_sems, row_sems, extra_sems = refs[-7:]
+    hops = refs[:-7]
     me = lax.axis_index("ctx")
-    rows, width = q_ref.shape
+    rows, width = g_ref.shape
     loads = [
-        pltpu.make_async_copy(src, dst, sems.at[at])
-        for at, (src, dst) in enumerate(
-            ((g_in, g_ref), (a_in, a_ref), (k_in, k_ref), (v_in, v_ref), (q_in, q_ref))
-        )
+        pltpu.make_async_copy(src, dst, in_sems.at[at])
+        for at, (src, dst) in enumerate(((g_in, g_ref), (a_in, a_ref), (n_in, n_ref)))
     ]
     for load in loads:
         load.start()
+
+    def moves(bit, first, second):
+        return [
+            pltpu.make_async_copy(
+                src, hops[bit].at[:rows, at * width : (at + 1) * width], row_sems.at[2 * bit + at]
+            )
+            for at, src in enumerate((first, second))
+        ]
+
+    for bit in range(len(hops)):
+        later = (me & (1 << bit)) == 0
+
+        @pl.when(later)
+        def _():
+            for move in moves(bit, k_in, v_in):
+                move.start()
+
+        @pl.when(jnp.logical_not(later))
+        def _():
+            for move in moves(bit, q_in, g_in):
+                move.start()
+
     for load in loads:
         load.wait()
     delta = delta_of(g_ref[...], a_ref[...])
@@ -183,35 +203,33 @@
     extra = jnp.zeros((EXTRA, rows), jnp.float32)
     for at, part in enumerate(pieces_of(n_ref[...]) + pieces_of(delta)):
         extra = jnp.where(row == at, part, extra)
-    extra = extra.astype(jnp.bfloat16)
-    for bit, hop in enumerate(hops):
-        later = (me & (1 << bit)) == 0
-
-        @pl.when(later)
-        def _():
-            hop[:rows, :width] = k_ref[...]
-            hop[:rows, width:] = v_ref[...]
-
-        @pl.when(jnp.logical_not(later))
-        def _():
-            hop[:rows, :width] = q_ref[...]
-            hop[:rows, width:] = g_ref[...]
-
-        hop[rows:, :width] = extra
-        hop[rows:, width:] = jnp.zeros((EXTRA, width), jnp.bfloat16)
+    extra_ref[:, :width] = extra.astype(jnp.bfloat16)
+    extra_ref[:, width:] = jnp.zeros((EXTRA, width), jnp.bfloat16)
+    tails = [
+        pltpu.make_async_copy(extra_ref, hop.at[rows:, :], extra_sems.at[bit])
+        for bit, hop in enumerate(hops)
+    ]
+    for tail in tails:
+        tail.start()
+    for bit in range(len(hops)):
+        for move in moves(bit, k_in, v_in):
+            move.wait()
+    for tail in tails:
+        tail.wait()
 
 
 def project(grads, w_ref, start, out_ref):
     part = out_ref.shape[1]
     cols = math.gcd(part, 512)
     for at in range(0, part, cols):
-        weight = w_ref[pl.ds(pl.multiple_of(start + at, cols), cols), :]
+        span = pl.ds(pl.multiple_of(start + at, cols), cols)
+        weight = jnp.concatenate([w_ref[i, span, :] for i in range(w_ref.shape[0])], axis=1)
         out_ref[:, at : at + cols] = dot_nt(grads[...], weight).astype(out_ref.dtype)
 
 
 def near_kernel(scale, part, q_ref, k_ref, v_ref, g_ref, a_ref, n_ref, w_ref, *refs):
-    grads, front, back = refs[-3:]
-    got = refs[:-3]
+    grads, front = refs[-2:]
+    got = refs[:-2]
     rows, width = q_ref.shape
     me, head = lax.axis_index("ctx"), lax.axis_index("head")
     exponent = scale * math.log2(math.e)
@@ -249,13 +267,13 @@
     grads[:, :width] = (scale * (query_sum + both_sum[:rows])).astype(jnp.bfloat16)
     grads[:, width : 2 * width] = (scale * (key_sum + both_sum[rows:])).astype(jnp.bfloat16)
     grads[:, 2 * width :] = value_sum.astype(jnp.bfloat16)
-    start = (head ^ 3) * part
-    project(grads, w_ref, start, front)
-    project(grads, w_ref, start + part // 2, back)
-
-
-def far_kernel(part, grads, w_ref, front, back):
-    start = (lax.axis_index("head") ^ 2) * part
+    project(grads, w_ref, (head ^ 3) * part, front)
+
+
+def far_kernel(part, grads, w_ref, last, front, back):
+    head = lax.axis_index("head")
+    project(grads, w_ref, (head ^ 3) * part + part // 2, last)
+    start = (head ^ 2) * part
     project(grads, w_ref, start, front)
     project(grads, w_ref, start + part // 2, back)
 
@@ -284,10 +302,16 @@
     sent = pl.pallas_call(
         send_kernel,
         out_shape=[hop] * bits,
-        in_specs=[hbm] * 5 + [vmem],
-        out_specs=[vmem] * bits,
-        scratch_shapes=[pltpu.VMEM((rows, width), jnp.bfloat16)] * 5
-        + [pltpu.SemaphoreType.DMA((5,))],
+        in_specs=[hbm] * 6,
+        out_specs=[hbm] * bits,
+        scratch_shapes=[pltpu.VMEM((rows, width), jnp.bfloat16)] * 2
+        + [
+            pltpu.VMEM((1, rows), jnp.float32),
+            pltpu.VMEM((EXTRA, 2 * width), jnp.bfloat16),
+            pltpu.SemaphoreType.DMA((3,)),
+            pltpu.SemaphoreType.DMA((2 * bits,)),
+            pltpu.SemaphoreType.DMA((bits,)),
+        ],
         compiler_params=pltpu.CompilerParams(vmem_limit_bytes=60 * MIB),
     )(*own)
     got = {}
@@ -296,17 +320,17 @@
     early = tuple(got[at] for at in range(ctx - 1, ctx // 2, -1))
     early, weights = lax.optimization_barrier((early, weights))
     got.update(zip(range(ctx - 1, ctx // 2, -1), early))
-    weight = jnp.concatenate(weights, axis=1)
+    weight = jnp.stack(weights)
     got = [got[at] for at in range(1, ctx)]
     half_low = jax.ShapeDtypeStruct((rows, part // 2), jnp.bfloat16)
     half = jax.ShapeDtypeStruct((rows, part // 2), jnp.float32)
     low = jax.ShapeDtypeStruct((rows, part), jnp.bfloat16)
     full = jax.ShapeDtypeStruct((rows, part), jnp.float32)
-    grads, front, back = pl.pallas_call(
+    grads, front = pl.pallas_call(
         functools.partial(near_kernel, scale, part),
-        out_shape=[jax.ShapeDtypeStruct((rows, 3 * width), jnp.bfloat16), half_low, half_low],
+        out_shape=[jax.ShapeDtypeStruct((rows, 3 * width), jnp.bfloat16), half_low],
         in_specs=[vmem] * (ctx + 6),
-        out_specs=[vmem] * 3,
+        out_specs=[vmem] * 2,
         compiler_params=params,
         cost_estimate=pl.CostEstimate(
             flops=14 * rows * rows * ctx * width + 6 * rows * width * part,
@@ -314,21 +338,22 @@
             transcendentals=rows * rows * ctx,
         ),
     )(*own, weight, *got)
-    front, back = swap(front, "head", 1), swap(back, "head", 1)
+    front = swap(front, "head", 1)
     def projected(kernel, outs, operands):
         count = sum(out.shape[1] for out in outs)
         return pl.pallas_call(
             functools.partial(kernel, part),
             out_shape=outs,
             in_specs=[vmem] * 2,
-            out_specs=[vmem] * 2,
+            out_specs=[vmem] * len(outs),
             compiler_params=params,
             cost_estimate=pl.CostEstimate(
                 flops=6 * rows * width * count, bytes_accessed=6 * count * width, transcendentals=0
             ),
         )(*operands)
 
-    two_front, two_back = projected(far_kernel, [half, half], (grads, weight))
+    back, two_front, two_back = projected(far_kernel, [half_low, half, half], (grads, weight))
+    back = swap(back, "head", 1)
     near, total = projected(close_kernel, [low, full], (grads, weight))
     near, back = lax.optimization_barrier((near, back))
     front = swap((two_front + front.astype(jnp.float32)).astype(jnp.bfloat16), "head", 2)

time: 39.1 us -> 42.8 us (1.095)
  Pallas kernels: 4.49 us -> 9.23 us
  local copies, waits for them, and re-layouts: 3.16 us -> 0.03 us
  other arithmetic: 0.86 us -> 3.1 us
    pallas_call x1, Pallas kernels: 2.42 us -> 7.17 us  [near_body(): pl.pallas_call(send_kernel, out_shape=[hop] * bits, in_specs=[hbm] * 6, o...]
    unnamed x16 -> x12, local copies, waits for them, and re-layouts: 2.91 us -> 0.03 us
    another operation x0 -> x1, other arithmetic: none -> 2.25 us  [near_body(): weight = jnp.stack(weights)]
  transfers between devices with their start and end apart: 12 -> 12, of which waited for: 6 -> 6; matrix products, arithmetic and copies ran while one was open for 8% -> 5% of each run, Pallas kernels for 3% -> 3%
where the time goes in v7:
time: 42.8 us; the launch traced here: 42.6 us
  starting transfers between devices  17.3 us (40%)
  waiting for transfers between devices  12.7 us (30%)
  Pallas kernels  9.23 us (22%)
  other arithmetic  3.1 us (7%)
    ppermute x12, starting transfers between devices, swap(): return lax.ppermute(value, axis, [(at, at ^ offset) for at in range(size)])  17.3 us
    ppermute x12, waiting for transfers between devices, swap(): return lax.ppermute(value, axis, [(at, at ^ offset) for at in range(size)])  12.7 us
    pallas_call x1, Pallas kernels, near_body(): pl.pallas_call(send_kernel, out_shape=[hop] * bits, in_specs=[hbm] * 6, o...  7.17 us
    another operation x1, other arithmetic, near_body(): weight = jnp.stack(weights)  2.25 us
    pallas_call x2, Pallas kernels, projected(): pl.pallas_call(functools.partial(kernel, part), out_shape=outs, in_specs=...  1.12 us
    pallas_call x1, Pallas kernels, near_body(): pl.pallas_call(functools.partial(near_kernel, scale, part), out_shape=[ja...  0.94 us
  transfers between devices with their start and end apart: 12, of which 6 were waited for; matrix products, arithmetic and copies ran while one was open for 5% of the time, Pallas kernels for 3%

profile of v7, /device:TPU:0, one launch (start us, length us, event | category | flops | bytes accessed | tf_op | source)
XLA Modules:
  0.0 42.6 jit_solution(12826505129497565905)
XLA Ops:
  0.0 7.2 %shard_map.91 = (bf16[144,256]{1,0:T(8,128)(2,1)}, bf16[144,256]{1,0:T(8,128)(2,1)}, bf16[144,256]{1,0:T(8,128)(2,1)}) custom-call(bf16[128,128]{1,0:T(8,128)(2,1)} %q_ref.1, bf16[128,128]{1,0:T(8,128)(2,1)} %k_ref.1, bf16[128,128]{1,0:T(8,128)(2,1)} %v_ref.1, bf16[128,128]{1,0:T(8,128)(2,1)} %g_ref.1, bf16[128,128]{1,0:T(8,128)(2,1)} %a_ref.1, f32[1,128]{1,0:T(1,128)} %bitcast.4), custom_call_target="tpu_custom_call" | custom-call | tf_op jit(solution)/shard_map/pallas_call | solution.py:302
  7.2 3.4 %collective-permute-start = (bf16[144,256]{1,0:T(8,128)(2,1)}, bf16[144,256]{1,0:T(8,128)(2,1)S(1)}, u32[]{:S(2)}, u32[]{:S(2)}) collective-permute-start(bf16[144,256]{1,0:T(8,128)(2,1)} %get-tuple-element.23), channel_id=1, source_target_pairs={{0,28},{4,24},{8,20},{12,16},{16,12},{20,8},{24,4},{28,0},{1,29},{... | collective-permute-start | bytes 221192 | tf_op jit(solution)/shard_map/ppermute | solution.py:289
  10.6 0.6 %collective-permute-start.1 = (bf16[144,256]{1,0:T(8,128)(2,1)}, bf16[144,256]{1,0:T(8,128)(2,1)S(1)}, u32[]{:S(2)}, u32[]{:S(2)}) collective-permute-start(bf16[144,256]{1,0:T(8,128)(2,1)} %get-tuple-element.23), channel_id=1, source_target_pairs={{0,24},{4,28},{8,16},{12,20},{16,8},{20,12},{24,0},{28,4},{1,25},{... | collective-permute-start | bytes 221192 | tf_op jit(solution)/shard_map/ppermute | solution.py:289
  11.2 1.4 %collective-permute-start.2 = (bf16[144,256]{1,0:T(8,128)(2,1)}, bf16[144,256]{1,0:T(8,128)(2,1)S(1)}, u32[]{:S(2)}, u32[]{:S(2)}) collective-permute-start(bf16[144,256]{1,0:T(8,128)(2,1)} %get-tuple-element.23), channel_id=1, source_target_pairs={{0,20},{4,16},{8,28},{12,24},{16,4},{20,0},{24,12},{28,8},{1,21},{... | collective-permute-start | bytes 221192 | tf_op jit(solution)/shard_map/ppermute | solution.py:289
  12.6 0.3 collective-permute-start.6
  12.9 1.7 %collective-permute-start.4 = (bf16[144,256]{1,0:T(8,128)(2,1)}, bf16[144,256]{1,0:T(8,128)(2,1)S(1)}, u32[]{:S(2)}, u32[]{:S(2)}) collective-permute-start(bf16[144,256]{1,0:T(8,128)(2,1)} %get-tuple-element.28), channel_id=1, source_target_pairs={{0,8},{4,12},{8,0},{12,4},{16,24},{20,28},{24,16},{28,20},{1,9},{5... | collective-permute-start | bytes 221192 | tf_op jit(solution)/shard_map/ppermute | solution.py:289
  14.6 0.0 collective-permute-done.refs_6_
  14.6 1.0 %collective-permute-start.5 = (bf16[144,256]{1,0:T(8,128)(2,1)}, bf16[144,256]{1,0:T(8,128)(2,1)S(1)}, u32[]{:S(2)}, u32[]{:S(2)}) collective-permute-start(bf16[144,256]{1,0:T(8,128)(2,1)} %get-tuple-element.28), channel_id=1, source_target_pairs={{0,12},{4,8},{8,4},{12,0},{16,28},{20,24},{24,20},{28,16},{1,13},{... | collective-permute-start | bytes 221192 | tf_op jit(solution)/shard_map/ppermute | solution.py:289
  15.6 1.1 %collective-permute-done.1.refs_5_ = bf16[144,256]{1,0:T(8,128)(2,1)S(1)} collective-permute-done((bf16[144,256]{1,0:T(8,128)(2,1)}, bf16[144,256]{1,0:T(8,128)(2,1)S(1)}, u32[]{:S(2)}, u32[]{:S(2)}) %collective-permute-start.1) | collective-permute-done | bytes 73760 | tf_op jit(solution)/shard_map/ppermute | solution.py:289
  16.6 0.0 collective-permute-start.3
  16.6 0.7 %collective-permute-done.2.refs_4_ = bf16[144,256]{1,0:T(8,128)(2,1)S(1)} collective-permute-done((bf16[144,256]{1,0:T(8,128)(2,1)}, bf16[144,256]{1,0:T(8,128)(2,1)S(1)}, u32[]{:S(2)}, u32[]{:S(2)}) %collective-permute-start.2) | collective-permute-done | bytes 73760 | tf_op jit(solution)/shard_map/ppermute | solution.py:289
  17.3 0.0 copy-start
  17.4 0.0 copy-start.1
  17.4 0.0 copy-start.2
  17.4 0.0 copy-start.3
  17.4 0.0 copy-start.4
  17.4 0.0 copy-start.5
  17.4 2.3 %pad_maximum_fusion.w_ref = bf16[3,4096,128]{2,1,0:T(8,128)(2,1)S(1)} fusion(bf16[1,4096,128]{2,1,0:T(8,128)(2,1)} %bitcast.6, bf16[1,4096,128]{2,1,0:T(8,128)(2,1)} %bitcast.7, bf16[1,4096,128]{2,1,0:T(8,128)(2,1)} %bitcast.8), kind=kLoop, calls=%fused_computation | loop fusion | flops 3145728 | bytes 6291456 | tf_op jit(solution)/shard_map/stack | solution.py:323
  19.6 0.0 collective-permute-done.6.refs_3_
  19.7 0.0 collective-permute-done.4.refs_1_
  19.7 0.0 collective-permute-done.5.refs_2_
  19.7 0.0 collective-permute-done.3.refs_0_
  19.7 0.0 copy-done
  19.7 0.0 copy-done.1
  19.7 0.0 copy-done.2
  19.7 0.0 copy-done.3
  19.7 0.0 copy-done.4
  19.7 0.0 copy-done.5
  19.7 0.9 %shard_map.92 = (bf16[128,384]{1,0:T(8,128)(2,1)S(1)}, bf16[128,512]{1,0:T(8,128)(2,1)S(1)}) custom-call(bf16[128,128]{1,0:T(8,128)(2,1)S(1)} %copy-done, bf16[128,128]{1,0:T(8,128)(2,1)S(1)} %copy-done.1, bf16[128,128]{1,0:T(8,128)(2,1)S(1)} %copy-done.2, bf16[128,128]{1,0:T(8,128)(2,1)S(1)} %copy-done.3, bf16[128,128]{1,0:T(8,128)(2,1)S(1)} %copy-done.4, ...), custom_call_target="tpu_custom_call" | custom-call | flops 335544320 | bytes 1310720 | tf_op jit(solution)/shard_map/pallas_call | solution.py:329
  20.7 1.5 %collective-permute-start.9 = (bf16[128,512]{1,0:T(8,128)(2,1)S(1)}, bf16[128,512]{1,0:T(8,128)(2,1)S(1)}, u32[]{:S(2)}, u32[]{:S(2)}) collective-permute-start(bf16[128,512]{1,0:T(8,128)(2,1)S(1)} %get-tuple-element.38), channel_id=1, source_target_pairs={{0,1},{1,0},{2,3},{3,2},{4,5},{5,4},{6,7},{7,6},{8,9},{9,8},{10,11... | collective-permute-start | bytes 393224 | tf_op jit(solution)/shard_map/ppermute | solution.py:289
  22.2 0.5 %shard_map.94 = (bf16[128,512]{1,0:T(8,128)(2,1)S(1)}, f32[128,512]{1,0:T(8,128)S(1)}, f32[128,512]{1,0:T(8,128)S(1)}) custom-call(bf16[128,384]{1,0:T(8,128)(2,1)S(1)} %get-tuple-element.32.grads, bf16[3,4096,128]{2,1,0:T(8,128)(2,1)S(1)} %pad_maximum_fusion.w_ref), custom_call_target="tpu_custom_call" | custom-call | flops 150994944 | bytes 1179648 | tf_op jit(solution)/shard_map/pallas_call | solution.py:344
  22.7 0.6 %collective-permute-start.7 = (bf16[128,512]{1,0:T(8,128)(2,1)S(1)}, bf16[128,512]{1,0:T(8,128)(2,1)S(1)}, u32[]{:S(2)}, u32[]{:S(2)}) collective-permute-start(bf16[128,512]{1,0:T(8,128)(2,1)S(1)} %get-tuple-element.35), channel_id=1, source_target_pairs={{0,1},{1,0},{2,3},{3,2},{4,5},{5,4},{6,7},{7,6},{8,9},{9,8},{10,11... | collective-permute-start | bytes 393224 | tf_op jit(solution)/shard_map/ppermute | solution.py:289
  23.4 0.6 %shard_map.93 = (bf16[128,1024]{1,0:T(8,128)(2,1)S(1)}, f32[128,1024]{1,0:T(8,128)S(1)}) custom-call(bf16[128,384]{1,0:T(8,128)(2,1)S(1)} %get-tuple-element.32.grads, bf16[3,4096,128]{2,1,0:T(8,128)(2,1)S(1)} %pad_maximum_fusion.w_ref), custom_call_target="tpu_custom_call" | custom-call | flops 201326592 | bytes 1572864 | tf_op jit(solution)/shard_map/pallas_call | solution.py:344
  24.0 3.1 %collective-permute-done.9 = bf16[128,512]{1,0:T(8,128)(2,1)S(1)} collective-permute-done((bf16[128,512]{1,0:T(8,128)(2,1)S(1)}, bf16[128,512]{1,0:T(8,128)(2,1)S(1)}, u32[]{:S(2)}, u32[]{:S(2)}) %collective-permute-start.9) | collective-permute-done | bytes 131104 | tf_op jit(solution)/shard_map/ppermute | solution.py:289
  27.1 2.6 %collective-permute-start.10 = (bf16[128,512]{1,0:T(8,128)(2,1)S(1)}, bf16[128,512]{1,0:T(8,128)(2,1)S(1)}, u32[]{:S(2)}, u32[]{:S(2)}) collective-permute-start(bf16[128,512]{1,0:T(8,128)(2,1)S(1)} %add_convert_fusion.2), channel_id=1, source_target_pairs={{0,2},{1,3},{2,0},{3,1},{4,6},{5,7},{6,4},{7,5},{8,10},{9,11},{10,... | collective-permute-start | bytes 393224 | tf_op jit(solution)/shard_map/ppermute | solution.py:289
  29.7 0.0 collective-permute-done.7
  29.7 1.6 %collective-permute-start.8 = (bf16[128,1024]{1,0:T(8,128)(2,1)S(1)}, bf16[128,1024]{1,0:T(8,128)(2,1)S(1)}, u32[]{:S(2)}, u32[]{:S(2)}) collective-permute-start(bf16[128,1024]{1,0:T(8,128)(2,1)S(1)} %get-tuple-element.36), channel_id=1, source_target_pairs={{0,1},{1,0},{2,3},{3,2},{4,5},{5,4},{6,7},{7,6},{8,9},{9,8},{10,11... | collective-permute-start | bytes 786440 | tf_op jit(solution)/shard_map/ppermute | solution.py:289
  31.3 2.6 %collective-permute-start.11 = (bf16[128,512]{1,0:T(8,128)(2,1)S(1)}, bf16[128,512]{1,0:T(8,128)(2,1)S(1)}, u32[]{:S(2)}, u32[]{:S(2)}) collective-permute-start(bf16[128,512]{1,0:T(8,128)(2,1)S(1)} %add_convert_fusion.1), channel_id=1, source_target_pairs={{0,2},{1,3},{2,0},{3,1},{4,6},{5,7},{6,4},{7,5},{8,10},{9,11},{10,... | collective-permute-start | bytes 393224 | tf_op jit(solution)/shard_map/ppermute | solution.py:289
  33.9 3.4 %collective-permute-done.10 = bf16[128,512]{1,0:T(8,128)(2,1)S(1)} collective-permute-done((bf16[128,512]{1,0:T(8,128)(2,1)S(1)}, bf16[128,512]{1,0:T(8,128)(2,1)S(1)}, u32[]{:S(2)}, u32[]{:S(2)}) %collective-permute-start.10) | collective-permute-done | bytes 131104 | tf_op jit(solution)/shard_map/ppermute | solution.py:289
  37.3 3.5 %collective-permute-done.11 = bf16[128,512]{1,0:T(8,128)(2,1)S(1)} collective-permute-done((bf16[128,512]{1,0:T(8,128)(2,1)S(1)}, bf16[128,512]{1,0:T(8,128)(2,1)S(1)}, u32[]{:S(2)}, u32[]{:S(2)}) %collective-permute-start.11) | collective-permute-done | bytes 131104 | tf_op jit(solution)/shard_map/ppermute | solution.py:289
  40.8 1.0 %collective-permute-done.8 = bf16[128,1024]{1,0:T(8,128)(2,1)S(1)} collective-permute-done((bf16[128,1024]{1,0:T(8,128)(2,1)S(1)}, bf16[128,1024]{1,0:T(8,128)(2,1)S(1)}, u32[]{:S(2)}, u32[]{:S(2)}) %collective-permute-start.8) | collective-permute-done | bytes 262176 | tf_op jit(solution)/shard_map/ppermute | solution.py:289
  41.8 0.8 %add_convert_fusion = bf16[128,1024]{1,0:T(8,128)(2,1)} fusion(f32[128,1024]{1,0:T(8,128)S(1)} %get-tuple-element.33, bf16[128,1024]{1,0:T(8,128)(2,1)S(1)} %collective-permute-done.8, bf16[128,512]{1,0:T(8,128)(2,1)S(1)} %collective-permute-done.11, bf16[128,512]{1,0:T(8,128)(2,1)S(1)} %collective-permute-done.10), kind=kLoop, calls=%fused_computation.1 | loop fusion | flops 1048576 | bytes 1310720 | tf_op jit(solution)/shard_map/convert_element_type | solution.py:363
  (2 shorter events, 0.1 us)
Async XLA Ops:
  7.2 7.4 %collective-permute-start = (bf16[144,256]{1,0:T(8,128)(2,1)}, bf16[144,256]{1,0:T(8,128)(2,1)S(1)}, u32[]{:S(2)}, u32[]{:S(2)}) collective-permute-start(bf16[144,256]{1,0:T(8,128)(2,1)} %get-tuple-element.23), channel_id=1, source_target_pairs={{0,28},{4,24},{8,20},{12,16},{16,12},{20,8},{24,4},{28,0},{1,29},{... | collective-permute-start | bytes 221192 | tf_op jit(solution)/shard_map/ppermute | solution.py:289
  10.6 6.1 %collective-permute-start.1 = (bf16[144,256]{1,0:T(8,128)(2,1)}, bf16[144,256]{1,0:T(8,128)(2,1)S(1)}, u32[]{:S(2)}, u32[]{:S(2)}) collective-permute-start(bf16[144,256]{1,0:T(8,128)(2,1)} %get-tuple-element.23), channel_id=1, source_target_pairs={{0,24},{4,28},{8,16},{12,20},{16,8},{20,12},{24,0},{28,4},{1,25},{... | collective-permute-start | bytes 221192 | tf_op jit(solution)/shard_map/ppermute | solution.py:289
  11.2 6.1 %collective-permute-start.2 = (bf16[144,256]{1,0:T(8,128)(2,1)}, bf16[144,256]{1,0:T(8,128)(2,1)S(1)}, u32[]{:S(2)}, u32[]{:S(2)}) collective-permute-start(bf16[144,256]{1,0:T(8,128)(2,1)} %get-tuple-element.23), channel_id=1, source_target_pairs={{0,20},{4,16},{8,28},{12,24},{16,4},{20,0},{24,12},{28,8},{1,21},{... | collective-permute-start | bytes 221192 | tf_op jit(solution)/shard_map/ppermute | solution.py:289
  12.6 7.0 %collective-permute-start.6 = (bf16[144,256]{1,0:T(8,128)(2,1)}, bf16[144,256]{1,0:T(8,128)(2,1)S(1)}, u32[]{:S(2)}, u32[]{:S(2)}) collective-permute-start(bf16[144,256]{1,0:T(8,128)(2,1)} %get-tuple-element.23), channel_id=1, source_target_pairs={{0,16},{4,20},{8,24},{12,28},{16,0},{20,4},{24,8},{28,12},{1,17},{... | collective-permute-start | bytes 221192 | tf_op jit(solution)/shard_map/ppermute | solution.py:289
  12.9 6.8 %collective-permute-start.4 = (bf16[144,256]{1,0:T(8,128)(2,1)}, bf16[144,256]{1,0:T(8,128)(2,1)S(1)}, u32[]{:S(2)}, u32[]{:S(2)}) collective-permute-start(bf16[144,256]{1,0:T(8,128)(2,1)} %get-tuple-element.28), channel_id=1, source_target_pairs={{0,8},{4,12},{8,0},{12,4},{16,24},{20,28},{24,16},{28,20},{1,9},{5... | collective-permute-start | bytes 221192 | tf_op jit(solution)/shard_map/ppermute | solution.py:289
  14.6 5.1 %collective-permute-start.5 = (bf16[144,256]{1,0:T(8,128)(2,1)}, bf16[144,256]{1,0:T(8,128)(2,1)S(1)}, u32[]{:S(2)}, u32[]{:S(2)}) collective-permute-start(bf16[144,256]{1,0:T(8,128)(2,1)} %get-tuple-element.28), channel_id=1, source_target_pairs={{0,12},{4,8},{8,4},{12,0},{16,28},{20,24},{24,20},{28,16},{1,13},{... | collective-permute-start | bytes 221192 | tf_op jit(solution)/shard_map/ppermute | solution.py:289
  16.6 3.0 %collective-permute-start.3 = (bf16[144,256]{1,0:T(8,128)(2,1)}, bf16[144,256]{1,0:T(8,128)(2,1)S(1)}, u32[]{:S(2)}, u32[]{:S(2)}) collective-permute-start(bf16[144,256]{1,0:T(8,128)(2,1)} %get-tuple-element.27), channel_id=1, source_target_pairs={{0,4},{4,0},{8,12},{12,8},{16,20},{20,16},{24,28},{28,24},{1,5},{5... | collective-permute-start | bytes 221192 | tf_op jit(solution)/shard_map/ppermute | solution.py:289
  17.3 2.3 %copy-start = (bf16[128,128]{1,0:T(8,128)(2,1)S(1)}, bf16[128,128]{1,0:T(8,128)(2,1)}, u32[]{:S(2)}) copy-start(bf16[128,128]{1,0:T(8,128)(2,1)} %q_ref.1) | copy-start | bytes 98308
  17.4 2.3 %copy-start.1 = (bf16[128,128]{1,0:T(8,128)(2,1)S(1)}, bf16[128,128]{1,0:T(8,128)(2,1)}, u32[]{:S(2)}) copy-start(bf16[128,128]{1,0:T(8,128)(2,1)} %k_ref.1) | copy-start | bytes 98308
  17.4 2.4 %copy-start.2 = (bf16[128,128]{1,0:T(8,128)(2,1)S(1)}, bf16[128,128]{1,0:T(8,128)(2,1)}, u32[]{:S(2)}) copy-start(bf16[128,128]{1,0:T(8,128)(2,1)} %v_ref.1) | copy-start | bytes 98308
  17.4 2.4 %copy-start.3 = (bf16[128,128]{1,0:T(8,128)(2,1)S(1)}, bf16[128,128]{1,0:T(8,128)(2,1)}, u32[]{:S(2)}) copy-start(bf16[128,128]{1,0:T(8,128)(2,1)} %g_ref.1) | copy-start | bytes 98308
  17.4 2.4 %copy-start.4 = (bf16[128,128]{1,0:T(8,128)(2,1)S(1)}, bf16[128,128]{1,0:T(8,128)(2,1)}, u32[]{:S(2)}) copy-start(bf16[128,128]{1,0:T(8,128)(2,1)} %a_ref.1) | copy-start | bytes 98308
  17.4 2.4 %copy-start.5 = (f32[128,1]{0,1:T(1,128)S(1)}, f32[128,1]{0,1:T(1,128)}, u32[]{:S(2)}) copy-start(f32[128,1]{0,1:T(1,128)} %param.14) | copy-start | bytes 1540
  20.7 6.4 %collective-permute-start.9 = (bf16[128,512]{1,0:T(8,128)(2,1)S(1)}, bf16[128,512]{1,0:T(8,128)(2,1)S(1)}, u32[]{:S(2)}, u32[]{:S(2)}) collective-permute-start(bf16[128,512]{1,0:T(8,128)(2,1)S(1)} %get-tuple-element.38), channel_id=1, source_target_pairs={{0,1},{1,0},{2,3},{3,2},{4,5},{5,4},{6,7},{7,6},{8,9},{9,8},{10,11... | collective-permute-start | bytes 393224 | tf_op jit(solution)/shard_map/ppermute | solution.py:289
  22.7 7.0 %collective-permute-start.7 = (bf16[128,512]{1,0:T(8,128)(2,1)S(1)}, bf16[128,512]{1,0:T(8,128)(2,1)S(1)}, u32[]{:S(2)}, u32[]{:S(2)}) collective-permute-start(bf16[128,512]{1,0:T(8,128)(2,1)S(1)} %get-tuple-element.35), channel_id=1, source_target_pairs={{0,1},{1,0},{2,3},{3,2},{4,5},{5,4},{6,7},{7,6},{8,9},{9,8},{10,11... | collective-permute-start | bytes 393224 | tf_op jit(solution)/shard_map/ppermute | solution.py:289
  27.1 10.2 %collective-permute-start.10 = (bf16[128,512]{1,0:T(8,128)(2,1)S(1)}, bf16[128,512]{1,0:T(8,128)(2,1)S(1)}, u32[]{:S(2)}, u32[]{:S(2)}) collective-permute-start(bf16[128,512]{1,0:T(8,128)(2,1)S(1)} %add_convert_fusion.2), channel_id=1, source_target_pairs={{0,2},{1,3},{2,0},{3,1},{4,6},{5,7},{6,4},{7,5},{8,10},{9,11},{10,... | collective-permute-start | bytes 393224 | tf_op jit(solution)/shard_map/ppermute | solution.py:289
  29.7 12.0 %collective-permute-start.8 = (bf16[128,1024]{1,0:T(8,128)(2,1)S(1)}, bf16[128,1024]{1,0:T(8,128)(2,1)S(1)}, u32[]{:S(2)}, u32[]{:S(2)}) collective-permute-start(bf16[128,1024]{1,0:T(8,128)(2,1)S(1)} %get-tuple-element.36), channel_id=1, source_target_pairs={{0,1},{1,0},{2,3},{3,2},{4,5},{5,4},{6,7},{7,6},{8,9},{9,8},{10,11... | collective-permute-start | bytes 786440 | tf_op jit(solution)/shard_map/ppermute | solution.py:289
  31.3 9.5 %collective-permute-start.11 = (bf16[128,512]{1,0:T(8,128)(2,1)S(1)}, bf16[128,512]{1,0:T(8,128)(2,1)S(1)}, u32[]{:S(2)}, u32[]{:S(2)}) collective-permute-start(bf16[128,512]{1,0:T(8,128)(2,1)S(1)} %add_convert_fusion.1), channel_id=1, source_target_pairs={{0,2},{1,3},{2,0},{3,1},{4,6},{5,7},{6,4},{7,5},{8,10},{9,11},{10,... | collective-permute-start | bytes 393224 | tf_op jit(solution)/shard_map/ppermute | solution.py:289

commit v8 on v7

--- a/solution.py
+++ b/solution.py
@@ -163,14 +163,19 @@
 
 
 def send_kernel(q_in, k_in, v_in, g_in, a_in, n_in, *refs):
-    g_ref, a_ref, n_ref, extra_ref, in_sems, row_sems, extra_sems = refs[-7:]
-    hops = refs[:-7]
+    q_ref, k_ref, v_ref, g_ref, a_ref, n_ref, extra_ref, in_sems, row_sems, extra_sems = refs[-10:]
+    hops = refs[:-10]
     me = lax.axis_index("ctx")
     rows, width = g_ref.shape
-    loads = [
-        pltpu.make_async_copy(src, dst, in_sems.at[at])
-        for at, (src, dst) in enumerate(((g_in, g_ref), (a_in, a_ref), (n_in, n_ref)))
-    ]
+    pairs = (
+        (k_in, k_ref),
+        (v_in, v_ref),
+        (q_in, q_ref),
+        (g_in, g_ref),
+        (a_in, a_ref),
+        (n_in, n_ref),
+    )
+    loads = [pltpu.make_async_copy(*pair, in_sems.at[at]) for at, pair in enumerate(pairs)]
     for load in loads:
         load.start()
 
@@ -182,21 +187,21 @@
             for at, src in enumerate((first, second))
         ]
 
+    for load in loads:
+        load.wait()
     for bit in range(len(hops)):
         later = (me & (1 << bit)) == 0
 
         @pl.when(later)
         def _():
-            for move in moves(bit, k_in, v_in):
+            for move in moves(bit, k_ref, v_ref):
                 move.start()
 
         @pl.when(jnp.logical_not(later))
         def _():
-            for move in moves(bit, q_in, g_in):
+            for move in moves(bit, q_ref, g_ref):
                 move.start()
 
-    for load in loads:
-        load.wait()
     delta = delta_of(g_ref[...], a_ref[...])
     delta = jnp.sum(jnp.where(diagonal(rows), delta, 0.0), axis=0, keepdims=True)
     row = lax.broadcasted_iota(jnp.int32, (EXTRA, rows), 0)
@@ -212,26 +217,26 @@
     for tail in tails:
         tail.start()
     for bit in range(len(hops)):
-        for move in moves(bit, k_in, v_in):
+        for move in moves(bit, k_ref, v_ref):
             move.wait()
     for tail in tails:
         tail.wait()
 
 
-def project(grads, w_ref, start, out_ref):
+def project(grads, w_refs, start, out_ref):
     part = out_ref.shape[1]
     cols = math.gcd(part, 512)
     for at in range(0, part, cols):
         span = pl.ds(pl.multiple_of(start + at, cols), cols)
-        weight = jnp.concatenate([w_ref[i, span, :] for i in range(w_ref.shape[0])], axis=1)
+        weight = jnp.concatenate([ref[span, :] for ref in w_refs], axis=1)
         out_ref[:, at : at + cols] = dot_nt(grads[...], weight).astype(out_ref.dtype)
 
 
-def near_kernel(scale, part, q_ref, k_ref, v_ref, g_ref, a_ref, n_ref, w_ref, *refs):
+def near_kernel(scale, q_ref, k_ref, v_ref, g_ref, a_ref, n_ref, w_ref, *refs):
     grads, front = refs[-2:]
     got = refs[:-2]
     rows, width = q_ref.shape
-    me, head = lax.axis_index("ctx"), lax.axis_index("head")
+    me = lax.axis_index("ctx")
     exponent = scale * math.log2(math.e)
     query, key, value, grad = q_ref[...], k_ref[...], v_ref[...], g_ref[...]
     norm = (1.0 / scale) * jnp.sum(
@@ -267,21 +272,23 @@
     grads[:, :width] = (scale * (query_sum + both_sum[:rows])).astype(jnp.bfloat16)
     grads[:, width : 2 * width] = (scale * (key_sum + both_sum[rows:])).astype(jnp.bfloat16)
     grads[:, 2 * width :] = value_sum.astype(jnp.bfloat16)
-    project(grads, w_ref, (head ^ 3) * part, front)
-
-
-def far_kernel(part, grads, w_ref, last, front, back):
+    project(grads, [w_ref.at[at] for at in range(w_ref.shape[0])], 0, front)
+
+
+def far_kernel(part, grads, wq_ref, wk_ref, wv_ref, last, front, back):
+    w_refs = (wq_ref, wk_ref, wv_ref)
     head = lax.axis_index("head")
-    project(grads, w_ref, (head ^ 3) * part + part // 2, last)
+    project(grads, w_refs, (head ^ 3) * part + part // 2, last)
     start = (head ^ 2) * part
-    project(grads, w_ref, start, front)
-    project(grads, w_ref, start + part // 2, back)
-
-
-def close_kernel(part, grads, w_ref, near, mine):
+    project(grads, w_refs, start, front)
+    project(grads, w_refs, start + part // 2, back)
+
+
+def close_kernel(part, grads, wq_ref, wk_ref, wv_ref, near, mine):
+    w_refs = (wq_ref, wk_ref, wv_ref)
     head = lax.axis_index("head")
-    project(grads, w_ref, (head ^ 1) * part, near)
-    project(grads, w_ref, head * part, mine)
+    project(grads, w_refs, (head ^ 1) * part, near)
+    project(grads, w_refs, head * part, mine)
 
 
 def swap(value, axis, offset):
@@ -304,11 +311,11 @@
         out_shape=[hop] * bits,
         in_specs=[hbm] * 6,
         out_specs=[hbm] * bits,
-        scratch_shapes=[pltpu.VMEM((rows, width), jnp.bfloat16)] * 2
+        scratch_shapes=[pltpu.VMEM((rows, width), jnp.bfloat16)] * 5
         + [
             pltpu.VMEM((1, rows), jnp.float32),
             pltpu.VMEM((EXTRA, 2 * width), jnp.bfloat16),
-            pltpu.SemaphoreType.DMA((3,)),
+            pltpu.SemaphoreType.DMA((6,)),
             pltpu.SemaphoreType.DMA((2 * bits,)),
             pltpu.SemaphoreType.DMA((bits,)),
         ],
@@ -318,16 +325,19 @@
     for at in range(ctx - 1, 0, -1):
         got[at] = swap(sent[at.bit_length() - 1], "ctx", at)
     early = tuple(got[at] for at in range(ctx - 1, ctx // 2, -1))
-    early, weights = lax.optimization_barrier((early, weights))
+    early, first_weights = lax.optimization_barrier((early, weights))
     got.update(zip(range(ctx - 1, ctx // 2, -1), early))
-    weight = jnp.stack(weights)
+    start = (lax.axis_index("head") ^ 3) * part
+    weight = jnp.stack(
+        [lax.dynamic_slice_in_dim(one, start, part // 2, 0) for one in first_weights]
+    )
     got = [got[at] for at in range(1, ctx)]
     half_low = jax.ShapeDtypeStruct((rows, part // 2), jnp.bfloat16)
     half = jax.ShapeDtypeStruct((rows, part // 2), jnp.float32)
     low = jax.ShapeDtypeStruct((rows, part), jnp.bfloat16)
     full = jax.ShapeDtypeStruct((rows, part), jnp.float32)
     grads, front = pl.pallas_call(
-        functools.partial(near_kernel, scale, part),
+        functools.partial(near_kernel, scale),
         out_shape=[jax.ShapeDtypeStruct((rows, 3 * width), jnp.bfloat16), half_low],
         in_specs=[vmem] * (ctx + 6),
         out_specs=[vmem] * 2,
@@ -344,7 +354,7 @@
         return pl.pallas_call(
             functools.partial(kernel, part),
             out_shape=outs,
-            in_specs=[vmem] * 2,
+            in_specs=[vmem] * (1 + len(weights)),
             out_specs=[vmem] * len(outs),
             compiler_params=params,
             cost_estimate=pl.CostEstimate(
@@ -352,9 +362,9 @@
             ),
         )(*operands)
 
-    back, two_front, two_back = projected(far_kernel, [half_low, half, half], (grads, weight))
+    back, two_front, two_back = projected(far_kernel, [half_low, half, half], (grads, *weights))
     back = swap(back, "head", 1)
-    near, total = projected(close_kernel, [low, full], (grads, weight))
+    near, total = projected(close_kernel, [low, full], (grads, *weights))
     near, back = lax.optimization_barrier((near, back))
     front = swap((two_front + front.astype(jnp.float32)).astype(jnp.bfloat16), "head", 2)
     back = swap((two_back + back.astype(jnp.float32)).astype(jnp.bfloat16), "head", 2)

time: 42.8 us -> 36.8 us (0.86)
  the two profiles are of different devices: /device:TPU:0 before, /device:TPU:10 now
where the time goes in v8:
time: 36.8 us; the launch traced here: 36.5 us
  starting transfers between devices  16.9 us (46%)
  waiting for transfers between devices  11.5 us (31%)
  Pallas kernels  3.74 us (10%)
  local copies, waits for them, and re-layouts  3.28 us (9%)
  other arithmetic  0.91 us (2%)
    ppermute x12, starting transfers between devices, swap(): return lax.ppermute(value, axis, [(at, at ^ offset) for at in range(size)])  16.9 us
    ppermute x12, waiting for transfers between devices, swap(): return lax.ppermute(value, axis, [(at, at ^ offset) for at in range(size)])  11.5 us
    another operation x2, local copies, waits for them, and re-layouts, near_body(): jnp.stack([lax.dynamic_slice_in_dim(one, start, part // 2, 0) for one in...  2 us
    pallas_call x1, Pallas kernels, near_body(): pl.pallas_call(send_kernel, out_shape=[hop] * bits, in_specs=[hbm] * 6, o...  1.67 us
    unnamed x18, local copies, waits for them, and re-layouts  1.28 us
    pallas_call x2, Pallas kernels, projected(): pl.pallas_call(functools.partial(kernel, part), out_shape=outs, in_specs=...  1.13 us
    pallas_call x1, Pallas kernels, near_body(): pl.pallas_call(functools.partial(near_kernel, scale), out_shape=[jax.Shap...  0.95 us
    convert_element_type x1, other arithmetic, near_body(): return (total + near.astype(jnp.float32) + far_sum).astype(jnp.bfloat16)  0.8 us
  transfers between devices with their start and end apart: 12, of which 5 were waited for; matrix products, arithmetic and copies ran while one was open for 6% of the time, Pallas kernels for 3%

profile of v8, /device:TPU:10, one launch (start us, length us, event | category | flops | bytes accessed | tf_op | source)
XLA Modules:
  0.0 36.5 jit_solution(15931941111087023782)
XLA Ops:
  0.0 1.7 %shard_map.91 = (bf16[144,256]{1,0:T(8,128)(2,1)}, bf16[144,256]{1,0:T(8,128)(2,1)}, bf16[144,256]{1,0:T(8,128)(2,1)}) custom-call(bf16[128,128]{1,0:T(8,128)(2,1)} %q_ref.1, bf16[128,128]{1,0:T(8,128)(2,1)} %k_ref.1, bf16[128,128]{1,0:T(8,128)(2,1)} %v_ref.1, bf16[128,128]{1,0:T(8,128)(2,1)} %g_ref.1, bf16[128,128]{1,0:T(8,128)(2,1)} %a_ref.1, f32[1,128]{1,0:T(1,128)} %bitcast.7), custom_call_target="tpu_custom_call" | custom-call | tf_op jit(solution)/shard_map/pallas_call | solution.py:309
  1.7 1.0 %collective-permute-start.2 = (bf16[144,256]{1,0:T(8,128)(2,1)}, bf16[144,256]{1,0:T(8,128)(2,1)S(1)}, u32[]{:S(2)}, u32[]{:S(2)}) collective-permute-start(bf16[144,256]{1,0:T(8,128)(2,1)} %get-tuple-element.23), channel_id=1, source_target_pairs={{0,20},{4,16},{8,28},{12,24},{16,4},{20,0},{24,12},{28,8},{1,21},{... | collective-permute-start | bytes 221192 | tf_op jit(solution)/shard_map/ppermute | solution.py:296
  2.7 0.6 %collective-permute-start.1 = (bf16[144,256]{1,0:T(8,128)(2,1)}, bf16[144,256]{1,0:T(8,128)(2,1)S(1)}, u32[]{:S(2)}, u32[]{:S(2)}) collective-permute-start(bf16[144,256]{1,0:T(8,128)(2,1)} %get-tuple-element.23), channel_id=1, source_target_pairs={{0,24},{4,28},{8,16},{12,20},{16,8},{20,12},{24,0},{28,4},{1,25},{... | collective-permute-start | bytes 221192 | tf_op jit(solution)/shard_map/ppermute | solution.py:296
  3.3 2.3 %collective-permute-start = (bf16[144,256]{1,0:T(8,128)(2,1)}, bf16[144,256]{1,0:T(8,128)(2,1)S(1)}, u32[]{:S(2)}, u32[]{:S(2)}) collective-permute-start(bf16[144,256]{1,0:T(8,128)(2,1)} %get-tuple-element.23), channel_id=1, source_target_pairs={{0,28},{4,24},{8,20},{12,16},{16,12},{20,8},{24,4},{28,0},{1,29},{... | collective-permute-start | bytes 221192 | tf_op jit(solution)/shard_map/ppermute | solution.py:296
  5.7 0.2 collective-permute-start.5
  5.9 1.5 %collective-permute-start.4 = (bf16[144,256]{1,0:T(8,128)(2,1)}, bf16[144,256]{1,0:T(8,128)(2,1)S(1)}, u32[]{:S(2)}, u32[]{:S(2)}) collective-permute-start(bf16[144,256]{1,0:T(8,128)(2,1)} %get-tuple-element.28), channel_id=1, source_target_pairs={{0,8},{4,12},{8,0},{12,4},{16,24},{20,28},{24,16},{28,20},{1,9},{5... | collective-permute-start | bytes 221192 | tf_op jit(solution)/shard_map/ppermute | solution.py:296
  7.4 1.4 %collective-permute-done.2.refs_4_ = bf16[144,256]{1,0:T(8,128)(2,1)S(1)} collective-permute-done((bf16[144,256]{1,0:T(8,128)(2,1)}, bf16[144,256]{1,0:T(8,128)(2,1)S(1)}, u32[]{:S(2)}, u32[]{:S(2)}) %collective-permute-start.2) | collective-permute-done | bytes 73760 | tf_op jit(solution)/shard_map/ppermute | solution.py:296
  8.7 2.4 %collective-permute-start.6 = (bf16[144,256]{1,0:T(8,128)(2,1)}, bf16[144,256]{1,0:T(8,128)(2,1)S(1)}, u32[]{:S(2)}, u32[]{:S(2)}) collective-permute-start(bf16[144,256]{1,0:T(8,128)(2,1)} %get-tuple-element.23), channel_id=1, source_target_pairs={{0,16},{4,20},{8,24},{12,28},{16,0},{20,4},{24,8},{28,12},{1,17},{... | collective-permute-start | bytes 221192 | tf_op jit(solution)/shard_map/ppermute | solution.py:296
  11.2 0.0 collective-permute-done.1.refs_5_
  11.2 0.0 collective-permute-start.3
  11.2 0.0 collective-permute-done.refs_6_
  11.2 0.9 %dynamic-slice_bitcast_fusion.2 = bf16[1,512,128]{2,1,0:T(8,128)(2,1)S(1)} fusion(bf16[4096,128]{1,0:T(8,128)(2,1)} %wq_ref.3, s32[]{:T(128)S(6)} %select_n.2), kind=kLoop, calls=%fused_computation.6 | loop fusion | bytes 262148 | tf_op jit(solution)/shard_map/stack | solution.py:331
  12.1 0.0 copy-start.3
  12.1 0.0 copy-start.4
  12.1 0.0 copy-start.5
  12.2 0.0 copy-start.6
  12.2 0.0 copy-start.7
  12.2 0.0 copy-start.8
  12.2 0.0 copy-start.1
  12.2 1.1 %dynamic-slice_bitcast_fusion = (bf16[1,512,128]{2,1,0:T(8,128)(2,1)S(1)}, bf16[1,512,128]{2,1,0:T(8,128)(2,1)S(1)}) fusion(bf16[4096,128]{1,0:T(8,128)(2,1)} %wv_ref.3, s32[]{:T(128)S(6)} %select_n.2, bf16[4096,128]{1,0:T(8,128)(2,1)} %wk_ref.3), kind=kLoop, calls=%fused_computation.4 | loop fusion | bytes 524292 | tf_op jit(solution)/shard_map/stack | solution.py:331
  13.3 0.0 copy-start
  13.4 0.0 collective-permute-done.3.refs_0_
  13.4 0.0 collective-permute-done.5.refs_2_
  13.4 0.0 collective-permute-done.4.refs_1_
  13.4 0.6 %collective-permute-done.6.refs_3_ = bf16[144,256]{1,0:T(8,128)(2,1)S(1)} collective-permute-done((bf16[144,256]{1,0:T(8,128)(2,1)}, bf16[144,256]{1,0:T(8,128)(2,1)S(1)}, u32[]{:S(2)}, u32[]{:S(2)}) %collective-permute-start.6) | collective-permute-done | bytes 73760 | tf_op jit(solution)/shard_map/ppermute | solution.py:296
  14.0 0.0 copy-done.3
  14.0 0.0 copy-done.4
  14.0 0.0 copy-done.5
  14.0 0.0 copy-done.6
  14.0 0.0 copy-done.7
  14.0 0.0 copy-done.8
  14.0 0.9 %shard_map.92 = (bf16[128,384]{1,0:T(8,128)(2,1)S(1)}, bf16[128,512]{1,0:T(8,128)(2,1)S(1)}) custom-call(bf16[128,128]{1,0:T(8,128)(2,1)S(1)} %copy-done.3, bf16[128,128]{1,0:T(8,128)(2,1)S(1)} %copy-done.4, bf16[128,128]{1,0:T(8,128)(2,1)S(1)} %copy-done.5, bf16[128,128]{1,0:T(8,128)(2,1)S(1)} %copy-done.6, bf16[128,128]{1,0:T(8,128)(2,1)S(1)} %copy-done.7, ...), custom_call_target="tpu_custom_call" | custom-call | flops 335544320 | bytes 1310720 | tf_op jit(solution)/shard_map/pallas_call | solution.py:339
  14.9 0.5 %collective-permute-start.9 = (bf16[128,512]{1,0:T(8,128)(2,1)S(1)}, bf16[128,512]{1,0:T(8,128)(2,1)S(1)}, u32[]{:S(2)}, u32[]{:S(2)}) collective-permute-start(bf16[128,512]{1,0:T(8,128)(2,1)S(1)} %get-tuple-element.38), channel_id=1, source_target_pairs={{0,1},{1,0},{2,3},{3,2},{4,5},{5,4},{6,7},{7,6},{8,9},{9,8},{10,11... | collective-permute-start | bytes 393224 | tf_op jit(solution)/shard_map/ppermute | solution.py:296
  15.5 0.0 copy-done.1
  15.5 0.0 copy-done
  15.5 0.0 copy-start.2
  15.5 1.2 %copy-done.2 = bf16[4096,128]{1,0:T(8,128)(2,1)S(1)} copy-done((bf16[4096,128]{1,0:T(8,128)(2,1)S(1)}, bf16[4096,128]{1,0:T(8,128)(2,1)}, u32[]{:S(2)}) %copy-start.2) | copy-done | bytes 1048600
  16.7 0.5 %shard_map.94 = (bf16[128,512]{1,0:T(8,128)(2,1)S(1)}, f32[128,512]{1,0:T(8,128)S(1)}, f32[128,512]{1,0:T(8,128)S(1)}) custom-call(bf16[128,384]{1,0:T(8,128)(2,1)S(1)} %get-tuple-element.32.grads, bf16[4096,128]{1,0:T(8,128)(2,1)S(1)} %copy-done.2, bf16[4096,128]{1,0:T(8,128)(2,1)S(1)} %copy-done.1, bf16[4096,128]{1,0:T(8,128)(2,1)S(1)} %copy-done), custom_call_target="tpu_custom_call" | custom-call | flops 150994944 | bytes 1179648 | tf_op jit(solution)/shard_map/pallas_call | solution.py:354
  17.2 1.6 %collective-permute-start.7 = (bf16[128,512]{1,0:T(8,128)(2,1)S(1)}, bf16[128,512]{1,0:T(8,128)(2,1)S(1)}, u32[]{:S(2)}, u32[]{:S(2)}) collective-permute-start(bf16[128,512]{1,0:T(8,128)(2,1)S(1)} %get-tuple-element.35), channel_id=1, source_target_pairs={{0,1},{1,0},{2,3},{3,2},{4,5},{5,4},{6,7},{7,6},{8,9},{9,8},{10,11... | collective-permute-start | bytes 393224 | tf_op jit(solution)/shard_map/ppermute | solution.py:296
  18.8 0.6 %shard_map.93 = (bf16[128,1024]{1,0:T(8,128)(2,1)S(1)}, f32[128,1024]{1,0:T(8,128)S(1)}) custom-call(bf16[128,384]{1,0:T(8,128)(2,1)S(1)} %get-tuple-element.32.grads, bf16[4096,128]{1,0:T(8,128)(2,1)S(1)} %copy-done.2, bf16[4096,128]{1,0:T(8,128)(2,1)S(1)} %copy-done.1, bf16[4096,128]{1,0:T(8,128)(2,1)S(1)} %copy-done), custom_call_target="tpu_custom_call" | custom-call | flops 201326592 | bytes 1572864 | tf_op jit(solution)/shard_map/pallas_call | solution.py:354
  19.5 1.7 %collective-permute-done.9 = bf16[128,512]{1,0:T(8,128)(2,1)S(1)} collective-permute-done((bf16[128,512]{1,0:T(8,128)(2,1)S(1)}, bf16[128,512]{1,0:T(8,128)(2,1)S(1)}, u32[]{:S(2)}, u32[]{:S(2)}) %collective-permute-start.9) | collective-permute-done | bytes 131104 | tf_op jit(solution)/shard_map/ppermute | solution.py:296
  21.2 2.6 %collective-permute-start.10 = (bf16[128,512]{1,0:T(8,128)(2,1)S(1)}, bf16[128,512]{1,0:T(8,128)(2,1)S(1)}, u32[]{:S(2)}, u32[]{:S(2)}) collective-permute-start(bf16[128,512]{1,0:T(8,128)(2,1)S(1)} %add_convert_fusion.2), channel_id=1, source_target_pairs={{0,2},{1,3},{2,0},{3,1},{4,6},{5,7},{6,4},{7,5},{8,10},{9,11},{10,... | collective-permute-start | bytes 393224 | tf_op jit(solution)/shard_map/ppermute | solution.py:296
  23.9 0.0 collective-permute-done.7
  23.9 1.4 %collective-permute-start.8 = (bf16[128,1024]{1,0:T(8,128)(2,1)S(1)}, bf16[128,1024]{1,0:T(8,128)(2,1)S(1)}, u32[]{:S(2)}, u32[]{:S(2)}) collective-permute-start(bf16[128,1024]{1,0:T(8,128)(2,1)S(1)} %get-tuple-element.36), channel_id=1, source_target_pairs={{0,1},{1,0},{2,3},{3,2},{4,5},{5,4},{6,7},{7,6},{8,9},{9,8},{10,11... | collective-permute-start | bytes 786440 | tf_op jit(solution)/shard_map/ppermute | solution.py:296
  25.4 2.6 %collective-permute-start.11 = (bf16[128,512]{1,0:T(8,128)(2,1)S(1)}, bf16[128,512]{1,0:T(8,128)(2,1)S(1)}, u32[]{:S(2)}, u32[]{:S(2)}) collective-permute-start(bf16[128,512]{1,0:T(8,128)(2,1)S(1)} %add_convert_fusion.1), channel_id=1, source_target_pairs={{0,2},{1,3},{2,0},{3,1},{4,6},{5,7},{6,4},{7,5},{8,10},{9,11},{10,... | collective-permute-start | bytes 393224 | tf_op jit(solution)/shard_map/ppermute | solution.py:296
  27.9 0.9 %collective-permute-done.10 = bf16[128,512]{1,0:T(8,128)(2,1)S(1)} collective-permute-done((bf16[128,512]{1,0:T(8,128)(2,1)S(1)}, bf16[128,512]{1,0:T(8,128)(2,1)S(1)}, u32[]{:S(2)}, u32[]{:S(2)}) %collective-permute-start.10) | collective-permute-done | bytes 131104 | tf_op jit(solution)/shard_map/ppermute | solution.py:296
  28.8 6.9 %collective-permute-done.11 = bf16[128,512]{1,0:T(8,128)(2,1)S(1)} collective-permute-done((bf16[128,512]{1,0:T(8,128)(2,1)S(1)}, bf16[128,512]{1,0:T(8,128)(2,1)S(1)}, u32[]{:S(2)}, u32[]{:S(2)}) %collective-permute-start.11) | collective-permute-done | bytes 131104 | tf_op jit(solution)/shard_map/ppermute | solution.py:296
  35.7 0.0 collective-permute-done.8
  35.7 0.8 %add_convert_fusion = bf16[128,1024]{1,0:T(8,128)(2,1)} fusion(f32[128,1024]{1,0:T(8,128)S(1)} %get-tuple-element.33, bf16[128,1024]{1,0:T(8,128)(2,1)S(1)} %collective-permute-done.8, bf16[128,512]{1,0:T(8,128)(2,1)S(1)} %collective-permute-done.11, bf16[128,512]{1,0:T(8,128)(2,1)S(1)} %collective-permute-done.10), kind=kLoop, calls=%fused_computation | loop fusion | flops 1048576 | bytes 1310720 | tf_op jit(solution)/shard_map/convert_element_type | solution.py:373
  (3 shorter events, 0.1 us)
Async XLA Ops:
  1.7 7.1 %collective-permute-start.2 = (bf16[144,256]{1,0:T(8,128)(2,1)}, bf16[144,256]{1,0:T(8,128)(2,1)S(1)}, u32[]{:S(2)}, u32[]{:S(2)}) collective-permute-start(bf16[144,256]{1,0:T(8,128)(2,1)} %get-tuple-element.23), channel_id=1, source_target_pairs={{0,20},{4,16},{8,28},{12,24},{16,4},{20,0},{24,12},{28,8},{1,21},{... | collective-permute-start | bytes 221192 | tf_op jit(solution)/shard_map/ppermute | solution.py:296
  2.7 8.5 %collective-permute-start.1 = (bf16[144,256]{1,0:T(8,128)(2,1)}, bf16[144,256]{1,0:T(8,128)(2,1)S(1)}, u32[]{:S(2)}, u32[]{:S(2)}) collective-permute-start(bf16[144,256]{1,0:T(8,128)(2,1)} %get-tuple-element.23), channel_id=1, source_target_pairs={{0,24},{4,28},{8,16},{12,20},{16,8},{20,12},{24,0},{28,4},{1,25},{... | collective-permute-start | bytes 221192 | tf_op jit(solution)/shard_map/ppermute | solution.py:296
  3.3 7.9 %collective-permute-start = (bf16[144,256]{1,0:T(8,128)(2,1)}, bf16[144,256]{1,0:T(8,128)(2,1)S(1)}, u32[]{:S(2)}, u32[]{:S(2)}) collective-permute-start(bf16[144,256]{1,0:T(8,128)(2,1)} %get-tuple-element.23), channel_id=1, source_target_pairs={{0,28},{4,24},{8,20},{12,16},{16,12},{20,8},{24,4},{28,0},{1,29},{... | collective-permute-start | bytes 221192 | tf_op jit(solution)/shard_map/ppermute | solution.py:296
  5.7 7.7 %collective-permute-start.5 = (bf16[144,256]{1,0:T(8,128)(2,1)}, bf16[144,256]{1,0:T(8,128)(2,1)S(1)}, u32[]{:S(2)}, u32[]{:S(2)}) collective-permute-start(bf16[144,256]{1,0:T(8,128)(2,1)} %get-tuple-element.28), channel_id=1, source_target_pairs={{0,12},{4,8},{8,4},{12,0},{16,28},{20,24},{24,20},{28,16},{1,13},{... | collective-permute-start | bytes 221192 | tf_op jit(solution)/shard_map/ppermute | solution.py:296
  5.9 7.5 %collective-permute-start.4 = (bf16[144,256]{1,0:T(8,128)(2,1)}, bf16[144,256]{1,0:T(8,128)(2,1)S(1)}, u32[]{:S(2)}, u32[]{:S(2)}) collective-permute-start(bf16[144,256]{1,0:T(8,128)(2,1)} %get-tuple-element.28), channel_id=1, source_target_pairs={{0,8},{4,12},{8,0},{12,4},{16,24},{20,28},{24,16},{28,20},{1,9},{5... | collective-permute-start | bytes 221192 | tf_op jit(solution)/shard_map/ppermute | solution.py:296
  8.7 5.2 %collective-permute-start.6 = (bf16[144,256]{1,0:T(8,128)(2,1)}, bf16[144,256]{1,0:T(8,128)(2,1)S(1)}, u32[]{:S(2)}, u32[]{:S(2)}) collective-permute-start(bf16[144,256]{1,0:T(8,128)(2,1)} %get-tuple-element.23), channel_id=1, source_target_pairs={{0,16},{4,20},{8,24},{12,28},{16,0},{20,4},{24,8},{28,12},{1,17},{... | collective-permute-start | bytes 221192 | tf_op jit(solution)/shard_map/ppermute | solution.py:296
  11.2 2.2 %collective-permute-start.3 = (bf16[144,256]{1,0:T(8,128)(2,1)}, bf16[144,256]{1,0:T(8,128)(2,1)S(1)}, u32[]{:S(2)}, u32[]{:S(2)}) collective-permute-start(bf16[144,256]{1,0:T(8,128)(2,1)} %get-tuple-element.27), channel_id=1, source_target_pairs={{0,4},{4,0},{8,12},{12,8},{16,20},{20,16},{24,28},{28,24},{1,5},{5... | collective-permute-start | bytes 221192 | tf_op jit(solution)/shard_map/ppermute | solution.py:296
  12.1 1.8 %copy-start.3 = (bf16[128,128]{1,0:T(8,128)(2,1)S(1)}, bf16[128,128]{1,0:T(8,128)(2,1)}, u32[]{:S(2)}) copy-start(bf16[128,128]{1,0:T(8,128)(2,1)} %q_ref.1) | copy-start | bytes 98308
  12.1 1.8 %copy-start.4 = (bf16[128,128]{1,0:T(8,128)(2,1)S(1)}, bf16[128,128]{1,0:T(8,128)(2,1)}, u32[]{:S(2)}) copy-start(bf16[128,128]{1,0:T(8,128)(2,1)} %k_ref.1) | copy-start | bytes 98308
  12.1 1.8 %copy-start.5 = (bf16[128,128]{1,0:T(8,128)(2,1)S(1)}, bf16[128,128]{1,0:T(8,128)(2,1)}, u32[]{:S(2)}) copy-start(bf16[128,128]{1,0:T(8,128)(2,1)} %v_ref.1) | copy-start | bytes 98308
  12.2 1.8 %copy-start.6 = (bf16[128,128]{1,0:T(8,128)(2,1)S(1)}, bf16[128,128]{1,0:T(8,128)(2,1)}, u32[]{:S(2)}) copy-start(bf16[128,128]{1,0:T(8,128)(2,1)} %g_ref.1) | copy-start | bytes 98308
  12.2 1.8 %copy-start.7 = (bf16[128,128]{1,0:T(8,128)(2,1)S(1)}, bf16[128,128]{1,0:T(8,128)(2,1)}, u32[]{:S(2)}) copy-start(bf16[128,128]{1,0:T(8,128)(2,1)} %a_ref.1) | copy-start | bytes 98308
  12.2 1.8 %copy-start.8 = (f32[128,1]{0,1:T(1,128)S(1)}, f32[128,1]{0,1:T(1,128)}, u32[]{:S(2)}) copy-start(f32[128,1]{0,1:T(1,128)} %param.14) | copy-start | bytes 1540
  12.2 3.3 %copy-start.1 = (bf16[4096,128]{1,0:T(8,128)(2,1)S(1)}, bf16[4096,128]{1,0:T(8,128)(2,1)}, u32[]{:S(2)}) copy-start(bf16[4096,128]{1,0:T(8,128)(2,1)} %wk_ref.3) | copy-start | bytes 3145732
  13.3 2.2 %copy-start = (bf16[4096,128]{1,0:T(8,128)(2,1)S(1)}, bf16[4096,128]{1,0:T(8,128)(2,1)}, u32[]{:S(2)}) copy-start(bf16[4096,128]{1,0:T(8,128)(2,1)} %wv_ref.3) | copy-start | bytes 3145732
  14.9 6.3 %collective-permute-start.9 = (bf16[128,512]{1,0:T(8,128)(2,1)S(1)}, bf16[128,512]{1,0:T(8,128)(2,1)S(1)}, u32[]{:S(2)}, u32[]{:S(2)}) collective-permute-start(bf16[128,512]{1,0:T(8,128)(2,1)S(1)} %get-tuple-element.38), channel_id=1, source_target_pairs={{0,1},{1,0},{2,3},{3,2},{4,5},{5,4},{6,7},{7,6},{8,9},{9,8},{10,11... | collective-permute-start | bytes 393224 | tf_op jit(solution)/shard_map/ppermute | solution.py:296
  15.5 1.2 %copy-start.2 = (bf16[4096,128]{1,0:T(8,128)(2,1)S(1)}, bf16[4096,128]{1,0:T(8,128)(2,1)}, u32[]{:S(2)}) copy-start(bf16[4096,128]{1,0:T(8,128)(2,1)} %wq_ref.3) | copy-start | bytes 3145732
  17.2 6.7 %collective-permute-start.7 = (bf16[128,512]{1,0:T(8,128)(2,1)S(1)}, bf16[128,512]{1,0:T(8,128)(2,1)S(1)}, u32[]{:S(2)}, u32[]{:S(2)}) collective-permute-start(bf16[128,512]{1,0:T(8,128)(2,1)S(1)} %get-tuple-element.35), channel_id=1, source_target_pairs={{0,1},{1,0},{2,3},{3,2},{4,5},{5,4},{6,7},{7,6},{8,9},{9,8},{10,11... | collective-permute-start | bytes 393224 | tf_op jit(solution)/shard_map/ppermute | solution.py:296
  21.2 7.6 %collective-permute-start.10 = (bf16[128,512]{1,0:T(8,128)(2,1)S(1)}, bf16[128,512]{1,0:T(8,128)(2,1)S(1)}, u32[]{:S(2)}, u32[]{:S(2)}) collective-permute-start(bf16[128,512]{1,0:T(8,128)(2,1)S(1)} %add_convert_fusion.2), channel_id=1, source_target_pairs={{0,2},{1,3},{2,0},{3,1},{4,6},{5,7},{6,4},{7,5},{8,10},{9,11},{10,... | collective-permute-start | bytes 393224 | tf_op jit(solution)/shard_map/ppermute | solution.py:296
  23.9 11.8 %collective-permute-start.8 = (bf16[128,1024]{1,0:T(8,128)(2,1)S(1)}, bf16[128,1024]{1,0:T(8,128)(2,1)S(1)}, u32[]{:S(2)}, u32[]{:S(2)}) collective-permute-start(bf16[128,1024]{1,0:T(8,128)(2,1)S(1)} %get-tuple-element.36), channel_id=1, source_target_pairs={{0,1},{1,0},{2,3},{3,2},{4,5},{5,4},{6,7},{7,6},{8,9},{9,8},{10,11... | collective-permute-start | bytes 786440 | tf_op jit(solution)/shard_map/ppermute | solution.py:296
  25.4 10.4 %collective-permute-start.11 = (bf16[128,512]{1,0:T(8,128)(2,1)S(1)}, bf16[128,512]{1,0:T(8,128)(2,1)S(1)}, u32[]{:S(2)}, u32[]{:S(2)}) collective-permute-start(bf16[128,512]{1,0:T(8,128)(2,1)S(1)} %add_convert_fusion.1), channel_id=1, source_target_pairs={{0,2},{1,3},{2,0},{3,1},{4,6},{5,7},{6,4},{7,5},{8,10},{9,11},{10,... | collective-permute-start | bytes 393224 | tf_op jit(solution)/shard_map/ppermute | solution.py:296

commit v9 on v8

--- a/solution.py
+++ b/solution.py
@@ -324,9 +324,10 @@
     got = {}
     for at in range(ctx - 1, 0, -1):
         got[at] = swap(sent[at.bit_length() - 1], "ctx", at)
-    early = tuple(got[at] for at in range(ctx - 1, ctx // 2, -1))
+    soon = [at for at in (1, 2, 6) if at < ctx]
+    early = tuple(got[at] for at in soon)
     early, first_weights = lax.optimization_barrier((early, weights))
-    got.update(zip(range(ctx - 1, ctx // 2, -1), early))
+    got.update(zip(soon, early))
     start = (lax.axis_index("head") ^ 3) * part
     weight = jnp.stack(
         [lax.dynamic_slice_in_dim(one, start, part // 2, 0) for one in first_weights]

time: 36.8 us -> 37.8 us (1.027)
  the two profiles are of different devices: /device:TPU:10 before, /device:TPU:0 now
where the time goes in v9:
time: 37.8 us; the launch traced here: 37.5 us
  starting transfers between devices  15.7 us (42%)
  waiting for transfers between devices  13.7 us (36%)
  Pallas kernels  3.73 us (10%)
  local copies, waits for them, and re-layouts  3.27 us (9%)
  other arithmetic  0.91 us (2%)
    ppermute x12, starting transfers between devices, swap(): return lax.ppermute(value, axis, [(at, at ^ offset) for at in range(size)])  15.7 us
    ppermute x12, waiting for transfers between devices, swap(): return lax.ppermute(value, axis, [(at, at ^ offset) for at in range(size)])  13.7 us
    another operation x2, local copies, waits for them, and re-layouts, near_body(): jnp.stack([lax.dynamic_slice_in_dim(one, start, part // 2, 0) for one in...  2 us
    pallas_call x1, Pallas kernels, near_body(): pl.pallas_call(send_kernel, out_shape=[hop] * bits, in_specs=[hbm] * 6, o...  1.67 us
    unnamed x18, local copies, waits for them, and re-layouts  1.28 us
    pallas_call x2, Pallas kernels, projected(): pl.pallas_call(functools.partial(kernel, part), out_shape=outs, in_specs=...  1.13 us
    pallas_call x1, Pallas kernels, near_body(): pl.pallas_call(functools.partial(near_kernel, scale), out_shape=[jax.Shap...  0.94 us
    convert_element_type x1, other arithmetic, near_body(): return (total + near.astype(jnp.float32) + far_sum).astype(jnp.bfloat16)  0.8 us
  transfers between devices with their start and end apart: 12, of which 8 were waited for; matrix products, arithmetic and copies ran while one was open for 6% of the time, Pallas kernels for 3%

profile of v9, /device:TPU:0, one launch (start us, length us, event | category | flops | bytes accessed | tf_op | source)
XLA Modules:
  0.0 37.5 jit_solution(13156414908634893645)
XLA Ops:
  0.0 1.7 %shard_map.91 = (bf16[144,256]{1,0:T(8,128)(2,1)}, bf16[144,256]{1,0:T(8,128)(2,1)}, bf16[144,256]{1,0:T(8,128)(2,1)}) custom-call(bf16[128,128]{1,0:T(8,128)(2,1)} %q_ref.1, bf16[128,128]{1,0:T(8,128)(2,1)} %k_ref.1, bf16[128,128]{1,0:T(8,128)(2,1)} %v_ref.1, bf16[128,128]{1,0:T(8,128)(2,1)} %g_ref.1, bf16[128,128]{1,0:T(8,128)(2,1)} %a_ref.1, f32[1,128]{1,0:T(1,128)} %bitcast.7), custom_call_target="tpu_custom_call" | custom-call | tf_op jit(solution)/shard_map/pallas_call | solution.py:309
  1.7 0.5 %collective-permute-start = (bf16[144,256]{1,0:T(8,128)(2,1)}, bf16[144,256]{1,0:T(8,128)(2,1)S(1)}, u32[]{:S(2)}, u32[]{:S(2)}) collective-permute-start(bf16[144,256]{1,0:T(8,128)(2,1)} %get-tuple-element.23), channel_id=1, source_target_pairs={{0,4},{4,0},{8,12},{12,8},{16,20},{20,16},{24,28},{28,24},{1,5},{5... | collective-permute-start | bytes 221192 | tf_op jit(solution)/shard_map/ppermute | solution.py:296
  2.2 2.6 %collective-permute-start.1 = (bf16[144,256]{1,0:T(8,128)(2,1)}, bf16[144,256]{1,0:T(8,128)(2,1)S(1)}, u32[]{:S(2)}, u32[]{:S(2)}) collective-permute-start(bf16[144,256]{1,0:T(8,128)(2,1)} %get-tuple-element.24), channel_id=1, source_target_pairs={{0,8},{4,12},{8,0},{12,4},{16,24},{20,28},{24,16},{28,20},{1,9},{5... | collective-permute-start | bytes 221192 | tf_op jit(solution)/shard_map/ppermute | solution.py:296
  4.8 1.5 %collective-permute-start.2 = (bf16[144,256]{1,0:T(8,128)(2,1)}, bf16[144,256]{1,0:T(8,128)(2,1)S(1)}, u32[]{:S(2)}, u32[]{:S(2)}) collective-permute-start(bf16[144,256]{1,0:T(8,128)(2,1)} %get-tuple-element.25), channel_id=1, source_target_pairs={{0,24},{4,28},{8,16},{12,20},{16,8},{20,12},{24,0},{28,4},{1,25},{... | collective-permute-start | bytes 221192 | tf_op jit(solution)/shard_map/ppermute | solution.py:296
  6.2 1.0 %collective-permute-start.3 = (bf16[144,256]{1,0:T(8,128)(2,1)}, bf16[144,256]{1,0:T(8,128)(2,1)S(1)}, u32[]{:S(2)}, u32[]{:S(2)}) collective-permute-start(bf16[144,256]{1,0:T(8,128)(2,1)} %get-tuple-element.24), channel_id=1, source_target_pairs={{0,12},{4,8},{8,4},{12,0},{16,28},{20,24},{24,20},{28,16},{1,13},{... | collective-permute-start | bytes 221192 | tf_op jit(solution)/shard_map/ppermute | solution.py:296
  7.2 0.3 collective-permute-start.6
  7.5 0.0 collective-permute-done.refs_0_
  7.5 1.5 %collective-permute-start.5 = (bf16[144,256]{1,0:T(8,128)(2,1)}, bf16[144,256]{1,0:T(8,128)(2,1)S(1)}, u32[]{:S(2)}, u32[]{:S(2)}) collective-permute-start(bf16[144,256]{1,0:T(8,128)(2,1)} %get-tuple-element.25), channel_id=1, source_target_pairs={{0,20},{4,16},{8,28},{12,24},{16,4},{20,0},{24,12},{28,8},{1,21},{... | collective-permute-start | bytes 221192 | tf_op jit(solution)/shard_map/ppermute | solution.py:296
  9.0 0.0 collective-permute-done.1.refs_1_
  9.0 1.1 %collective-permute-start.4 = (bf16[144,256]{1,0:T(8,128)(2,1)}, bf16[144,256]{1,0:T(8,128)(2,1)S(1)}, u32[]{:S(2)}, u32[]{:S(2)}) collective-permute-start(bf16[144,256]{1,0:T(8,128)(2,1)} %get-tuple-element.25), channel_id=1, source_target_pairs={{0,16},{4,20},{8,24},{12,28},{16,0},{20,4},{24,8},{28,12},{1,17},{... | collective-permute-start | bytes 221192 | tf_op jit(solution)/shard_map/ppermute | solution.py:296
  10.1 1.0 %collective-permute-done.2.refs_5_ = bf16[144,256]{1,0:T(8,128)(2,1)S(1)} collective-permute-done((bf16[144,256]{1,0:T(8,128)(2,1)}, bf16[144,256]{1,0:T(8,128)(2,1)S(1)}, u32[]{:S(2)}, u32[]{:S(2)}) %collective-permute-start.2) | collective-permute-done | bytes 73760 | tf_op jit(solution)/shard_map/ppermute | solution.py:296
  11.1 0.9 %dynamic-slice_bitcast_fusion.2 = bf16[1,512,128]{2,1,0:T(8,128)(2,1)S(1)} fusion(bf16[4096,128]{1,0:T(8,128)(2,1)} %wq_ref.3, s32[]{:T(128)S(6)} %select_n.2), kind=kLoop, calls=%fused_computation.6 | loop fusion | bytes 262148 | tf_op jit(solution)/shard_map/stack | solution.py:332
  12.0 0.0 copy-start.3
  12.0 0.0 copy-start.4
  12.0 0.0 copy-start.5
  12.1 0.0 copy-start.6
  12.1 0.0 copy-start.7
  12.1 0.0 copy-start.8
  12.1 0.0 copy-start.1
  12.1 1.1 %dynamic-slice_bitcast_fusion = (bf16[1,512,128]{2,1,0:T(8,128)(2,1)S(1)}, bf16[1,512,128]{2,1,0:T(8,128)(2,1)S(1)}) fusion(bf16[4096,128]{1,0:T(8,128)(2,1)} %wv_ref.3, s32[]{:T(128)S(6)} %select_n.2, bf16[4096,128]{1,0:T(8,128)(2,1)} %wk_ref.3), kind=kLoop, calls=%fused_computation.4 | loop fusion | bytes 524292 | tf_op jit(solution)/shard_map/stack | solution.py:332
  13.2 0.0 copy-start
  13.3 0.0 collective-permute-done.3.refs_2_
  13.3 0.1 collective-permute-done.6.refs_6_
  13.4 0.0 collective-permute-done.5.refs_4_
  13.4 2.2 %collective-permute-done.4.refs_3_ = bf16[144,256]{1,0:T(8,128)(2,1)S(1)} collective-permute-done((bf16[144,256]{1,0:T(8,128)(2,1)}, bf16[144,256]{1,0:T(8,128)(2,1)S(1)}, u32[]{:S(2)}, u32[]{:S(2)}) %collective-permute-start.4) | collective-permute-done | bytes 73760 | tf_op jit(solution)/shard_map/ppermute | solution.py:296
  15.7 0.0 copy-done.3
  15.7 0.0 copy-done.4
  15.7 0.0 copy-done.5
  15.7 0.0 copy-done.6
  15.7 0.0 copy-done.7
  15.7 0.0 copy-done.8
  15.7 0.9 %shard_map.92 = (bf16[128,384]{1,0:T(8,128)(2,1)S(1)}, bf16[128,512]{1,0:T(8,128)(2,1)S(1)}) custom-call(bf16[128,128]{1,0:T(8,128)(2,1)S(1)} %copy-done.3, bf16[128,128]{1,0:T(8,128)(2,1)S(1)} %copy-done.4, bf16[128,128]{1,0:T(8,128)(2,1)S(1)} %copy-done.5, bf16[128,128]{1,0:T(8,128)(2,1)S(1)} %copy-done.6, bf16[128,128]{1,0:T(8,128)(2,1)S(1)} %copy-done.7, ...), custom_call_target="tpu_custom_call" | custom-call | flops 335544320 | bytes 1310720 | tf_op jit(solution)/shard_map/pallas_call | solution.py:340
  16.6 1.9 %collective-permute-start.9 = (bf16[128,512]{1,0:T(8,128)(2,1)S(1)}, bf16[128,512]{1,0:T(8,128)(2,1)S(1)}, u32[]{:S(2)}, u32[]{:S(2)}) collective-permute-start(bf16[128,512]{1,0:T(8,128)(2,1)S(1)} %get-tuple-element.38), channel_id=1, source_target_pairs={{0,1},{1,0},{2,3},{3,2},{4,5},{5,4},{6,7},{7,6},{8,9},{9,8},{10,11... | collective-permute-start | bytes 393224 | tf_op jit(solution)/shard_map/ppermute | solution.py:296
  18.5 0.0 copy-done.1
  18.5 0.0 copy-done
  18.5 0.0 copy-start.2
  18.5 1.2 %copy-done.2 = bf16[4096,128]{1,0:T(8,128)(2,1)S(1)} copy-done((bf16[4096,128]{1,0:T(8,128)(2,1)S(1)}, bf16[4096,128]{1,0:T(8,128)(2,1)}, u32[]{:S(2)}) %copy-start.2) | copy-done | bytes 1048600
  19.7 0.5 %shard_map.94 = (bf16[128,512]{1,0:T(8,128)(2,1)S(1)}, f32[128,512]{1,0:T(8,128)S(1)}, f32[128,512]{1,0:T(8,128)S(1)}) custom-call(bf16[128,384]{1,0:T(8,128)(2,1)S(1)} %get-tuple-element.32.grads, bf16[4096,128]{1,0:T(8,128)(2,1)S(1)} %copy-done.2, bf16[4096,128]{1,0:T(8,128)(2,1)S(1)} %copy-done.1, bf16[4096,128]{1,0:T(8,128)(2,1)S(1)} %copy-done), custom_call_target="tpu_custom_call" | custom-call | flops 150994944 | bytes 1179648 | tf_op jit(solution)/shard_map/pallas_call | solution.py:355
  20.2 0.3 collective-permute-start.7
  20.5 0.6 %shard_map.93 = (bf16[128,1024]{1,0:T(8,128)(2,1)S(1)}, f32[128,1024]{1,0:T(8,128)S(1)}) custom-call(bf16[128,384]{1,0:T(8,128)(2,1)S(1)} %get-tuple-element.32.grads, bf16[4096,128]{1,0:T(8,128)(2,1)S(1)} %copy-done.2, bf16[4096,128]{1,0:T(8,128)(2,1)S(1)} %copy-done.1, bf16[4096,128]{1,0:T(8,128)(2,1)S(1)} %copy-done), custom_call_target="tpu_custom_call" | custom-call | flops 201326592 | bytes 1572864 | tf_op jit(solution)/shard_map/pallas_call | solution.py:355
  21.2 1.2 %collective-permute-done.9 = bf16[128,512]{1,0:T(8,128)(2,1)S(1)} collective-permute-done((bf16[128,512]{1,0:T(8,128)(2,1)S(1)}, bf16[128,512]{1,0:T(8,128)(2,1)S(1)}, u32[]{:S(2)}, u32[]{:S(2)}) %collective-permute-start.9) | collective-permute-done | bytes 131104 | tf_op jit(solution)/shard_map/ppermute | solution.py:296
  22.4 2.6 %collective-permute-start.10 = (bf16[128,512]{1,0:T(8,128)(2,1)S(1)}, bf16[128,512]{1,0:T(8,128)(2,1)S(1)}, u32[]{:S(2)}, u32[]{:S(2)}) collective-permute-start(bf16[128,512]{1,0:T(8,128)(2,1)S(1)} %add_convert_fusion.2), channel_id=1, source_target_pairs={{0,2},{1,3},{2,0},{3,1},{4,6},{5,7},{6,4},{7,5},{8,10},{9,11},{10,... | collective-permute-start | bytes 393224 | tf_op jit(solution)/shard_map/ppermute | solution.py:296
  25.0 1.8 %collective-permute-done.7 = bf16[128,512]{1,0:T(8,128)(2,1)S(1)} collective-permute-done((bf16[128,512]{1,0:T(8,128)(2,1)S(1)}, bf16[128,512]{1,0:T(8,128)(2,1)S(1)}, u32[]{:S(2)}, u32[]{:S(2)}) %collective-permute-start.7) | collective-permute-done | bytes 131104 | tf_op jit(solution)/shard_map/ppermute | solution.py:296
  26.9 0.6 %collective-permute-start.8 = (bf16[128,1024]{1,0:T(8,128)(2,1)S(1)}, bf16[128,1024]{1,0:T(8,128)(2,1)S(1)}, u32[]{:S(2)}, u32[]{:S(2)}) collective-permute-start(bf16[128,1024]{1,0:T(8,128)(2,1)S(1)} %get-tuple-element.36), channel_id=1, source_target_pairs={{0,1},{1,0},{2,3},{3,2},{4,5},{5,4},{6,7},{7,6},{8,9},{9,8},{10,11... | collective-permute-start | bytes 786440 | tf_op jit(solution)/shard_map/ppermute | solution.py:296
  27.5 2.0 %collective-permute-start.11 = (bf16[128,512]{1,0:T(8,128)(2,1)S(1)}, bf16[128,512]{1,0:T(8,128)(2,1)S(1)}, u32[]{:S(2)}, u32[]{:S(2)}) collective-permute-start(bf16[128,512]{1,0:T(8,128)(2,1)S(1)} %add_convert_fusion.1), channel_id=1, source_target_pairs={{0,2},{1,3},{2,0},{3,1},{4,6},{5,7},{6,4},{7,5},{8,10},{9,11},{10,... | collective-permute-start | bytes 393224 | tf_op jit(solution)/shard_map/ppermute | solution.py:296
  29.4 1.0 %collective-permute-done.10 = bf16[128,512]{1,0:T(8,128)(2,1)S(1)} collective-permute-done((bf16[128,512]{1,0:T(8,128)(2,1)S(1)}, bf16[128,512]{1,0:T(8,128)(2,1)S(1)}, u32[]{:S(2)}, u32[]{:S(2)}) %collective-permute-start.10) | collective-permute-done | bytes 131104 | tf_op jit(solution)/shard_map/ppermute | solution.py:296
  30.4 5.4 %collective-permute-done.11 = bf16[128,512]{1,0:T(8,128)(2,1)S(1)} collective-permute-done((bf16[128,512]{1,0:T(8,128)(2,1)S(1)}, bf16[128,512]{1,0:T(8,128)(2,1)S(1)}, u32[]{:S(2)}, u32[]{:S(2)}) %collective-permute-start.11) | collective-permute-done | bytes 131104 | tf_op jit(solution)/shard_map/ppermute | solution.py:296
  35.8 0.9 %collective-permute-done.8 = bf16[128,1024]{1,0:T(8,128)(2,1)S(1)} collective-permute-done((bf16[128,1024]{1,0:T(8,128)(2,1)S(1)}, bf16[128,1024]{1,0:T(8,128)(2,1)S(1)}, u32[]{:S(2)}, u32[]{:S(2)}) %collective-permute-start.8) | collective-permute-done | bytes 262176 | tf_op jit(solution)/shard_map/ppermute | solution.py:296
  36.7 0.8 %add_convert_fusion = bf16[128,1024]{1,0:T(8,128)(2,1)} fusion(f32[128,1024]{1,0:T(8,128)S(1)} %get-tuple-element.33, bf16[128,1024]{1,0:T(8,128)(2,1)S(1)} %collective-permute-done.8, bf16[128,512]{1,0:T(8,128)(2,1)S(1)} %collective-permute-done.11, bf16[128,512]{1,0:T(8,128)(2,1)S(1)} %collective-permute-done.10), kind=kLoop, calls=%fused_computation | loop fusion | flops 1048576 | bytes 1310720 | tf_op jit(solution)/shard_map/convert_element_type | solution.py:374
  (3 shorter events, 0.1 us)
Async XLA Ops:
  1.7 5.8 %collective-permute-start = (bf16[144,256]{1,0:T(8,128)(2,1)}, bf16[144,256]{1,0:T(8,128)(2,1)S(1)}, u32[]{:S(2)}, u32[]{:S(2)}) collective-permute-start(bf16[144,256]{1,0:T(8,128)(2,1)} %get-tuple-element.23), channel_id=1, source_target_pairs={{0,4},{4,0},{8,12},{12,8},{16,20},{20,16},{24,28},{28,24},{1,5},{5... | collective-permute-start | bytes 221192 | tf_op jit(solution)/shard_map/ppermute | solution.py:296
  2.2 6.8 %collective-permute-start.1 = (bf16[144,256]{1,0:T(8,128)(2,1)}, bf16[144,256]{1,0:T(8,128)(2,1)S(1)}, u32[]{:S(2)}, u32[]{:S(2)}) collective-permute-start(bf16[144,256]{1,0:T(8,128)(2,1)} %get-tuple-element.24), channel_id=1, source_target_pairs={{0,8},{4,12},{8,0},{12,4},{16,24},{20,28},{24,16},{28,20},{1,9},{5... | collective-permute-start | bytes 221192 | tf_op jit(solution)/shard_map/ppermute | solution.py:296
  4.8 6.4 %collective-permute-start.2 = (bf16[144,256]{1,0:T(8,128)(2,1)}, bf16[144,256]{1,0:T(8,128)(2,1)S(1)}, u32[]{:S(2)}, u32[]{:S(2)}) collective-permute-start(bf16[144,256]{1,0:T(8,128)(2,1)} %get-tuple-element.25), channel_id=1, source_target_pairs={{0,24},{4,28},{8,16},{12,20},{16,8},{20,12},{24,0},{28,4},{1,25},{... | collective-permute-start | bytes 221192 | tf_op jit(solution)/shard_map/ppermute | solution.py:296
  6.2 7.0 %collective-permute-start.3 = (bf16[144,256]{1,0:T(8,128)(2,1)}, bf16[144,256]{1,0:T(8,128)(2,1)S(1)}, u32[]{:S(2)}, u32[]{:S(2)}) collective-permute-start(bf16[144,256]{1,0:T(8,128)(2,1)} %get-tuple-element.24), channel_id=1, source_target_pairs={{0,12},{4,8},{8,4},{12,0},{16,28},{20,24},{24,20},{28,16},{1,13},{... | collective-permute-start | bytes 221192 | tf_op jit(solution)/shard_map/ppermute | solution.py:296
  7.2 6.2 %collective-permute-start.6 = (bf16[144,256]{1,0:T(8,128)(2,1)}, bf16[144,256]{1,0:T(8,128)(2,1)S(1)}, u32[]{:S(2)}, u32[]{:S(2)}) collective-permute-start(bf16[144,256]{1,0:T(8,128)(2,1)} %get-tuple-element.25), channel_id=1, source_target_pairs={{0,28},{4,24},{8,20},{12,16},{16,12},{20,8},{24,4},{28,0},{1,29},{... | collective-permute-start | bytes 221192 | tf_op jit(solution)/shard_map/ppermute | solution.py:296
  7.5 5.9 %collective-permute-start.5 = (bf16[144,256]{1,0:T(8,128)(2,1)}, bf16[144,256]{1,0:T(8,128)(2,1)S(1)}, u32[]{:S(2)}, u32[]{:S(2)}) collective-permute-start(bf16[144,256]{1,0:T(8,128)(2,1)} %get-tuple-element.25), channel_id=1, source_target_pairs={{0,20},{4,16},{8,28},{12,24},{16,4},{20,0},{24,12},{28,8},{1,21},{... | collective-permute-start | bytes 221192 | tf_op jit(solution)/shard_map/ppermute | solution.py:296
  9.0 6.7 %collective-permute-start.4 = (bf16[144,256]{1,0:T(8,128)(2,1)}, bf16[144,256]{1,0:T(8,128)(2,1)S(1)}, u32[]{:S(2)}, u32[]{:S(2)}) collective-permute-start(bf16[144,256]{1,0:T(8,128)(2,1)} %get-tuple-element.25), channel_id=1, source_target_pairs={{0,16},{4,20},{8,24},{12,28},{16,0},{20,4},{24,8},{28,12},{1,17},{... | collective-permute-start | bytes 221192 | tf_op jit(solution)/shard_map/ppermute | solution.py:296
  12.0 3.6 %copy-start.3 = (bf16[128,128]{1,0:T(8,128)(2,1)S(1)}, bf16[128,128]{1,0:T(8,128)(2,1)}, u32[]{:S(2)}) copy-start(bf16[128,128]{1,0:T(8,128)(2,1)} %q_ref.1) | copy-start | bytes 98308
  12.0 3.6 %copy-start.4 = (bf16[128,128]{1,0:T(8,128)(2,1)S(1)}, bf16[128,128]{1,0:T(8,128)(2,1)}, u32[]{:S(2)}) copy-start(bf16[128,128]{1,0:T(8,128)(2,1)} %k_ref.1) | copy-start | bytes 98308
  12.0 3.6 %copy-start.5 = (bf16[128,128]{1,0:T(8,128)(2,1)S(1)}, bf16[128,128]{1,0:T(8,128)(2,1)}, u32[]{:S(2)}) copy-start(bf16[128,128]{1,0:T(8,128)(2,1)} %v_ref.1) | copy-start | bytes 98308
  12.1 3.6 %copy-start.6 = (bf16[128,128]{1,0:T(8,128)(2,1)S(1)}, bf16[128,128]{1,0:T(8,128)(2,1)}, u32[]{:S(2)}) copy-start(bf16[128,128]{1,0:T(8,128)(2,1)} %g_ref.1) | copy-start | bytes 98308
  12.1 3.6 %copy-start.7 = (bf16[128,128]{1,0:T(8,128)(2,1)S(1)}, bf16[128,128]{1,0:T(8,128)(2,1)}, u32[]{:S(2)}) copy-start(bf16[128,128]{1,0:T(8,128)(2,1)} %a_ref.1) | copy-start | bytes 98308
  12.1 3.6 %copy-start.8 = (f32[128,1]{0,1:T(1,128)S(1)}, f32[128,1]{0,1:T(1,128)}, u32[]{:S(2)}) copy-start(f32[128,1]{0,1:T(1,128)} %param.14) | copy-start | bytes 1540
  12.1 6.4 %copy-start.1 = (bf16[4096,128]{1,0:T(8,128)(2,1)S(1)}, bf16[4096,128]{1,0:T(8,128)(2,1)}, u32[]{:S(2)}) copy-start(bf16[4096,128]{1,0:T(8,128)(2,1)} %wk_ref.3) | copy-start | bytes 3145732
  13.2 5.3 %copy-start = (bf16[4096,128]{1,0:T(8,128)(2,1)S(1)}, bf16[4096,128]{1,0:T(8,128)(2,1)}, u32[]{:S(2)}) copy-start(bf16[4096,128]{1,0:T(8,128)(2,1)} %wv_ref.3) | copy-start | bytes 3145732
  16.6 5.7 %collective-permute-start.9 = (bf16[128,512]{1,0:T(8,128)(2,1)S(1)}, bf16[128,512]{1,0:T(8,128)(2,1)S(1)}, u32[]{:S(2)}, u32[]{:S(2)}) collective-permute-start(bf16[128,512]{1,0:T(8,128)(2,1)S(1)} %get-tuple-element.38), channel_id=1, source_target_pairs={{0,1},{1,0},{2,3},{3,2},{4,5},{5,4},{6,7},{7,6},{8,9},{9,8},{10,11... | collective-permute-start | bytes 393224 | tf_op jit(solution)/shard_map/ppermute | solution.py:296
  18.5 1.2 %copy-start.2 = (bf16[4096,128]{1,0:T(8,128)(2,1)S(1)}, bf16[4096,128]{1,0:T(8,128)(2,1)}, u32[]{:S(2)}) copy-start(bf16[4096,128]{1,0:T(8,128)(2,1)} %wq_ref.3) | copy-start | bytes 3145732
  20.2 6.6 %collective-permute-start.7 = (bf16[128,512]{1,0:T(8,128)(2,1)S(1)}, bf16[128,512]{1,0:T(8,128)(2,1)S(1)}, u32[]{:S(2)}, u32[]{:S(2)}) collective-permute-start(bf16[128,512]{1,0:T(8,128)(2,1)S(1)} %get-tuple-element.35), channel_id=1, source_target_pairs={{0,1},{1,0},{2,3},{3,2},{4,5},{5,4},{6,7},{7,6},{8,9},{9,8},{10,11... | collective-permute-start | bytes 393224 | tf_op jit(solution)/shard_map/ppermute | solution.py:296
  22.4 8.0 %collective-permute-start.10 = (bf16[128,512]{1,0:T(8,128)(2,1)S(1)}, bf16[128,512]{1,0:T(8,128)(2,1)S(1)}, u32[]{:S(2)}, u32[]{:S(2)}) collective-permute-start(bf16[128,512]{1,0:T(8,128)(2,1)S(1)} %add_convert_fusion.2), channel_id=1, source_target_pairs={{0,2},{1,3},{2,0},{3,1},{4,6},{5,7},{6,4},{7,5},{8,10},{9,11},{10,... | collective-permute-start | bytes 393224 | tf_op jit(solution)/shard_map/ppermute | solution.py:296
  26.9 9.9 %collective-permute-start.8 = (bf16[128,1024]{1,0:T(8,128)(2,1)S(1)}, bf16[128,1024]{1,0:T(8,128)(2,1)S(1)}, u32[]{:S(2)}, u32[]{:S(2)}) collective-permute-start(bf16[128,1024]{1,0:T(8,128)(2,1)S(1)} %get-tuple-element.36), channel_id=1, source_target_pairs={{0,1},{1,0},{2,3},{3,2},{4,5},{5,4},{6,7},{7,6},{8,9},{9,8},{10,11... | collective-permute-start | bytes 786440 | tf_op jit(solution)/shard_map/ppermute | solution.py:296
  27.5 8.4 %collective-permute-start.11 = (bf16[128,512]{1,0:T(8,128)(2,1)S(1)}, bf16[128,512]{1,0:T(8,128)(2,1)S(1)}, u32[]{:S(2)}, u32[]{:S(2)}) collective-permute-start(bf16[128,512]{1,0:T(8,128)(2,1)S(1)} %add_convert_fusion.1), channel_id=1, source_target_pairs={{0,2},{1,3},{2,0},{3,1},{4,6},{5,7},{6,4},{7,5},{8,10},{9,11},{10,... | collective-permute-start | bytes 393224 | tf_op jit(solution)/shard_map/ppermute | solution.py:296

commit v10 on v9

--- a/solution.py
+++ b/solution.py
@@ -324,7 +324,7 @@
     got = {}
     for at in range(ctx - 1, 0, -1):
         got[at] = swap(sent[at.bit_length() - 1], "ctx", at)
-    soon = [at for at in (1, 2, 6) if at < ctx]
+    soon = [at for at in (1, 6, 4, 7, 5) if at < ctx]
     early = tuple(got[at] for at in soon)
     early, first_weights = lax.optimization_barrier((early, weights))
     got.update(zip(soon, early))

time: 37.8 us -> 37.7 us (level)
  waiting for transfers between devices: 13.7 us -> 14.4 us
  starting transfers between devices: 15.7 us -> 15 us
    ppermute x12, starting transfers between devices: 15.7 us -> 15 us  [swap(): return lax.ppermute(value, axis, [(at, at ^ offset) for at in range(size)])]
    ppermute x12, waiting for transfers between devices: 13.7 us -> 14.4 us  [swap(): return lax.ppermute(value, axis, [(at, at ^ offset) for at in range(size)])]
where the time goes in v10:
time: 37.7 us; the launch traced here: 37.5 us
  starting transfers between devices  15 us (40%)
  waiting for transfers between devices  14.4 us (38%)
  Pallas kernels  3.74 us (10%)
  local copies, waits for them, and re-layouts  3.27 us (9%)
  other arithmetic  0.91 us (2%)
    ppermute x12, starting transfers between devices, swap(): return lax.ppermute(value, axis, [(at, at ^ offset) for at in range(size)])  15 us
    ppermute x12, waiting for transfers between devices, swap(): return lax.ppermute(value, axis, [(at, at ^ offset) for at in range(size)])  14.4 us
    another operation x2, local copies, waits for them, and re-layouts, near_body(): jnp.stack([lax.dynamic_slice_in_dim(one, start, part // 2, 0) for one in...  2 us
    pallas_call x1, Pallas kernels, near_body(): pl.pallas_call(send_kernel, out_shape=[hop] * bits, in_specs=[hbm] * 6, o...  1.67 us
    unnamed x18, local copies, waits for them, and re-layouts  1.28 us
    pallas_call x2, Pallas kernels, projected(): pl.pallas_call(functools.partial(kernel, part), out_shape=outs, in_specs=...  1.13 us
    pallas_call x1, Pallas kernels, near_body(): pl.pallas_call(functools.partial(near_kernel, scale), out_shape=[jax.Shap...  0.95 us
    convert_element_type x1, other arithmetic, near_body(): return (total + near.astype(jnp.float32) + far_sum).astype(jnp.bfloat16)  0.8 us
  transfers between devices with their start and end apart: 12, of which 8 were waited for; matrix products, arithmetic and copies ran while one was open for 6% of the time, Pallas kernels for 3%

profile of v10, /device:TPU:0, one launch (start us, length us, event | category | flops | bytes accessed | tf_op | source)
XLA Modules:
  0.0 37.5 jit_solution(13208638696248679248)
XLA Ops:
  0.0 1.7 %shard_map.91 = (bf16[144,256]{1,0:T(8,128)(2,1)}, bf16[144,256]{1,0:T(8,128)(2,1)}, bf16[144,256]{1,0:T(8,128)(2,1)}) custom-call(bf16[128,128]{1,0:T(8,128)(2,1)} %q_ref.1, bf16[128,128]{1,0:T(8,128)(2,1)} %k_ref.1, bf16[128,128]{1,0:T(8,128)(2,1)} %v_ref.1, bf16[128,128]{1,0:T(8,128)(2,1)} %g_ref.1, bf16[128,128]{1,0:T(8,128)(2,1)} %a_ref.1, f32[1,128]{1,0:T(1,128)} %bitcast.7), custom_call_target="tpu_custom_call" | custom-call | tf_op jit(solution)/shard_map/pallas_call | solution.py:309
  1.7 0.5 %collective-permute-start = (bf16[144,256]{1,0:T(8,128)(2,1)}, bf16[144,256]{1,0:T(8,128)(2,1)S(1)}, u32[]{:S(2)}, u32[]{:S(2)}) collective-permute-start(bf16[144,256]{1,0:T(8,128)(2,1)} %get-tuple-element.25), channel_id=1, source_target_pairs={{0,4},{4,0},{8,12},{12,8},{16,20},{20,16},{24,28},{28,24},{1,5},{5... | collective-permute-start | bytes 221192 | tf_op jit(solution)/shard_map/ppermute | solution.py:296
  2.2 2.6 %collective-permute-start.4 = (bf16[144,256]{1,0:T(8,128)(2,1)}, bf16[144,256]{1,0:T(8,128)(2,1)S(1)}, u32[]{:S(2)}, u32[]{:S(2)}) collective-permute-start(bf16[144,256]{1,0:T(8,128)(2,1)} %get-tuple-element.26), channel_id=1, source_target_pairs={{0,20},{4,16},{8,28},{12,24},{16,4},{20,0},{24,12},{28,8},{1,21},{... | collective-permute-start | bytes 221192 | tf_op jit(solution)/shard_map/ppermute | solution.py:296
  4.8 1.1 %collective-permute-start.3 = (bf16[144,256]{1,0:T(8,128)(2,1)}, bf16[144,256]{1,0:T(8,128)(2,1)S(1)}, u32[]{:S(2)}, u32[]{:S(2)}) collective-permute-start(bf16[144,256]{1,0:T(8,128)(2,1)} %get-tuple-element.26), channel_id=1, source_target_pairs={{0,28},{4,24},{8,20},{12,16},{16,12},{20,8},{24,4},{28,0},{1,29},{... | collective-permute-start | bytes 221192 | tf_op jit(solution)/shard_map/ppermute | solution.py:296
  5.9 1.5 %collective-permute-start.2 = (bf16[144,256]{1,0:T(8,128)(2,1)}, bf16[144,256]{1,0:T(8,128)(2,1)S(1)}, u32[]{:S(2)}, u32[]{:S(2)}) collective-permute-start(bf16[144,256]{1,0:T(8,128)(2,1)} %get-tuple-element.26), channel_id=1, source_target_pairs={{0,16},{4,20},{8,24},{12,28},{16,0},{20,4},{24,8},{28,12},{1,17},{... | collective-permute-start | bytes 221192 | tf_op jit(solution)/shard_map/ppermute | solution.py:296
  7.5 0.3 collective-permute-start.1
  7.8 0.0 collective-permute-done.refs_0_
  7.8 1.1 %collective-permute-start.6 = (bf16[144,256]{1,0:T(8,128)(2,1)}, bf16[144,256]{1,0:T(8,128)(2,1)S(1)}, u32[]{:S(2)}, u32[]{:S(2)}) collective-permute-start(bf16[144,256]{1,0:T(8,128)(2,1)} %get-tuple-element.31), channel_id=1, source_target_pairs={{0,12},{4,8},{8,4},{12,0},{16,28},{20,24},{24,20},{28,16},{1,13},{... | collective-permute-start | bytes 221192 | tf_op jit(solution)/shard_map/ppermute | solution.py:296
  8.9 0.2 collective-permute-done.4.refs_4_
  9.1 0.4 collective-permute-start.5
  9.5 0.9 %collective-permute-done.3.refs_6_ = bf16[144,256]{1,0:T(8,128)(2,1)S(1)} collective-permute-done((bf16[144,256]{1,0:T(8,128)(2,1)}, bf16[144,256]{1,0:T(8,128)(2,1)S(1)}, u32[]{:S(2)}, u32[]{:S(2)}) %collective-permute-start.3) | collective-permute-done | bytes 73760 | tf_op jit(solution)/shard_map/ppermute | solution.py:296
  10.4 3.3 %collective-permute-done.2.refs_3_ = bf16[144,256]{1,0:T(8,128)(2,1)S(1)} collective-permute-done((bf16[144,256]{1,0:T(8,128)(2,1)}, bf16[144,256]{1,0:T(8,128)(2,1)S(1)}, u32[]{:S(2)}, u32[]{:S(2)}) %collective-permute-start.2) | collective-permute-done | bytes 73760 | tf_op jit(solution)/shard_map/ppermute | solution.py:296
  13.7 0.0 collective-permute-done.1.refs_5_
  13.7 0.9 %dynamic-slice_bitcast_fusion.2 = bf16[1,512,128]{2,1,0:T(8,128)(2,1)S(1)} fusion(bf16[4096,128]{1,0:T(8,128)(2,1)} %wq_ref.3, s32[]{:T(128)S(6)} %select_n.2), kind=kLoop, calls=%fused_computation.6 | loop fusion | bytes 262148 | tf_op jit(solution)/shard_map/stack | solution.py:332
  14.6 0.0 copy-start.3
  14.6 0.0 copy-start.4
  14.6 0.0 copy-start.5
  14.6 0.0 copy-start.6
  14.6 0.0 copy-start.7
  14.7 0.0 copy-start.8
  14.7 0.0 copy-start.1
  14.7 1.1 %dynamic-slice_bitcast_fusion = (bf16[1,512,128]{2,1,0:T(8,128)(2,1)S(1)}, bf16[1,512,128]{2,1,0:T(8,128)(2,1)S(1)}) fusion(bf16[4096,128]{1,0:T(8,128)(2,1)} %wv_ref.3, s32[]{:T(128)S(6)} %select_n.2, bf16[4096,128]{1,0:T(8,128)(2,1)} %wk_ref.3), kind=kLoop, calls=%fused_computation.4 | loop fusion | bytes 524292 | tf_op jit(solution)/shard_map/stack | solution.py:332
  15.8 0.0 copy-start
  15.8 0.0 collective-permute-done.6.refs_2_
  15.8 0.0 collective-permute-done.5.refs_1_
  15.9 0.0 copy-done.3
  15.9 0.0 copy-done.4
  15.9 0.0 copy-done.5
  15.9 0.0 copy-done.6
  15.9 0.0 copy-done.7
  15.9 0.0 copy-done.8
  15.9 0.9 %shard_map.92 = (bf16[128,384]{1,0:T(8,128)(2,1)S(1)}, bf16[128,512]{1,0:T(8,128)(2,1)S(1)}) custom-call(bf16[128,128]{1,0:T(8,128)(2,1)S(1)} %copy-done.3, bf16[128,128]{1,0:T(8,128)(2,1)S(1)} %copy-done.4, bf16[128,128]{1,0:T(8,128)(2,1)S(1)} %copy-done.5, bf16[128,128]{1,0:T(8,128)(2,1)S(1)} %copy-done.6, bf16[128,128]{1,0:T(8,128)(2,1)S(1)} %copy-done.7, ...), custom_call_target="tpu_custom_call" | custom-call | flops 335544320 | bytes 1310720 | tf_op jit(solution)/shard_map/pallas_call | solution.py:340
  16.9 1.6 %collective-permute-start.9 = (bf16[128,512]{1,0:T(8,128)(2,1)S(1)}, bf16[128,512]{1,0:T(8,128)(2,1)S(1)}, u32[]{:S(2)}, u32[]{:S(2)}) collective-permute-start(bf16[128,512]{1,0:T(8,128)(2,1)S(1)} %get-tuple-element.42), channel_id=1, source_target_pairs={{0,1},{1,0},{2,3},{3,2},{4,5},{5,4},{6,7},{7,6},{8,9},{9,8},{10,11... | collective-permute-start | bytes 393224 | tf_op jit(solution)/shard_map/ppermute | solution.py:296
  18.5 0.0 copy-done.1
  18.5 0.0 copy-done
  18.5 0.0 copy-start.2
  18.5 1.2 %copy-done.2 = bf16[4096,128]{1,0:T(8,128)(2,1)S(1)} copy-done((bf16[4096,128]{1,0:T(8,128)(2,1)S(1)}, bf16[4096,128]{1,0:T(8,128)(2,1)}, u32[]{:S(2)}) %copy-start.2) | copy-done | bytes 1048600
  19.7 0.5 %shard_map.94 = (bf16[128,512]{1,0:T(8,128)(2,1)S(1)}, f32[128,512]{1,0:T(8,128)S(1)}, f32[128,512]{1,0:T(8,128)S(1)}) custom-call(bf16[128,384]{1,0:T(8,128)(2,1)S(1)} %get-tuple-element.36.grads, bf16[4096,128]{1,0:T(8,128)(2,1)S(1)} %copy-done.2, bf16[4096,128]{1,0:T(8,128)(2,1)S(1)} %copy-done.1, bf16[4096,128]{1,0:T(8,128)(2,1)S(1)} %copy-done), custom_call_target="tpu_custom_call" | custom-call | flops 150994944 | bytes 1179648 | tf_op jit(solution)/shard_map/pallas_call | solution.py:355
  20.2 0.5 %collective-permute-start.7 = (bf16[128,512]{1,0:T(8,128)(2,1)S(1)}, bf16[128,512]{1,0:T(8,128)(2,1)S(1)}, u32[]{:S(2)}, u32[]{:S(2)}) collective-permute-start(bf16[128,512]{1,0:T(8,128)(2,1)S(1)} %get-tuple-element.39), channel_id=1, source_target_pairs={{0,1},{1,0},{2,3},{3,2},{4,5},{5,4},{6,7},{7,6},{8,9},{9,8},{10,11... | collective-permute-start | bytes 393224 | tf_op jit(solution)/shard_map/ppermute | solution.py:296
  20.8 0.6 %shard_map.93 = (bf16[128,1024]{1,0:T(8,128)(2,1)S(1)}, f32[128,1024]{1,0:T(8,128)S(1)}) custom-call(bf16[128,384]{1,0:T(8,128)(2,1)S(1)} %get-tuple-element.36.grads, bf16[4096,128]{1,0:T(8,128)(2,1)S(1)} %copy-done.2, bf16[4096,128]{1,0:T(8,128)(2,1)S(1)} %copy-done.1, bf16[4096,128]{1,0:T(8,128)(2,1)S(1)} %copy-done), custom_call_target="tpu_custom_call" | custom-call | flops 201326592 | bytes 1572864 | tf_op jit(solution)/shard_map/pallas_call | solution.py:355
  21.4 0.9 %collective-permute-done.9 = bf16[128,512]{1,0:T(8,128)(2,1)S(1)} collective-permute-done((bf16[128,512]{1,0:T(8,128)(2,1)S(1)}, bf16[128,512]{1,0:T(8,128)(2,1)S(1)}, u32[]{:S(2)}, u32[]{:S(2)}) %collective-permute-start.9) | collective-permute-done | bytes 131104 | tf_op jit(solution)/shard_map/ppermute | solution.py:296
  22.4 2.6 %collective-permute-start.10 = (bf16[128,512]{1,0:T(8,128)(2,1)S(1)}, bf16[128,512]{1,0:T(8,128)(2,1)S(1)}, u32[]{:S(2)}, u32[]{:S(2)}) collective-permute-start(bf16[128,512]{1,0:T(8,128)(2,1)S(1)} %add_convert_fusion.2), channel_id=1, source_target_pairs={{0,2},{1,3},{2,0},{3,1},{4,6},{5,7},{6,4},{7,5},{8,10},{9,11},{10,... | collective-permute-start | bytes 393224 | tf_op jit(solution)/shard_map/ppermute | solution.py:296
  25.0 1.8 %collective-permute-done.7 = bf16[128,512]{1,0:T(8,128)(2,1)S(1)} collective-permute-done((bf16[128,512]{1,0:T(8,128)(2,1)S(1)}, bf16[128,512]{1,0:T(8,128)(2,1)S(1)}, u32[]{:S(2)}, u32[]{:S(2)}) %collective-permute-start.7) | collective-permute-done | bytes 131104 | tf_op jit(solution)/shard_map/ppermute | solution.py:296
  26.8 0.6 %collective-permute-start.8 = (bf16[128,1024]{1,0:T(8,128)(2,1)S(1)}, bf16[128,1024]{1,0:T(8,128)(2,1)S(1)}, u32[]{:S(2)}, u32[]{:S(2)}) collective-permute-start(bf16[128,1024]{1,0:T(8,128)(2,1)S(1)} %get-tuple-element.40), channel_id=1, source_target_pairs={{0,1},{1,0},{2,3},{3,2},{4,5},{5,4},{6,7},{7,6},{8,9},{9,8},{10,11... | collective-permute-start | bytes 786440 | tf_op jit(solution)/shard_map/ppermute | solution.py:296
  27.5 1.9 %collective-permute-start.11 = (bf16[128,512]{1,0:T(8,128)(2,1)S(1)}, bf16[128,512]{1,0:T(8,128)(2,1)S(1)}, u32[]{:S(2)}, u32[]{:S(2)}) collective-permute-start(bf16[128,512]{1,0:T(8,128)(2,1)S(1)} %add_convert_fusion.1), channel_id=1, source_target_pairs={{0,2},{1,3},{2,0},{3,1},{4,6},{5,7},{6,4},{7,5},{8,10},{9,11},{10,... | collective-permute-start | bytes 393224 | tf_op jit(solution)/shard_map/ppermute | solution.py:296
  29.4 0.9 %collective-permute-done.10 = bf16[128,512]{1,0:T(8,128)(2,1)S(1)} collective-permute-done((bf16[128,512]{1,0:T(8,128)(2,1)S(1)}, bf16[128,512]{1,0:T(8,128)(2,1)S(1)}, u32[]{:S(2)}, u32[]{:S(2)}) %collective-permute-start.10) | collective-permute-done | bytes 131104 | tf_op jit(solution)/shard_map/ppermute | solution.py:296
  30.3 5.6 %collective-permute-done.11 = bf16[128,512]{1,0:T(8,128)(2,1)S(1)} collective-permute-done((bf16[128,512]{1,0:T(8,128)(2,1)S(1)}, bf16[128,512]{1,0:T(8,128)(2,1)S(1)}, u32[]{:S(2)}, u32[]{:S(2)}) %collective-permute-start.11) | collective-permute-done | bytes 131104 | tf_op jit(solution)/shard_map/ppermute | solution.py:296
  35.9 0.8 %collective-permute-done.8 = bf16[128,1024]{1,0:T(8,128)(2,1)S(1)} collective-permute-done((bf16[128,1024]{1,0:T(8,128)(2,1)S(1)}, bf16[128,1024]{1,0:T(8,128)(2,1)S(1)}, u32[]{:S(2)}, u32[]{:S(2)}) %collective-permute-start.8) | collective-permute-done | bytes 262176 | tf_op jit(solution)/shard_map/ppermute | solution.py:296
  36.7 0.8 %add_convert_fusion = bf16[128,1024]{1,0:T(8,128)(2,1)} fusion(f32[128,1024]{1,0:T(8,128)S(1)} %get-tuple-element.37, bf16[128,1024]{1,0:T(8,128)(2,1)S(1)} %collective-permute-done.8, bf16[128,512]{1,0:T(8,128)(2,1)S(1)} %collective-permute-done.11, bf16[128,512]{1,0:T(8,128)(2,1)S(1)} %collective-permute-done.10), kind=kLoop, calls=%fused_computation | loop fusion | flops 1048576 | bytes 1310720 | tf_op jit(solution)/shard_map/convert_element_type | solution.py:374
  (3 shorter events, 0.1 us)
Async XLA Ops:
  1.7 6.1 %collective-permute-start = (bf16[144,256]{1,0:T(8,128)(2,1)}, bf16[144,256]{1,0:T(8,128)(2,1)S(1)}, u32[]{:S(2)}, u32[]{:S(2)}) collective-permute-start(bf16[144,256]{1,0:T(8,128)(2,1)} %get-tuple-element.25), channel_id=1, source_target_pairs={{0,4},{4,0},{8,12},{12,8},{16,20},{20,16},{24,28},{28,24},{1,5},{5... | collective-permute-start | bytes 221192 | tf_op jit(solution)/shard_map/ppermute | solution.py:296
  2.2 6.9 %collective-permute-start.4 = (bf16[144,256]{1,0:T(8,128)(2,1)}, bf16[144,256]{1,0:T(8,128)(2,1)S(1)}, u32[]{:S(2)}, u32[]{:S(2)}) collective-permute-start(bf16[144,256]{1,0:T(8,128)(2,1)} %get-tuple-element.26), channel_id=1, source_target_pairs={{0,20},{4,16},{8,28},{12,24},{16,4},{20,0},{24,12},{28,8},{1,21},{... | collective-permute-start | bytes 221192 | tf_op jit(solution)/shard_map/ppermute | solution.py:296
  4.8 5.5 %collective-permute-start.3 = (bf16[144,256]{1,0:T(8,128)(2,1)}, bf16[144,256]{1,0:T(8,128)(2,1)S(1)}, u32[]{:S(2)}, u32[]{:S(2)}) collective-permute-start(bf16[144,256]{1,0:T(8,128)(2,1)} %get-tuple-element.26), channel_id=1, source_target_pairs={{0,28},{4,24},{8,20},{12,16},{16,12},{20,8},{24,4},{28,0},{1,29},{... | collective-permute-start | bytes 221192 | tf_op jit(solution)/shard_map/ppermute | solution.py:296
  5.9 7.7 %collective-permute-start.2 = (bf16[144,256]{1,0:T(8,128)(2,1)}, bf16[144,256]{1,0:T(8,128)(2,1)S(1)}, u32[]{:S(2)}, u32[]{:S(2)}) collective-permute-start(bf16[144,256]{1,0:T(8,128)(2,1)} %get-tuple-element.26), channel_id=1, source_target_pairs={{0,16},{4,20},{8,24},{12,28},{16,0},{20,4},{24,8},{28,12},{1,17},{... | collective-permute-start | bytes 221192 | tf_op jit(solution)/shard_map/ppermute | solution.py:296
  7.5 6.2 %collective-permute-start.1 = (bf16[144,256]{1,0:T(8,128)(2,1)}, bf16[144,256]{1,0:T(8,128)(2,1)S(1)}, u32[]{:S(2)}, u32[]{:S(2)}) collective-permute-start(bf16[144,256]{1,0:T(8,128)(2,1)} %get-tuple-element.26), channel_id=1, source_target_pairs={{0,24},{4,28},{8,16},{12,20},{16,8},{20,12},{24,0},{28,4},{1,25},{... | collective-permute-start | bytes 221192 | tf_op jit(solution)/shard_map/ppermute | solution.py:296
  7.8 8.0 %collective-permute-start.6 = (bf16[144,256]{1,0:T(8,128)(2,1)}, bf16[144,256]{1,0:T(8,128)(2,1)S(1)}, u32[]{:S(2)}, u32[]{:S(2)}) collective-permute-start(bf16[144,256]{1,0:T(8,128)(2,1)} %get-tuple-element.31), channel_id=1, source_target_pairs={{0,12},{4,8},{8,4},{12,0},{16,28},{20,24},{24,20},{28,16},{1,13},{... | collective-permute-start | bytes 221192 | tf_op jit(solution)/shard_map/ppermute | solution.py:296
  9.1 6.7 %collective-permute-start.5 = (bf16[144,256]{1,0:T(8,128)(2,1)}, bf16[144,256]{1,0:T(8,128)(2,1)S(1)}, u32[]{:S(2)}, u32[]{:S(2)}) collective-permute-start(bf16[144,256]{1,0:T(8,128)(2,1)} %get-tuple-element.31), channel_id=1, source_target_pairs={{0,8},{4,12},{8,0},{12,4},{16,24},{20,28},{24,16},{28,20},{1,9},{5... | collective-permute-start | bytes 221192 | tf_op jit(solution)/shard_map/ppermute | solution.py:296
  14.6 1.3 %copy-start.3 = (bf16[128,128]{1,0:T(8,128)(2,1)S(1)}, bf16[128,128]{1,0:T(8,128)(2,1)}, u32[]{:S(2)}) copy-start(bf16[128,128]{1,0:T(8,128)(2,1)} %q_ref.1) | copy-start | bytes 98308
  14.6 1.3 %copy-start.4 = (bf16[128,128]{1,0:T(8,128)(2,1)S(1)}, bf16[128,128]{1,0:T(8,128)(2,1)}, u32[]{:S(2)}) copy-start(bf16[128,128]{1,0:T(8,128)(2,1)} %k_ref.1) | copy-start | bytes 98308
  14.6 1.3 %copy-start.5 = (bf16[128,128]{1,0:T(8,128)(2,1)S(1)}, bf16[128,128]{1,0:T(8,128)(2,1)}, u32[]{:S(2)}) copy-start(bf16[128,128]{1,0:T(8,128)(2,1)} %v_ref.1) | copy-start | bytes 98308
  14.6 1.3 %copy-start.6 = (bf16[128,128]{1,0:T(8,128)(2,1)S(1)}, bf16[128,128]{1,0:T(8,128)(2,1)}, u32[]{:S(2)}) copy-start(bf16[128,128]{1,0:T(8,128)(2,1)} %g_ref.1) | copy-start | bytes 98308
  14.6 1.3 %copy-start.7 = (bf16[128,128]{1,0:T(8,128)(2,1)S(1)}, bf16[128,128]{1,0:T(8,128)(2,1)}, u32[]{:S(2)}) copy-start(bf16[128,128]{1,0:T(8,128)(2,1)} %a_ref.1) | copy-start | bytes 98308
  14.7 1.2 %copy-start.8 = (f32[128,1]{0,1:T(1,128)S(1)}, f32[128,1]{0,1:T(1,128)}, u32[]{:S(2)}) copy-start(f32[128,1]{0,1:T(1,128)} %param.14) | copy-start | bytes 1540
  14.7 3.8 %copy-start.1 = (bf16[4096,128]{1,0:T(8,128)(2,1)S(1)}, bf16[4096,128]{1,0:T(8,128)(2,1)}, u32[]{:S(2)}) copy-start(bf16[4096,128]{1,0:T(8,128)(2,1)} %wk_ref.3) | copy-start | bytes 3145732
  15.8 2.7 %copy-start = (bf16[4096,128]{1,0:T(8,128)(2,1)S(1)}, bf16[4096,128]{1,0:T(8,128)(2,1)}, u32[]{:S(2)}) copy-start(bf16[4096,128]{1,0:T(8,128)(2,1)} %wv_ref.3) | copy-start | bytes 3145732
  16.9 5.5 %collective-permute-start.9 = (bf16[128,512]{1,0:T(8,128)(2,1)S(1)}, bf16[128,512]{1,0:T(8,128)(2,1)S(1)}, u32[]{:S(2)}, u32[]{:S(2)}) collective-permute-start(bf16[128,512]{1,0:T(8,128)(2,1)S(1)} %get-tuple-element.42), channel_id=1, source_target_pairs={{0,1},{1,0},{2,3},{3,2},{4,5},{5,4},{6,7},{7,6},{8,9},{9,8},{10,11... | collective-permute-start | bytes 393224 | tf_op jit(solution)/shard_map/ppermute | solution.py:296
  18.5 1.2 %copy-start.2 = (bf16[4096,128]{1,0:T(8,128)(2,1)S(1)}, bf16[4096,128]{1,0:T(8,128)(2,1)}, u32[]{:S(2)}) copy-start(bf16[4096,128]{1,0:T(8,128)(2,1)} %wq_ref.3) | copy-start | bytes 3145732
  20.2 6.6 %collective-permute-start.7 = (bf16[128,512]{1,0:T(8,128)(2,1)S(1)}, bf16[128,512]{1,0:T(8,128)(2,1)S(1)}, u32[]{:S(2)}, u32[]{:S(2)}) collective-permute-start(bf16[128,512]{1,0:T(8,128)(2,1)S(1)} %get-tuple-element.39), channel_id=1, source_target_pairs={{0,1},{1,0},{2,3},{3,2},{4,5},{5,4},{6,7},{7,6},{8,9},{9,8},{10,11... | collective-permute-start | bytes 393224 | tf_op jit(solution)/shard_map/ppermute | solution.py:296
  22.4 7.9 %collective-permute-start.10 = (bf16[128,512]{1,0:T(8,128)(2,1)S(1)}, bf16[128,512]{1,0:T(8,128)(2,1)S(1)}, u32[]{:S(2)}, u32[]{:S(2)}) collective-permute-start(bf16[128,512]{1,0:T(8,128)(2,1)S(1)} %add_convert_fusion.2), channel_id=1, source_target_pairs={{0,2},{1,3},{2,0},{3,1},{4,6},{5,7},{6,4},{7,5},{8,10},{9,11},{10,... | collective-permute-start | bytes 393224 | tf_op jit(solution)/shard_map/ppermute | solution.py:296
  26.8 9.9 %collective-permute-start.8 = (bf16[128,1024]{1,0:T(8,128)(2,1)S(1)}, bf16[128,1024]{1,0:T(8,128)(2,1)S(1)}, u32[]{:S(2)}, u32[]{:S(2)}) collective-permute-start(bf16[128,1024]{1,0:T(8,128)(2,1)S(1)} %get-tuple-element.40), channel_id=1, source_target_pairs={{0,1},{1,0},{2,3},{3,2},{4,5},{5,4},{6,7},{7,6},{8,9},{9,8},{10,11... | collective-permute-start | bytes 786440 | tf_op jit(solution)/shard_map/ppermute | solution.py:296
  27.5 8.5 %collective-permute-start.11 = (bf16[128,512]{1,0:T(8,128)(2,1)S(1)}, bf16[128,512]{1,0:T(8,128)(2,1)S(1)}, u32[]{:S(2)}, u32[]{:S(2)}) collective-permute-start(bf16[128,512]{1,0:T(8,128)(2,1)S(1)} %add_convert_fusion.1), channel_id=1, source_target_pairs={{0,2},{1,3},{2,0},{3,1},{4,6},{5,7},{6,4},{7,5},{8,10},{9,11},{10,... | collective-permute-start | bytes 393224 | tf_op jit(solution)/shard_map/ppermute | solution.py:296

commit v11 on v10

--- a/solution.py
+++ b/solution.py
@@ -232,16 +232,14 @@
         out_ref[:, at : at + cols] = dot_nt(grads[...], weight).astype(out_ref.dtype)
 
 
-def near_kernel(scale, q_ref, k_ref, v_ref, g_ref, a_ref, n_ref, w_ref, *refs):
+def near_kernel(scale, part, q_ref, k_ref, v_ref, g_ref, a_ref, n_ref, wq_ref, wk_ref, wv_ref, *refs):
     grads, front = refs[-2:]
     got = refs[:-2]
     rows, width = q_ref.shape
     me = lax.axis_index("ctx")
     exponent = scale * math.log2(math.e)
     query, key, value, grad = q_ref[...], k_ref[...], v_ref[...], g_ref[...]
-    norm = (1.0 / scale) * jnp.sum(
-        jnp.where(diagonal(rows), n_ref[...], 0.0), axis=1, keepdims=True
-    )
+    norm = jnp.sum(jnp.where(diagonal(rows), n_ref[...], 0.0), axis=1, keepdims=True)
     delta = delta_of(grad, a_ref[...])
     row_at = lax.broadcasted_iota(jnp.int32, (rows, rows), 0)
     col_at = lax.broadcasted_iota(jnp.int32, (rows, rows), 1)
@@ -272,7 +270,8 @@
     grads[:, :width] = (scale * (query_sum + both_sum[:rows])).astype(jnp.bfloat16)
     grads[:, width : 2 * width] = (scale * (key_sum + both_sum[rows:])).astype(jnp.bfloat16)
     grads[:, 2 * width :] = value_sum.astype(jnp.bfloat16)
-    project(grads, [w_ref.at[at] for at in range(w_ref.shape[0])], 0, front)
+    start = (lax.axis_index("head") ^ 3) * part
+    project(grads, (wq_ref, wk_ref, wv_ref), start, front)
 
 
 def far_kernel(part, grads, wq_ref, wk_ref, wv_ref, last, front, back):
@@ -319,28 +318,27 @@
             pltpu.SemaphoreType.DMA((2 * bits,)),
             pltpu.SemaphoreType.DMA((bits,)),
         ],
-        compiler_params=pltpu.CompilerParams(vmem_limit_bytes=60 * MIB),
+        compiler_params=pltpu.CompilerParams(vmem_limit_bytes=56 * MIB),
+        cost_estimate=pl.CostEstimate(
+            flops=5000000000, bytes_accessed=20 * rows * width, transcendentals=0
+        ),
     )(*own)
     got = {}
     for at in range(ctx - 1, 0, -1):
         got[at] = swap(sent[at.bit_length() - 1], "ctx", at)
-    soon = [at for at in (1, 6, 4, 7, 5) if at < ctx]
-    early = tuple(got[at] for at in soon)
-    early, first_weights = lax.optimization_barrier((early, weights))
+    soon = [at for at in (1,6,4,7,5) if at < ctx]
+    early, norm = lax.optimization_barrier((tuple(got[at] for at in soon), own[-1]))
     got.update(zip(soon, early))
-    start = (lax.axis_index("head") ^ 3) * part
-    weight = jnp.stack(
-        [lax.dynamic_slice_in_dim(one, start, part // 2, 0) for one in first_weights]
-    )
+    own = own[:-1] + (norm * (1.0 / scale),)
     got = [got[at] for at in range(1, ctx)]
     half_low = jax.ShapeDtypeStruct((rows, part // 2), jnp.bfloat16)
     half = jax.ShapeDtypeStruct((rows, part // 2), jnp.float32)
     low = jax.ShapeDtypeStruct((rows, part), jnp.bfloat16)
     full = jax.ShapeDtypeStruct((rows, part), jnp.float32)
     grads, front = pl.pallas_call(
-        functools.partial(near_kernel, scale),
+        functools.partial(near_kernel, scale, part),
         out_shape=[jax.ShapeDtypeStruct((rows, 3 * width), jnp.bfloat16), half_low],
-        in_specs=[vmem] * (ctx + 6),
+        in_specs=[vmem] * (ctx + 8),
         out_specs=[vmem] * 2,
         compiler_params=params,
         cost_estimate=pl.CostEstimate(
@@ -348,7 +346,7 @@
             bytes_accessed=4 * rows * ctx * width + 6 * part * width,
             transcendentals=rows * rows * ctx,
         ),
-    )(*own, weight, *got)
+    )(*own, *weights, *got)
     front = swap(front, "head", 1)
     def projected(kernel, outs, operands):
         count = sum(out.shape[1] for out in outs)

time: 37.7 us -> 37.1 us (0.984)
  the two profiles are of different devices: /device:TPU:0 before, /device:TPU:30 now
where the time goes in v11:
time: 37.1 us; the launch traced here: 36.9 us
  waiting for transfers between devices  22.3 us (60%)
  starting transfers between devices  9.75 us (26%)
  Pallas kernels  3.86 us (10%)
  other arithmetic  0.85 us (2%)
    ppermute x12, waiting for transfers between devices, swap(): return lax.ppermute(value, axis, [(at, at ^ offset) for at in range(size)])  22.3 us
    ppermute x12, starting transfers between devices, swap(): return lax.ppermute(value, axis, [(at, at ^ offset) for at in range(size)])  9.75 us
    pallas_call x1, Pallas kernels, near_body(): pl.pallas_call(send_kernel, out_shape=[hop] * bits, in_specs=[hbm] * 6, o...  1.82 us
    pallas_call x2, Pallas kernels, projected(): pl.pallas_call(functools.partial(kernel, part), out_shape=outs, in_specs=...  1.12 us
    pallas_call x1, Pallas kernels, near_body(): pl.pallas_call(functools.partial(near_kernel, scale, part), out_shape=[ja...  0.93 us
    convert_element_type x1, other arithmetic, near_body(): return (total + near.astype(jnp.float32) + far_sum).astype(jnp.bfloat16)  0.79 us
  transfers between devices with their start and end apart: 12, of which 7 were waited for; matrix products, arithmetic and copies ran while one was open for 0% of the time, Pallas kernels for 3%

profile of v11, /device:TPU:30, one launch (start us, length us, event | category | flops | bytes accessed | tf_op | source)
XLA Modules:
  0.0 36.9 jit_solution(17764895569022309639)
XLA Ops:
  0.0 0.0 copy-start
  0.0 0.0 copy-start.1
  0.0 0.0 copy-start.2
  0.0 0.0 copy-start.3
  0.0 0.0 copy-start.4
  0.0 0.0 copy-start.5
  0.0 0.0 copy-start.6
  0.0 0.0 copy-start.7
  0.1 1.8 %shard_map.91 = (bf16[144,256]{1,0:T(8,128)(2,1)}, bf16[144,256]{1,0:T(8,128)(2,1)}, bf16[144,256]{1,0:T(8,128)(2,1)}) custom-call(bf16[128,128]{1,0:T(8,128)(2,1)} %q_ref.1, bf16[128,128]{1,0:T(8,128)(2,1)} %k_ref.1, bf16[128,128]{1,0:T(8,128)(2,1)} %v_ref.1, bf16[128,128]{1,0:T(8,128)(2,1)} %g_ref.1, bf16[128,128]{1,0:T(8,128)(2,1)} %a_ref.1, f32[1,128]{1,0:T(1,128)} %bitcast.1), custom_call_target="tpu_custom_call" | custom-call | flops 5000000000 | bytes 327680 | tf_op jit(solution)/shard_map/pallas_call | solution.py:308
  1.9 0.1 collective-permute-start
  2.0 0.0 copy-start.8
  2.0 0.6 %collective-permute-start.4 = (bf16[144,256]{1,0:T(8,128)(2,1)}, bf16[144,256]{1,0:T(8,128)(2,1)S(1)}, u32[]{:S(2)}, u32[]{:S(2)}) collective-permute-start(bf16[144,256]{1,0:T(8,128)(2,1)} %get-tuple-element.24), channel_id=1, source_target_pairs={{0,20},{4,16},{8,28},{12,24},{16,4},{20,0},{24,12},{28,8},{1,21},{... | collective-permute-start | bytes 221192 | tf_op jit(solution)/shard_map/ppermute | solution.py:295
  2.6 1.2 %collective-permute-start.3 = (bf16[144,256]{1,0:T(8,128)(2,1)}, bf16[144,256]{1,0:T(8,128)(2,1)S(1)}, u32[]{:S(2)}, u32[]{:S(2)}) collective-permute-start(bf16[144,256]{1,0:T(8,128)(2,1)} %get-tuple-element.24), channel_id=1, source_target_pairs={{0,28},{4,24},{8,20},{12,16},{16,12},{20,8},{24,4},{28,0},{1,29},{... | collective-permute-start | bytes 221192 | tf_op jit(solution)/shard_map/ppermute | solution.py:295
  3.8 0.5 %collective-permute-start.2 = (bf16[144,256]{1,0:T(8,128)(2,1)}, bf16[144,256]{1,0:T(8,128)(2,1)S(1)}, u32[]{:S(2)}, u32[]{:S(2)}) collective-permute-start(bf16[144,256]{1,0:T(8,128)(2,1)} %get-tuple-element.24), channel_id=1, source_target_pairs={{0,16},{4,20},{8,24},{12,28},{16,0},{20,4},{24,8},{28,12},{1,17},{... | collective-permute-start | bytes 221192 | tf_op jit(solution)/shard_map/ppermute | solution.py:295
  4.3 2.4 %collective-permute-start.1 = (bf16[144,256]{1,0:T(8,128)(2,1)}, bf16[144,256]{1,0:T(8,128)(2,1)S(1)}, u32[]{:S(2)}, u32[]{:S(2)}) collective-permute-start(bf16[144,256]{1,0:T(8,128)(2,1)} %get-tuple-element.24), channel_id=1, source_target_pairs={{0,24},{4,28},{8,16},{12,20},{16,8},{20,12},{24,0},{28,4},{1,25},{... | collective-permute-start | bytes 221192 | tf_op jit(solution)/shard_map/ppermute | solution.py:295
  6.7 0.0 collective-permute-done.refs_0_
  6.7 0.0 collective-permute-start.6
  6.7 0.0 collective-permute-done.4.refs_4_
  6.7 1.5 %collective-permute-start.5 = (bf16[144,256]{1,0:T(8,128)(2,1)}, bf16[144,256]{1,0:T(8,128)(2,1)S(1)}, u32[]{:S(2)}, u32[]{:S(2)}) collective-permute-start(bf16[144,256]{1,0:T(8,128)(2,1)} %get-tuple-element.27), channel_id=1, source_target_pairs={{0,8},{4,12},{8,0},{12,4},{16,24},{20,28},{24,16},{28,20},{1,9},{5... | collective-permute-start | bytes 221192 | tf_op jit(solution)/shard_map/ppermute | solution.py:295
  8.2 0.0 collective-permute-done.3.refs_6_
  8.2 3.3 %collective-permute-done.2.refs_3_ = bf16[144,256]{1,0:T(8,128)(2,1)S(1)} collective-permute-done((bf16[144,256]{1,0:T(8,128)(2,1)}, bf16[144,256]{1,0:T(8,128)(2,1)S(1)}, u32[]{:S(2)}, u32[]{:S(2)}) %collective-permute-start.2) | collective-permute-done | bytes 73760 | tf_op jit(solution)/shard_map/ppermute | solution.py:295
  11.6 0.0 collective-permute-done.1.refs_5_
  11.6 0.0 copy-done.8
  11.6 0.0 collective-permute-done.6.refs_2_
  11.6 0.7 %collective-permute-done.5.refs_1_ = bf16[144,256]{1,0:T(8,128)(2,1)S(1)} collective-permute-done((bf16[144,256]{1,0:T(8,128)(2,1)}, bf16[144,256]{1,0:T(8,128)(2,1)S(1)}, u32[]{:S(2)}, u32[]{:S(2)}) %collective-permute-start.5) | collective-permute-done | bytes 73760 | tf_op jit(solution)/shard_map/ppermute | solution.py:295
  12.3 0.0 copy-done
  12.3 0.0 copy-done.1
  12.3 0.0 copy-done.2
  12.3 0.0 copy-done.3
  12.3 0.0 copy-done.4
  12.3 0.0 copy-done.5
  12.4 0.0 copy-done.6
  12.4 0.0 copy-done.7
  12.4 0.9 %shard_map.92 = (bf16[128,384]{1,0:T(8,128)(2,1)S(1)}, bf16[128,512]{1,0:T(8,128)(2,1)S(1)}) custom-call(bf16[128,128]{1,0:T(8,128)(2,1)S(1)} %copy-done.3, bf16[128,128]{1,0:T(8,128)(2,1)S(1)} %copy-done.4, bf16[128,128]{1,0:T(8,128)(2,1)S(1)} %copy-done.5, bf16[128,128]{1,0:T(8,128)(2,1)S(1)} %copy-done.6, bf16[128,128]{1,0:T(8,128)(2,1)S(1)} %copy-done.7, ...), custom_call_target="tpu_custom_call" | custom-call | flops 335544320 | bytes 1310720 | tf_op jit(solution)/shard_map/pallas_call | solution.py:338
  13.3 0.5 %collective-permute-start.9 = (bf16[128,512]{1,0:T(8,128)(2,1)S(1)}, bf16[128,512]{1,0:T(8,128)(2,1)S(1)}, u32[]{:S(2)}, u32[]{:S(2)}) collective-permute-start(bf16[128,512]{1,0:T(8,128)(2,1)S(1)} %get-tuple-element.38), channel_id=1, source_target_pairs={{0,1},{1,0},{2,3},{3,2},{4,5},{5,4},{6,7},{7,6},{8,9},{9,8},{10,11... | collective-permute-start | bytes 393224 | tf_op jit(solution)/shard_map/ppermute | solution.py:295
  13.8 0.5 %shard_map.94 = (bf16[128,512]{1,0:T(8,128)(2,1)S(1)}, f32[128,512]{1,0:T(8,128)S(1)}, f32[128,512]{1,0:T(8,128)S(1)}) custom-call(bf16[128,384]{1,0:T(8,128)(2,1)S(1)} %get-tuple-element.32.grads, bf16[4096,128]{1,0:T(8,128)(2,1)S(1)} %copy-done, bf16[4096,128]{1,0:T(8,128)(2,1)S(1)} %copy-done.1, bf16[4096,128]{1,0:T(8,128)(2,1)S(1)} %copy-done.2), custom_call_target="tpu_custom_call" | custom-call | flops 150994944 | bytes 1179648 | tf_op jit(solution)/shard_map/pallas_call | solution.py:353
  14.3 1.6 %collective-permute-start.7 = (bf16[128,512]{1,0:T(8,128)(2,1)S(1)}, bf16[128,512]{1,0:T(8,128)(2,1)S(1)}, u32[]{:S(2)}, u32[]{:S(2)}) collective-permute-start(bf16[128,512]{1,0:T(8,128)(2,1)S(1)} %get-tuple-element.35), channel_id=1, source_target_pairs={{0,1},{1,0},{2,3},{3,2},{4,5},{5,4},{6,7},{7,6},{8,9},{9,8},{10,11... | collective-permute-start | bytes 393224 | tf_op jit(solution)/shard_map/ppermute | solution.py:295
  16.0 0.6 %shard_map.93 = (bf16[128,1024]{1,0:T(8,128)(2,1)S(1)}, f32[128,1024]{1,0:T(8,128)S(1)}) custom-call(bf16[128,384]{1,0:T(8,128)(2,1)S(1)} %get-tuple-element.32.grads, bf16[4096,128]{1,0:T(8,128)(2,1)S(1)} %copy-done, bf16[4096,128]{1,0:T(8,128)(2,1)S(1)} %copy-done.1, bf16[4096,128]{1,0:T(8,128)(2,1)S(1)} %copy-done.2), custom_call_target="tpu_custom_call" | custom-call | flops 201326592 | bytes 1572864 | tf_op jit(solution)/shard_map/pallas_call | solution.py:353
  16.6 2.9 %collective-permute-done.9 = bf16[128,512]{1,0:T(8,128)(2,1)S(1)} collective-permute-done((bf16[128,512]{1,0:T(8,128)(2,1)S(1)}, bf16[128,512]{1,0:T(8,128)(2,1)S(1)}, u32[]{:S(2)}, u32[]{:S(2)}) %collective-permute-start.9) | collective-permute-done | bytes 131104 | tf_op jit(solution)/shard_map/ppermute | solution.py:295
  19.5 0.4 %collective-permute-start.10 = (bf16[128,512]{1,0:T(8,128)(2,1)S(1)}, bf16[128,512]{1,0:T(8,128)(2,1)S(1)}, u32[]{:S(2)}, u32[]{:S(2)}) collective-permute-start(bf16[128,512]{1,0:T(8,128)(2,1)S(1)} %add_convert_fusion.2), channel_id=1, source_target_pairs={{0,2},{1,3},{2,0},{3,1},{4,6},{5,7},{6,4},{7,5},{8,10},{9,11},{10,... | collective-permute-start | bytes 393224 | tf_op jit(solution)/shard_map/ppermute | solution.py:295
  19.9 2.4 %collective-permute-done.7 = bf16[128,512]{1,0:T(8,128)(2,1)S(1)} collective-permute-done((bf16[128,512]{1,0:T(8,128)(2,1)S(1)}, bf16[128,512]{1,0:T(8,128)(2,1)S(1)}, u32[]{:S(2)}, u32[]{:S(2)}) %collective-permute-start.7) | collective-permute-done | bytes 131104 | tf_op jit(solution)/shard_map/ppermute | solution.py:295
  22.3 0.5 %collective-permute-start.8 = (bf16[128,1024]{1,0:T(8,128)(2,1)S(1)}, bf16[128,1024]{1,0:T(8,128)(2,1)S(1)}, u32[]{:S(2)}, u32[]{:S(2)}) collective-permute-start(bf16[128,1024]{1,0:T(8,128)(2,1)S(1)} %get-tuple-element.36), channel_id=1, source_target_pairs={{0,1},{1,0},{2,3},{3,2},{4,5},{5,4},{6,7},{7,6},{8,9},{9,8},{10,11... | collective-permute-start | bytes 786440 | tf_op jit(solution)/shard_map/ppermute | solution.py:295
  22.8 0.4 %collective-permute-start.11 = (bf16[128,512]{1,0:T(8,128)(2,1)S(1)}, bf16[128,512]{1,0:T(8,128)(2,1)S(1)}, u32[]{:S(2)}, u32[]{:S(2)}) collective-permute-start(bf16[128,512]{1,0:T(8,128)(2,1)S(1)} %add_convert_fusion.1), channel_id=1, source_target_pairs={{0,2},{1,3},{2,0},{3,1},{4,6},{5,7},{6,4},{7,5},{8,10},{9,11},{10,... | collective-permute-start | bytes 393224 | tf_op jit(solution)/shard_map/ppermute | solution.py:295
  23.2 6.1 %collective-permute-done.10 = bf16[128,512]{1,0:T(8,128)(2,1)S(1)} collective-permute-done((bf16[128,512]{1,0:T(8,128)(2,1)S(1)}, bf16[128,512]{1,0:T(8,128)(2,1)S(1)}, u32[]{:S(2)}, u32[]{:S(2)}) %collective-permute-start.10) | collective-permute-done | bytes 131104 | tf_op jit(solution)/shard_map/ppermute | solution.py:295
  29.3 3.0 %collective-permute-done.11 = bf16[128,512]{1,0:T(8,128)(2,1)S(1)} collective-permute-done((bf16[128,512]{1,0:T(8,128)(2,1)S(1)}, bf16[128,512]{1,0:T(8,128)(2,1)S(1)}, u32[]{:S(2)}, u32[]{:S(2)}) %collective-permute-start.11) | collective-permute-done | bytes 131104 | tf_op jit(solution)/shard_map/ppermute | solution.py:295
  32.3 3.8 %collective-permute-done.8 = bf16[128,1024]{1,0:T(8,128)(2,1)S(1)} collective-permute-done((bf16[128,1024]{1,0:T(8,128)(2,1)S(1)}, bf16[128,1024]{1,0:T(8,128)(2,1)S(1)}, u32[]{:S(2)}, u32[]{:S(2)}) %collective-permute-start.8) | collective-permute-done | bytes 262176 | tf_op jit(solution)/shard_map/ppermute | solution.py:295
  36.2 0.8 %add_convert_fusion = bf16[128,1024]{1,0:T(8,128)(2,1)} fusion(f32[128,1024]{1,0:T(8,128)S(1)} %get-tuple-element.33, bf16[128,1024]{1,0:T(8,128)(2,1)S(1)} %collective-permute-done.8, bf16[128,512]{1,0:T(8,128)(2,1)S(1)} %collective-permute-done.11, bf16[128,512]{1,0:T(8,128)(2,1)S(1)} %collective-permute-done.10), kind=kLoop, calls=%fused_computation | loop fusion | flops 1048576 | bytes 1310720 | tf_op jit(solution)/shard_map/convert_element_type | solution.py:372
  (3 shorter events, 0.1 us)
Async XLA Ops:
  0.0 12.3 %copy-start = (bf16[4096,128]{1,0:T(8,128)(2,1)S(1)}, bf16[4096,128]{1,0:T(8,128)(2,1)}, u32[]{:S(2)}) copy-start(bf16[4096,128]{1,0:T(8,128)(2,1)} %wq_ref.5) | copy-start | bytes 3145732
  0.0 12.3 %copy-start.1 = (bf16[4096,128]{1,0:T(8,128)(2,1)S(1)}, bf16[4096,128]{1,0:T(8,128)(2,1)}, u32[]{:S(2)}) copy-start(bf16[4096,128]{1,0:T(8,128)(2,1)} %wk_ref.5) | copy-start | bytes 3145732
  0.0 12.3 %copy-start.2 = (bf16[4096,128]{1,0:T(8,128)(2,1)S(1)}, bf16[4096,128]{1,0:T(8,128)(2,1)}, u32[]{:S(2)}) copy-start(bf16[4096,128]{1,0:T(8,128)(2,1)} %wv_ref.5) | copy-start | bytes 3145732
  0.0 12.3 %copy-start.3 = (bf16[128,128]{1,0:T(8,128)(2,1)S(1)}, bf16[128,128]{1,0:T(8,128)(2,1)}, u32[]{:S(2)}) copy-start(bf16[128,128]{1,0:T(8,128)(2,1)} %q_ref.1) | copy-start | bytes 98308
  0.0 12.3 %copy-start.4 = (bf16[128,128]{1,0:T(8,128)(2,1)S(1)}, bf16[128,128]{1,0:T(8,128)(2,1)}, u32[]{:S(2)}) copy-start(bf16[128,128]{1,0:T(8,128)(2,1)} %k_ref.1) | copy-start | bytes 98308
  0.0 12.3 %copy-start.5 = (bf16[128,128]{1,0:T(8,128)(2,1)S(1)}, bf16[128,128]{1,0:T(8,128)(2,1)}, u32[]{:S(2)}) copy-start(bf16[128,128]{1,0:T(8,128)(2,1)} %v_ref.1) | copy-start | bytes 98308
  0.0 12.3 %copy-start.6 = (bf16[128,128]{1,0:T(8,128)(2,1)S(1)}, bf16[128,128]{1,0:T(8,128)(2,1)}, u32[]{:S(2)}) copy-start(bf16[128,128]{1,0:T(8,128)(2,1)} %g_ref.1) | copy-start | bytes 98308
  0.0 12.3 %copy-start.7 = (bf16[128,128]{1,0:T(8,128)(2,1)S(1)}, bf16[128,128]{1,0:T(8,128)(2,1)}, u32[]{:S(2)}) copy-start(bf16[128,128]{1,0:T(8,128)(2,1)} %a_ref.1) | copy-start | bytes 98308
  1.9 4.8 %collective-permute-start = (bf16[144,256]{1,0:T(8,128)(2,1)}, bf16[144,256]{1,0:T(8,128)(2,1)S(1)}, u32[]{:S(2)}, u32[]{:S(2)}) collective-permute-start(bf16[144,256]{1,0:T(8,128)(2,1)} %get-tuple-element.23), channel_id=1, source_target_pairs={{0,4},{4,0},{8,12},{12,8},{16,20},{20,16},{24,28},{28,24},{1,5},{5... | collective-permute-start | bytes 221192 | tf_op jit(solution)/shard_map/ppermute | solution.py:295
  2.0 9.6 %copy-start.8 = (f32[128,1]{0,1:T(1,128)S(1)}, f32[128,1]{0,1:T(1,128)}, u32[]{:S(2)}) copy-start(f32[128,1]{0,1:T(1,128)} %param.14) | copy-start | bytes 1540
  2.0 4.8 %collective-permute-start.4 = (bf16[144,256]{1,0:T(8,128)(2,1)}, bf16[144,256]{1,0:T(8,128)(2,1)S(1)}, u32[]{:S(2)}, u32[]{:S(2)}) collective-permute-start(bf16[144,256]{1,0:T(8,128)(2,1)} %get-tuple-element.24), channel_id=1, source_target_pairs={{0,20},{4,16},{8,28},{12,24},{16,4},{20,0},{24,12},{28,8},{1,21},{... | collective-permute-start | bytes 221192 | tf_op jit(solution)/shard_map/ppermute | solution.py:295
  2.6 5.6 %collective-permute-start.3 = (bf16[144,256]{1,0:T(8,128)(2,1)}, bf16[144,256]{1,0:T(8,128)(2,1)S(1)}, u32[]{:S(2)}, u32[]{:S(2)}) collective-permute-start(bf16[144,256]{1,0:T(8,128)(2,1)} %get-tuple-element.24), channel_id=1, source_target_pairs={{0,28},{4,24},{8,20},{12,16},{16,12},{20,8},{24,4},{28,0},{1,29},{... | collective-permute-start | bytes 221192 | tf_op jit(solution)/shard_map/ppermute | solution.py:295
  3.8 7.8 %collective-permute-start.2 = (bf16[144,256]{1,0:T(8,128)(2,1)}, bf16[144,256]{1,0:T(8,128)(2,1)S(1)}, u32[]{:S(2)}, u32[]{:S(2)}) collective-permute-start(bf16[144,256]{1,0:T(8,128)(2,1)} %get-tuple-element.24), channel_id=1, source_target_pairs={{0,16},{4,20},{8,24},{12,28},{16,0},{20,4},{24,8},{28,12},{1,17},{... | collective-permute-start | bytes 221192 | tf_op jit(solution)/shard_map/ppermute | solution.py:295
  4.3 7.3 %collective-permute-start.1 = (bf16[144,256]{1,0:T(8,128)(2,1)}, bf16[144,256]{1,0:T(8,128)(2,1)S(1)}, u32[]{:S(2)}, u32[]{:S(2)}) collective-permute-start(bf16[144,256]{1,0:T(8,128)(2,1)} %get-tuple-element.24), channel_id=1, source_target_pairs={{0,24},{4,28},{8,16},{12,20},{16,8},{20,12},{24,0},{28,4},{1,25},{... | collective-permute-start | bytes 221192 | tf_op jit(solution)/shard_map/ppermute | solution.py:295
  6.7 4.9 %collective-permute-start.6 = (bf16[144,256]{1,0:T(8,128)(2,1)}, bf16[144,256]{1,0:T(8,128)(2,1)S(1)}, u32[]{:S(2)}, u32[]{:S(2)}) collective-permute-start(bf16[144,256]{1,0:T(8,128)(2,1)} %get-tuple-element.27), channel_id=1, source_target_pairs={{0,12},{4,8},{8,4},{12,0},{16,28},{20,24},{24,20},{28,16},{1,13},{... | collective-permute-start | bytes 221192 | tf_op jit(solution)/shard_map/ppermute | solution.py:295
  6.7 5.6 %collective-permute-start.5 = (bf16[144,256]{1,0:T(8,128)(2,1)}, bf16[144,256]{1,0:T(8,128)(2,1)S(1)}, u32[]{:S(2)}, u32[]{:S(2)}) collective-permute-start(bf16[144,256]{1,0:T(8,128)(2,1)} %get-tuple-element.27), channel_id=1, source_target_pairs={{0,8},{4,12},{8,0},{12,4},{16,24},{20,28},{24,16},{28,20},{1,9},{5... | collective-permute-start | bytes 221192 | tf_op jit(solution)/shard_map/ppermute | solution.py:295
  13.3 6.2 %collective-permute-start.9 = (bf16[128,512]{1,0:T(8,128)(2,1)S(1)}, bf16[128,512]{1,0:T(8,128)(2,1)S(1)}, u32[]{:S(2)}, u32[]{:S(2)}) collective-permute-start(bf16[128,512]{1,0:T(8,128)(2,1)S(1)} %get-tuple-element.38), channel_id=1, source_target_pairs={{0,1},{1,0},{2,3},{3,2},{4,5},{5,4},{6,7},{7,6},{8,9},{9,8},{10,11... | collective-permute-start | bytes 393224 | tf_op jit(solution)/shard_map/ppermute | solution.py:295
  14.3 8.0 %collective-permute-start.7 = (bf16[128,512]{1,0:T(8,128)(2,1)S(1)}, bf16[128,512]{1,0:T(8,128)(2,1)S(1)}, u32[]{:S(2)}, u32[]{:S(2)}) collective-permute-start(bf16[128,512]{1,0:T(8,128)(2,1)S(1)} %get-tuple-element.35), channel_id=1, source_target_pairs={{0,1},{1,0},{2,3},{3,2},{4,5},{5,4},{6,7},{7,6},{8,9},{9,8},{10,11... | collective-permute-start | bytes 393224 | tf_op jit(solution)/shard_map/ppermute | solution.py:295
  19.5 9.8 %collective-permute-start.10 = (bf16[128,512]{1,0:T(8,128)(2,1)S(1)}, bf16[128,512]{1,0:T(8,128)(2,1)S(1)}, u32[]{:S(2)}, u32[]{:S(2)}) collective-permute-start(bf16[128,512]{1,0:T(8,128)(2,1)S(1)} %add_convert_fusion.2), channel_id=1, source_target_pairs={{0,2},{1,3},{2,0},{3,1},{4,6},{5,7},{6,4},{7,5},{8,10},{9,11},{10,... | collective-permute-start | bytes 393224 | tf_op jit(solution)/shard_map/ppermute | solution.py:295
  22.3 13.8 %collective-permute-start.8 = (bf16[128,1024]{1,0:T(8,128)(2,1)S(1)}, bf16[128,1024]{1,0:T(8,128)(2,1)S(1)}, u32[]{:S(2)}, u32[]{:S(2)}) collective-permute-start(bf16[128,1024]{1,0:T(8,128)(2,1)S(1)} %get-tuple-element.36), channel_id=1, source_target_pairs={{0,1},{1,0},{2,3},{3,2},{4,5},{5,4},{6,7},{7,6},{8,9},{9,8},{10,11... | collective-permute-start | bytes 786440 | tf_op jit(solution)/shard_map/ppermute | solution.py:295
  22.8 9.5 %collective-permute-start.11 = (bf16[128,512]{1,0:T(8,128)(2,1)S(1)}, bf16[128,512]{1,0:T(8,128)(2,1)S(1)}, u32[]{:S(2)}, u32[]{:S(2)}) collective-permute-start(bf16[128,512]{1,0:T(8,128)(2,1)S(1)} %add_convert_fusion.1), channel_id=1, source_target_pairs={{0,2},{1,3},{2,0},{3,1},{4,6},{5,7},{6,4},{7,5},{8,10},{9,11},{10,... | collective-permute-start | bytes 393224 | tf_op jit(solution)/shard_map/ppermute | solution.py:295

commit v12 on v11

--- a/solution.py
+++ b/solution.py
@@ -274,18 +274,18 @@
     project(grads, (wq_ref, wk_ref, wv_ref), start, front)
 
 
-def far_kernel(part, grads, wq_ref, wk_ref, wv_ref, last, front, back):
+def far_kernel(part, grads, wq_ref, wk_ref, wv_ref, front, back):
+    w_refs = (wq_ref, wk_ref, wv_ref)
+    head = lax.axis_index("head")
+    start = (head ^ 2) * part
+    project(grads, w_refs, start, front)
+    project(grads, w_refs, start + part // 2, back)
+
+
+def close_kernel(part, grads, wq_ref, wk_ref, wv_ref, last, near, mine):
     w_refs = (wq_ref, wk_ref, wv_ref)
     head = lax.axis_index("head")
     project(grads, w_refs, (head ^ 3) * part + part // 2, last)
-    start = (head ^ 2) * part
-    project(grads, w_refs, start, front)
-    project(grads, w_refs, start + part // 2, back)
-
-
-def close_kernel(part, grads, wq_ref, wk_ref, wv_ref, near, mine):
-    w_refs = (wq_ref, wk_ref, wv_ref)
-    head = lax.axis_index("head")
     project(grads, w_refs, (head ^ 1) * part, near)
     project(grads, w_refs, head * part, mine)
 
@@ -326,7 +326,7 @@
     got = {}
     for at in range(ctx - 1, 0, -1):
         got[at] = swap(sent[at.bit_length() - 1], "ctx", at)
-    soon = [at for at in (1,6,4,7,5) if at < ctx]
+    soon = [at for at in (7,6,5) if at < ctx]
     early, norm = lax.optimization_barrier((tuple(got[at] for at in soon), own[-1]))
     got.update(zip(soon, early))
     own = own[:-1] + (norm * (1.0 / scale),)
@@ -361,9 +361,10 @@
             ),
         )(*operands)
 
-    back, two_front, two_back = projected(far_kernel, [half_low, half, half], (grads, *weights))
+    two_front, two_back = projected(far_kernel, [half, half], (grads, *weights))
+    grads, two_front = lax.optimization_barrier((grads, two_front))
+    back, near, total = projected(close_kernel, [half_low, low, full], (grads, *weights))
     back = swap(back, "head", 1)
-    near, total = projected(close_kernel, [low, full], (grads, *weights))
     near, back = lax.optimization_barrier((near, back))
     front = swap((two_front + front.astype(jnp.float32)).astype(jnp.bfloat16), "head", 2)
     back = swap((two_back + back.astype(jnp.float32)).astype(jnp.bfloat16), "head", 2)

time: 37.1 us -> 36.5 us (0.984)
  the two profiles are of different devices: /device:TPU:30 before, /device:TPU:14 now
where the time goes in v12:
time: 36.5 us; the launch traced here: 36.3 us
  waiting for transfers between devices  17.7 us (48%)
  starting transfers between devices  13.7 us (38%)
  Pallas kernels  3.9 us (11%)
  other arithmetic  0.85 us (2%)
    ppermute x12, waiting for transfers between devices, swap(): return lax.ppermute(value, axis, [(at, at ^ offset) for at in range(size)])  17.7 us
    ppermute x12, starting transfers between devices, swap(): return lax.ppermute(value, axis, [(at, at ^ offset) for at in range(size)])  13.7 us
    pallas_call x1, Pallas kernels, near_body(): pl.pallas_call(send_kernel, out_shape=[hop] * bits, in_specs=[hbm] * 6, o...  1.82 us
    pallas_call x2, Pallas kernels, projected(): pl.pallas_call(functools.partial(kernel, part), out_shape=outs, in_specs=...  1.14 us
    pallas_call x1, Pallas kernels, near_body(): pl.pallas_call(functools.partial(near_kernel, scale, part), out_shape=[ja...  0.94 us
    convert_element_type x1, other arithmetic, near_body(): return (total + near.astype(jnp.float32) + far_sum).astype(jnp.bfloat16)  0.79 us
  transfers between devices with their start and end apart: 12, of which 7 were waited for; matrix products, arithmetic and copies ran while one was open for 0% of the time, Pallas kernels for 3%

profile of v12, /device:TPU:14, one launch (start us, length us, event | category | flops | bytes accessed | tf_op | source)
XLA Modules:
  0.0 36.3 jit_solution(18031496593915602658)
XLA Ops:
  0.0 0.0 copy-start
  0.0 0.0 copy-start.1
  0.0 0.0 copy-start.2
  0.0 0.0 copy-start.3
  0.0 0.0 copy-start.4
  0.0 0.0 copy-start.5
  0.0 0.0 copy-start.6
  0.0 0.0 copy-start.7
  0.1 1.8 %shard_map.91 = (bf16[144,256]{1,0:T(8,128)(2,1)}, bf16[144,256]{1,0:T(8,128)(2,1)}, bf16[144,256]{1,0:T(8,128)(2,1)}) custom-call(bf16[128,128]{1,0:T(8,128)(2,1)} %q_ref.1, bf16[128,128]{1,0:T(8,128)(2,1)} %k_ref.1, bf16[128,128]{1,0:T(8,128)(2,1)} %v_ref.1, bf16[128,128]{1,0:T(8,128)(2,1)} %g_ref.1, bf16[128,128]{1,0:T(8,128)(2,1)} %a_ref.1, f32[1,128]{1,0:T(1,128)} %bitcast.1), custom_call_target="tpu_custom_call" | custom-call | flops 5000000000 | bytes 327680 | tf_op jit(solution)/shard_map/pallas_call | solution.py:308
  1.9 0.1 collective-permute-start.2
  2.0 1.4 %collective-permute-start.1 = (bf16[144,256]{1,0:T(8,128)(2,1)}, bf16[144,256]{1,0:T(8,128)(2,1)S(1)}, u32[]{:S(2)}, u32[]{:S(2)}) collective-permute-start(bf16[144,256]{1,0:T(8,128)(2,1)} %get-tuple-element.23), channel_id=1, source_target_pairs={{0,24},{4,28},{8,16},{12,20},{16,8},{20,12},{24,0},{28,4},{1,25},{... | collective-permute-start | bytes 221192 | tf_op jit(solution)/shard_map/ppermute | solution.py:295
  3.4 1.4 %collective-permute-start = (bf16[144,256]{1,0:T(8,128)(2,1)}, bf16[144,256]{1,0:T(8,128)(2,1)S(1)}, u32[]{:S(2)}, u32[]{:S(2)}) collective-permute-start(bf16[144,256]{1,0:T(8,128)(2,1)} %get-tuple-element.23), channel_id=1, source_target_pairs={{0,28},{4,24},{8,20},{12,16},{16,12},{20,8},{24,4},{28,0},{1,29},{... | collective-permute-start | bytes 221192 | tf_op jit(solution)/shard_map/ppermute | solution.py:295
  4.8 0.0 copy-start.8
  4.8 0.4 %collective-permute-start.5 = (bf16[144,256]{1,0:T(8,128)(2,1)}, bf16[144,256]{1,0:T(8,128)(2,1)S(1)}, u32[]{:S(2)}, u32[]{:S(2)}) collective-permute-start(bf16[144,256]{1,0:T(8,128)(2,1)} %get-tuple-element.26), channel_id=1, source_target_pairs={{0,12},{4,8},{8,4},{12,0},{16,28},{20,24},{24,20},{28,16},{1,13},{... | collective-permute-start | bytes 221192 | tf_op jit(solution)/shard_map/ppermute | solution.py:295
  5.2 1.5 %collective-permute-start.4 = (bf16[144,256]{1,0:T(8,128)(2,1)}, bf16[144,256]{1,0:T(8,128)(2,1)S(1)}, u32[]{:S(2)}, u32[]{:S(2)}) collective-permute-start(bf16[144,256]{1,0:T(8,128)(2,1)} %get-tuple-element.26), channel_id=1, source_target_pairs={{0,8},{4,12},{8,0},{12,4},{16,24},{20,28},{24,16},{28,20},{1,9},{5... | collective-permute-start | bytes 221192 | tf_op jit(solution)/shard_map/ppermute | solution.py:295
  6.7 3.2 %collective-permute-done.2.refs_4_ = bf16[144,256]{1,0:T(8,128)(2,1)S(1)} collective-permute-done((bf16[144,256]{1,0:T(8,128)(2,1)}, bf16[144,256]{1,0:T(8,128)(2,1)S(1)}, u32[]{:S(2)}, u32[]{:S(2)}) %collective-permute-start.2) | collective-permute-done | bytes 73760 | tf_op jit(solution)/shard_map/ppermute | solution.py:295
  9.9 0.0 collective-permute-start.6
  9.9 0.0 collective-permute-done.1.refs_5_
  9.9 0.1 collective-permute-start.3
  10.0 0.0 collective-permute-done.refs_6_
  10.0 0.0 copy-done.8
  10.0 1.3 %collective-permute-done.3.refs_0_ = bf16[144,256]{1,0:T(8,128)(2,1)S(1)} collective-permute-done((bf16[144,256]{1,0:T(8,128)(2,1)}, bf16[144,256]{1,0:T(8,128)(2,1)S(1)}, u32[]{:S(2)}, u32[]{:S(2)}) %collective-permute-start.3) | collective-permute-done | bytes 73760 | tf_op jit(solution)/shard_map/ppermute | solution.py:295
  11.4 0.0 collective-permute-done.5.refs_2_
  11.4 1.3 %collective-permute-done.4.refs_1_ = bf16[144,256]{1,0:T(8,128)(2,1)S(1)} collective-permute-done((bf16[144,256]{1,0:T(8,128)(2,1)}, bf16[144,256]{1,0:T(8,128)(2,1)S(1)}, u32[]{:S(2)}, u32[]{:S(2)}) %collective-permute-start.4) | collective-permute-done | bytes 73760 | tf_op jit(solution)/shard_map/ppermute | solution.py:295
  12.7 1.8 %collective-permute-done.6.refs_3_ = bf16[144,256]{1,0:T(8,128)(2,1)S(1)} collective-permute-done((bf16[144,256]{1,0:T(8,128)(2,1)}, bf16[144,256]{1,0:T(8,128)(2,1)S(1)}, u32[]{:S(2)}, u32[]{:S(2)}) %collective-permute-start.6) | collective-permute-done | bytes 73760 | tf_op jit(solution)/shard_map/ppermute | solution.py:295
  14.4 0.0 copy-done
  14.4 0.0 copy-done.1
  14.4 0.0 copy-done.2
  14.4 0.0 copy-done.3
  14.5 0.0 copy-done.4
  14.5 0.0 copy-done.5
  14.5 0.0 copy-done.6
  14.5 0.0 copy-done.7
  14.5 0.9 %shard_map.92 = (bf16[128,384]{1,0:T(8,128)(2,1)S(1)}, bf16[128,512]{1,0:T(8,128)(2,1)S(1)}) custom-call(bf16[128,128]{1,0:T(8,128)(2,1)S(1)} %copy-done.3, bf16[128,128]{1,0:T(8,128)(2,1)S(1)} %copy-done.4, bf16[128,128]{1,0:T(8,128)(2,1)S(1)} %copy-done.5, bf16[128,128]{1,0:T(8,128)(2,1)S(1)} %copy-done.6, bf16[128,128]{1,0:T(8,128)(2,1)S(1)} %copy-done.7, ...), custom_call_target="tpu_custom_call" | custom-call | flops 335544320 | bytes 1310720 | tf_op jit(solution)/shard_map/pallas_call | solution.py:338
  15.4 0.5 %collective-permute-start.9 = (bf16[128,512]{1,0:T(8,128)(2,1)S(1)}, bf16[128,512]{1,0:T(8,128)(2,1)S(1)}, u32[]{:S(2)}, u32[]{:S(2)}) collective-permute-start(bf16[128,512]{1,0:T(8,128)(2,1)S(1)} %get-tuple-element.38), channel_id=1, source_target_pairs={{0,1},{1,0},{2,3},{3,2},{4,5},{5,4},{6,7},{7,6},{8,9},{9,8},{10,11... | collective-permute-start | bytes 393224 | tf_op jit(solution)/shard_map/ppermute | solution.py:295
  16.0 0.4 %shard_map.93 = (f32[128,512]{1,0:T(8,128)S(1)}, f32[128,512]{1,0:T(8,128)S(1)}) custom-call(bf16[128,384]{1,0:T(8,128)(2,1)S(1)} %get-tuple-element.32.grads, bf16[4096,128]{1,0:T(8,128)(2,1)S(1)} %copy-done, bf16[4096,128]{1,0:T(8,128)(2,1)S(1)} %copy-done.1, bf16[4096,128]{1,0:T(8,128)(2,1)S(1)} %copy-done.2), custom_call_target="tpu_custom_call" | custom-call | flops 100663296 | bytes 786432 | tf_op jit(solution)/shard_map/pallas_call | solution.py:353
  16.3 0.8 %shard_map.94 = (bf16[128,512]{1,0:T(8,128)(2,1)S(1)}, bf16[128,1024]{1,0:T(8,128)(2,1)S(1)}, f32[128,1024]{1,0:T(8,128)S(1)}) custom-call(bf16[128,384]{1,0:T(8,128)(2,1)S(1)} %get-tuple-element.32.grads, bf16[4096,128]{1,0:T(8,128)(2,1)S(1)} %copy-done, bf16[4096,128]{1,0:T(8,128)(2,1)S(1)} %copy-done.1, bf16[4096,128]{1,0:T(8,128)(2,1)S(1)} %copy-done.2), custom_call_target="tpu_custom_call" | custom-call | flops 251658240 | bytes 1966080 | tf_op jit(solution)/shard_map/pallas_call | solution.py:353
  17.1 1.7 %collective-permute-start.7 = (bf16[128,512]{1,0:T(8,128)(2,1)S(1)}, bf16[128,512]{1,0:T(8,128)(2,1)S(1)}, u32[]{:S(2)}, u32[]{:S(2)}) collective-permute-start(bf16[128,512]{1,0:T(8,128)(2,1)S(1)} %get-tuple-element.35), channel_id=1, source_target_pairs={{0,1},{1,0},{2,3},{3,2},{4,5},{5,4},{6,7},{7,6},{8,9},{9,8},{10,11... | collective-permute-start | bytes 393224 | tf_op jit(solution)/shard_map/ppermute | solution.py:295
  18.8 2.5 %collective-permute-done.9 = bf16[128,512]{1,0:T(8,128)(2,1)S(1)} collective-permute-done((bf16[128,512]{1,0:T(8,128)(2,1)S(1)}, bf16[128,512]{1,0:T(8,128)(2,1)S(1)}, u32[]{:S(2)}, u32[]{:S(2)}) %collective-permute-start.9) | collective-permute-done | bytes 131104 | tf_op jit(solution)/shard_map/ppermute | solution.py:295
  21.3 2.7 %collective-permute-start.10 = (bf16[128,512]{1,0:T(8,128)(2,1)S(1)}, bf16[128,512]{1,0:T(8,128)(2,1)S(1)}, u32[]{:S(2)}, u32[]{:S(2)}) collective-permute-start(bf16[128,512]{1,0:T(8,128)(2,1)S(1)} %add_convert_fusion.2), channel_id=1, source_target_pairs={{0,2},{1,3},{2,0},{3,1},{4,6},{5,7},{6,4},{7,5},{8,10},{9,11},{10,... | collective-permute-start | bytes 393224 | tf_op jit(solution)/shard_map/ppermute | solution.py:295
  24.0 0.0 collective-permute-done.7
  24.0 1.5 %collective-permute-start.8 = (bf16[128,1024]{1,0:T(8,128)(2,1)S(1)}, bf16[128,1024]{1,0:T(8,128)(2,1)S(1)}, u32[]{:S(2)}, u32[]{:S(2)}) collective-permute-start(bf16[128,1024]{1,0:T(8,128)(2,1)S(1)} %get-tuple-element.36), channel_id=1, source_target_pairs={{0,1},{1,0},{2,3},{3,2},{4,5},{5,4},{6,7},{7,6},{8,9},{9,8},{10,11... | collective-permute-start | bytes 786440 | tf_op jit(solution)/shard_map/ppermute | solution.py:295
  25.5 2.4 %collective-permute-start.11 = (bf16[128,512]{1,0:T(8,128)(2,1)S(1)}, bf16[128,512]{1,0:T(8,128)(2,1)S(1)}, u32[]{:S(2)}, u32[]{:S(2)}) collective-permute-start(bf16[128,512]{1,0:T(8,128)(2,1)S(1)} %add_convert_fusion.1), channel_id=1, source_target_pairs={{0,2},{1,3},{2,0},{3,1},{4,6},{5,7},{6,4},{7,5},{8,10},{9,11},{10,... | collective-permute-start | bytes 393224 | tf_op jit(solution)/shard_map/ppermute | solution.py:295
  27.9 2.4 %collective-permute-done.10 = bf16[128,512]{1,0:T(8,128)(2,1)S(1)} collective-permute-done((bf16[128,512]{1,0:T(8,128)(2,1)S(1)}, bf16[128,512]{1,0:T(8,128)(2,1)S(1)}, u32[]{:S(2)}, u32[]{:S(2)}) %collective-permute-start.10) | collective-permute-done | bytes 131104 | tf_op jit(solution)/shard_map/ppermute | solution.py:295
  30.3 5.2 %collective-permute-done.11 = bf16[128,512]{1,0:T(8,128)(2,1)S(1)} collective-permute-done((bf16[128,512]{1,0:T(8,128)(2,1)S(1)}, bf16[128,512]{1,0:T(8,128)(2,1)S(1)}, u32[]{:S(2)}, u32[]{:S(2)}) %collective-permute-start.11) | collective-permute-done | bytes 131104 | tf_op jit(solution)/shard_map/ppermute | solution.py:295
  35.5 0.0 collective-permute-done.8
  35.5 0.8 %add_convert_fusion = bf16[128,1024]{1,0:T(8,128)(2,1)} fusion(f32[128,1024]{1,0:T(8,128)S(1)} %get-tuple-element.33, bf16[128,1024]{1,0:T(8,128)(2,1)S(1)} %collective-permute-done.8, bf16[128,512]{1,0:T(8,128)(2,1)S(1)} %collective-permute-done.11, bf16[128,512]{1,0:T(8,128)(2,1)S(1)} %collective-permute-done.10), kind=kLoop, calls=%fused_computation | loop fusion | flops 1048576 | bytes 1310720 | tf_op jit(solution)/shard_map/convert_element_type | solution.py:373
  (3 shorter events, 0.1 us)
Async XLA Ops:
  0.0 14.4 %copy-start = (bf16[4096,128]{1,0:T(8,128)(2,1)S(1)}, bf16[4096,128]{1,0:T(8,128)(2,1)}, u32[]{:S(2)}) copy-start(bf16[4096,128]{1,0:T(8,128)(2,1)} %wq_ref.5) | copy-start | bytes 3145732
  0.0 14.4 %copy-start.1 = (bf16[4096,128]{1,0:T(8,128)(2,1)S(1)}, bf16[4096,128]{1,0:T(8,128)(2,1)}, u32[]{:S(2)}) copy-start(bf16[4096,128]{1,0:T(8,128)(2,1)} %wk_ref.5) | copy-start | bytes 3145732
  0.0 14.4 %copy-start.2 = (bf16[4096,128]{1,0:T(8,128)(2,1)S(1)}, bf16[4096,128]{1,0:T(8,128)(2,1)}, u32[]{:S(2)}) copy-start(bf16[4096,128]{1,0:T(8,128)(2,1)} %wv_ref.5) | copy-start | bytes 3145732
  0.0 14.4 %copy-start.3 = (bf16[128,128]{1,0:T(8,128)(2,1)S(1)}, bf16[128,128]{1,0:T(8,128)(2,1)}, u32[]{:S(2)}) copy-start(bf16[128,128]{1,0:T(8,128)(2,1)} %q_ref.1) | copy-start | bytes 98308
  0.0 14.4 %copy-start.4 = (bf16[128,128]{1,0:T(8,128)(2,1)S(1)}, bf16[128,128]{1,0:T(8,128)(2,1)}, u32[]{:S(2)}) copy-start(bf16[128,128]{1,0:T(8,128)(2,1)} %k_ref.1) | copy-start | bytes 98308
  0.0 14.4 %copy-start.5 = (bf16[128,128]{1,0:T(8,128)(2,1)S(1)}, bf16[128,128]{1,0:T(8,128)(2,1)}, u32[]{:S(2)}) copy-start(bf16[128,128]{1,0:T(8,128)(2,1)} %v_ref.1) | copy-start | bytes 98308
  0.0 14.4 %copy-start.6 = (bf16[128,128]{1,0:T(8,128)(2,1)S(1)}, bf16[128,128]{1,0:T(8,128)(2,1)}, u32[]{:S(2)}) copy-start(bf16[128,128]{1,0:T(8,128)(2,1)} %g_ref.1) | copy-start | bytes 98308
  0.0 14.4 %copy-start.7 = (bf16[128,128]{1,0:T(8,128)(2,1)S(1)}, bf16[128,128]{1,0:T(8,128)(2,1)}, u32[]{:S(2)}) copy-start(bf16[128,128]{1,0:T(8,128)(2,1)} %a_ref.1) | copy-start | bytes 98308
  1.9 8.0 %collective-permute-start.2 = (bf16[144,256]{1,0:T(8,128)(2,1)}, bf16[144,256]{1,0:T(8,128)(2,1)S(1)}, u32[]{:S(2)}, u32[]{:S(2)}) collective-permute-start(bf16[144,256]{1,0:T(8,128)(2,1)} %get-tuple-element.23), channel_id=1, source_target_pairs={{0,20},{4,16},{8,28},{12,24},{16,4},{20,0},{24,12},{28,8},{1,21},{... | collective-permute-start | bytes 221192 | tf_op jit(solution)/shard_map/ppermute | solution.py:295
  2.0 7.9 %collective-permute-start.1 = (bf16[144,256]{1,0:T(8,128)(2,1)}, bf16[144,256]{1,0:T(8,128)(2,1)S(1)}, u32[]{:S(2)}, u32[]{:S(2)}) collective-permute-start(bf16[144,256]{1,0:T(8,128)(2,1)} %get-tuple-element.23), channel_id=1, source_target_pairs={{0,24},{4,28},{8,16},{12,20},{16,8},{20,12},{24,0},{28,4},{1,25},{... | collective-permute-start | bytes 221192 | tf_op jit(solution)/shard_map/ppermute | solution.py:295
  3.4 6.6 %collective-permute-start = (bf16[144,256]{1,0:T(8,128)(2,1)}, bf16[144,256]{1,0:T(8,128)(2,1)S(1)}, u32[]{:S(2)}, u32[]{:S(2)}) collective-permute-start(bf16[144,256]{1,0:T(8,128)(2,1)} %get-tuple-element.23), channel_id=1, source_target_pairs={{0,28},{4,24},{8,20},{12,16},{16,12},{20,8},{24,4},{28,0},{1,29},{... | collective-permute-start | bytes 221192 | tf_op jit(solution)/shard_map/ppermute | solution.py:295
  4.8 5.2 %copy-start.8 = (f32[128,1]{0,1:T(1,128)S(1)}, f32[128,1]{0,1:T(1,128)}, u32[]{:S(2)}) copy-start(f32[128,1]{0,1:T(1,128)} %param.14) | copy-start | bytes 1540
  4.8 6.5 %collective-permute-start.5 = (bf16[144,256]{1,0:T(8,128)(2,1)}, bf16[144,256]{1,0:T(8,128)(2,1)S(1)}, u32[]{:S(2)}, u32[]{:S(2)}) collective-permute-start(bf16[144,256]{1,0:T(8,128)(2,1)} %get-tuple-element.26), channel_id=1, source_target_pairs={{0,12},{4,8},{8,4},{12,0},{16,28},{20,24},{24,20},{28,16},{1,13},{... | collective-permute-start | bytes 221192 | tf_op jit(solution)/shard_map/ppermute | solution.py:295
  5.2 7.4 %collective-permute-start.4 = (bf16[144,256]{1,0:T(8,128)(2,1)}, bf16[144,256]{1,0:T(8,128)(2,1)S(1)}, u32[]{:S(2)}, u32[]{:S(2)}) collective-permute-start(bf16[144,256]{1,0:T(8,128)(2,1)} %get-tuple-element.26), channel_id=1, source_target_pairs={{0,8},{4,12},{8,0},{12,4},{16,24},{20,28},{24,16},{28,20},{1,9},{5... | collective-permute-start | bytes 221192 | tf_op jit(solution)/shard_map/ppermute | solution.py:295
  9.9 4.6 %collective-permute-start.6 = (bf16[144,256]{1,0:T(8,128)(2,1)}, bf16[144,256]{1,0:T(8,128)(2,1)S(1)}, u32[]{:S(2)}, u32[]{:S(2)}) collective-permute-start(bf16[144,256]{1,0:T(8,128)(2,1)} %get-tuple-element.23), channel_id=1, source_target_pairs={{0,16},{4,20},{8,24},{12,28},{16,0},{20,4},{24,8},{28,12},{1,17},{... | collective-permute-start | bytes 221192 | tf_op jit(solution)/shard_map/ppermute | solution.py:295
  9.9 1.5 %collective-permute-start.3 = (bf16[144,256]{1,0:T(8,128)(2,1)}, bf16[144,256]{1,0:T(8,128)(2,1)S(1)}, u32[]{:S(2)}, u32[]{:S(2)}) collective-permute-start(bf16[144,256]{1,0:T(8,128)(2,1)} %get-tuple-element.25), channel_id=1, source_target_pairs={{0,4},{4,0},{8,12},{12,8},{16,20},{20,16},{24,28},{28,24},{1,5},{5... | collective-permute-start | bytes 221192 | tf_op jit(solution)/shard_map/ppermute | solution.py:295
  15.4 5.9 %collective-permute-start.9 = (bf16[128,512]{1,0:T(8,128)(2,1)S(1)}, bf16[128,512]{1,0:T(8,128)(2,1)S(1)}, u32[]{:S(2)}, u32[]{:S(2)}) collective-permute-start(bf16[128,512]{1,0:T(8,128)(2,1)S(1)} %get-tuple-element.38), channel_id=1, source_target_pairs={{0,1},{1,0},{2,3},{3,2},{4,5},{5,4},{6,7},{7,6},{8,9},{9,8},{10,11... | collective-permute-start | bytes 393224 | tf_op jit(solution)/shard_map/ppermute | solution.py:295
  17.1 6.9 %collective-permute-start.7 = (bf16[128,512]{1,0:T(8,128)(2,1)S(1)}, bf16[128,512]{1,0:T(8,128)(2,1)S(1)}, u32[]{:S(2)}, u32[]{:S(2)}) collective-permute-start(bf16[128,512]{1,0:T(8,128)(2,1)S(1)} %get-tuple-element.35), channel_id=1, source_target_pairs={{0,1},{1,0},{2,3},{3,2},{4,5},{5,4},{6,7},{7,6},{8,9},{9,8},{10,11... | collective-permute-start | bytes 393224 | tf_op jit(solution)/shard_map/ppermute | solution.py:295
  21.3 9.0 %collective-permute-start.10 = (bf16[128,512]{1,0:T(8,128)(2,1)S(1)}, bf16[128,512]{1,0:T(8,128)(2,1)S(1)}, u32[]{:S(2)}, u32[]{:S(2)}) collective-permute-start(bf16[128,512]{1,0:T(8,128)(2,1)S(1)} %add_convert_fusion.2), channel_id=1, source_target_pairs={{0,2},{1,3},{2,0},{3,1},{4,6},{5,7},{6,4},{7,5},{8,10},{9,11},{10,... | collective-permute-start | bytes 393224 | tf_op jit(solution)/shard_map/ppermute | solution.py:295
  24.0 11.6 %collective-permute-start.8 = (bf16[128,1024]{1,0:T(8,128)(2,1)S(1)}, bf16[128,1024]{1,0:T(8,128)(2,1)S(1)}, u32[]{:S(2)}, u32[]{:S(2)}) collective-permute-start(bf16[128,1024]{1,0:T(8,128)(2,1)S(1)} %get-tuple-element.36), channel_id=1, source_target_pairs={{0,1},{1,0},{2,3},{3,2},{4,5},{5,4},{6,7},{7,6},{8,9},{9,8},{10,11... | collective-permute-start | bytes 786440 | tf_op jit(solution)/shard_map/ppermute | solution.py:295
  25.5 10.0 %collective-permute-start.11 = (bf16[128,512]{1,0:T(8,128)(2,1)S(1)}, bf16[128,512]{1,0:T(8,128)(2,1)S(1)}, u32[]{:S(2)}, u32[]{:S(2)}) collective-permute-start(bf16[128,512]{1,0:T(8,128)(2,1)S(1)} %add_convert_fusion.1), channel_id=1, source_target_pairs={{0,2},{1,3},{2,0},{3,1},{4,6},{5,7},{6,4},{7,5},{8,10},{9,11},{10,... | collective-permute-start | bytes 393224 | tf_op jit(solution)/shard_map/ppermute | solution.py:295

commit v13 on v12

--- a/solution.py
+++ b/solution.py
@@ -323,13 +323,13 @@
             flops=5000000000, bytes_accessed=20 * rows * width, transcendentals=0
         ),
     )(*own)
-    got = {}
-    for at in range(ctx - 1, 0, -1):
-        got[at] = swap(sent[at.bit_length() - 1], "ctx", at)
-    soon = [at for at in (7,6,5) if at < ctx]
+    got = {at: swap(sent[at.bit_length() - 1], "ctx", at) for at in (1, *range(2, ctx, 2))}
+    soon = [at for at in (6,) if at < ctx]
     early, norm = lax.optimization_barrier((tuple(got[at] for at in soon), own[-1]))
     got.update(zip(soon, early))
     own = own[:-1] + (norm * (1.0 / scale),)
+    for at in range(2, ctx, 2):
+        got[at + 1] = swap(got[at], "ctx", 1)
     got = [got[at] for at in range(1, ctx)]
     half_low = jax.ShapeDtypeStruct((rows, part // 2), jnp.bfloat16)
     half = jax.ShapeDtypeStruct((rows, part // 2), jnp.float32)

time: 36.5 us -> 34.3 us (0.940)
  the two profiles are of different devices: /device:TPU:14 before, /device:TPU:0 now
where the time goes in v13:
time: 34.3 us; the launch traced here: 34.2 us
  waiting for transfers between devices  15.6 us (45%)
  starting transfers between devices  13.6 us (40%)
  Pallas kernels  3.9 us (11%)
  other arithmetic  0.85 us (2%)
    ppermute x12, waiting for transfers between devices, swap(): return lax.ppermute(value, axis, [(at, at ^ offset) for at in range(size)])  15.6 us
    ppermute x12, starting transfers between devices, swap(): return lax.ppermute(value, axis, [(at, at ^ offset) for at in range(size)])  13.6 us
    pallas_call x1, Pallas kernels, near_body(): pl.pallas_call(send_kernel, out_shape=[hop] * bits, in_specs=[hbm] * 6, o...  1.82 us
    pallas_call x2, Pallas kernels, projected(): pl.pallas_call(functools.partial(kernel, part), out_shape=outs, in_specs=...  1.14 us
    pallas_call x1, Pallas kernels, near_body(): pl.pallas_call(functools.partial(near_kernel, scale, part), out_shape=[ja...  0.94 us
    convert_element_type x1, other arithmetic, near_body(): return (total + near.astype(jnp.float32) + far_sum).astype(jnp.bfloat16)  0.79 us
  transfers between devices with their start and end apart: 12, of which 9 were waited for; matrix products, arithmetic and copies ran while one was open for 0% of the time, Pallas kernels for 3%

profile of v13, /device:TPU:0, one launch (start us, length us, event | category | flops | bytes accessed | tf_op | source)
XLA Modules:
  0.0 34.2 jit_solution(3673004706758849820)
XLA Ops:
  0.0 0.0 copy-start
  0.0 0.0 copy-start.1
  0.0 0.0 copy-start.2
  0.0 0.0 copy-start.3
  0.0 0.0 copy-start.4
  0.0 0.0 copy-start.5
  0.0 0.0 copy-start.6
  0.0 0.0 copy-start.7
  0.0 1.8 %shard_map.91 = (bf16[144,256]{1,0:T(8,128)(2,1)}, bf16[144,256]{1,0:T(8,128)(2,1)}, bf16[144,256]{1,0:T(8,128)(2,1)}) custom-call(bf16[128,128]{1,0:T(8,128)(2,1)} %q_ref.1, bf16[128,128]{1,0:T(8,128)(2,1)} %k_ref.1, bf16[128,128]{1,0:T(8,128)(2,1)} %v_ref.1, bf16[128,128]{1,0:T(8,128)(2,1)} %g_ref.1, bf16[128,128]{1,0:T(8,128)(2,1)} %a_ref.1, f32[1,128]{1,0:T(1,128)} %bitcast.1), custom_call_target="tpu_custom_call" | custom-call | flops 5000000000 | bytes 327680 | tf_op jit(solution)/shard_map/pallas_call | solution.py:308
  1.9 4.0 %collective-permute-start = (bf16[144,256]{1,0:T(8,128)(2,1)}, bf16[144,256]{1,0:T(8,128)(2,1)S(1)}, u32[]{:S(2)}, u32[]{:S(2)}) collective-permute-start(bf16[144,256]{1,0:T(8,128)(2,1)} %get-tuple-element.21), channel_id=1, source_target_pairs={{0,24},{4,28},{8,16},{12,20},{16,8},{20,12},{24,0},{28,4},{1,25},{... | collective-permute-start | bytes 221192 | tf_op jit(solution)/shard_map/ppermute | solution.py:295
  5.8 0.0 copy-start.8
  5.8 0.5 %collective-permute-start.2 = (bf16[144,256]{1,0:T(8,128)(2,1)}, bf16[144,256]{1,0:T(8,128)(2,1)S(1)}, u32[]{:S(2)}, u32[]{:S(2)}) collective-permute-start(bf16[144,256]{1,0:T(8,128)(2,1)} %get-tuple-element.24), channel_id=1, source_target_pairs={{0,8},{4,12},{8,0},{12,4},{16,24},{20,28},{24,16},{28,20},{1,9},{5... | collective-permute-start | bytes 221192 | tf_op jit(solution)/shard_map/ppermute | solution.py:295
  6.4 0.1 collective-permute-start.4
  6.5 0.0 collective-permute-start.1
  6.5 2.2 %collective-permute-done.refs_5_ = bf16[144,256]{1,0:T(8,128)(2,1)S(1)} collective-permute-done((bf16[144,256]{1,0:T(8,128)(2,1)}, bf16[144,256]{1,0:T(8,128)(2,1)S(1)}, u32[]{:S(2)}, u32[]{:S(2)}) %collective-permute-start) | collective-permute-done | bytes 73760 | tf_op jit(solution)/shard_map/ppermute | solution.py:295
  8.7 0.0 collective-permute-start.6
  8.7 1.8 %collective-permute-done.2.refs_1_ = bf16[144,256]{1,0:T(8,128)(2,1)S(1)} collective-permute-done((bf16[144,256]{1,0:T(8,128)(2,1)}, bf16[144,256]{1,0:T(8,128)(2,1)S(1)}, u32[]{:S(2)}, u32[]{:S(2)}) %collective-permute-start.2) | collective-permute-done | bytes 73760 | tf_op jit(solution)/shard_map/ppermute | solution.py:295
  10.5 0.0 collective-permute-start.3
  10.5 0.4 %collective-permute-done.4.refs_3_ = bf16[144,256]{1,0:T(8,128)(2,1)S(1)} collective-permute-done((bf16[144,256]{1,0:T(8,128)(2,1)}, bf16[144,256]{1,0:T(8,128)(2,1)S(1)}, u32[]{:S(2)}, u32[]{:S(2)}) %collective-permute-start.4) | collective-permute-done | bytes 73760 | tf_op jit(solution)/shard_map/ppermute | solution.py:295
  10.9 0.1 collective-permute-start.5
  11.0 0.0 copy-done.8
  11.0 0.0 collective-permute-done.1.refs_0_
  11.0 0.7 %collective-permute-done.3.refs_2_ = bf16[144,256]{1,0:T(8,128)(2,1)S(1)} collective-permute-done((bf16[144,256]{1,0:T(8,128)(2,1)S(1)}, bf16[144,256]{1,0:T(8,128)(2,1)S(1)}, u32[]{:S(2)}, u32[]{:S(2)}) %collective-permute-start.3) | collective-permute-done | bytes 73760 | tf_op jit(solution)/shard_map/ppermute | solution.py:295
  11.8 0.4 %collective-permute-done.5.refs_4_ = bf16[144,256]{1,0:T(8,128)(2,1)S(1)} collective-permute-done((bf16[144,256]{1,0:T(8,128)(2,1)S(1)}, bf16[144,256]{1,0:T(8,128)(2,1)S(1)}, u32[]{:S(2)}, u32[]{:S(2)}) %collective-permute-start.5) | collective-permute-done | bytes 73760 | tf_op jit(solution)/shard_map/ppermute | solution.py:295
  12.2 0.0 collective-permute-done.6.refs_6_
  12.2 0.0 copy-done
  12.2 0.0 copy-done.1
  12.2 0.0 copy-done.2
  12.2 0.0 copy-done.3
  12.2 0.0 copy-done.4
  12.3 0.0 copy-done.5
  12.3 0.0 copy-done.6
  12.3 0.0 copy-done.7
  12.3 0.9 %shard_map.92 = (bf16[128,384]{1,0:T(8,128)(2,1)S(1)}, bf16[128,512]{1,0:T(8,128)(2,1)S(1)}) custom-call(bf16[128,128]{1,0:T(8,128)(2,1)S(1)} %copy-done.3, bf16[128,128]{1,0:T(8,128)(2,1)S(1)} %copy-done.4, bf16[128,128]{1,0:T(8,128)(2,1)S(1)} %copy-done.5, bf16[128,128]{1,0:T(8,128)(2,1)S(1)} %copy-done.6, bf16[128,128]{1,0:T(8,128)(2,1)S(1)} %copy-done.7, ...), custom_call_target="tpu_custom_call" | custom-call | flops 335544320 | bytes 1310720 | tf_op jit(solution)/shard_map/pallas_call | solution.py:338
  13.2 1.6 %collective-permute-start.9 = (bf16[128,512]{1,0:T(8,128)(2,1)S(1)}, bf16[128,512]{1,0:T(8,128)(2,1)S(1)}, u32[]{:S(2)}, u32[]{:S(2)}) collective-permute-start(bf16[128,512]{1,0:T(8,128)(2,1)S(1)} %get-tuple-element.34), channel_id=1, source_target_pairs={{0,1},{1,0},{2,3},{3,2},{4,5},{5,4},{6,7},{7,6},{8,9},{9,8},{10,11... | collective-permute-start | bytes 393224 | tf_op jit(solution)/shard_map/ppermute | solution.py:295
  14.9 0.4 %shard_map.93 = (f32[128,512]{1,0:T(8,128)S(1)}, f32[128,512]{1,0:T(8,128)S(1)}) custom-call(bf16[128,384]{1,0:T(8,128)(2,1)S(1)} %get-tuple-element.28.grads, bf16[4096,128]{1,0:T(8,128)(2,1)S(1)} %copy-done, bf16[4096,128]{1,0:T(8,128)(2,1)S(1)} %copy-done.1, bf16[4096,128]{1,0:T(8,128)(2,1)S(1)} %copy-done.2), custom_call_target="tpu_custom_call" | custom-call | flops 100663296 | bytes 786432 | tf_op jit(solution)/shard_map/pallas_call | solution.py:353
  15.3 0.8 %shard_map.94 = (bf16[128,512]{1,0:T(8,128)(2,1)S(1)}, bf16[128,1024]{1,0:T(8,128)(2,1)S(1)}, f32[128,1024]{1,0:T(8,128)S(1)}) custom-call(bf16[128,384]{1,0:T(8,128)(2,1)S(1)} %get-tuple-element.28.grads, bf16[4096,128]{1,0:T(8,128)(2,1)S(1)} %copy-done, bf16[4096,128]{1,0:T(8,128)(2,1)S(1)} %copy-done.1, bf16[4096,128]{1,0:T(8,128)(2,1)S(1)} %copy-done.2), custom_call_target="tpu_custom_call" | custom-call | flops 251658240 | bytes 1966080 | tf_op jit(solution)/shard_map/pallas_call | solution.py:353
  16.0 0.5 %collective-permute-start.7 = (bf16[128,512]{1,0:T(8,128)(2,1)S(1)}, bf16[128,512]{1,0:T(8,128)(2,1)S(1)}, u32[]{:S(2)}, u32[]{:S(2)}) collective-permute-start(bf16[128,512]{1,0:T(8,128)(2,1)S(1)} %get-tuple-element.31), channel_id=1, source_target_pairs={{0,1},{1,0},{2,3},{3,2},{4,5},{5,4},{6,7},{7,6},{8,9},{9,8},{10,11... | collective-permute-start | bytes 393224 | tf_op jit(solution)/shard_map/ppermute | solution.py:295
  16.5 2.5 %collective-permute-done.9 = bf16[128,512]{1,0:T(8,128)(2,1)S(1)} collective-permute-done((bf16[128,512]{1,0:T(8,128)(2,1)S(1)}, bf16[128,512]{1,0:T(8,128)(2,1)S(1)}, u32[]{:S(2)}, u32[]{:S(2)}) %collective-permute-start.9) | collective-permute-done | bytes 131104 | tf_op jit(solution)/shard_map/ppermute | solution.py:295
  19.1 2.7 %collective-permute-start.10 = (bf16[128,512]{1,0:T(8,128)(2,1)S(1)}, bf16[128,512]{1,0:T(8,128)(2,1)S(1)}, u32[]{:S(2)}, u32[]{:S(2)}) collective-permute-start(bf16[128,512]{1,0:T(8,128)(2,1)S(1)} %add_convert_fusion.2), channel_id=1, source_target_pairs={{0,2},{1,3},{2,0},{3,1},{4,6},{5,7},{6,4},{7,5},{8,10},{9,11},{10,... | collective-permute-start | bytes 393224 | tf_op jit(solution)/shard_map/ppermute | solution.py:295
  21.8 0.0 collective-permute-done.7
  21.8 2.1 %collective-permute-start.8 = (bf16[128,1024]{1,0:T(8,128)(2,1)S(1)}, bf16[128,1024]{1,0:T(8,128)(2,1)S(1)}, u32[]{:S(2)}, u32[]{:S(2)}) collective-permute-start(bf16[128,1024]{1,0:T(8,128)(2,1)S(1)} %get-tuple-element.32), channel_id=1, source_target_pairs={{0,1},{1,0},{2,3},{3,2},{4,5},{5,4},{6,7},{7,6},{8,9},{9,8},{10,11... | collective-permute-start | bytes 786440 | tf_op jit(solution)/shard_map/ppermute | solution.py:295
  23.9 2.0 %collective-permute-start.11 = (bf16[128,512]{1,0:T(8,128)(2,1)S(1)}, bf16[128,512]{1,0:T(8,128)(2,1)S(1)}, u32[]{:S(2)}, u32[]{:S(2)}) collective-permute-start(bf16[128,512]{1,0:T(8,128)(2,1)S(1)} %add_convert_fusion.1), channel_id=1, source_target_pairs={{0,2},{1,3},{2,0},{3,1},{4,6},{5,7},{6,4},{7,5},{8,10},{9,11},{10,... | collective-permute-start | bytes 393224 | tf_op jit(solution)/shard_map/ppermute | solution.py:295
  25.9 2.1 %collective-permute-done.10 = bf16[128,512]{1,0:T(8,128)(2,1)S(1)} collective-permute-done((bf16[128,512]{1,0:T(8,128)(2,1)S(1)}, bf16[128,512]{1,0:T(8,128)(2,1)S(1)}, u32[]{:S(2)}, u32[]{:S(2)}) %collective-permute-start.10) | collective-permute-done | bytes 131104 | tf_op jit(solution)/shard_map/ppermute | solution.py:295
  28.1 4.4 %collective-permute-done.11 = bf16[128,512]{1,0:T(8,128)(2,1)S(1)} collective-permute-done((bf16[128,512]{1,0:T(8,128)(2,1)S(1)}, bf16[128,512]{1,0:T(8,128)(2,1)S(1)}, u32[]{:S(2)}, u32[]{:S(2)}) %collective-permute-start.11) | collective-permute-done | bytes 131104 | tf_op jit(solution)/shard_map/ppermute | solution.py:295
  32.5 0.9 %collective-permute-done.8 = bf16[128,1024]{1,0:T(8,128)(2,1)S(1)} collective-permute-done((bf16[128,1024]{1,0:T(8,128)(2,1)S(1)}, bf16[128,1024]{1,0:T(8,128)(2,1)S(1)}, u32[]{:S(2)}, u32[]{:S(2)}) %collective-permute-start.8) | collective-permute-done | bytes 262176 | tf_op jit(solution)/shard_map/ppermute | solution.py:295
  33.4 0.8 %add_convert_fusion = bf16[128,1024]{1,0:T(8,128)(2,1)} fusion(f32[128,1024]{1,0:T(8,128)S(1)} %get-tuple-element.29, bf16[128,1024]{1,0:T(8,128)(2,1)S(1)} %collective-permute-done.8, bf16[128,512]{1,0:T(8,128)(2,1)S(1)} %collective-permute-done.11, bf16[128,512]{1,0:T(8,128)(2,1)S(1)} %collective-permute-done.10), kind=kLoop, calls=%fused_computation | loop fusion | flops 1048576 | bytes 1310720 | tf_op jit(solution)/shard_map/convert_element_type | solution.py:373
  (3 shorter events, 0.1 us)
Async XLA Ops:
  0.0 12.2 %copy-start = (bf16[4096,128]{1,0:T(8,128)(2,1)S(1)}, bf16[4096,128]{1,0:T(8,128)(2,1)}, u32[]{:S(2)}) copy-start(bf16[4096,128]{1,0:T(8,128)(2,1)} %wq_ref.5) | copy-start | bytes 3145732
  0.0 12.2 %copy-start.1 = (bf16[4096,128]{1,0:T(8,128)(2,1)S(1)}, bf16[4096,128]{1,0:T(8,128)(2,1)}, u32[]{:S(2)}) copy-start(bf16[4096,128]{1,0:T(8,128)(2,1)} %wk_ref.5) | copy-start | bytes 3145732
  0.0 12.2 %copy-start.2 = (bf16[4096,128]{1,0:T(8,128)(2,1)S(1)}, bf16[4096,128]{1,0:T(8,128)(2,1)}, u32[]{:S(2)}) copy-start(bf16[4096,128]{1,0:T(8,128)(2,1)} %wv_ref.5) | copy-start | bytes 3145732
  0.0 12.2 %copy-start.3 = (bf16[128,128]{1,0:T(8,128)(2,1)S(1)}, bf16[128,128]{1,0:T(8,128)(2,1)}, u32[]{:S(2)}) copy-start(bf16[128,128]{1,0:T(8,128)(2,1)} %q_ref.1) | copy-start | bytes 98308
  0.0 12.2 %copy-start.4 = (bf16[128,128]{1,0:T(8,128)(2,1)S(1)}, bf16[128,128]{1,0:T(8,128)(2,1)}, u32[]{:S(2)}) copy-start(bf16[128,128]{1,0:T(8,128)(2,1)} %k_ref.1) | copy-start | bytes 98308
  0.0 12.2 %copy-start.5 = (bf16[128,128]{1,0:T(8,128)(2,1)S(1)}, bf16[128,128]{1,0:T(8,128)(2,1)}, u32[]{:S(2)}) copy-start(bf16[128,128]{1,0:T(8,128)(2,1)} %v_ref.1) | copy-start | bytes 98308
  0.0 12.2 %copy-start.6 = (bf16[128,128]{1,0:T(8,128)(2,1)S(1)}, bf16[128,128]{1,0:T(8,128)(2,1)}, u32[]{:S(2)}) copy-start(bf16[128,128]{1,0:T(8,128)(2,1)} %g_ref.1) | copy-start | bytes 98308
  0.0 12.2 %copy-start.7 = (bf16[128,128]{1,0:T(8,128)(2,1)S(1)}, bf16[128,128]{1,0:T(8,128)(2,1)}, u32[]{:S(2)}) copy-start(bf16[128,128]{1,0:T(8,128)(2,1)} %a_ref.1) | copy-start | bytes 98308
  1.9 6.8 %collective-permute-start = (bf16[144,256]{1,0:T(8,128)(2,1)}, bf16[144,256]{1,0:T(8,128)(2,1)S(1)}, u32[]{:S(2)}, u32[]{:S(2)}) collective-permute-start(bf16[144,256]{1,0:T(8,128)(2,1)} %get-tuple-element.21), channel_id=1, source_target_pairs={{0,24},{4,28},{8,16},{12,20},{16,8},{20,12},{24,0},{28,4},{1,25},{... | collective-permute-start | bytes 221192 | tf_op jit(solution)/shard_map/ppermute | solution.py:295
  5.8 5.2 %copy-start.8 = (f32[128,1]{0,1:T(1,128)S(1)}, f32[128,1]{0,1:T(1,128)}, u32[]{:S(2)}) copy-start(f32[128,1]{0,1:T(1,128)} %param.14) | copy-start | bytes 1540
  5.8 4.7 %collective-permute-start.2 = (bf16[144,256]{1,0:T(8,128)(2,1)}, bf16[144,256]{1,0:T(8,128)(2,1)S(1)}, u32[]{:S(2)}, u32[]{:S(2)}) collective-permute-start(bf16[144,256]{1,0:T(8,128)(2,1)} %get-tuple-element.24), channel_id=1, source_target_pairs={{0,8},{4,12},{8,0},{12,4},{16,24},{20,28},{24,16},{28,20},{1,9},{5... | collective-permute-start | bytes 221192 | tf_op jit(solution)/shard_map/ppermute | solution.py:295
  6.4 4.6 %collective-permute-start.4 = (bf16[144,256]{1,0:T(8,128)(2,1)}, bf16[144,256]{1,0:T(8,128)(2,1)S(1)}, u32[]{:S(2)}, u32[]{:S(2)}) collective-permute-start(bf16[144,256]{1,0:T(8,128)(2,1)} %get-tuple-element.21), channel_id=1, source_target_pairs={{0,16},{4,20},{8,24},{12,28},{16,0},{20,4},{24,8},{28,12},{1,17},{... | collective-permute-start | bytes 221192 | tf_op jit(solution)/shard_map/ppermute | solution.py:295
  6.5 4.5 %collective-permute-start.1 = (bf16[144,256]{1,0:T(8,128)(2,1)}, bf16[144,256]{1,0:T(8,128)(2,1)S(1)}, u32[]{:S(2)}, u32[]{:S(2)}) collective-permute-start(bf16[144,256]{1,0:T(8,128)(2,1)} %get-tuple-element.23), channel_id=1, source_target_pairs={{0,4},{4,0},{8,12},{12,8},{16,20},{20,16},{24,28},{28,24},{1,5},{5... | collective-permute-start | bytes 221192 | tf_op jit(solution)/shard_map/ppermute | solution.py:295
  8.7 3.5 %collective-permute-start.6 = (bf16[144,256]{1,0:T(8,128)(2,1)S(1)}, bf16[144,256]{1,0:T(8,128)(2,1)S(1)}, u32[]{:S(2)}, u32[]{:S(2)}) collective-permute-start(bf16[144,256]{1,0:T(8,128)(2,1)S(1)} %collective-permute-done.refs_5_), channel_id=1, source_target_pairs={{0,4},{4,0},{8,12},{12,8},{16,20},{20,16},{24,28},{28,24},{1,5},{5... | collective-permute-start | bytes 221192 | tf_op jit(solution)/shard_map/ppermute | solution.py:295
  10.5 1.3 %collective-permute-start.3 = (bf16[144,256]{1,0:T(8,128)(2,1)S(1)}, bf16[144,256]{1,0:T(8,128)(2,1)S(1)}, u32[]{:S(2)}, u32[]{:S(2)}) collective-permute-start(bf16[144,256]{1,0:T(8,128)(2,1)S(1)} %collective-permute-done.2.refs_1_), channel_id=1, source_target_pairs={{0,4},{4,0},{8,12},{12,8},{16,20},{20,16},{24,28},{28,24},{1,5},{5... | collective-permute-start | bytes 221192 | tf_op jit(solution)/shard_map/ppermute | solution.py:295
  10.9 1.3 %collective-permute-start.5 = (bf16[144,256]{1,0:T(8,128)(2,1)S(1)}, bf16[144,256]{1,0:T(8,128)(2,1)S(1)}, u32[]{:S(2)}, u32[]{:S(2)}) collective-permute-start(bf16[144,256]{1,0:T(8,128)(2,1)S(1)} %collective-permute-done.4.refs_3_), channel_id=1, source_target_pairs={{0,4},{4,0},{8,12},{12,8},{16,20},{20,16},{24,28},{28,24},{1,5},{5... | collective-permute-start | bytes 221192 | tf_op jit(solution)/shard_map/ppermute | solution.py:295
  13.2 5.8 %collective-permute-start.9 = (bf16[128,512]{1,0:T(8,128)(2,1)S(1)}, bf16[128,512]{1,0:T(8,128)(2,1)S(1)}, u32[]{:S(2)}, u32[]{:S(2)}) collective-permute-start(bf16[128,512]{1,0:T(8,128)(2,1)S(1)} %get-tuple-element.34), channel_id=1, source_target_pairs={{0,1},{1,0},{2,3},{3,2},{4,5},{5,4},{6,7},{7,6},{8,9},{9,8},{10,11... | collective-permute-start | bytes 393224 | tf_op jit(solution)/shard_map/ppermute | solution.py:295
  16.0 5.7 %collective-permute-start.7 = (bf16[128,512]{1,0:T(8,128)(2,1)S(1)}, bf16[128,512]{1,0:T(8,128)(2,1)S(1)}, u32[]{:S(2)}, u32[]{:S(2)}) collective-permute-start(bf16[128,512]{1,0:T(8,128)(2,1)S(1)} %get-tuple-element.31), channel_id=1, source_target_pairs={{0,1},{1,0},{2,3},{3,2},{4,5},{5,4},{6,7},{7,6},{8,9},{9,8},{10,11... | collective-permute-start | bytes 393224 | tf_op jit(solution)/shard_map/ppermute | solution.py:295
  19.1 9.0 %collective-permute-start.10 = (bf16[128,512]{1,0:T(8,128)(2,1)S(1)}, bf16[128,512]{1,0:T(8,128)(2,1)S(1)}, u32[]{:S(2)}, u32[]{:S(2)}) collective-permute-start(bf16[128,512]{1,0:T(8,128)(2,1)S(1)} %add_convert_fusion.2), channel_id=1, source_target_pairs={{0,2},{1,3},{2,0},{3,1},{4,6},{5,7},{6,4},{7,5},{8,10},{9,11},{10,... | collective-permute-start | bytes 393224 | tf_op jit(solution)/shard_map/ppermute | solution.py:295
  21.8 11.6 %collective-permute-start.8 = (bf16[128,1024]{1,0:T(8,128)(2,1)S(1)}, bf16[128,1024]{1,0:T(8,128)(2,1)S(1)}, u32[]{:S(2)}, u32[]{:S(2)}) collective-permute-start(bf16[128,1024]{1,0:T(8,128)(2,1)S(1)} %get-tuple-element.32), channel_id=1, source_target_pairs={{0,1},{1,0},{2,3},{3,2},{4,5},{5,4},{6,7},{7,6},{8,9},{9,8},{10,11... | collective-permute-start | bytes 786440 | tf_op jit(solution)/shard_map/ppermute | solution.py:295
  23.9 8.6 %collective-permute-start.11 = (bf16[128,512]{1,0:T(8,128)(2,1)S(1)}, bf16[128,512]{1,0:T(8,128)(2,1)S(1)}, u32[]{:S(2)}, u32[]{:S(2)}) collective-permute-start(bf16[128,512]{1,0:T(8,128)(2,1)S(1)} %add_convert_fusion.1), channel_id=1, source_target_pairs={{0,2},{1,3},{2,0},{3,1},{4,6},{5,7},{6,4},{7,5},{8,10},{9,11},{10,... | collective-permute-start | bytes 393224 | tf_op jit(solution)/shard_map/ppermute | solution.py:295

commit v14 on v13

--- a/solution.py
+++ b/solution.py
@@ -225,9 +225,9 @@
 
 def project(grads, w_refs, start, out_ref):
     part = out_ref.shape[1]
-    cols = math.gcd(part, 512)
+    cols = part if part < 512 else math.gcd(part, 512)
     for at in range(0, part, cols):
-        span = pl.ds(pl.multiple_of(start + at, cols), cols)
+        span = pl.ds(pl.multiple_of(start + at, 128), cols)
         weight = jnp.concatenate([ref[span, :] for ref in w_refs], axis=1)
         out_ref[:, at : at + cols] = dot_nt(grads[...], weight).astype(out_ref.dtype)
 
@@ -274,18 +274,21 @@
     project(grads, (wq_ref, wk_ref, wv_ref), start, front)
 
 
-def far_kernel(part, grads, wq_ref, wk_ref, wv_ref, front, back):
+def far_kernel(part, grads, wq_ref, wk_ref, wv_ref, front, back, third, second):
     w_refs = (wq_ref, wk_ref, wv_ref)
     head = lax.axis_index("head")
     start = (head ^ 2) * part
+    size = front.shape[1]
+    project(grads, w_refs, (head ^ 3) * part + 2 * size, third)
+    project(grads, w_refs, start + 2 * size, second)
     project(grads, w_refs, start, front)
-    project(grads, w_refs, start + part // 2, back)
+    project(grads, w_refs, start + size, back)
 
 
 def close_kernel(part, grads, wq_ref, wk_ref, wv_ref, last, near, mine):
     w_refs = (wq_ref, wk_ref, wv_ref)
     head = lax.axis_index("head")
-    project(grads, w_refs, (head ^ 3) * part + part // 2, last)
+    project(grads, w_refs, (head ^ 3) * part + last.shape[1], last)
     project(grads, w_refs, (head ^ 1) * part, near)
     project(grads, w_refs, head * part, mine)
 
@@ -331,8 +334,11 @@
     for at in range(2, ctx, 2):
         got[at + 1] = swap(got[at], "ctx", 1)
     got = [got[at] for at in range(1, ctx)]
-    half_low = jax.ShapeDtypeStruct((rows, part // 2), jnp.bfloat16)
-    half = jax.ShapeDtypeStruct((rows, part // 2), jnp.float32)
+    straight = part // 4
+    size = (part - straight) // 2
+    half_low = jax.ShapeDtypeStruct((rows, size), jnp.bfloat16)
+    half = jax.ShapeDtypeStruct((rows, size), jnp.float32)
+    piece = jax.ShapeDtypeStruct((rows, straight), jnp.bfloat16)
     low = jax.ShapeDtypeStruct((rows, part), jnp.bfloat16)
     full = jax.ShapeDtypeStruct((rows, part), jnp.float32)
     grads, front = pl.pallas_call(
@@ -361,7 +367,10 @@
             ),
         )(*operands)
 
-    two_front, two_back = projected(far_kernel, [half, half], (grads, *weights))
+    two_front, two_back, third, second = projected(
+        far_kernel, [half, half, piece, piece], (grads, *weights)
+    )
+    third, second = swap(third, "head", 3), swap(second, "head", 2)
     grads, two_front = lax.optimization_barrier((grads, two_front))
     back, near, total = projected(close_kernel, [half_low, low, full], (grads, *weights))
     back = swap(back, "head", 1)
@@ -369,7 +378,9 @@
     front = swap((two_front + front.astype(jnp.float32)).astype(jnp.bfloat16), "head", 2)
     back = swap((two_back + back.astype(jnp.float32)).astype(jnp.bfloat16), "head", 2)
     near = swap(near, "head", 1)
+    direct = second.astype(jnp.float32) + third.astype(jnp.float32)
     far_sum = jnp.concatenate([front, back], axis=1).astype(jnp.float32)
+    far_sum = jnp.concatenate([far_sum, direct], axis=1)
     return (total + near.astype(jnp.float32) + far_sum).astype(jnp.bfloat16)
 
 

time: 34.3 us -> 37.6 us (1.096)
  starting transfers between devices: 13.6 us -> 17.7 us
  waiting for transfers between devices: 15.6 us -> 14.9 us
    ppermute x12 -> x14, starting transfers between devices: 13.6 us -> 17.7 us  [swap(): return lax.ppermute(value, axis, [(at, at ^ offset) for at in range(size)])]
    ppermute x12 -> x14, waiting for transfers between devices: 15.6 us -> 14.9 us  [swap(): return lax.ppermute(value, axis, [(at, at ^ offset) for at in range(size)])]
  transfers between devices with their start and end apart: 12 -> 14, of which waited for: 9 -> 9; matrix products, arithmetic and copies ran while one was open for 0% -> 0% of each run, Pallas kernels for 3% -> 3%
where the time goes in v14:
time: 37.6 us; the launch traced here: 37.4 us
  starting transfers between devices  17.7 us (47%)
  waiting for transfers between devices  14.9 us (40%)
  Pallas kernels  3.87 us (10%)
  other arithmetic  0.87 us (2%)
    ppermute x14, starting transfers between devices, swap(): return lax.ppermute(value, axis, [(at, at ^ offset) for at in range(size)])  17.7 us
    ppermute x14, waiting for transfers between devices, swap(): return lax.ppermute(value, axis, [(at, at ^ offset) for at in range(size)])  14.9 us
    pallas_call x1, Pallas kernels, near_body(): pl.pallas_call(send_kernel, out_shape=[hop] * bits, in_specs=[hbm] * 6, o...  1.82 us
    pallas_call x2, Pallas kernels, projected(): pl.pallas_call(functools.partial(kernel, part), out_shape=outs, in_specs=...  1.1 us
    pallas_call x1, Pallas kernels, near_body(): pl.pallas_call(functools.partial(near_kernel, scale, part), out_shape=[ja...  0.95 us
    convert_element_type x1, other arithmetic, near_body(): return (total + near.astype(jnp.float32) + far_sum).astype(jnp.bfloat16)  0.78 us
  transfers between devices with their start and end apart: 14, of which 9 were waited for; matrix products, arithmetic and copies ran while one was open for 0% of the time, Pallas kernels for 3%

profile of v14, /device:TPU:0, one launch (start us, length us, event | category | flops | bytes accessed | tf_op | source)
XLA Modules:
  0.0 37.4 jit_solution(8740644921244451445)
XLA Ops:
  0.0 0.0 copy-start
  0.0 0.0 copy-start.1
  0.0 0.0 copy-start.2
  0.0 0.0 copy-start.3
  0.0 0.0 copy-start.4
  0.0 0.0 copy-start.5
  0.0 0.0 copy-start.6
  0.0 0.0 copy-start.7
  0.0 1.8 %shard_map.91 = (bf16[144,256]{1,0:T(8,128)(2,1)}, bf16[144,256]{1,0:T(8,128)(2,1)}, bf16[144,256]{1,0:T(8,128)(2,1)}) custom-call(bf16[128,128]{1,0:T(8,128)(2,1)} %q_ref.1, bf16[128,128]{1,0:T(8,128)(2,1)} %k_ref.1, bf16[128,128]{1,0:T(8,128)(2,1)} %v_ref.1, bf16[128,128]{1,0:T(8,128)(2,1)} %g_ref.1, bf16[128,128]{1,0:T(8,128)(2,1)} %a_ref.1, f32[1,128]{1,0:T(1,128)} %bitcast.1), custom_call_target="tpu_custom_call" | custom-call | flops 5000000000 | bytes 327680 | tf_op jit(solution)/shard_map/pallas_call | solution.py:311
  1.9 4.0 %collective-permute-start = (bf16[144,256]{1,0:T(8,128)(2,1)}, bf16[144,256]{1,0:T(8,128)(2,1)S(1)}, u32[]{:S(2)}, u32[]{:S(2)}) collective-permute-start(bf16[144,256]{1,0:T(8,128)(2,1)} %get-tuple-element.23), channel_id=1, source_target_pairs={{0,24},{4,28},{8,16},{12,20},{16,8},{20,12},{24,0},{28,4},{1,25},{... | collective-permute-start | bytes 221192 | tf_op jit(solution)/shard_map/ppermute | solution.py:298
  5.8 0.0 copy-start.8
  5.8 0.5 %collective-permute-start.2 = (bf16[144,256]{1,0:T(8,128)(2,1)}, bf16[144,256]{1,0:T(8,128)(2,1)S(1)}, u32[]{:S(2)}, u32[]{:S(2)}) collective-permute-start(bf16[144,256]{1,0:T(8,128)(2,1)} %get-tuple-element.26), channel_id=1, source_target_pairs={{0,8},{4,12},{8,0},{12,4},{16,24},{20,28},{24,16},{28,20},{1,9},{5... | collective-permute-start | bytes 221192 | tf_op jit(solution)/shard_map/ppermute | solution.py:298
  6.4 0.1 collective-permute-start.4
  6.5 0.0 collective-permute-start.1
  6.5 2.2 %collective-permute-done.refs_5_ = bf16[144,256]{1,0:T(8,128)(2,1)S(1)} collective-permute-done((bf16[144,256]{1,0:T(8,128)(2,1)}, bf16[144,256]{1,0:T(8,128)(2,1)S(1)}, u32[]{:S(2)}, u32[]{:S(2)}) %collective-permute-start) | collective-permute-done | bytes 73760 | tf_op jit(solution)/shard_map/ppermute | solution.py:298
  8.7 0.0 collective-permute-start.6
  8.7 1.8 %collective-permute-done.2.refs_1_ = bf16[144,256]{1,0:T(8,128)(2,1)S(1)} collective-permute-done((bf16[144,256]{1,0:T(8,128)(2,1)}, bf16[144,256]{1,0:T(8,128)(2,1)S(1)}, u32[]{:S(2)}, u32[]{:S(2)}) %collective-permute-start.2) | collective-permute-done | bytes 73760 | tf_op jit(solution)/shard_map/ppermute | solution.py:298
  10.5 0.0 collective-permute-start.3
  10.5 0.4 %collective-permute-done.4.refs_3_ = bf16[144,256]{1,0:T(8,128)(2,1)S(1)} collective-permute-done((bf16[144,256]{1,0:T(8,128)(2,1)}, bf16[144,256]{1,0:T(8,128)(2,1)S(1)}, u32[]{:S(2)}, u32[]{:S(2)}) %collective-permute-start.4) | collective-permute-done | bytes 73760 | tf_op jit(solution)/shard_map/ppermute | solution.py:298
  10.9 0.1 collective-permute-start.5
  11.0 0.0 copy-done.8
  11.0 0.0 collective-permute-done.1.refs_0_
  11.0 0.7 %collective-permute-done.3.refs_2_ = bf16[144,256]{1,0:T(8,128)(2,1)S(1)} collective-permute-done((bf16[144,256]{1,0:T(8,128)(2,1)S(1)}, bf16[144,256]{1,0:T(8,128)(2,1)S(1)}, u32[]{:S(2)}, u32[]{:S(2)}) %collective-permute-start.3) | collective-permute-done | bytes 73760 | tf_op jit(solution)/shard_map/ppermute | solution.py:298
  11.8 0.4 %collective-permute-done.5.refs_4_ = bf16[144,256]{1,0:T(8,128)(2,1)S(1)} collective-permute-done((bf16[144,256]{1,0:T(8,128)(2,1)S(1)}, bf16[144,256]{1,0:T(8,128)(2,1)S(1)}, u32[]{:S(2)}, u32[]{:S(2)}) %collective-permute-start.5) | collective-permute-done | bytes 73760 | tf_op jit(solution)/shard_map/ppermute | solution.py:298
  12.2 0.0 collective-permute-done.6.refs_6_
  12.2 0.0 copy-done
  12.2 0.0 copy-done.1
  12.2 0.0 copy-done.2
  12.2 0.0 copy-done.3
  12.2 0.0 copy-done.4
  12.3 0.0 copy-done.5
  12.3 0.0 copy-done.6
  12.3 0.0 copy-done.7
  12.3 0.9 %shard_map.92 = (bf16[128,384]{1,0:T(8,128)(2,1)S(1)}, bf16[128,384]{1,0:T(8,128)(2,1)S(1)}) custom-call(bf16[128,128]{1,0:T(8,128)(2,1)S(1)} %copy-done.3, bf16[128,128]{1,0:T(8,128)(2,1)S(1)} %copy-done.4, bf16[128,128]{1,0:T(8,128)(2,1)S(1)} %copy-done.5, bf16[128,128]{1,0:T(8,128)(2,1)S(1)} %copy-done.6, bf16[128,128]{1,0:T(8,128)(2,1)S(1)} %copy-done.7, ...), custom_call_target="tpu_custom_call" | custom-call | flops 335544320 | bytes 1310720 | tf_op jit(solution)/shard_map/pallas_call | solution.py:344
  13.2 1.6 %collective-permute-start.9 = (bf16[128,384]{1,0:T(8,128)(2,1)S(1)}, bf16[128,384]{1,0:T(8,128)(2,1)S(1)}, u32[]{:S(2)}, u32[]{:S(2)}) collective-permute-start(bf16[128,384]{1,0:T(8,128)(2,1)S(1)} %get-tuple-element.36), channel_id=1, source_target_pairs={{0,1},{1,0},{2,3},{3,2},{4,5},{5,4},{6,7},{7,6},{8,9},{9,8},{10,11... | collective-permute-start | bytes 294920 | tf_op jit(solution)/shard_map/ppermute | solution.py:298
  14.9 0.4 %shard_map.93 = (f32[128,384]{1,0:T(8,128)S(1)}, f32[128,384]{1,0:T(8,128)S(1)}, bf16[128,256]{1,0:T(8,128)(2,1)S(1)}, bf16[128,256]{1,0:T(8,128)(2,1)S(1)}) custom-call(bf16[128,384]{1,0:T(8,128)(2,1)S(1)} %get-tuple-element.30.grads, bf16[4096,128]{1,0:T(8,128)(2,1)S(1)} %copy-done, bf16[4096,128]{1,0:T(8,128)(2,1)S(1)} %copy-done.1, ...), custom_call_target="tpu_custom_call" | custom-call | flops 125829120 | bytes 983040 | tf_op jit(solution)/shard_map/pallas_call | solution.py:359
  15.3 2.7 %collective-permute-start.12 = (bf16[128,256]{1,0:T(8,128)(2,1)S(1)}, bf16[128,256]{1,0:T(8,128)(2,1)S(1)}, u32[]{:S(2)}, u32[]{:S(2)}) collective-permute-start(bf16[128,256]{1,0:T(8,128)(2,1)S(1)} %get-tuple-element.39), channel_id=1, source_target_pairs={{0,2},{1,3},{2,0},{3,1},{4,6},{5,7},{6,4},{7,5},{8,10},{9,11},{10,... | collective-permute-start | bytes 196616 | tf_op jit(solution)/shard_map/ppermute | solution.py:298
  18.0 0.2 collective-permute-start.13
  18.2 0.7 %shard_map.94 = (bf16[128,384]{1,0:T(8,128)(2,1)S(1)}, bf16[128,1024]{1,0:T(8,128)(2,1)S(1)}, f32[128,1024]{1,0:T(8,128)S(1)}) custom-call(bf16[128,384]{1,0:T(8,128)(2,1)S(1)} %get-tuple-element.30.grads, bf16[4096,128]{1,0:T(8,128)(2,1)S(1)} %copy-done, bf16[4096,128]{1,0:T(8,128)(2,1)S(1)} %copy-done.1, bf16[4096,128]{1,0:T(8,128)(2,1)S(1)} %copy-done.2), custom_call_target="tpu_custom_call" | custom-call | flops 239075328 | bytes 1867776 | tf_op jit(solution)/shard_map/pallas_call | solution.py:359
  18.9 0.7 %collective-permute-start.7 = (bf16[128,384]{1,0:T(8,128)(2,1)S(1)}, bf16[128,384]{1,0:T(8,128)(2,1)S(1)}, u32[]{:S(2)}, u32[]{:S(2)}) collective-permute-start(bf16[128,384]{1,0:T(8,128)(2,1)S(1)} %get-tuple-element.33), channel_id=1, source_target_pairs={{0,1},{1,0},{2,3},{3,2},{4,5},{5,4},{6,7},{7,6},{8,9},{9,8},{10,11... | collective-permute-start | bytes 294920 | tf_op jit(solution)/shard_map/ppermute | solution.py:298
  19.6 0.0 collective-permute-done.9
  19.6 3.5 %collective-permute-start.10 = (bf16[128,384]{1,0:T(8,128)(2,1)S(1)}, bf16[128,384]{1,0:T(8,128)(2,1)S(1)}, u32[]{:S(2)}, u32[]{:S(2)}) collective-permute-start(bf16[128,384]{1,0:T(8,128)(2,1)S(1)} %add_convert_fusion.1), channel_id=1, source_target_pairs={{0,2},{1,3},{2,0},{3,1},{4,6},{5,7},{6,4},{7,5},{8,10},{9,11},{10,... | collective-permute-start | bytes 294920 | tf_op jit(solution)/shard_map/ppermute | solution.py:298
  23.2 2.0 %collective-permute-done.7 = bf16[128,384]{1,0:T(8,128)(2,1)S(1)} collective-permute-done((bf16[128,384]{1,0:T(8,128)(2,1)S(1)}, bf16[128,384]{1,0:T(8,128)(2,1)S(1)}, u32[]{:S(2)}, u32[]{:S(2)}) %collective-permute-start.7) | collective-permute-done | bytes 98336 | tf_op jit(solution)/shard_map/ppermute | solution.py:298
  25.2 2.0 %collective-permute-start.11 = (bf16[128,384]{1,0:T(8,128)(2,1)S(1)}, bf16[128,384]{1,0:T(8,128)(2,1)S(1)}, u32[]{:S(2)}, u32[]{:S(2)}) collective-permute-start(bf16[128,384]{1,0:T(8,128)(2,1)S(1)} %add_convert_fusion), channel_id=1, source_target_pairs={{0,2},{1,3},{2,0},{3,1},{4,6},{5,7},{6,4},{7,5},{8,10},{9,11},{10,... | collective-permute-start | bytes 294920 | tf_op jit(solution)/shard_map/ppermute | solution.py:298
  27.2 2.1 %collective-permute-start.8 = (bf16[128,1024]{1,0:T(8,128)(2,1)S(1)}, bf16[128,1024]{1,0:T(8,128)(2,1)S(1)}, u32[]{:S(2)}, u32[]{:S(2)}) collective-permute-start(bf16[128,1024]{1,0:T(8,128)(2,1)S(1)} %get-tuple-element.34), channel_id=1, source_target_pairs={{0,1},{1,0},{2,3},{3,2},{4,5},{5,4},{6,7},{7,6},{8,9},{9,8},{10,11... | collective-permute-start | bytes 786440 | tf_op jit(solution)/shard_map/ppermute | solution.py:298
  29.3 0.0 collective-permute-done.12
  29.3 0.0 collective-permute-done.13
  29.4 1.1 %collective-permute-done.10 = bf16[128,384]{1,0:T(8,128)(2,1)S(1)} collective-permute-done((bf16[128,384]{1,0:T(8,128)(2,1)S(1)}, bf16[128,384]{1,0:T(8,128)(2,1)S(1)}, u32[]{:S(2)}, u32[]{:S(2)}) %collective-permute-start.10) | collective-permute-done | bytes 98336 | tf_op jit(solution)/shard_map/ppermute | solution.py:298
  30.5 2.5 %collective-permute-done.11 = bf16[128,384]{1,0:T(8,128)(2,1)S(1)} collective-permute-done((bf16[128,384]{1,0:T(8,128)(2,1)S(1)}, bf16[128,384]{1,0:T(8,128)(2,1)S(1)}, u32[]{:S(2)}, u32[]{:S(2)}) %collective-permute-start.11) | collective-permute-done | bytes 98336 | tf_op jit(solution)/shard_map/ppermute | solution.py:298
  33.0 3.6 %collective-permute-done.8 = bf16[128,1024]{1,0:T(8,128)(2,1)S(1)} collective-permute-done((bf16[128,1024]{1,0:T(8,128)(2,1)S(1)}, bf16[128,1024]{1,0:T(8,128)(2,1)S(1)}, u32[]{:S(2)}, u32[]{:S(2)}) %collective-permute-start.8) | collective-permute-done | bytes 262176 | tf_op jit(solution)/shard_map/ppermute | solution.py:298
  36.7 0.8 %fusion = bf16[128,1024]{1,0:T(8,128)(2,1)} fusion(f32[128,256]{1,0:T(8,128)S(1)} %convert_add_fusion, f32[128,768]{1,0:T(8,128)S(1)} %maximum_convert_fusion, f32[128,1024]{1,0:T(8,128)S(1)} %get-tuple-element.31, bf16[128,1024]{1,0:T(8,128)(2,1)S(1)} %collective-permute-done.8), kind=kLoop, calls=%fused_computation.1 | loop fusion | flops 655360 | bytes 1572864 | tf_op jit(solution)/shard_map/convert_element_type | solution.py:384
  (5 shorter events, 0.1 us)
Async XLA Ops:
  0.0 12.2 %copy-start = (bf16[4096,128]{1,0:T(8,128)(2,1)S(1)}, bf16[4096,128]{1,0:T(8,128)(2,1)}, u32[]{:S(2)}) copy-start(bf16[4096,128]{1,0:T(8,128)(2,1)} %wq_ref.5) | copy-start | bytes 3145732
  0.0 12.2 %copy-start.1 = (bf16[4096,128]{1,0:T(8,128)(2,1)S(1)}, bf16[4096,128]{1,0:T(8,128)(2,1)}, u32[]{:S(2)}) copy-start(bf16[4096,128]{1,0:T(8,128)(2,1)} %wk_ref.5) | copy-start | bytes 3145732
  0.0 12.2 %copy-start.2 = (bf16[4096,128]{1,0:T(8,128)(2,1)S(1)}, bf16[4096,128]{1,0:T(8,128)(2,1)}, u32[]{:S(2)}) copy-start(bf16[4096,128]{1,0:T(8,128)(2,1)} %wv_ref.5) | copy-start | bytes 3145732
  0.0 12.2 %copy-start.3 = (bf16[128,128]{1,0:T(8,128)(2,1)S(1)}, bf16[128,128]{1,0:T(8,128)(2,1)}, u32[]{:S(2)}) copy-start(bf16[128,128]{1,0:T(8,128)(2,1)} %q_ref.1) | copy-start | bytes 98308
  0.0 12.2 %copy-start.4 = (bf16[128,128]{1,0:T(8,128)(2,1)S(1)}, bf16[128,128]{1,0:T(8,128)(2,1)}, u32[]{:S(2)}) copy-start(bf16[128,128]{1,0:T(8,128)(2,1)} %k_ref.1) | copy-start | bytes 98308
  0.0 12.2 %copy-start.5 = (bf16[128,128]{1,0:T(8,128)(2,1)S(1)}, bf16[128,128]{1,0:T(8,128)(2,1)}, u32[]{:S(2)}) copy-start(bf16[128,128]{1,0:T(8,128)(2,1)} %v_ref.1) | copy-start | bytes 98308
  0.0 12.2 %copy-start.6 = (bf16[128,128]{1,0:T(8,128)(2,1)S(1)}, bf16[128,128]{1,0:T(8,128)(2,1)}, u32[]{:S(2)}) copy-start(bf16[128,128]{1,0:T(8,128)(2,1)} %g_ref.1) | copy-start | bytes 98308
  0.0 12.2 %copy-start.7 = (bf16[128,128]{1,0:T(8,128)(2,1)S(1)}, bf16[128,128]{1,0:T(8,128)(2,1)}, u32[]{:S(2)}) copy-start(bf16[128,128]{1,0:T(8,128)(2,1)} %a_ref.1) | copy-start | bytes 98308
  1.9 6.8 %collective-permute-start = (bf16[144,256]{1,0:T(8,128)(2,1)}, bf16[144,256]{1,0:T(8,128)(2,1)S(1)}, u32[]{:S(2)}, u32[]{:S(2)}) collective-permute-start(bf16[144,256]{1,0:T(8,128)(2,1)} %get-tuple-element.23), channel_id=1, source_target_pairs={{0,24},{4,28},{8,16},{12,20},{16,8},{20,12},{24,0},{28,4},{1,25},{... | collective-permute-start | bytes 221192 | tf_op jit(solution)/shard_map/ppermute | solution.py:298
  5.8 5.2 %copy-start.8 = (f32[128,1]{0,1:T(1,128)S(1)}, f32[128,1]{0,1:T(1,128)}, u32[]{:S(2)}) copy-start(f32[128,1]{0,1:T(1,128)} %param.14) | copy-start | bytes 1540
  5.8 4.7 %collective-permute-start.2 = (bf16[144,256]{1,0:T(8,128)(2,1)}, bf16[144,256]{1,0:T(8,128)(2,1)S(1)}, u32[]{:S(2)}, u32[]{:S(2)}) collective-permute-start(bf16[144,256]{1,0:T(8,128)(2,1)} %get-tuple-element.26), channel_id=1, source_target_pairs={{0,8},{4,12},{8,0},{12,4},{16,24},{20,28},{24,16},{28,20},{1,9},{5... | collective-permute-start | bytes 221192 | tf_op jit(solution)/shard_map/ppermute | solution.py:298
  6.4 4.6 %collective-permute-start.4 = (bf16[144,256]{1,0:T(8,128)(2,1)}, bf16[144,256]{1,0:T(8,128)(2,1)S(1)}, u32[]{:S(2)}, u32[]{:S(2)}) collective-permute-start(bf16[144,256]{1,0:T(8,128)(2,1)} %get-tuple-element.23), channel_id=1, source_target_pairs={{0,16},{4,20},{8,24},{12,28},{16,0},{20,4},{24,8},{28,12},{1,17},{... | collective-permute-start | bytes 221192 | tf_op jit(solution)/shard_map/ppermute | solution.py:298
  6.5 4.5 %collective-permute-start.1 = (bf16[144,256]{1,0:T(8,128)(2,1)}, bf16[144,256]{1,0:T(8,128)(2,1)S(1)}, u32[]{:S(2)}, u32[]{:S(2)}) collective-permute-start(bf16[144,256]{1,0:T(8,128)(2,1)} %get-tuple-element.25), channel_id=1, source_target_pairs={{0,4},{4,0},{8,12},{12,8},{16,20},{20,16},{24,28},{28,24},{1,5},{5... | collective-permute-start | bytes 221192 | tf_op jit(solution)/shard_map/ppermute | solution.py:298
  8.7 3.5 %collective-permute-start.6 = (bf16[144,256]{1,0:T(8,128)(2,1)S(1)}, bf16[144,256]{1,0:T(8,128)(2,1)S(1)}, u32[]{:S(2)}, u32[]{:S(2)}) collective-permute-start(bf16[144,256]{1,0:T(8,128)(2,1)S(1)} %collective-permute-done.refs_5_), channel_id=1, source_target_pairs={{0,4},{4,0},{8,12},{12,8},{16,20},{20,16},{24,28},{28,24},{1,5},{5... | collective-permute-start | bytes 221192 | tf_op jit(solution)/shard_map/ppermute | solution.py:298
  10.5 1.3 %collective-permute-start.3 = (bf16[144,256]{1,0:T(8,128)(2,1)S(1)}, bf16[144,256]{1,0:T(8,128)(2,1)S(1)}, u32[]{:S(2)}, u32[]{:S(2)}) collective-permute-start(bf16[144,256]{1,0:T(8,128)(2,1)S(1)} %collective-permute-done.2.refs_1_), channel_id=1, source_target_pairs={{0,4},{4,0},{8,12},{12,8},{16,20},{20,16},{24,28},{28,24},{1,5},{5... | collective-permute-start | bytes 221192 | tf_op jit(solution)/shard_map/ppermute | solution.py:298
  10.9 1.3 %collective-permute-start.5 = (bf16[144,256]{1,0:T(8,128)(2,1)S(1)}, bf16[144,256]{1,0:T(8,128)(2,1)S(1)}, u32[]{:S(2)}, u32[]{:S(2)}) collective-permute-start(bf16[144,256]{1,0:T(8,128)(2,1)S(1)} %collective-permute-done.4.refs_3_), channel_id=1, source_target_pairs={{0,4},{4,0},{8,12},{12,8},{16,20},{20,16},{24,28},{28,24},{1,5},{5... | collective-permute-start | bytes 221192 | tf_op jit(solution)/shard_map/ppermute | solution.py:298
  13.2 6.4 %collective-permute-start.9 = (bf16[128,384]{1,0:T(8,128)(2,1)S(1)}, bf16[128,384]{1,0:T(8,128)(2,1)S(1)}, u32[]{:S(2)}, u32[]{:S(2)}) collective-permute-start(bf16[128,384]{1,0:T(8,128)(2,1)S(1)} %get-tuple-element.36), channel_id=1, source_target_pairs={{0,1},{1,0},{2,3},{3,2},{4,5},{5,4},{6,7},{7,6},{8,9},{9,8},{10,11... | collective-permute-start | bytes 294920 | tf_op jit(solution)/shard_map/ppermute | solution.py:298
  15.3 14.0 %collective-permute-start.12 = (bf16[128,256]{1,0:T(8,128)(2,1)S(1)}, bf16[128,256]{1,0:T(8,128)(2,1)S(1)}, u32[]{:S(2)}, u32[]{:S(2)}) collective-permute-start(bf16[128,256]{1,0:T(8,128)(2,1)S(1)} %get-tuple-element.39), channel_id=1, source_target_pairs={{0,2},{1,3},{2,0},{3,1},{4,6},{5,7},{6,4},{7,5},{8,10},{9,11},{10,... | collective-permute-start | bytes 196616 | tf_op jit(solution)/shard_map/ppermute | solution.py:298
  18.0 11.4 %collective-permute-start.13 = (bf16[128,256]{1,0:T(8,128)(2,1)S(1)}, bf16[128,256]{1,0:T(8,128)(2,1)S(1)}, u32[]{:S(2)}, u32[]{:S(2)}) collective-permute-start(bf16[128,256]{1,0:T(8,128)(2,1)S(1)} %get-tuple-element.40), channel_id=1, source_target_pairs={{0,3},{1,2},{2,1},{3,0},{4,7},{5,6},{6,5},{7,4},{8,11},{9,10},{10,... | collective-permute-start | bytes 196616 | tf_op jit(solution)/shard_map/ppermute | solution.py:298
  18.9 6.3 %collective-permute-start.7 = (bf16[128,384]{1,0:T(8,128)(2,1)S(1)}, bf16[128,384]{1,0:T(8,128)(2,1)S(1)}, u32[]{:S(2)}, u32[]{:S(2)}) collective-permute-start(bf16[128,384]{1,0:T(8,128)(2,1)S(1)} %get-tuple-element.33), channel_id=1, source_target_pairs={{0,1},{1,0},{2,3},{3,2},{4,5},{5,4},{6,7},{7,6},{8,9},{9,8},{10,11... | collective-permute-start | bytes 294920 | tf_op jit(solution)/shard_map/ppermute | solution.py:298
  19.6 10.9 %collective-permute-start.10 = (bf16[128,384]{1,0:T(8,128)(2,1)S(1)}, bf16[128,384]{1,0:T(8,128)(2,1)S(1)}, u32[]{:S(2)}, u32[]{:S(2)}) collective-permute-start(bf16[128,384]{1,0:T(8,128)(2,1)S(1)} %add_convert_fusion.1), channel_id=1, source_target_pairs={{0,2},{1,3},{2,0},{3,1},{4,6},{5,7},{6,4},{7,5},{8,10},{9,11},{10,... | collective-permute-start | bytes 294920 | tf_op jit(solution)/shard_map/ppermute | solution.py:298
  25.2 7.8 %collective-permute-start.11 = (bf16[128,384]{1,0:T(8,128)(2,1)S(1)}, bf16[128,384]{1,0:T(8,128)(2,1)S(1)}, u32[]{:S(2)}, u32[]{:S(2)}) collective-permute-start(bf16[128,384]{1,0:T(8,128)(2,1)S(1)} %add_convert_fusion), channel_id=1, source_target_pairs={{0,2},{1,3},{2,0},{3,1},{4,6},{5,7},{6,4},{7,5},{8,10},{9,11},{10,... | collective-permute-start | bytes 294920 | tf_op jit(solution)/shard_map/ppermute | solution.py:298
  27.2 9.4 %collective-permute-start.8 = (bf16[128,1024]{1,0:T(8,128)(2,1)S(1)}, bf16[128,1024]{1,0:T(8,128)(2,1)S(1)}, u32[]{:S(2)}, u32[]{:S(2)}) collective-permute-start(bf16[128,1024]{1,0:T(8,128)(2,1)S(1)} %get-tuple-element.34), channel_id=1, source_target_pairs={{0,1},{1,0},{2,3},{3,2},{4,5},{5,4},{6,7},{7,6},{8,9},{9,8},{10,11... | collective-permute-start | bytes 786440 | tf_op jit(solution)/shard_map/ppermute | solution.py:298

commit v15 on v13

--- a/solution.py
+++ b/solution.py
@@ -365,7 +365,7 @@
     grads, two_front = lax.optimization_barrier((grads, two_front))
     back, near, total = projected(close_kernel, [half_low, low, full], (grads, *weights))
     back = swap(back, "head", 1)
-    near, back = lax.optimization_barrier((near, back))
+    near, front = lax.optimization_barrier((near, front))
     front = swap((two_front + front.astype(jnp.float32)).astype(jnp.bfloat16), "head", 2)
     back = swap((two_back + back.astype(jnp.float32)).astype(jnp.bfloat16), "head", 2)
     near = swap(near, "head", 1)

time: 34.3 us -> 34.1 us (level)
  starting transfers between devices: 13.6 us -> 12.9 us
  waiting for transfers between devices: 15.6 us -> 16.1 us
    ppermute x12, starting transfers between devices: 13.6 us -> 12.9 us  [swap(): return lax.ppermute(value, axis, [(at, at ^ offset) for at in range(size)])]
    ppermute x12, waiting for transfers between devices: 15.6 us -> 16.1 us  [swap(): return lax.ppermute(value, axis, [(at, at ^ offset) for at in range(size)])]
where the time goes in v15:
time: 34.1 us; the launch traced here: 33.9 us
  waiting for transfers between devices  16.1 us (47%)
  starting transfers between devices  12.9 us (38%)
  Pallas kernels  3.9 us (11%)
  other arithmetic  0.85 us (2%)
    ppermute x12, waiting for transfers between devices, swap(): return lax.ppermute(value, axis, [(at, at ^ offset) for at in range(size)])  16.1 us
    ppermute x12, starting transfers between devices, swap(): return lax.ppermute(value, axis, [(at, at ^ offset) for at in range(size)])  12.9 us
    pallas_call x1, Pallas kernels, near_body(): pl.pallas_call(send_kernel, out_shape=[hop] * bits, in_specs=[hbm] * 6, o...  1.82 us
    pallas_call x2, Pallas kernels, projected(): pl.pallas_call(functools.partial(kernel, part), out_shape=outs, in_specs=...  1.14 us
    pallas_call x1, Pallas kernels, near_body(): pl.pallas_call(functools.partial(near_kernel, scale, part), out_shape=[ja...  0.94 us
    convert_element_type x1, other arithmetic, near_body(): return (total + near.astype(jnp.float32) + far_sum).astype(jnp.bfloat16)  0.79 us
  transfers between devices with their start and end apart: 12, of which 9 were waited for; matrix products, arithmetic and copies ran while one was open for 0% of the time, Pallas kernels for 3%

profile of v15, /device:TPU:0, one launch (start us, length us, event | category | flops | bytes accessed | tf_op | source)
XLA Modules:
  0.0 33.9 jit_solution(6096224478692819059)
XLA Ops:
  0.0 0.0 copy-start
  0.0 0.0 copy-start.1
  0.0 0.0 copy-start.2
  0.0 0.0 copy-start.3
  0.0 0.0 copy-start.4
  0.0 0.0 copy-start.5
  0.0 0.0 copy-start.6
  0.0 0.0 copy-start.7
  0.0 1.8 %shard_map.91 = (bf16[144,256]{1,0:T(8,128)(2,1)}, bf16[144,256]{1,0:T(8,128)(2,1)}, bf16[144,256]{1,0:T(8,128)(2,1)}) custom-call(bf16[128,128]{1,0:T(8,128)(2,1)} %q_ref.1, bf16[128,128]{1,0:T(8,128)(2,1)} %k_ref.1, bf16[128,128]{1,0:T(8,128)(2,1)} %v_ref.1, bf16[128,128]{1,0:T(8,128)(2,1)} %g_ref.1, bf16[128,128]{1,0:T(8,128)(2,1)} %a_ref.1, f32[1,128]{1,0:T(1,128)} %bitcast.1), custom_call_target="tpu_custom_call" | custom-call | flops 5000000000 | bytes 327680 | tf_op jit(solution)/shard_map/pallas_call | solution.py:308
  1.9 4.0 %collective-permute-start = (bf16[144,256]{1,0:T(8,128)(2,1)}, bf16[144,256]{1,0:T(8,128)(2,1)S(1)}, u32[]{:S(2)}, u32[]{:S(2)}) collective-permute-start(bf16[144,256]{1,0:T(8,128)(2,1)} %get-tuple-element.21), channel_id=1, source_target_pairs={{0,24},{4,28},{8,16},{12,20},{16,8},{20,12},{24,0},{28,4},{1,25},{... | collective-permute-start | bytes 221192 | tf_op jit(solution)/shard_map/ppermute | solution.py:295
  5.8 0.0 copy-start.8
  5.8 0.5 %collective-permute-start.2 = (bf16[144,256]{1,0:T(8,128)(2,1)}, bf16[144,256]{1,0:T(8,128)(2,1)S(1)}, u32[]{:S(2)}, u32[]{:S(2)}) collective-permute-start(bf16[144,256]{1,0:T(8,128)(2,1)} %get-tuple-element.24), channel_id=1, source_target_pairs={{0,8},{4,12},{8,0},{12,4},{16,24},{20,28},{24,16},{28,20},{1,9},{5... | collective-permute-start | bytes 221192 | tf_op jit(solution)/shard_map/ppermute | solution.py:295
  6.4 0.1 collective-permute-start.4
  6.5 0.0 collective-permute-start.1
  6.5 2.2 %collective-permute-done.refs_5_ = bf16[144,256]{1,0:T(8,128)(2,1)S(1)} collective-permute-done((bf16[144,256]{1,0:T(8,128)(2,1)}, bf16[144,256]{1,0:T(8,128)(2,1)S(1)}, u32[]{:S(2)}, u32[]{:S(2)}) %collective-permute-start) | collective-permute-done | bytes 73760 | tf_op jit(solution)/shard_map/ppermute | solution.py:295
  8.7 0.0 collective-permute-start.6
  8.7 1.8 %collective-permute-done.2.refs_1_ = bf16[144,256]{1,0:T(8,128)(2,1)S(1)} collective-permute-done((bf16[144,256]{1,0:T(8,128)(2,1)}, bf16[144,256]{1,0:T(8,128)(2,1)S(1)}, u32[]{:S(2)}, u32[]{:S(2)}) %collective-permute-start.2) | collective-permute-done | bytes 73760 | tf_op jit(solution)/shard_map/ppermute | solution.py:295
  10.5 0.0 collective-permute-start.3
  10.5 0.4 %collective-permute-done.4.refs_3_ = bf16[144,256]{1,0:T(8,128)(2,1)S(1)} collective-permute-done((bf16[144,256]{1,0:T(8,128)(2,1)}, bf16[144,256]{1,0:T(8,128)(2,1)S(1)}, u32[]{:S(2)}, u32[]{:S(2)}) %collective-permute-start.4) | collective-permute-done | bytes 73760 | tf_op jit(solution)/shard_map/ppermute | solution.py:295
  10.9 0.1 collective-permute-start.5
  11.0 0.0 copy-done.8
  11.0 0.0 collective-permute-done.1.refs_0_
  11.0 0.7 %collective-permute-done.3.refs_2_ = bf16[144,256]{1,0:T(8,128)(2,1)S(1)} collective-permute-done((bf16[144,256]{1,0:T(8,128)(2,1)S(1)}, bf16[144,256]{1,0:T(8,128)(2,1)S(1)}, u32[]{:S(2)}, u32[]{:S(2)}) %collective-permute-start.3) | collective-permute-done | bytes 73760 | tf_op jit(solution)/shard_map/ppermute | solution.py:295
  11.8 0.4 %collective-permute-done.5.refs_4_ = bf16[144,256]{1,0:T(8,128)(2,1)S(1)} collective-permute-done((bf16[144,256]{1,0:T(8,128)(2,1)S(1)}, bf16[144,256]{1,0:T(8,128)(2,1)S(1)}, u32[]{:S(2)}, u32[]{:S(2)}) %collective-permute-start.5) | collective-permute-done | bytes 73760 | tf_op jit(solution)/shard_map/ppermute | solution.py:295
  12.2 0.0 collective-permute-done.6.refs_6_
  12.2 0.0 copy-done
  12.2 0.0 copy-done.1
  12.2 0.0 copy-done.2
  12.2 0.0 copy-done.3
  12.2 0.0 copy-done.4
  12.3 0.0 copy-done.5
  12.3 0.0 copy-done.6
  12.3 0.0 copy-done.7
  12.3 0.9 %shard_map.92 = (bf16[128,384]{1,0:T(8,128)(2,1)S(1)}, bf16[128,512]{1,0:T(8,128)(2,1)S(1)}) custom-call(bf16[128,128]{1,0:T(8,128)(2,1)S(1)} %copy-done.3, bf16[128,128]{1,0:T(8,128)(2,1)S(1)} %copy-done.4, bf16[128,128]{1,0:T(8,128)(2,1)S(1)} %copy-done.5, bf16[128,128]{1,0:T(8,128)(2,1)S(1)} %copy-done.6, bf16[128,128]{1,0:T(8,128)(2,1)S(1)} %copy-done.7, ...), custom_call_target="tpu_custom_call" | custom-call | flops 335544320 | bytes 1310720 | tf_op jit(solution)/shard_map/pallas_call | solution.py:338
  13.2 1.6 %collective-permute-start.7 = (bf16[128,512]{1,0:T(8,128)(2,1)S(1)}, bf16[128,512]{1,0:T(8,128)(2,1)S(1)}, u32[]{:S(2)}, u32[]{:S(2)}) collective-permute-start(bf16[128,512]{1,0:T(8,128)(2,1)S(1)} %get-tuple-element.31), channel_id=1, source_target_pairs={{0,1},{1,0},{2,3},{3,2},{4,5},{5,4},{6,7},{7,6},{8,9},{9,8},{10,11... | collective-permute-start | bytes 393224 | tf_op jit(solution)/shard_map/ppermute | solution.py:295
  14.9 0.4 %shard_map.93 = (f32[128,512]{1,0:T(8,128)S(1)}, f32[128,512]{1,0:T(8,128)S(1)}) custom-call(bf16[128,384]{1,0:T(8,128)(2,1)S(1)} %get-tuple-element.28.grads, bf16[4096,128]{1,0:T(8,128)(2,1)S(1)} %copy-done, bf16[4096,128]{1,0:T(8,128)(2,1)S(1)} %copy-done.1, bf16[4096,128]{1,0:T(8,128)(2,1)S(1)} %copy-done.2), custom_call_target="tpu_custom_call" | custom-call | flops 100663296 | bytes 786432 | tf_op jit(solution)/shard_map/pallas_call | solution.py:353
  15.3 0.8 %shard_map.94 = (bf16[128,512]{1,0:T(8,128)(2,1)S(1)}, bf16[128,1024]{1,0:T(8,128)(2,1)S(1)}, f32[128,1024]{1,0:T(8,128)S(1)}) custom-call(bf16[128,384]{1,0:T(8,128)(2,1)S(1)} %get-tuple-element.28.grads, bf16[4096,128]{1,0:T(8,128)(2,1)S(1)} %copy-done, bf16[4096,128]{1,0:T(8,128)(2,1)S(1)} %copy-done.1, bf16[4096,128]{1,0:T(8,128)(2,1)S(1)} %copy-done.2), custom_call_target="tpu_custom_call" | custom-call | flops 251658240 | bytes 1966080 | tf_op jit(solution)/shard_map/pallas_call | solution.py:353
  16.0 0.5 %collective-permute-start.10 = (bf16[128,512]{1,0:T(8,128)(2,1)S(1)}, bf16[128,512]{1,0:T(8,128)(2,1)S(1)}, u32[]{:S(2)}, u32[]{:S(2)}) collective-permute-start(bf16[128,512]{1,0:T(8,128)(2,1)S(1)} %get-tuple-element.36), channel_id=1, source_target_pairs={{0,1},{1,0},{2,3},{3,2},{4,5},{5,4},{6,7},{7,6},{8,9},{9,8},{10,11... | collective-permute-start | bytes 393224 | tf_op jit(solution)/shard_map/ppermute | solution.py:295
  16.5 2.5 %collective-permute-done.7 = bf16[128,512]{1,0:T(8,128)(2,1)S(1)} collective-permute-done((bf16[128,512]{1,0:T(8,128)(2,1)S(1)}, bf16[128,512]{1,0:T(8,128)(2,1)S(1)}, u32[]{:S(2)}, u32[]{:S(2)}) %collective-permute-start.7) | collective-permute-done | bytes 131104 | tf_op jit(solution)/shard_map/ppermute | solution.py:295
  19.1 2.7 %collective-permute-start.9 = (bf16[128,512]{1,0:T(8,128)(2,1)S(1)}, bf16[128,512]{1,0:T(8,128)(2,1)S(1)}, u32[]{:S(2)}, u32[]{:S(2)}) collective-permute-start(bf16[128,512]{1,0:T(8,128)(2,1)S(1)} %add_convert_fusion.2), channel_id=1, source_target_pairs={{0,2},{1,3},{2,0},{3,1},{4,6},{5,7},{6,4},{7,5},{8,10},{9,11},{10,... | collective-permute-start | bytes 393224 | tf_op jit(solution)/shard_map/ppermute | solution.py:295
  21.8 2.1 %collective-permute-start.8 = (bf16[128,1024]{1,0:T(8,128)(2,1)S(1)}, bf16[128,1024]{1,0:T(8,128)(2,1)S(1)}, u32[]{:S(2)}, u32[]{:S(2)}) collective-permute-start(bf16[128,1024]{1,0:T(8,128)(2,1)S(1)} %get-tuple-element.32), channel_id=1, source_target_pairs={{0,1},{1,0},{2,3},{3,2},{4,5},{5,4},{6,7},{7,6},{8,9},{9,8},{10,11... | collective-permute-start | bytes 786440 | tf_op jit(solution)/shard_map/ppermute | solution.py:295
  23.9 0.0 collective-permute-done.10
  23.9 1.2 %collective-permute-start.11 = (bf16[128,512]{1,0:T(8,128)(2,1)S(1)}, bf16[128,512]{1,0:T(8,128)(2,1)S(1)}, u32[]{:S(2)}, u32[]{:S(2)}) collective-permute-start(bf16[128,512]{1,0:T(8,128)(2,1)S(1)} %add_convert_fusion.1), channel_id=1, source_target_pairs={{0,2},{1,3},{2,0},{3,1},{4,6},{5,7},{6,4},{7,5},{8,10},{9,11},{10,... | collective-permute-start | bytes 393224 | tf_op jit(solution)/shard_map/ppermute | solution.py:295
  25.2 2.9 %collective-permute-done.9 = bf16[128,512]{1,0:T(8,128)(2,1)S(1)} collective-permute-done((bf16[128,512]{1,0:T(8,128)(2,1)S(1)}, bf16[128,512]{1,0:T(8,128)(2,1)S(1)}, u32[]{:S(2)}, u32[]{:S(2)}) %collective-permute-start.9) | collective-permute-done | bytes 131104 | tf_op jit(solution)/shard_map/ppermute | solution.py:295
  28.1 4.1 %collective-permute-done.11 = bf16[128,512]{1,0:T(8,128)(2,1)S(1)} collective-permute-done((bf16[128,512]{1,0:T(8,128)(2,1)S(1)}, bf16[128,512]{1,0:T(8,128)(2,1)S(1)}, u32[]{:S(2)}, u32[]{:S(2)}) %collective-permute-start.11) | collective-permute-done | bytes 131104 | tf_op jit(solution)/shard_map/ppermute | solution.py:295
  32.2 0.9 %collective-permute-done.8 = bf16[128,1024]{1,0:T(8,128)(2,1)S(1)} collective-permute-done((bf16[128,1024]{1,0:T(8,128)(2,1)S(1)}, bf16[128,1024]{1,0:T(8,128)(2,1)S(1)}, u32[]{:S(2)}, u32[]{:S(2)}) %collective-permute-start.8) | collective-permute-done | bytes 262176 | tf_op jit(solution)/shard_map/ppermute | solution.py:295
  33.1 0.8 %add_convert_fusion = bf16[128,1024]{1,0:T(8,128)(2,1)} fusion(f32[128,1024]{1,0:T(8,128)S(1)} %get-tuple-element.29, bf16[128,1024]{1,0:T(8,128)(2,1)S(1)} %collective-permute-done.8, bf16[128,512]{1,0:T(8,128)(2,1)S(1)} %collective-permute-done.11, bf16[128,512]{1,0:T(8,128)(2,1)S(1)} %collective-permute-done.9), kind=kLoop, calls=%fused_computation | loop fusion | flops 1048576 | bytes 1310720 | tf_op jit(solution)/shard_map/convert_element_type | solution.py:373
  (3 shorter events, 0.1 us)
Async XLA Ops:
  0.0 12.2 %copy-start = (bf16[4096,128]{1,0:T(8,128)(2,1)S(1)}, bf16[4096,128]{1,0:T(8,128)(2,1)}, u32[]{:S(2)}) copy-start(bf16[4096,128]{1,0:T(8,128)(2,1)} %wq_ref.5) | copy-start | bytes 3145732
  0.0 12.2 %copy-start.1 = (bf16[4096,128]{1,0:T(8,128)(2,1)S(1)}, bf16[4096,128]{1,0:T(8,128)(2,1)}, u32[]{:S(2)}) copy-start(bf16[4096,128]{1,0:T(8,128)(2,1)} %wk_ref.5) | copy-start | bytes 3145732
  0.0 12.2 %copy-start.2 = (bf16[4096,128]{1,0:T(8,128)(2,1)S(1)}, bf16[4096,128]{1,0:T(8,128)(2,1)}, u32[]{:S(2)}) copy-start(bf16[4096,128]{1,0:T(8,128)(2,1)} %wv_ref.5) | copy-start | bytes 3145732
  0.0 12.2 %copy-start.3 = (bf16[128,128]{1,0:T(8,128)(2,1)S(1)}, bf16[128,128]{1,0:T(8,128)(2,1)}, u32[]{:S(2)}) copy-start(bf16[128,128]{1,0:T(8,128)(2,1)} %q_ref.1) | copy-start | bytes 98308
  0.0 12.2 %copy-start.4 = (bf16[128,128]{1,0:T(8,128)(2,1)S(1)}, bf16[128,128]{1,0:T(8,128)(2,1)}, u32[]{:S(2)}) copy-start(bf16[128,128]{1,0:T(8,128)(2,1)} %k_ref.1) | copy-start | bytes 98308
  0.0 12.2 %copy-start.5 = (bf16[128,128]{1,0:T(8,128)(2,1)S(1)}, bf16[128,128]{1,0:T(8,128)(2,1)}, u32[]{:S(2)}) copy-start(bf16[128,128]{1,0:T(8,128)(2,1)} %v_ref.1) | copy-start | bytes 98308
  0.0 12.2 %copy-start.6 = (bf16[128,128]{1,0:T(8,128)(2,1)S(1)}, bf16[128,128]{1,0:T(8,128)(2,1)}, u32[]{:S(2)}) copy-start(bf16[128,128]{1,0:T(8,128)(2,1)} %g_ref.1) | copy-start | bytes 98308
  0.0 12.2 %copy-start.7 = (bf16[128,128]{1,0:T(8,128)(2,1)S(1)}, bf16[128,128]{1,0:T(8,128)(2,1)}, u32[]{:S(2)}) copy-start(bf16[128,128]{1,0:T(8,128)(2,1)} %a_ref.1) | copy-start | bytes 98308
  1.9 6.8 %collective-permute-start = (bf16[144,256]{1,0:T(8,128)(2,1)}, bf16[144,256]{1,0:T(8,128)(2,1)S(1)}, u32[]{:S(2)}, u32[]{:S(2)}) collective-permute-start(bf16[144,256]{1,0:T(8,128)(2,1)} %get-tuple-element.21), channel_id=1, source_target_pairs={{0,24},{4,28},{8,16},{12,20},{16,8},{20,12},{24,0},{28,4},{1,25},{... | collective-permute-start | bytes 221192 | tf_op jit(solution)/shard_map/ppermute | solution.py:295
  5.8 5.2 %copy-start.8 = (f32[128,1]{0,1:T(1,128)S(1)}, f32[128,1]{0,1:T(1,128)}, u32[]{:S(2)}) copy-start(f32[128,1]{0,1:T(1,128)} %param.14) | copy-start | bytes 1540
  5.8 4.7 %collective-permute-start.2 = (bf16[144,256]{1,0:T(8,128)(2,1)}, bf16[144,256]{1,0:T(8,128)(2,1)S(1)}, u32[]{:S(2)}, u32[]{:S(2)}) collective-permute-start(bf16[144,256]{1,0:T(8,128)(2,1)} %get-tuple-element.24), channel_id=1, source_target_pairs={{0,8},{4,12},{8,0},{12,4},{16,24},{20,28},{24,16},{28,20},{1,9},{5... | collective-permute-start | bytes 221192 | tf_op jit(solution)/shard_map/ppermute | solution.py:295
  6.4 4.6 %collective-permute-start.4 = (bf16[144,256]{1,0:T(8,128)(2,1)}, bf16[144,256]{1,0:T(8,128)(2,1)S(1)}, u32[]{:S(2)}, u32[]{:S(2)}) collective-permute-start(bf16[144,256]{1,0:T(8,128)(2,1)} %get-tuple-element.21), channel_id=1, source_target_pairs={{0,16},{4,20},{8,24},{12,28},{16,0},{20,4},{24,8},{28,12},{1,17},{... | collective-permute-start | bytes 221192 | tf_op jit(solution)/shard_map/ppermute | solution.py:295
  6.5 4.5 %collective-permute-start.1 = (bf16[144,256]{1,0:T(8,128)(2,1)}, bf16[144,256]{1,0:T(8,128)(2,1)S(1)}, u32[]{:S(2)}, u32[]{:S(2)}) collective-permute-start(bf16[144,256]{1,0:T(8,128)(2,1)} %get-tuple-element.23), channel_id=1, source_target_pairs={{0,4},{4,0},{8,12},{12,8},{16,20},{20,16},{24,28},{28,24},{1,5},{5... | collective-permute-start | bytes 221192 | tf_op jit(solution)/shard_map/ppermute | solution.py:295
  8.7 3.5 %collective-permute-start.6 = (bf16[144,256]{1,0:T(8,128)(2,1)S(1)}, bf16[144,256]{1,0:T(8,128)(2,1)S(1)}, u32[]{:S(2)}, u32[]{:S(2)}) collective-permute-start(bf16[144,256]{1,0:T(8,128)(2,1)S(1)} %collective-permute-done.refs_5_), channel_id=1, source_target_pairs={{0,4},{4,0},{8,12},{12,8},{16,20},{20,16},{24,28},{28,24},{1,5},{5... | collective-permute-start | bytes 221192 | tf_op jit(solution)/shard_map/ppermute | solution.py:295
  10.5 1.3 %collective-permute-start.3 = (bf16[144,256]{1,0:T(8,128)(2,1)S(1)}, bf16[144,256]{1,0:T(8,128)(2,1)S(1)}, u32[]{:S(2)}, u32[]{:S(2)}) collective-permute-start(bf16[144,256]{1,0:T(8,128)(2,1)S(1)} %collective-permute-done.2.refs_1_), channel_id=1, source_target_pairs={{0,4},{4,0},{8,12},{12,8},{16,20},{20,16},{24,28},{28,24},{1,5},{5... | collective-permute-start | bytes 221192 | tf_op jit(solution)/shard_map/ppermute | solution.py:295
  10.9 1.3 %collective-permute-start.5 = (bf16[144,256]{1,0:T(8,128)(2,1)S(1)}, bf16[144,256]{1,0:T(8,128)(2,1)S(1)}, u32[]{:S(2)}, u32[]{:S(2)}) collective-permute-start(bf16[144,256]{1,0:T(8,128)(2,1)S(1)} %collective-permute-done.4.refs_3_), channel_id=1, source_target_pairs={{0,4},{4,0},{8,12},{12,8},{16,20},{20,16},{24,28},{28,24},{1,5},{5... | collective-permute-start | bytes 221192 | tf_op jit(solution)/shard_map/ppermute | solution.py:295
  13.2 5.8 %collective-permute-start.7 = (bf16[128,512]{1,0:T(8,128)(2,1)S(1)}, bf16[128,512]{1,0:T(8,128)(2,1)S(1)}, u32[]{:S(2)}, u32[]{:S(2)}) collective-permute-start(bf16[128,512]{1,0:T(8,128)(2,1)S(1)} %get-tuple-element.31), channel_id=1, source_target_pairs={{0,1},{1,0},{2,3},{3,2},{4,5},{5,4},{6,7},{7,6},{8,9},{9,8},{10,11... | collective-permute-start | bytes 393224 | tf_op jit(solution)/shard_map/ppermute | solution.py:295
  16.0 7.9 %collective-permute-start.10 = (bf16[128,512]{1,0:T(8,128)(2,1)S(1)}, bf16[128,512]{1,0:T(8,128)(2,1)S(1)}, u32[]{:S(2)}, u32[]{:S(2)}) collective-permute-start(bf16[128,512]{1,0:T(8,128)(2,1)S(1)} %get-tuple-element.36), channel_id=1, source_target_pairs={{0,1},{1,0},{2,3},{3,2},{4,5},{5,4},{6,7},{7,6},{8,9},{9,8},{10,11... | collective-permute-start | bytes 393224 | tf_op jit(solution)/shard_map/ppermute | solution.py:295
  19.1 9.0 %collective-permute-start.9 = (bf16[128,512]{1,0:T(8,128)(2,1)S(1)}, bf16[128,512]{1,0:T(8,128)(2,1)S(1)}, u32[]{:S(2)}, u32[]{:S(2)}) collective-permute-start(bf16[128,512]{1,0:T(8,128)(2,1)S(1)} %add_convert_fusion.2), channel_id=1, source_target_pairs={{0,2},{1,3},{2,0},{3,1},{4,6},{5,7},{6,4},{7,5},{8,10},{9,11},{10,... | collective-permute-start | bytes 393224 | tf_op jit(solution)/shard_map/ppermute | solution.py:295
  21.8 11.4 %collective-permute-start.8 = (bf16[128,1024]{1,0:T(8,128)(2,1)S(1)}, bf16[128,1024]{1,0:T(8,128)(2,1)S(1)}, u32[]{:S(2)}, u32[]{:S(2)}) collective-permute-start(bf16[128,1024]{1,0:T(8,128)(2,1)S(1)} %get-tuple-element.32), channel_id=1, source_target_pairs={{0,1},{1,0},{2,3},{3,2},{4,5},{5,4},{6,7},{7,6},{8,9},{9,8},{10,11... | collective-permute-start | bytes 786440 | tf_op jit(solution)/shard_map/ppermute | solution.py:295
  23.9 8.3 %collective-permute-start.11 = (bf16[128,512]{1,0:T(8,128)(2,1)S(1)}, bf16[128,512]{1,0:T(8,128)(2,1)S(1)}, u32[]{:S(2)}, u32[]{:S(2)}) collective-permute-start(bf16[128,512]{1,0:T(8,128)(2,1)S(1)} %add_convert_fusion.1), channel_id=1, source_target_pairs={{0,2},{1,3},{2,0},{3,1},{4,6},{5,7},{6,4},{7,5},{8,10},{9,11},{10,... | collective-permute-start | bytes 393224 | tf_op jit(solution)/shard_map/ppermute | solution.py:295

commit v16 on v15

--- a/solution.py
+++ b/solution.py
@@ -232,30 +232,20 @@
         out_ref[:, at : at + cols] = dot_nt(grads[...], weight).astype(out_ref.dtype)
 
 
-def near_kernel(scale, part, q_ref, k_ref, v_ref, g_ref, a_ref, n_ref, wq_ref, wk_ref, wv_ref, *refs):
-    grads, front = refs[-2:]
-    got = refs[:-2]
-    rows, width = q_ref.shape
+def pair_sums(scale, offsets, got, query, key, value, grad, norm, delta):
+    rows, width = query.shape
     me = lax.axis_index("ctx")
     exponent = scale * math.log2(math.e)
-    query, key, value, grad = q_ref[...], k_ref[...], v_ref[...], g_ref[...]
-    norm = jnp.sum(jnp.where(diagonal(rows), n_ref[...], 0.0), axis=1, keepdims=True)
-    delta = delta_of(grad, a_ref[...])
-    row_at = lax.broadcasted_iota(jnp.int32, (rows, rows), 0)
-    col_at = lax.broadcasted_iota(jnp.int32, (rows, rows), 1)
-    probs = jnp.where(col_at <= row_at, jnp.exp2(exponent * (dot_nt(query, key) - norm)), 0.0)
-    score_low = (probs * (dot_nt(grad, value) - delta)).astype(jnp.bfloat16)
-    query_sum = dot_nn(score_low, key)
-    key_sum = dot_tn(score_low, query)
-    value_sum = dot_tn(probs.astype(jnp.bfloat16), grad)
-
     first = jnp.concatenate([ref[:rows, :width] for ref in got], axis=0)
     second = jnp.concatenate([ref[:rows, width:] for ref in got], axis=0)
     extra = jnp.concatenate([ref[rows:, :width] for ref in got], axis=1).astype(jnp.float32)
     norms = (1.0 / scale) * jnp.sum(extra[:PIECES], axis=0, keepdims=True)
     deltas = jnp.sum(extra[PIECES : 2 * PIECES], axis=0, keepdims=True)
     lanes = lax.broadcasted_iota(jnp.int32, (rows, len(got) * rows), 1)
-    earlier = ((lanes // rows + 1) ^ me) < me
+    offset = jnp.zeros_like(lanes)
+    for at, value_at in enumerate(offsets):
+        offset = jnp.where(lanes // rows == at, value_at, offset)
+    earlier = (offset ^ me) < me
     scores = dot_nt(jnp.concatenate([query, key], axis=0), first)
     scores = jnp.where(earlier, scores[:rows] - norm, scores[rows:] - norms)
     probs = jnp.exp2(exponent * scores)
@@ -266,12 +256,44 @@
         [jnp.where(earlier, score_grad, 0.0), jnp.where(earlier, 0.0, score_grad)], axis=0
     ).astype(jnp.bfloat16)
     both_sum = dot_nn(sides, first)
-    value_sum += dot_nn(jnp.where(earlier, 0.0, probs).astype(jnp.bfloat16), second)
-    grads[:, :width] = (scale * (query_sum + both_sum[:rows])).astype(jnp.bfloat16)
-    grads[:, width : 2 * width] = (scale * (key_sum + both_sum[rows:])).astype(jnp.bfloat16)
-    grads[:, 2 * width :] = value_sum.astype(jnp.bfloat16)
-    start = (lax.axis_index("head") ^ 3) * part
-    project(grads, (wq_ref, wk_ref, wv_ref), start, front)
+    value_sum = dot_nn(jnp.where(earlier, 0.0, probs).astype(jnp.bfloat16), second)
+    return both_sum[:rows], both_sum[rows:], value_sum
+
+
+def own_columns(q_ref, k_ref, v_ref, g_ref, a_ref, n_ref):
+    grad = g_ref[...]
+    norm = jnp.sum(jnp.where(diagonal(q_ref.shape[0]), n_ref[...], 0.0), axis=1, keepdims=True)
+    return q_ref[...], k_ref[...], v_ref[...], grad, norm, delta_of(grad, a_ref[...])
+
+
+def first_kernel(scale, offsets, *refs):
+    out_ref = refs[-1]
+    own = own_columns(*refs[:6])
+    query, key, value, grad, norm, delta = own
+    rows, width = query.shape
+    exponent = scale * math.log2(math.e)
+    row_at = lax.broadcasted_iota(jnp.int32, (rows, rows), 0)
+    col_at = lax.broadcasted_iota(jnp.int32, (rows, rows), 1)
+    probs = jnp.where(col_at <= row_at, jnp.exp2(exponent * (dot_nt(query, key) - norm)), 0.0)
+    score_low = (probs * (dot_nt(grad, value) - delta)).astype(jnp.bfloat16)
+    sums = pair_sums(scale, offsets, refs[6:-1], *own)
+    out_ref[:, :width] = sums[0] + dot_nn(score_low, key)
+    out_ref[:, width : 2 * width] = sums[1] + dot_tn(score_low, query)
+    out_ref[:, 2 * width :] = sums[2] + dot_tn(probs.astype(jnp.bfloat16), grad)
+
+
+def near_kernel(scale, part, offsets, *refs):
+    grads, front = refs[-2:]
+    w_refs, sum_ref, got = refs[6:9], refs[9], refs[10:-2]
+    own = own_columns(*refs[:6])
+    width = own[0].shape[1]
+    sums = pair_sums(scale, offsets, got, *own)
+    grads[:, :width] = (scale * (sum_ref[:, :width] + sums[0])).astype(jnp.bfloat16)
+    grads[:, width : 2 * width] = (
+        scale * (sum_ref[:, width : 2 * width] + sums[1])
+    ).astype(jnp.bfloat16)
+    grads[:, 2 * width :] = (sum_ref[:, 2 * width :] + sums[2]).astype(jnp.bfloat16)
+    project(grads, w_refs, (lax.axis_index("head") ^ 3) * part, front)
 
 
 def far_kernel(part, grads, wq_ref, wk_ref, wv_ref, front, back):
@@ -330,15 +352,28 @@
     own = own[:-1] + (norm * (1.0 / scale),)
     for at in range(2, ctx, 2):
         got[at + 1] = swap(got[at], "ctx", 1)
-    got = [got[at] for at in range(1, ctx)]
+    soon = tuple(at for at in got if at == 1 or at % 2 == 0)
+    late = tuple(at for at in got if at not in soon)
     half_low = jax.ShapeDtypeStruct((rows, part // 2), jnp.bfloat16)
     half = jax.ShapeDtypeStruct((rows, part // 2), jnp.float32)
     low = jax.ShapeDtypeStruct((rows, part), jnp.bfloat16)
     full = jax.ShapeDtypeStruct((rows, part), jnp.float32)
+    sums = pl.pallas_call(
+        functools.partial(first_kernel, scale, soon),
+        out_shape=jax.ShapeDtypeStruct((rows, 3 * width), jnp.float32),
+        in_specs=[vmem] * (6 + len(soon)),
+        out_specs=vmem,
+        compiler_params=params,
+        cost_estimate=pl.CostEstimate(
+            flops=14 * rows * rows * len(soon) * width,
+            bytes_accessed=4 * rows * len(soon) * width,
+            transcendentals=rows * rows * len(soon),
+        ),
+    )(*own, *[got[at] for at in soon])
     grads, front = pl.pallas_call(
-        functools.partial(near_kernel, scale, part),
+        functools.partial(near_kernel, scale, part, late),
         out_shape=[jax.ShapeDtypeStruct((rows, 3 * width), jnp.bfloat16), half_low],
-        in_specs=[vmem] * (ctx + 8),
+        in_specs=[vmem] * (10 + len(late)),
         out_specs=[vmem] * 2,
         compiler_params=params,
         cost_estimate=pl.CostEstimate(
@@ -346,7 +381,7 @@
             bytes_accessed=4 * rows * ctx * width + 6 * part * width,
             transcendentals=rows * rows * ctx,
         ),
-    )(*own, *weights, *got)
+    )(*own, *weights, sums, *[got[at] for at in late])
     front = swap(front, "head", 1)
     def projected(kernel, outs, operands):
         count = sum(out.shape[1] for out in outs)

time: 34.1 us -> 33.7 us (0.988)
  waiting for transfers between devices: 16.1 us -> 15.5 us
    ppermute x12, waiting for transfers between devices: 16.1 us -> 15.5 us  [swap(): return lax.ppermute(value, axis, [(at, at ^ offset) for at in range(size)])]
    pallas_call x1 -> x2, Pallas kernels: 0.94 us -> 1.23 us  [the longest x1 0.64 us: near_body(): pl.pallas_call(functools.partial(near_kernel, scale, part, late), out_sha...]
  transfers between devices with their start and end apart: 12 -> 12, of which waited for: 9 -> 9; matrix products, arithmetic and copies ran while one was open for 0% -> 0% of each run, Pallas kernels for 3% -> 5%
where the time goes in v16:
time: 33.7 us; the launch traced here: 33.6 us
  waiting for transfers between devices  15.5 us (46%)
  starting transfers between devices  12.9 us (38%)
  Pallas kernels  4.2 us (12%)
  other arithmetic  0.85 us (3%)
    ppermute x12, waiting for transfers between devices, swap(): return lax.ppermute(value, axis, [(at, at ^ offset) for at in range(size)])  15.5 us
    ppermute x12, starting transfers between devices, swap(): return lax.ppermute(value, axis, [(at, at ^ offset) for at in range(size)])  12.9 us
    pallas_call x1, Pallas kernels, near_body(): pl.pallas_call(send_kernel, out_shape=[hop] * bits, in_specs=[hbm] * 6, o...  1.82 us
    pallas_call x2, Pallas kernels, projected(): pl.pallas_call(functools.partial(kernel, part), out_shape=outs, in_specs=...  1.15 us
    convert_element_type x1, other arithmetic, near_body(): return (total + near.astype(jnp.float32) + far_sum).astype(jnp.bfloat16)  0.8 us
  transfers between devices with their start and end apart: 12, of which 9 were waited for; matrix products, arithmetic and copies ran while one was open for 0% of the time, Pallas kernels for 5%

profile of v16, /device:TPU:0, one launch (start us, length us, event | category | flops | bytes accessed | tf_op | source)
XLA Modules:
  0.0 33.6 jit_solution(11256983637149024422)
XLA Ops:
  0.0 0.0 copy-start.3
  0.0 0.0 copy-start.4
  0.0 0.0 copy-start.5
  0.0 0.0 copy-start.6
  0.0 0.0 copy-start.7
  0.0 0.0 copy-start
  0.0 0.0 copy-start.1
  0.0 0.0 copy-start.2
  0.0 1.8 %shard_map.91 = (bf16[144,256]{1,0:T(8,128)(2,1)}, bf16[144,256]{1,0:T(8,128)(2,1)}, bf16[144,256]{1,0:T(8,128)(2,1)}) custom-call(bf16[128,128]{1,0:T(8,128)(2,1)} %refs_0_.3, bf16[128,128]{1,0:T(8,128)(2,1)} %refs_1_.3, bf16[128,128]{1,0:T(8,128)(2,1)} %refs_2_.3, bf16[128,128]{1,0:T(8,128)(2,1)} %refs_3_.3, bf16[128,128]{1,0:T(8,128)(2,1)} %refs_4_.3, ...), custom_call_target="tpu_custom_call" | custom-call | flops 5000000000 | bytes 327680 | tf_op jit(solution)/shard_map/pallas_call | solution.py:330
  1.9 4.0 %collective-permute-start = (bf16[144,256]{1,0:T(8,128)(2,1)}, bf16[144,256]{1,0:T(8,128)(2,1)S(1)}, u32[]{:S(2)}, u32[]{:S(2)}) collective-permute-start(bf16[144,256]{1,0:T(8,128)(2,1)} %get-tuple-element.21), channel_id=1, source_target_pairs={{0,24},{4,28},{8,16},{12,20},{16,8},{20,12},{24,0},{28,4},{1,25},{... | collective-permute-start | bytes 221192 | tf_op jit(solution)/shard_map/ppermute | solution.py:317
  5.8 0.0 copy-start.8
  5.8 0.5 %collective-permute-start.2 = (bf16[144,256]{1,0:T(8,128)(2,1)}, bf16[144,256]{1,0:T(8,128)(2,1)S(1)}, u32[]{:S(2)}, u32[]{:S(2)}) collective-permute-start(bf16[144,256]{1,0:T(8,128)(2,1)} %get-tuple-element.24), channel_id=1, source_target_pairs={{0,8},{4,12},{8,0},{12,4},{16,24},{20,28},{24,16},{28,20},{1,9},{5... | collective-permute-start | bytes 221192 | tf_op jit(solution)/shard_map/ppermute | solution.py:317
  6.4 0.1 collective-permute-start.3
  6.5 0.0 collective-permute-start.1
  6.5 2.2 %collective-permute-done.refs_9_ = bf16[144,256]{1,0:T(8,128)(2,1)S(1)} collective-permute-done((bf16[144,256]{1,0:T(8,128)(2,1)}, bf16[144,256]{1,0:T(8,128)(2,1)S(1)}, u32[]{:S(2)}, u32[]{:S(2)}) %collective-permute-start) | collective-permute-done | bytes 73760 | tf_op jit(solution)/shard_map/ppermute | solution.py:317
  8.7 0.0 collective-permute-start.6
  8.7 1.8 %collective-permute-done.2.refs_7_ = bf16[144,256]{1,0:T(8,128)(2,1)S(1)} collective-permute-done((bf16[144,256]{1,0:T(8,128)(2,1)}, bf16[144,256]{1,0:T(8,128)(2,1)S(1)}, u32[]{:S(2)}, u32[]{:S(2)}) %collective-permute-start.2) | collective-permute-done | bytes 73760 | tf_op jit(solution)/shard_map/ppermute | solution.py:317
  10.5 0.0 collective-permute-start.4
  10.5 0.4 %collective-permute-done.3.refs_8_ = bf16[144,256]{1,0:T(8,128)(2,1)S(1)} collective-permute-done((bf16[144,256]{1,0:T(8,128)(2,1)}, bf16[144,256]{1,0:T(8,128)(2,1)S(1)}, u32[]{:S(2)}, u32[]{:S(2)}) %collective-permute-start.3) | collective-permute-done | bytes 73760 | tf_op jit(solution)/shard_map/ppermute | solution.py:317
  10.9 0.1 collective-permute-start.5
  11.0 0.0 copy-done.8
  11.0 0.0 collective-permute-done.1.refs_6_
  11.0 0.0 copy-done.3
  11.0 0.0 copy-done.4
  11.0 0.0 copy-done.5
  11.1 0.0 copy-done.6
  11.1 0.0 copy-done.7
  11.1 0.6 %shard_map.92.refs_9_ = f32[128,384]{1,0:T(8,128)S(1)} custom-call(bf16[128,128]{1,0:T(8,128)(2,1)S(1)} %copy-done.3, bf16[128,128]{1,0:T(8,128)(2,1)S(1)} %copy-done.4, bf16[128,128]{1,0:T(8,128)(2,1)S(1)} %copy-done.5, bf16[128,128]{1,0:T(8,128)(2,1)S(1)} %copy-done.6, bf16[128,128]{1,0:T(8,128)(2,1)S(1)} %copy-done.7, ...), custom_call_target="tpu_custom_call" | custom-call | flops 117440512 | bytes 262144 | tf_op jit(solution)/shard_map/pallas_call | solution.py:361
  11.7 0.1 collective-permute-done.4.refs_10_
  11.8 0.4 %collective-permute-done.5.refs_11_ = bf16[144,256]{1,0:T(8,128)(2,1)S(1)} collective-permute-done((bf16[144,256]{1,0:T(8,128)(2,1)S(1)}, bf16[144,256]{1,0:T(8,128)(2,1)S(1)}, u32[]{:S(2)}, u32[]{:S(2)}) %collective-permute-start.5) | collective-permute-done | bytes 73760 | tf_op jit(solution)/shard_map/ppermute | solution.py:317
  12.2 0.0 collective-permute-done.6.refs_12_
  12.2 0.0 copy-done
  12.2 0.0 copy-done.1
  12.2 0.0 copy-done.2
  12.2 0.6 %shard_map.93 = (bf16[128,384]{1,0:T(8,128)(2,1)S(1)}, bf16[128,512]{1,0:T(8,128)(2,1)S(1)}) custom-call(bf16[128,128]{1,0:T(8,128)(2,1)S(1)} %copy-done.3, bf16[128,128]{1,0:T(8,128)(2,1)S(1)} %copy-done.4, bf16[128,128]{1,0:T(8,128)(2,1)S(1)} %copy-done.5, bf16[128,128]{1,0:T(8,128)(2,1)S(1)} %copy-done.6, bf16[128,128]{1,0:T(8,128)(2,1)S(1)} %copy-done.7, ...), custom_call_target="tpu_custom_call" | custom-call | flops 335544320 | bytes 1310720 | tf_op jit(solution)/shard_map/pallas_call | solution.py:373
  12.9 1.6 %collective-permute-start.7 = (bf16[128,512]{1,0:T(8,128)(2,1)S(1)}, bf16[128,512]{1,0:T(8,128)(2,1)S(1)}, u32[]{:S(2)}, u32[]{:S(2)}) collective-permute-start(bf16[128,512]{1,0:T(8,128)(2,1)S(1)} %get-tuple-element.31), channel_id=1, source_target_pairs={{0,1},{1,0},{2,3},{3,2},{4,5},{5,4},{6,7},{7,6},{8,9},{9,8},{10,11... | collective-permute-start | bytes 393224 | tf_op jit(solution)/shard_map/ppermute | solution.py:317
  14.5 0.4 %shard_map.94 = (f32[128,512]{1,0:T(8,128)S(1)}, f32[128,512]{1,0:T(8,128)S(1)}) custom-call(bf16[128,384]{1,0:T(8,128)(2,1)S(1)} %get-tuple-element.28.grads, bf16[4096,128]{1,0:T(8,128)(2,1)S(1)} %copy-done, bf16[4096,128]{1,0:T(8,128)(2,1)S(1)} %copy-done.1, bf16[4096,128]{1,0:T(8,128)(2,1)S(1)} %copy-done.2), custom_call_target="tpu_custom_call" | custom-call | flops 100663296 | bytes 786432 | tf_op jit(solution)/shard_map/pallas_call | solution.py:388
  14.9 0.8 %shard_map.95 = (bf16[128,512]{1,0:T(8,128)(2,1)S(1)}, bf16[128,1024]{1,0:T(8,128)(2,1)S(1)}, f32[128,1024]{1,0:T(8,128)S(1)}) custom-call(bf16[128,384]{1,0:T(8,128)(2,1)S(1)} %get-tuple-element.28.grads, bf16[4096,128]{1,0:T(8,128)(2,1)S(1)} %copy-done, bf16[4096,128]{1,0:T(8,128)(2,1)S(1)} %copy-done.1, bf16[4096,128]{1,0:T(8,128)(2,1)S(1)} %copy-done.2), custom_call_target="tpu_custom_call" | custom-call | flops 251658240 | bytes 1966080 | tf_op jit(solution)/shard_map/pallas_call | solution.py:388
  15.7 0.5 %collective-permute-start.10 = (bf16[128,512]{1,0:T(8,128)(2,1)S(1)}, bf16[128,512]{1,0:T(8,128)(2,1)S(1)}, u32[]{:S(2)}, u32[]{:S(2)}) collective-permute-start(bf16[128,512]{1,0:T(8,128)(2,1)S(1)} %get-tuple-element.36), channel_id=1, source_target_pairs={{0,1},{1,0},{2,3},{3,2},{4,5},{5,4},{6,7},{7,6},{8,9},{9,8},{10,11... | collective-permute-start | bytes 393224 | tf_op jit(solution)/shard_map/ppermute | solution.py:317
  16.2 2.5 %collective-permute-done.7 = bf16[128,512]{1,0:T(8,128)(2,1)S(1)} collective-permute-done((bf16[128,512]{1,0:T(8,128)(2,1)S(1)}, bf16[128,512]{1,0:T(8,128)(2,1)S(1)}, u32[]{:S(2)}, u32[]{:S(2)}) %collective-permute-start.7) | collective-permute-done | bytes 131104 | tf_op jit(solution)/shard_map/ppermute | solution.py:317
  18.8 2.7 %collective-permute-start.9 = (bf16[128,512]{1,0:T(8,128)(2,1)S(1)}, bf16[128,512]{1,0:T(8,128)(2,1)S(1)}, u32[]{:S(2)}, u32[]{:S(2)}) collective-permute-start(bf16[128,512]{1,0:T(8,128)(2,1)S(1)} %add_convert_fusion.2), channel_id=1, source_target_pairs={{0,2},{1,3},{2,0},{3,1},{4,6},{5,7},{6,4},{7,5},{8,10},{9,11},{10,... | collective-permute-start | bytes 393224 | tf_op jit(solution)/shard_map/ppermute | solution.py:317
  21.4 2.1 %collective-permute-start.8 = (bf16[128,1024]{1,0:T(8,128)(2,1)S(1)}, bf16[128,1024]{1,0:T(8,128)(2,1)S(1)}, u32[]{:S(2)}, u32[]{:S(2)}) collective-permute-start(bf16[128,1024]{1,0:T(8,128)(2,1)S(1)} %get-tuple-element.32), channel_id=1, source_target_pairs={{0,1},{1,0},{2,3},{3,2},{4,5},{5,4},{6,7},{7,6},{8,9},{9,8},{10,11... | collective-permute-start | bytes 786440 | tf_op jit(solution)/shard_map/ppermute | solution.py:317
  23.6 0.0 collective-permute-done.10
  23.6 1.2 %collective-permute-start.11 = (bf16[128,512]{1,0:T(8,128)(2,1)S(1)}, bf16[128,512]{1,0:T(8,128)(2,1)S(1)}, u32[]{:S(2)}, u32[]{:S(2)}) collective-permute-start(bf16[128,512]{1,0:T(8,128)(2,1)S(1)} %add_convert_fusion.1), channel_id=1, source_target_pairs={{0,2},{1,3},{2,0},{3,1},{4,6},{5,7},{6,4},{7,5},{8,10},{9,11},{10,... | collective-permute-start | bytes 393224 | tf_op jit(solution)/shard_map/ppermute | solution.py:317
  24.8 2.9 %collective-permute-done.9 = bf16[128,512]{1,0:T(8,128)(2,1)S(1)} collective-permute-done((bf16[128,512]{1,0:T(8,128)(2,1)S(1)}, bf16[128,512]{1,0:T(8,128)(2,1)S(1)}, u32[]{:S(2)}, u32[]{:S(2)}) %collective-permute-start.9) | collective-permute-done | bytes 131104 | tf_op jit(solution)/shard_map/ppermute | solution.py:317
  27.7 4.2 %collective-permute-done.11 = bf16[128,512]{1,0:T(8,128)(2,1)S(1)} collective-permute-done((bf16[128,512]{1,0:T(8,128)(2,1)S(1)}, bf16[128,512]{1,0:T(8,128)(2,1)S(1)}, u32[]{:S(2)}, u32[]{:S(2)}) %collective-permute-start.11) | collective-permute-done | bytes 131104 | tf_op jit(solution)/shard_map/ppermute | solution.py:317
  31.8 0.9 %collective-permute-done.8 = bf16[128,1024]{1,0:T(8,128)(2,1)S(1)} collective-permute-done((bf16[128,1024]{1,0:T(8,128)(2,1)S(1)}, bf16[128,1024]{1,0:T(8,128)(2,1)S(1)}, u32[]{:S(2)}, u32[]{:S(2)}) %collective-permute-start.8) | collective-permute-done | bytes 262176 | tf_op jit(solution)/shard_map/ppermute | solution.py:317
  32.8 0.8 %add_convert_fusion = bf16[128,1024]{1,0:T(8,128)(2,1)} fusion(f32[128,1024]{1,0:T(8,128)S(1)} %get-tuple-element.29, bf16[128,1024]{1,0:T(8,128)(2,1)S(1)} %collective-permute-done.8, bf16[128,512]{1,0:T(8,128)(2,1)S(1)} %collective-permute-done.11, bf16[128,512]{1,0:T(8,128)(2,1)S(1)} %collective-permute-done.9), kind=kLoop, calls=%fused_computation | loop fusion | flops 1048576 | bytes 1310720 | tf_op jit(solution)/shard_map/convert_element_type | solution.py:408
  (3 shorter events, 0.1 us)
Async XLA Ops:
  0.0 11.0 %copy-start.3 = (bf16[128,128]{1,0:T(8,128)(2,1)S(1)}, bf16[128,128]{1,0:T(8,128)(2,1)}, u32[]{:S(2)}) copy-start(bf16[128,128]{1,0:T(8,128)(2,1)} %refs_0_.3) | copy-start | bytes 98308
  0.0 11.0 %copy-start.4 = (bf16[128,128]{1,0:T(8,128)(2,1)S(1)}, bf16[128,128]{1,0:T(8,128)(2,1)}, u32[]{:S(2)}) copy-start(bf16[128,128]{1,0:T(8,128)(2,1)} %refs_1_.3) | copy-start | bytes 98308
  0.0 11.0 %copy-start.5 = (bf16[128,128]{1,0:T(8,128)(2,1)S(1)}, bf16[128,128]{1,0:T(8,128)(2,1)}, u32[]{:S(2)}) copy-start(bf16[128,128]{1,0:T(8,128)(2,1)} %refs_2_.3) | copy-start | bytes 98308
  0.0 11.1 %copy-start.6 = (bf16[128,128]{1,0:T(8,128)(2,1)S(1)}, bf16[128,128]{1,0:T(8,128)(2,1)}, u32[]{:S(2)}) copy-start(bf16[128,128]{1,0:T(8,128)(2,1)} %refs_3_.3) | copy-start | bytes 98308
  0.0 11.1 %copy-start.7 = (bf16[128,128]{1,0:T(8,128)(2,1)S(1)}, bf16[128,128]{1,0:T(8,128)(2,1)}, u32[]{:S(2)}) copy-start(bf16[128,128]{1,0:T(8,128)(2,1)} %refs_4_.3) | copy-start | bytes 98308
  0.0 12.2 %copy-start = (bf16[4096,128]{1,0:T(8,128)(2,1)S(1)}, bf16[4096,128]{1,0:T(8,128)(2,1)}, u32[]{:S(2)}) copy-start(bf16[4096,128]{1,0:T(8,128)(2,1)} %wq_ref.3) | copy-start | bytes 3145732
  0.0 12.2 %copy-start.1 = (bf16[4096,128]{1,0:T(8,128)(2,1)S(1)}, bf16[4096,128]{1,0:T(8,128)(2,1)}, u32[]{:S(2)}) copy-start(bf16[4096,128]{1,0:T(8,128)(2,1)} %wk_ref.3) | copy-start | bytes 3145732
  0.0 12.2 %copy-start.2 = (bf16[4096,128]{1,0:T(8,128)(2,1)S(1)}, bf16[4096,128]{1,0:T(8,128)(2,1)}, u32[]{:S(2)}) copy-start(bf16[4096,128]{1,0:T(8,128)(2,1)} %wv_ref.3) | copy-start | bytes 3145732
  1.9 6.8 %collective-permute-start = (bf16[144,256]{1,0:T(8,128)(2,1)}, bf16[144,256]{1,0:T(8,128)(2,1)S(1)}, u32[]{:S(2)}, u32[]{:S(2)}) collective-permute-start(bf16[144,256]{1,0:T(8,128)(2,1)} %get-tuple-element.21), channel_id=1, source_target_pairs={{0,24},{4,28},{8,16},{12,20},{16,8},{20,12},{24,0},{28,4},{1,25},{... | collective-permute-start | bytes 221192 | tf_op jit(solution)/shard_map/ppermute | solution.py:317
  5.8 5.2 %copy-start.8 = (f32[128,1]{0,1:T(1,128)S(1)}, f32[128,1]{0,1:T(1,128)}, u32[]{:S(2)}) copy-start(f32[128,1]{0,1:T(1,128)} %param.14) | copy-start | bytes 1540
  5.8 4.7 %collective-permute-start.2 = (bf16[144,256]{1,0:T(8,128)(2,1)}, bf16[144,256]{1,0:T(8,128)(2,1)S(1)}, u32[]{:S(2)}, u32[]{:S(2)}) collective-permute-start(bf16[144,256]{1,0:T(8,128)(2,1)} %get-tuple-element.24), channel_id=1, source_target_pairs={{0,8},{4,12},{8,0},{12,4},{16,24},{20,28},{24,16},{28,20},{1,9},{5... | collective-permute-start | bytes 221192 | tf_op jit(solution)/shard_map/ppermute | solution.py:317
  6.4 4.6 %collective-permute-start.3 = (bf16[144,256]{1,0:T(8,128)(2,1)}, bf16[144,256]{1,0:T(8,128)(2,1)S(1)}, u32[]{:S(2)}, u32[]{:S(2)}) collective-permute-start(bf16[144,256]{1,0:T(8,128)(2,1)} %get-tuple-element.21), channel_id=1, source_target_pairs={{0,16},{4,20},{8,24},{12,28},{16,0},{20,4},{24,8},{28,12},{1,17},{... | collective-permute-start | bytes 221192 | tf_op jit(solution)/shard_map/ppermute | solution.py:317
  6.5 4.5 %collective-permute-start.1 = (bf16[144,256]{1,0:T(8,128)(2,1)}, bf16[144,256]{1,0:T(8,128)(2,1)S(1)}, u32[]{:S(2)}, u32[]{:S(2)}) collective-permute-start(bf16[144,256]{1,0:T(8,128)(2,1)} %get-tuple-element.23), channel_id=1, source_target_pairs={{0,4},{4,0},{8,12},{12,8},{16,20},{20,16},{24,28},{28,24},{1,5},{5... | collective-permute-start | bytes 221192 | tf_op jit(solution)/shard_map/ppermute | solution.py:317
  8.7 3.5 %collective-permute-start.6 = (bf16[144,256]{1,0:T(8,128)(2,1)S(1)}, bf16[144,256]{1,0:T(8,128)(2,1)S(1)}, u32[]{:S(2)}, u32[]{:S(2)}) collective-permute-start(bf16[144,256]{1,0:T(8,128)(2,1)S(1)} %collective-permute-done.refs_9_), channel_id=1, source_target_pairs={{0,4},{4,0},{8,12},{12,8},{16,20},{20,16},{24,28},{28,24},{1,5},{5... | collective-permute-start | bytes 221192 | tf_op jit(solution)/shard_map/ppermute | solution.py:317
  10.5 1.3 %collective-permute-start.4 = (bf16[144,256]{1,0:T(8,128)(2,1)S(1)}, bf16[144,256]{1,0:T(8,128)(2,1)S(1)}, u32[]{:S(2)}, u32[]{:S(2)}) collective-permute-start(bf16[144,256]{1,0:T(8,128)(2,1)S(1)} %collective-permute-done.2.refs_7_), channel_id=1, source_target_pairs={{0,4},{4,0},{8,12},{12,8},{16,20},{20,16},{24,28},{28,24},{1,5},{5... | collective-permute-start | bytes 221192 | tf_op jit(solution)/shard_map/ppermute | solution.py:317
  10.9 1.3 %collective-permute-start.5 = (bf16[144,256]{1,0:T(8,128)(2,1)S(1)}, bf16[144,256]{1,0:T(8,128)(2,1)S(1)}, u32[]{:S(2)}, u32[]{:S(2)}) collective-permute-start(bf16[144,256]{1,0:T(8,128)(2,1)S(1)} %collective-permute-done.3.refs_8_), channel_id=1, source_target_pairs={{0,4},{4,0},{8,12},{12,8},{16,20},{20,16},{24,28},{28,24},{1,5},{5... | collective-permute-start | bytes 221192 | tf_op jit(solution)/shard_map/ppermute | solution.py:317
  12.9 5.8 %collective-permute-start.7 = (bf16[128,512]{1,0:T(8,128)(2,1)S(1)}, bf16[128,512]{1,0:T(8,128)(2,1)S(1)}, u32[]{:S(2)}, u32[]{:S(2)}) collective-permute-start(bf16[128,512]{1,0:T(8,128)(2,1)S(1)} %get-tuple-element.31), channel_id=1, source_target_pairs={{0,1},{1,0},{2,3},{3,2},{4,5},{5,4},{6,7},{7,6},{8,9},{9,8},{10,11... | collective-permute-start | bytes 393224 | tf_op jit(solution)/shard_map/ppermute | solution.py:317
  15.7 7.9 %collective-permute-start.10 = (bf16[128,512]{1,0:T(8,128)(2,1)S(1)}, bf16[128,512]{1,0:T(8,128)(2,1)S(1)}, u32[]{:S(2)}, u32[]{:S(2)}) collective-permute-start(bf16[128,512]{1,0:T(8,128)(2,1)S(1)} %get-tuple-element.36), channel_id=1, source_target_pairs={{0,1},{1,0},{2,3},{3,2},{4,5},{5,4},{6,7},{7,6},{8,9},{9,8},{10,11... | collective-permute-start | bytes 393224 | tf_op jit(solution)/shard_map/ppermute | solution.py:317
  18.8 8.9 %collective-permute-start.9 = (bf16[128,512]{1,0:T(8,128)(2,1)S(1)}, bf16[128,512]{1,0:T(8,128)(2,1)S(1)}, u32[]{:S(2)}, u32[]{:S(2)}) collective-permute-start(bf16[128,512]{1,0:T(8,128)(2,1)S(1)} %add_convert_fusion.2), channel_id=1, source_target_pairs={{0,2},{1,3},{2,0},{3,1},{4,6},{5,7},{6,4},{7,5},{8,10},{9,11},{10,... | collective-permute-start | bytes 393224 | tf_op jit(solution)/shard_map/ppermute | solution.py:317
  21.4 11.4 %collective-permute-start.8 = (bf16[128,1024]{1,0:T(8,128)(2,1)S(1)}, bf16[128,1024]{1,0:T(8,128)(2,1)S(1)}, u32[]{:S(2)}, u32[]{:S(2)}) collective-permute-start(bf16[128,1024]{1,0:T(8,128)(2,1)S(1)} %get-tuple-element.32), channel_id=1, source_target_pairs={{0,1},{1,0},{2,3},{3,2},{4,5},{5,4},{6,7},{7,6},{8,9},{9,8},{10,11... | collective-permute-start | bytes 786440 | tf_op jit(solution)/shard_map/ppermute | solution.py:317
  23.6 8.3 %collective-permute-start.11 = (bf16[128,512]{1,0:T(8,128)(2,1)S(1)}, bf16[128,512]{1,0:T(8,128)(2,1)S(1)}, u32[]{:S(2)}, u32[]{:S(2)}) collective-permute-start(bf16[128,512]{1,0:T(8,128)(2,1)S(1)} %add_convert_fusion.1), channel_id=1, source_target_pairs={{0,2},{1,3},{2,0},{3,1},{4,6},{5,7},{6,4},{7,5},{8,10},{9,11},{10,... | collective-permute-start | bytes 393224 | tf_op jit(solution)/shard_map/ppermute | solution.py:317

commit v17 on v16

--- a/solution.py
+++ b/solution.py
@@ -187,7 +187,7 @@
             for at, src in enumerate((first, second))
         ]
 
-    for load in loads:
+    for load in loads[:4]:
         load.wait()
     for bit in range(len(hops)):
         later = (me & (1 << bit)) == 0
@@ -202,6 +202,8 @@
             for move in moves(bit, q_ref, g_ref):
                 move.start()
 
+    for load in loads[4:]:
+        load.wait()
     delta = delta_of(g_ref[...], a_ref[...])
     delta = jnp.sum(jnp.where(diagonal(rows), delta, 0.0), axis=0, keepdims=True)
     row = lax.broadcasted_iota(jnp.int32, (EXTRA, rows), 0)
@@ -279,20 +281,23 @@
     sums = pair_sums(scale, offsets, refs[6:-1], *own)
     out_ref[:, :width] = sums[0] + dot_nn(score_low, key)
     out_ref[:, width : 2 * width] = sums[1] + dot_tn(score_low, query)
-    out_ref[:, 2 * width :] = sums[2] + dot_tn(probs.astype(jnp.bfloat16), grad)
+    lane = lax.broadcasted_iota(jnp.int32, (rows, width), 1)
+    out_ref[:, 3 * width :] = jnp.where(lane == 0, norm, delta)
+    out_ref[:, 2 * width : 3 * width] = sums[2] + dot_tn(probs.astype(jnp.bfloat16), grad)
 
 
 def near_kernel(scale, part, offsets, *refs):
     grads, front = refs[-2:]
-    w_refs, sum_ref, got = refs[6:9], refs[9], refs[10:-2]
-    own = own_columns(*refs[:6])
-    width = own[0].shape[1]
+    w_refs, sum_ref, got = refs[4:7], refs[7], refs[8:-2]
+    width = refs[0].shape[1]
+    columns = sum_ref[:, 3 * width : 3 * width + 1], sum_ref[:, 3 * width + 1 : 3 * width + 2]
+    own = [ref[...] for ref in refs[:4]] + list(columns)
     sums = pair_sums(scale, offsets, got, *own)
     grads[:, :width] = (scale * (sum_ref[:, :width] + sums[0])).astype(jnp.bfloat16)
     grads[:, width : 2 * width] = (
         scale * (sum_ref[:, width : 2 * width] + sums[1])
     ).astype(jnp.bfloat16)
-    grads[:, 2 * width :] = (sum_ref[:, 2 * width :] + sums[2]).astype(jnp.bfloat16)
+    grads[:, 2 * width :] = (sum_ref[:, 2 * width : 3 * width] + sums[2]).astype(jnp.bfloat16)
     project(grads, w_refs, (lax.axis_index("head") ^ 3) * part, front)
 
 
@@ -360,7 +365,7 @@
     full = jax.ShapeDtypeStruct((rows, part), jnp.float32)
     sums = pl.pallas_call(
         functools.partial(first_kernel, scale, soon),
-        out_shape=jax.ShapeDtypeStruct((rows, 3 * width), jnp.float32),
+        out_shape=jax.ShapeDtypeStruct((rows, 4 * width), jnp.float32),
         in_specs=[vmem] * (6 + len(soon)),
         out_specs=vmem,
         compiler_params=params,
@@ -373,7 +378,7 @@
     grads, front = pl.pallas_call(
         functools.partial(near_kernel, scale, part, late),
         out_shape=[jax.ShapeDtypeStruct((rows, 3 * width), jnp.bfloat16), half_low],
-        in_specs=[vmem] * (10 + len(late)),
+        in_specs=[vmem] * (8 + len(late)),
         out_specs=[vmem] * 2,
         compiler_params=params,
         cost_estimate=pl.CostEstimate(
@@ -381,7 +386,7 @@
             bytes_accessed=4 * rows * ctx * width + 6 * part * width,
             transcendentals=rows * rows * ctx,
         ),
-    )(*own, *weights, sums, *[got[at] for at in late])
+    )(*own[:4], *weights, sums, *[got[at] for at in late])
     front = swap(front, "head", 1)
     def projected(kernel, outs, operands):
         count = sum(out.shape[1] for out in outs)

time: 33.7 us -> 33.7 us (level)
  no operation moved by 1% of the time
where the time goes in v17:
time: 33.7 us; the launch traced here: 33.6 us
  waiting for transfers between devices  15.4 us (46%)
  starting transfers between devices  12.9 us (38%)
  Pallas kernels  4.22 us (13%)
  other arithmetic  0.85 us (3%)
    ppermute x12, waiting for transfers between devices, swap(): return lax.ppermute(value, axis, [(at, at ^ offset) for at in range(size)])  15.4 us
    ppermute x12, starting transfers between devices, swap(): return lax.ppermute(value, axis, [(at, at ^ offset) for at in range(size)])  12.9 us
    pallas_call x1, Pallas kernels, near_body(): pl.pallas_call(send_kernel, out_shape=[hop] * bits, in_specs=[hbm] * 6, o...  1.82 us
    pallas_call x2, Pallas kernels, projected(): pl.pallas_call(functools.partial(kernel, part), out_shape=outs, in_specs=...  1.15 us
    convert_element_type x1, other arithmetic, near_body(): return (total + near.astype(jnp.float32) + far_sum).astype(jnp.bfloat16)  0.8 us
  transfers between devices with their start and end apart: 12, of which 9 were waited for; matrix products, arithmetic and copies ran while one was open for 0% of the time, Pallas kernels for 5%

profile of v17, /device:TPU:0, one launch (start us, length us, event | category | flops | bytes accessed | tf_op | source)
XLA Modules:
  0.0 33.6 jit_solution(16360354455643841000)
XLA Ops:
  0.0 0.0 copy-start.3
  0.0 0.0 copy-start.4
  0.0 0.0 copy-start.5
  0.0 0.0 copy-start.6
  0.0 0.0 copy-start.7
  0.0 0.0 copy-start
  0.0 0.0 copy-start.1
  0.0 0.0 copy-start.2
  0.0 1.8 %shard_map.91 = (bf16[144,256]{1,0:T(8,128)(2,1)}, bf16[144,256]{1,0:T(8,128)(2,1)}, bf16[144,256]{1,0:T(8,128)(2,1)}) custom-call(bf16[128,128]{1,0:T(8,128)(2,1)} %refs_0_.3, bf16[128,128]{1,0:T(8,128)(2,1)} %refs_1_.3, bf16[128,128]{1,0:T(8,128)(2,1)} %refs_2_.3, bf16[128,128]{1,0:T(8,128)(2,1)} %refs_3_.3, bf16[128,128]{1,0:T(8,128)(2,1)} %refs_4_.2, ...), custom_call_target="tpu_custom_call" | custom-call | flops 5000000000 | bytes 327680 | tf_op jit(solution)/shard_map/pallas_call | solution.py:335
  1.9 4.0 %collective-permute-start = (bf16[144,256]{1,0:T(8,128)(2,1)}, bf16[144,256]{1,0:T(8,128)(2,1)S(1)}, u32[]{:S(2)}, u32[]{:S(2)}) collective-permute-start(bf16[144,256]{1,0:T(8,128)(2,1)} %get-tuple-element.21), channel_id=1, source_target_pairs={{0,24},{4,28},{8,16},{12,20},{16,8},{20,12},{24,0},{28,4},{1,25},{... | collective-permute-start | bytes 221192 | tf_op jit(solution)/shard_map/ppermute | solution.py:322
  5.8 0.0 copy-start.8
  5.8 0.5 %collective-permute-start.2 = (bf16[144,256]{1,0:T(8,128)(2,1)}, bf16[144,256]{1,0:T(8,128)(2,1)S(1)}, u32[]{:S(2)}, u32[]{:S(2)}) collective-permute-start(bf16[144,256]{1,0:T(8,128)(2,1)} %get-tuple-element.24), channel_id=1, source_target_pairs={{0,8},{4,12},{8,0},{12,4},{16,24},{20,28},{24,16},{28,20},{1,9},{5... | collective-permute-start | bytes 221192 | tf_op jit(solution)/shard_map/ppermute | solution.py:322
  6.4 0.1 collective-permute-start.3
  6.5 0.0 collective-permute-start.1
  6.5 2.2 %collective-permute-done.refs_9_ = bf16[144,256]{1,0:T(8,128)(2,1)S(1)} collective-permute-done((bf16[144,256]{1,0:T(8,128)(2,1)}, bf16[144,256]{1,0:T(8,128)(2,1)S(1)}, u32[]{:S(2)}, u32[]{:S(2)}) %collective-permute-start) | collective-permute-done | bytes 73760 | tf_op jit(solution)/shard_map/ppermute | solution.py:322
  8.7 0.0 collective-permute-start.6
  8.7 1.8 %collective-permute-done.2.refs_7_ = bf16[144,256]{1,0:T(8,128)(2,1)S(1)} collective-permute-done((bf16[144,256]{1,0:T(8,128)(2,1)}, bf16[144,256]{1,0:T(8,128)(2,1)S(1)}, u32[]{:S(2)}, u32[]{:S(2)}) %collective-permute-start.2) | collective-permute-done | bytes 73760 | tf_op jit(solution)/shard_map/ppermute | solution.py:322
  10.5 0.0 collective-permute-start.4
  10.5 0.4 %collective-permute-done.3.refs_8_ = bf16[144,256]{1,0:T(8,128)(2,1)S(1)} collective-permute-done((bf16[144,256]{1,0:T(8,128)(2,1)}, bf16[144,256]{1,0:T(8,128)(2,1)S(1)}, u32[]{:S(2)}, u32[]{:S(2)}) %collective-permute-start.3) | collective-permute-done | bytes 73760 | tf_op jit(solution)/shard_map/ppermute | solution.py:322
  10.9 0.1 collective-permute-start.5
  11.0 0.0 copy-done.8
  11.0 0.0 collective-permute-done.1.refs_6_
  11.0 0.0 copy-done.3
  11.0 0.0 copy-done.4
  11.0 0.0 copy-done.5
  11.1 0.0 copy-done.6
  11.1 0.0 copy-done.7
  11.1 0.6 %shard_map.92.refs_7_ = f32[128,512]{1,0:T(8,128)S(1)} custom-call(bf16[128,128]{1,0:T(8,128)(2,1)S(1)} %copy-done.3, bf16[128,128]{1,0:T(8,128)(2,1)S(1)} %copy-done.4, bf16[128,128]{1,0:T(8,128)(2,1)S(1)} %copy-done.5, bf16[128,128]{1,0:T(8,128)(2,1)S(1)} %copy-done.6, bf16[128,128]{1,0:T(8,128)(2,1)S(1)} %copy-done.7, ...), custom_call_target="tpu_custom_call" | custom-call | flops 117440512 | bytes 262144 | tf_op jit(solution)/shard_map/pallas_call | solution.py:366
  11.7 0.1 collective-permute-done.4.refs_8_
  11.8 0.4 %collective-permute-done.5.refs_9_ = bf16[144,256]{1,0:T(8,128)(2,1)S(1)} collective-permute-done((bf16[144,256]{1,0:T(8,128)(2,1)S(1)}, bf16[144,256]{1,0:T(8,128)(2,1)S(1)}, u32[]{:S(2)}, u32[]{:S(2)}) %collective-permute-start.5) | collective-permute-done | bytes 73760 | tf_op jit(solution)/shard_map/ppermute | solution.py:322
  12.2 0.0 collective-permute-done.6.refs_10_
  12.2 0.0 copy-done
  12.2 0.0 copy-done.1
  12.2 0.0 copy-done.2
  12.2 0.6 %shard_map.93 = (bf16[128,384]{1,0:T(8,128)(2,1)S(1)}, bf16[128,512]{1,0:T(8,128)(2,1)S(1)}) custom-call(bf16[128,128]{1,0:T(8,128)(2,1)S(1)} %copy-done.3, bf16[128,128]{1,0:T(8,128)(2,1)S(1)} %copy-done.4, bf16[128,128]{1,0:T(8,128)(2,1)S(1)} %copy-done.5, bf16[128,128]{1,0:T(8,128)(2,1)S(1)} %copy-done.6, bf16[4096,128]{1,0:T(8,128)(2,1)S(1)} %copy-done, ...), custom_call_target="tpu_custom_call" | custom-call | flops 335544320 | bytes 1310720 | tf_op jit(solution)/shard_map/pallas_call | solution.py:378
  12.9 1.6 %collective-permute-start.7 = (bf16[128,512]{1,0:T(8,128)(2,1)S(1)}, bf16[128,512]{1,0:T(8,128)(2,1)S(1)}, u32[]{:S(2)}, u32[]{:S(2)}) collective-permute-start(bf16[128,512]{1,0:T(8,128)(2,1)S(1)} %get-tuple-element.31), channel_id=1, source_target_pairs={{0,1},{1,0},{2,3},{3,2},{4,5},{5,4},{6,7},{7,6},{8,9},{9,8},{10,11... | collective-permute-start | bytes 393224 | tf_op jit(solution)/shard_map/ppermute | solution.py:322
  14.5 0.4 %shard_map.94 = (f32[128,512]{1,0:T(8,128)S(1)}, f32[128,512]{1,0:T(8,128)S(1)}) custom-call(bf16[128,384]{1,0:T(8,128)(2,1)S(1)} %get-tuple-element.28.grads, bf16[4096,128]{1,0:T(8,128)(2,1)S(1)} %copy-done, bf16[4096,128]{1,0:T(8,128)(2,1)S(1)} %copy-done.1, bf16[4096,128]{1,0:T(8,128)(2,1)S(1)} %copy-done.2), custom_call_target="tpu_custom_call" | custom-call | flops 100663296 | bytes 786432 | tf_op jit(solution)/shard_map/pallas_call | solution.py:393
  14.9 0.8 %shard_map.95 = (bf16[128,512]{1,0:T(8,128)(2,1)S(1)}, bf16[128,1024]{1,0:T(8,128)(2,1)S(1)}, f32[128,1024]{1,0:T(8,128)S(1)}) custom-call(bf16[128,384]{1,0:T(8,128)(2,1)S(1)} %get-tuple-element.28.grads, bf16[4096,128]{1,0:T(8,128)(2,1)S(1)} %copy-done, bf16[4096,128]{1,0:T(8,128)(2,1)S(1)} %copy-done.1, bf16[4096,128]{1,0:T(8,128)(2,1)S(1)} %copy-done.2), custom_call_target="tpu_custom_call" | custom-call | flops 251658240 | bytes 1966080 | tf_op jit(solution)/shard_map/pallas_call | solution.py:393
  15.7 0.5 %collective-permute-start.10 = (bf16[128,512]{1,0:T(8,128)(2,1)S(1)}, bf16[128,512]{1,0:T(8,128)(2,1)S(1)}, u32[]{:S(2)}, u32[]{:S(2)}) collective-permute-start(bf16[128,512]{1,0:T(8,128)(2,1)S(1)} %get-tuple-element.36), channel_id=1, source_target_pairs={{0,1},{1,0},{2,3},{3,2},{4,5},{5,4},{6,7},{7,6},{8,9},{9,8},{10,11... | collective-permute-start | bytes 393224 | tf_op jit(solution)/shard_map/ppermute | solution.py:322
  16.2 2.5 %collective-permute-done.7 = bf16[128,512]{1,0:T(8,128)(2,1)S(1)} collective-permute-done((bf16[128,512]{1,0:T(8,128)(2,1)S(1)}, bf16[128,512]{1,0:T(8,128)(2,1)S(1)}, u32[]{:S(2)}, u32[]{:S(2)}) %collective-permute-start.7) | collective-permute-done | bytes 131104 | tf_op jit(solution)/shard_map/ppermute | solution.py:322
  18.7 2.7 %collective-permute-start.9 = (bf16[128,512]{1,0:T(8,128)(2,1)S(1)}, bf16[128,512]{1,0:T(8,128)(2,1)S(1)}, u32[]{:S(2)}, u32[]{:S(2)}) collective-permute-start(bf16[128,512]{1,0:T(8,128)(2,1)S(1)} %add_convert_fusion.2), channel_id=1, source_target_pairs={{0,2},{1,3},{2,0},{3,1},{4,6},{5,7},{6,4},{7,5},{8,10},{9,11},{10,... | collective-permute-start | bytes 393224 | tf_op jit(solution)/shard_map/ppermute | solution.py:322
  21.4 2.1 %collective-permute-start.8 = (bf16[128,1024]{1,0:T(8,128)(2,1)S(1)}, bf16[128,1024]{1,0:T(8,128)(2,1)S(1)}, u32[]{:S(2)}, u32[]{:S(2)}) collective-permute-start(bf16[128,1024]{1,0:T(8,128)(2,1)S(1)} %get-tuple-element.32), channel_id=1, source_target_pairs={{0,1},{1,0},{2,3},{3,2},{4,5},{5,4},{6,7},{7,6},{8,9},{9,8},{10,11... | collective-permute-start | bytes 786440 | tf_op jit(solution)/shard_map/ppermute | solution.py:322
  23.6 0.0 collective-permute-done.10
  23.6 1.2 %collective-permute-start.11 = (bf16[128,512]{1,0:T(8,128)(2,1)S(1)}, bf16[128,512]{1,0:T(8,128)(2,1)S(1)}, u32[]{:S(2)}, u32[]{:S(2)}) collective-permute-start(bf16[128,512]{1,0:T(8,128)(2,1)S(1)} %add_convert_fusion.1), channel_id=1, source_target_pairs={{0,2},{1,3},{2,0},{3,1},{4,6},{5,7},{6,4},{7,5},{8,10},{9,11},{10,... | collective-permute-start | bytes 393224 | tf_op jit(solution)/shard_map/ppermute | solution.py:322
  24.8 2.8 %collective-permute-done.9 = bf16[128,512]{1,0:T(8,128)(2,1)S(1)} collective-permute-done((bf16[128,512]{1,0:T(8,128)(2,1)S(1)}, bf16[128,512]{1,0:T(8,128)(2,1)S(1)}, u32[]{:S(2)}, u32[]{:S(2)}) %collective-permute-start.9) | collective-permute-done | bytes 131104 | tf_op jit(solution)/shard_map/ppermute | solution.py:322
  27.7 4.2 %collective-permute-done.11 = bf16[128,512]{1,0:T(8,128)(2,1)S(1)} collective-permute-done((bf16[128,512]{1,0:T(8,128)(2,1)S(1)}, bf16[128,512]{1,0:T(8,128)(2,1)S(1)}, u32[]{:S(2)}, u32[]{:S(2)}) %collective-permute-start.11) | collective-permute-done | bytes 131104 | tf_op jit(solution)/shard_map/ppermute | solution.py:322
  31.9 0.9 %collective-permute-done.8 = bf16[128,1024]{1,0:T(8,128)(2,1)S(1)} collective-permute-done((bf16[128,1024]{1,0:T(8,128)(2,1)S(1)}, bf16[128,1024]{1,0:T(8,128)(2,1)S(1)}, u32[]{:S(2)}, u32[]{:S(2)}) %collective-permute-start.8) | collective-permute-done | bytes 262176 | tf_op jit(solution)/shard_map/ppermute | solution.py:322
  32.8 0.8 %add_convert_fusion = bf16[128,1024]{1,0:T(8,128)(2,1)} fusion(f32[128,1024]{1,0:T(8,128)S(1)} %get-tuple-element.29, bf16[128,1024]{1,0:T(8,128)(2,1)S(1)} %collective-permute-done.8, bf16[128,512]{1,0:T(8,128)(2,1)S(1)} %collective-permute-done.11, bf16[128,512]{1,0:T(8,128)(2,1)S(1)} %collective-permute-done.9), kind=kLoop, calls=%fused_computation | loop fusion | flops 1048576 | bytes 1310720 | tf_op jit(solution)/shard_map/convert_element_type | solution.py:413
  (3 shorter events, 0.1 us)
Async XLA Ops:
  0.0 11.0 %copy-start.3 = (bf16[128,128]{1,0:T(8,128)(2,1)S(1)}, bf16[128,128]{1,0:T(8,128)(2,1)}, u32[]{:S(2)}) copy-start(bf16[128,128]{1,0:T(8,128)(2,1)} %refs_0_.3) | copy-start | bytes 98308
  0.0 11.0 %copy-start.4 = (bf16[128,128]{1,0:T(8,128)(2,1)S(1)}, bf16[128,128]{1,0:T(8,128)(2,1)}, u32[]{:S(2)}) copy-start(bf16[128,128]{1,0:T(8,128)(2,1)} %refs_1_.3) | copy-start | bytes 98308
  0.0 11.0 %copy-start.5 = (bf16[128,128]{1,0:T(8,128)(2,1)S(1)}, bf16[128,128]{1,0:T(8,128)(2,1)}, u32[]{:S(2)}) copy-start(bf16[128,128]{1,0:T(8,128)(2,1)} %refs_2_.3) | copy-start | bytes 98308
  0.0 11.1 %copy-start.6 = (bf16[128,128]{1,0:T(8,128)(2,1)S(1)}, bf16[128,128]{1,0:T(8,128)(2,1)}, u32[]{:S(2)}) copy-start(bf16[128,128]{1,0:T(8,128)(2,1)} %refs_3_.3) | copy-start | bytes 98308
  0.0 11.1 %copy-start.7 = (bf16[128,128]{1,0:T(8,128)(2,1)S(1)}, bf16[128,128]{1,0:T(8,128)(2,1)}, u32[]{:S(2)}) copy-start(bf16[128,128]{1,0:T(8,128)(2,1)} %refs_4_.2) | copy-start | bytes 98308
  0.0 12.2 %copy-start = (bf16[4096,128]{1,0:T(8,128)(2,1)S(1)}, bf16[4096,128]{1,0:T(8,128)(2,1)}, u32[]{:S(2)}) copy-start(bf16[4096,128]{1,0:T(8,128)(2,1)} %wq_ref.3) | copy-start | bytes 3145732
  0.0 12.2 %copy-start.1 = (bf16[4096,128]{1,0:T(8,128)(2,1)S(1)}, bf16[4096,128]{1,0:T(8,128)(2,1)}, u32[]{:S(2)}) copy-start(bf16[4096,128]{1,0:T(8,128)(2,1)} %wk_ref.3) | copy-start | bytes 3145732
  0.0 12.2 %copy-start.2 = (bf16[4096,128]{1,0:T(8,128)(2,1)S(1)}, bf16[4096,128]{1,0:T(8,128)(2,1)}, u32[]{:S(2)}) copy-start(bf16[4096,128]{1,0:T(8,128)(2,1)} %wv_ref.3) | copy-start | bytes 3145732
  1.9 6.8 %collective-permute-start = (bf16[144,256]{1,0:T(8,128)(2,1)}, bf16[144,256]{1,0:T(8,128)(2,1)S(1)}, u32[]{:S(2)}, u32[]{:S(2)}) collective-permute-start(bf16[144,256]{1,0:T(8,128)(2,1)} %get-tuple-element.21), channel_id=1, source_target_pairs={{0,24},{4,28},{8,16},{12,20},{16,8},{20,12},{24,0},{28,4},{1,25},{... | collective-permute-start | bytes 221192 | tf_op jit(solution)/shard_map/ppermute | solution.py:322
  5.8 5.2 %copy-start.8 = (f32[128,1]{0,1:T(1,128)S(1)}, f32[128,1]{0,1:T(1,128)}, u32[]{:S(2)}) copy-start(f32[128,1]{0,1:T(1,128)} %param.14) | copy-start | bytes 1540
  5.8 4.7 %collective-permute-start.2 = (bf16[144,256]{1,0:T(8,128)(2,1)}, bf16[144,256]{1,0:T(8,128)(2,1)S(1)}, u32[]{:S(2)}, u32[]{:S(2)}) collective-permute-start(bf16[144,256]{1,0:T(8,128)(2,1)} %get-tuple-element.24), channel_id=1, source_target_pairs={{0,8},{4,12},{8,0},{12,4},{16,24},{20,28},{24,16},{28,20},{1,9},{5... | collective-permute-start | bytes 221192 | tf_op jit(solution)/shard_map/ppermute | solution.py:322
  6.4 4.6 %collective-permute-start.3 = (bf16[144,256]{1,0:T(8,128)(2,1)}, bf16[144,256]{1,0:T(8,128)(2,1)S(1)}, u32[]{:S(2)}, u32[]{:S(2)}) collective-permute-start(bf16[144,256]{1,0:T(8,128)(2,1)} %get-tuple-element.21), channel_id=1, source_target_pairs={{0,16},{4,20},{8,24},{12,28},{16,0},{20,4},{24,8},{28,12},{1,17},{... | collective-permute-start | bytes 221192 | tf_op jit(solution)/shard_map/ppermute | solution.py:322
  6.5 4.5 %collective-permute-start.1 = (bf16[144,256]{1,0:T(8,128)(2,1)}, bf16[144,256]{1,0:T(8,128)(2,1)S(1)}, u32[]{:S(2)}, u32[]{:S(2)}) collective-permute-start(bf16[144,256]{1,0:T(8,128)(2,1)} %get-tuple-element.23), channel_id=1, source_target_pairs={{0,4},{4,0},{8,12},{12,8},{16,20},{20,16},{24,28},{28,24},{1,5},{5... | collective-permute-start | bytes 221192 | tf_op jit(solution)/shard_map/ppermute | solution.py:322
  8.7 3.5 %collective-permute-start.6 = (bf16[144,256]{1,0:T(8,128)(2,1)S(1)}, bf16[144,256]{1,0:T(8,128)(2,1)S(1)}, u32[]{:S(2)}, u32[]{:S(2)}) collective-permute-start(bf16[144,256]{1,0:T(8,128)(2,1)S(1)} %collective-permute-done.refs_9_), channel_id=1, source_target_pairs={{0,4},{4,0},{8,12},{12,8},{16,20},{20,16},{24,28},{28,24},{1,5},{5... | collective-permute-start | bytes 221192 | tf_op jit(solution)/shard_map/ppermute | solution.py:322
  10.5 1.3 %collective-permute-start.4 = (bf16[144,256]{1,0:T(8,128)(2,1)S(1)}, bf16[144,256]{1,0:T(8,128)(2,1)S(1)}, u32[]{:S(2)}, u32[]{:S(2)}) collective-permute-start(bf16[144,256]{1,0:T(8,128)(2,1)S(1)} %collective-permute-done.2.refs_7_), channel_id=1, source_target_pairs={{0,4},{4,0},{8,12},{12,8},{16,20},{20,16},{24,28},{28,24},{1,5},{5... | collective-permute-start | bytes 221192 | tf_op jit(solution)/shard_map/ppermute | solution.py:322
  10.9 1.3 %collective-permute-start.5 = (bf16[144,256]{1,0:T(8,128)(2,1)S(1)}, bf16[144,256]{1,0:T(8,128)(2,1)S(1)}, u32[]{:S(2)}, u32[]{:S(2)}) collective-permute-start(bf16[144,256]{1,0:T(8,128)(2,1)S(1)} %collective-permute-done.3.refs_8_), channel_id=1, source_target_pairs={{0,4},{4,0},{8,12},{12,8},{16,20},{20,16},{24,28},{28,24},{1,5},{5... | collective-permute-start | bytes 221192 | tf_op jit(solution)/shard_map/ppermute | solution.py:322
  12.9 5.8 %collective-permute-start.7 = (bf16[128,512]{1,0:T(8,128)(2,1)S(1)}, bf16[128,512]{1,0:T(8,128)(2,1)S(1)}, u32[]{:S(2)}, u32[]{:S(2)}) collective-permute-start(bf16[128,512]{1,0:T(8,128)(2,1)S(1)} %get-tuple-element.31), channel_id=1, source_target_pairs={{0,1},{1,0},{2,3},{3,2},{4,5},{5,4},{6,7},{7,6},{8,9},{9,8},{10,11... | collective-permute-start | bytes 393224 | tf_op jit(solution)/shard_map/ppermute | solution.py:322
  15.7 7.9 %collective-permute-start.10 = (bf16[128,512]{1,0:T(8,128)(2,1)S(1)}, bf16[128,512]{1,0:T(8,128)(2,1)S(1)}, u32[]{:S(2)}, u32[]{:S(2)}) collective-permute-start(bf16[128,512]{1,0:T(8,128)(2,1)S(1)} %get-tuple-element.36), channel_id=1, source_target_pairs={{0,1},{1,0},{2,3},{3,2},{4,5},{5,4},{6,7},{7,6},{8,9},{9,8},{10,11... | collective-permute-start | bytes 393224 | tf_op jit(solution)/shard_map/ppermute | solution.py:322
  18.7 8.9 %collective-permute-start.9 = (bf16[128,512]{1,0:T(8,128)(2,1)S(1)}, bf16[128,512]{1,0:T(8,128)(2,1)S(1)}, u32[]{:S(2)}, u32[]{:S(2)}) collective-permute-start(bf16[128,512]{1,0:T(8,128)(2,1)S(1)} %add_convert_fusion.2), channel_id=1, source_target_pairs={{0,2},{1,3},{2,0},{3,1},{4,6},{5,7},{6,4},{7,5},{8,10},{9,11},{10,... | collective-permute-start | bytes 393224 | tf_op jit(solution)/shard_map/ppermute | solution.py:322
  21.4 11.4 %collective-permute-start.8 = (bf16[128,1024]{1,0:T(8,128)(2,1)S(1)}, bf16[128,1024]{1,0:T(8,128)(2,1)S(1)}, u32[]{:S(2)}, u32[]{:S(2)}) collective-permute-start(bf16[128,1024]{1,0:T(8,128)(2,1)S(1)} %get-tuple-element.32), channel_id=1, source_target_pairs={{0,1},{1,0},{2,3},{3,2},{4,5},{5,4},{6,7},{7,6},{8,9},{9,8},{10,11... | collective-permute-start | bytes 786440 | tf_op jit(solution)/shard_map/ppermute | solution.py:322
  23.6 8.3 %collective-permute-start.11 = (bf16[128,512]{1,0:T(8,128)(2,1)S(1)}, bf16[128,512]{1,0:T(8,128)(2,1)S(1)}, u32[]{:S(2)}, u32[]{:S(2)}) collective-permute-start(bf16[128,512]{1,0:T(8,128)(2,1)S(1)} %add_convert_fusion.1), channel_id=1, source_target_pairs={{0,2},{1,3},{2,0},{3,1},{4,6},{5,7},{6,4},{7,5},{8,10},{9,11},{10,... | collective-permute-start | bytes 393224 | tf_op jit(solution)/shard_map/ppermute | solution.py:322

commit v18 on v17

--- a/solution.py
+++ b/solution.py
@@ -351,7 +351,7 @@
         ),
     )(*own)
     got = {at: swap(sent[at.bit_length() - 1], "ctx", at) for at in (1, *range(2, ctx, 2))}
-    soon = [at for at in (6,) if at < ctx]
+    soon = [at for at in (4, 6) if at < ctx]
     early, norm = lax.optimization_barrier((tuple(got[at] for at in soon), own[-1]))
     got.update(zip(soon, early))
     own = own[:-1] + (norm * (1.0 / scale),)

time: 33.7 us -> 33.7 us (level)
  starting transfers between devices: 12.9 us -> 13.3 us
  waiting for transfers between devices: 15.4 us -> 15 us
    ppermute x12, waiting for transfers between devices: 15.4 us -> 15 us  [swap(): return lax.ppermute(value, axis, [(at, at ^ offset) for at in range(size)])]
    ppermute x12, starting transfers between devices: 12.9 us -> 13.3 us  [swap(): return lax.ppermute(value, axis, [(at, at ^ offset) for at in range(size)])]
  transfers between devices with their start and end apart: 12 -> 12, of which waited for: 9 -> 7; matrix products, arithmetic and copies ran while one was open for 0% -> 0% of each run, Pallas kernels for 5% -> 5%
where the time goes in v18:
time: 33.7 us; the launch traced here: 33.6 us
  waiting for transfers between devices  15 us (45%)
  starting transfers between devices  13.3 us (39%)
  Pallas kernels  4.21 us (12%)
  other arithmetic  0.85 us (3%)
    ppermute x12, waiting for transfers between devices, swap(): return lax.ppermute(value, axis, [(at, at ^ offset) for at in range(size)])  15 us
    ppermute x12, starting transfers between devices, swap(): return lax.ppermute(value, axis, [(at, at ^ offset) for at in range(size)])  13.3 us
    pallas_call x1, Pallas kernels, near_body(): pl.pallas_call(send_kernel, out_shape=[hop] * bits, in_specs=[hbm] * 6, o...  1.82 us
    pallas_call x2, Pallas kernels, projected(): pl.pallas_call(functools.partial(kernel, part), out_shape=outs, in_specs=...  1.15 us
    convert_element_type x1, other arithmetic, near_body(): return (total + near.astype(jnp.float32) + far_sum).astype(jnp.bfloat16)  0.8 us
  transfers between devices with their start and end apart: 12, of which 7 were waited for; matrix products, arithmetic and copies ran while one was open for 0% of the time, Pallas kernels for 5%

profile of v18, /device:TPU:0, one launch (start us, length us, event | category | flops | bytes accessed | tf_op | source)
XLA Modules:
  0.0 33.6 jit_solution(14116710656727678178)
XLA Ops:
  0.0 0.0 copy-start.3
  0.0 0.0 copy-start.4
  0.0 0.0 copy-start.5
  0.0 0.0 copy-start.6
  0.0 0.0 copy-start.7
  0.0 0.0 copy-start
  0.0 0.0 copy-start.1
  0.0 0.0 copy-start.2
  0.0 1.8 %shard_map.91 = (bf16[144,256]{1,0:T(8,128)(2,1)}, bf16[144,256]{1,0:T(8,128)(2,1)}, bf16[144,256]{1,0:T(8,128)(2,1)}) custom-call(bf16[128,128]{1,0:T(8,128)(2,1)} %refs_0_.3, bf16[128,128]{1,0:T(8,128)(2,1)} %refs_1_.3, bf16[128,128]{1,0:T(8,128)(2,1)} %refs_2_.3, bf16[128,128]{1,0:T(8,128)(2,1)} %refs_3_.3, bf16[128,128]{1,0:T(8,128)(2,1)} %refs_4_.2, ...), custom_call_target="tpu_custom_call" | custom-call | flops 5000000000 | bytes 327680 | tf_op jit(solution)/shard_map/pallas_call | solution.py:335
  1.9 4.0 %collective-permute-start.1 = (bf16[144,256]{1,0:T(8,128)(2,1)}, bf16[144,256]{1,0:T(8,128)(2,1)S(1)}, u32[]{:S(2)}, u32[]{:S(2)}) collective-permute-start(bf16[144,256]{1,0:T(8,128)(2,1)} %get-tuple-element.22), channel_id=1, source_target_pairs={{0,24},{4,28},{8,16},{12,20},{16,8},{20,12},{24,0},{28,4},{1,25},{... | collective-permute-start | bytes 221192 | tf_op jit(solution)/shard_map/ppermute | solution.py:322
  5.8 0.5 %collective-permute-start = (bf16[144,256]{1,0:T(8,128)(2,1)}, bf16[144,256]{1,0:T(8,128)(2,1)S(1)}, u32[]{:S(2)}, u32[]{:S(2)}) collective-permute-start(bf16[144,256]{1,0:T(8,128)(2,1)} %get-tuple-element.22), channel_id=1, source_target_pairs={{0,16},{4,20},{8,24},{12,28},{16,0},{20,4},{24,8},{28,12},{1,17},{... | collective-permute-start | bytes 221192 | tf_op jit(solution)/shard_map/ppermute | solution.py:322
  6.4 0.0 copy-start.8
  6.4 0.1 collective-permute-start.3
  6.5 0.0 collective-permute-start.2
  6.5 2.0 %collective-permute-done.1.refs_9_ = bf16[144,256]{1,0:T(8,128)(2,1)S(1)} collective-permute-done((bf16[144,256]{1,0:T(8,128)(2,1)}, bf16[144,256]{1,0:T(8,128)(2,1)S(1)}, u32[]{:S(2)}, u32[]{:S(2)}) %collective-permute-start.1) | collective-permute-done | bytes 73760 | tf_op jit(solution)/shard_map/ppermute | solution.py:322
  8.5 1.9 %collective-permute-done.refs_8_ = bf16[144,256]{1,0:T(8,128)(2,1)S(1)} collective-permute-done((bf16[144,256]{1,0:T(8,128)(2,1)}, bf16[144,256]{1,0:T(8,128)(2,1)S(1)}, u32[]{:S(2)}, u32[]{:S(2)}) %collective-permute-start) | collective-permute-done | bytes 73760 | tf_op jit(solution)/shard_map/ppermute | solution.py:322
  10.4 0.0 collective-permute-start.5
  10.4 0.5 %collective-permute-start.6 = (bf16[144,256]{1,0:T(8,128)(2,1)S(1)}, bf16[144,256]{1,0:T(8,128)(2,1)S(1)}, u32[]{:S(2)}, u32[]{:S(2)}) collective-permute-start(bf16[144,256]{1,0:T(8,128)(2,1)S(1)} %collective-permute-done.1.refs_9_), channel_id=1, source_target_pairs={{0,4},{4,0},{8,12},{12,8},{16,20},{20,16},{24,28},{28,24},{1,5},{5... | collective-permute-start | bytes 221192 | tf_op jit(solution)/shard_map/ppermute | solution.py:322
  10.9 0.0 collective-permute-done.3.refs_7_
  10.9 0.0 collective-permute-start.4
  10.9 0.0 copy-done.8
  10.9 0.0 collective-permute-done.2.refs_6_
  11.0 0.0 copy-done.3
  11.0 0.0 copy-done.4
  11.0 0.0 copy-done.5
  11.0 0.0 copy-done.6
  11.0 0.0 copy-done.7
  11.0 0.6 %shard_map.92.refs_7_ = f32[128,512]{1,0:T(8,128)S(1)} custom-call(bf16[128,128]{1,0:T(8,128)(2,1)S(1)} %copy-done.3, bf16[128,128]{1,0:T(8,128)(2,1)S(1)} %copy-done.4, bf16[128,128]{1,0:T(8,128)(2,1)S(1)} %copy-done.5, bf16[128,128]{1,0:T(8,128)(2,1)S(1)} %copy-done.6, bf16[128,128]{1,0:T(8,128)(2,1)S(1)} %copy-done.7, ...), custom_call_target="tpu_custom_call" | custom-call | flops 117440512 | bytes 262144 | tf_op jit(solution)/shard_map/pallas_call | solution.py:366
  11.6 0.6 %collective-permute-done.4.refs_8_ = bf16[144,256]{1,0:T(8,128)(2,1)S(1)} collective-permute-done((bf16[144,256]{1,0:T(8,128)(2,1)S(1)}, bf16[144,256]{1,0:T(8,128)(2,1)S(1)}, u32[]{:S(2)}, u32[]{:S(2)}) %collective-permute-start.4) | collective-permute-done | bytes 73760 | tf_op jit(solution)/shard_map/ppermute | solution.py:322
  12.2 0.0 collective-permute-done.5.refs_9_
  12.2 0.0 collective-permute-done.6.refs_10_
  12.2 0.0 copy-done
  12.2 0.0 copy-done.1
  12.2 0.0 copy-done.2
  12.2 0.6 %shard_map.93 = (bf16[128,384]{1,0:T(8,128)(2,1)S(1)}, bf16[128,512]{1,0:T(8,128)(2,1)S(1)}) custom-call(bf16[128,128]{1,0:T(8,128)(2,1)S(1)} %copy-done.3, bf16[128,128]{1,0:T(8,128)(2,1)S(1)} %copy-done.4, bf16[128,128]{1,0:T(8,128)(2,1)S(1)} %copy-done.5, bf16[128,128]{1,0:T(8,128)(2,1)S(1)} %copy-done.6, bf16[4096,128]{1,0:T(8,128)(2,1)S(1)} %copy-done, ...), custom_call_target="tpu_custom_call" | custom-call | flops 335544320 | bytes 1310720 | tf_op jit(solution)/shard_map/pallas_call | solution.py:378
  12.9 1.7 %collective-permute-start.7 = (bf16[128,512]{1,0:T(8,128)(2,1)S(1)}, bf16[128,512]{1,0:T(8,128)(2,1)S(1)}, u32[]{:S(2)}, u32[]{:S(2)}) collective-permute-start(bf16[128,512]{1,0:T(8,128)(2,1)S(1)} %get-tuple-element.33), channel_id=1, source_target_pairs={{0,1},{1,0},{2,3},{3,2},{4,5},{5,4},{6,7},{7,6},{8,9},{9,8},{10,11... | collective-permute-start | bytes 393224 | tf_op jit(solution)/shard_map/ppermute | solution.py:322
  14.5 0.4 %shard_map.94 = (f32[128,512]{1,0:T(8,128)S(1)}, f32[128,512]{1,0:T(8,128)S(1)}) custom-call(bf16[128,384]{1,0:T(8,128)(2,1)S(1)} %get-tuple-element.30.grads, bf16[4096,128]{1,0:T(8,128)(2,1)S(1)} %copy-done, bf16[4096,128]{1,0:T(8,128)(2,1)S(1)} %copy-done.1, bf16[4096,128]{1,0:T(8,128)(2,1)S(1)} %copy-done.2), custom_call_target="tpu_custom_call" | custom-call | flops 100663296 | bytes 786432 | tf_op jit(solution)/shard_map/pallas_call | solution.py:393
  14.9 0.8 %shard_map.95 = (bf16[128,512]{1,0:T(8,128)(2,1)S(1)}, bf16[128,1024]{1,0:T(8,128)(2,1)S(1)}, f32[128,1024]{1,0:T(8,128)S(1)}) custom-call(bf16[128,384]{1,0:T(8,128)(2,1)S(1)} %get-tuple-element.30.grads, bf16[4096,128]{1,0:T(8,128)(2,1)S(1)} %copy-done, bf16[4096,128]{1,0:T(8,128)(2,1)S(1)} %copy-done.1, bf16[4096,128]{1,0:T(8,128)(2,1)S(1)} %copy-done.2), custom_call_target="tpu_custom_call" | custom-call | flops 251658240 | bytes 1966080 | tf_op jit(solution)/shard_map/pallas_call | solution.py:393
  15.7 0.5 %collective-permute-start.10 = (bf16[128,512]{1,0:T(8,128)(2,1)S(1)}, bf16[128,512]{1,0:T(8,128)(2,1)S(1)}, u32[]{:S(2)}, u32[]{:S(2)}) collective-permute-start(bf16[128,512]{1,0:T(8,128)(2,1)S(1)} %get-tuple-element.38), channel_id=1, source_target_pairs={{0,1},{1,0},{2,3},{3,2},{4,5},{5,4},{6,7},{7,6},{8,9},{9,8},{10,11... | collective-permute-start | bytes 393224 | tf_op jit(solution)/shard_map/ppermute | solution.py:322
  16.2 2.5 %collective-permute-done.7 = bf16[128,512]{1,0:T(8,128)(2,1)S(1)} collective-permute-done((bf16[128,512]{1,0:T(8,128)(2,1)S(1)}, bf16[128,512]{1,0:T(8,128)(2,1)S(1)}, u32[]{:S(2)}, u32[]{:S(2)}) %collective-permute-start.7) | collective-permute-done | bytes 131104 | tf_op jit(solution)/shard_map/ppermute | solution.py:322
  18.7 2.7 %collective-permute-start.9 = (bf16[128,512]{1,0:T(8,128)(2,1)S(1)}, bf16[128,512]{1,0:T(8,128)(2,1)S(1)}, u32[]{:S(2)}, u32[]{:S(2)}) collective-permute-start(bf16[128,512]{1,0:T(8,128)(2,1)S(1)} %add_convert_fusion.2), channel_id=1, source_target_pairs={{0,2},{1,3},{2,0},{3,1},{4,6},{5,7},{6,4},{7,5},{8,10},{9,11},{10,... | collective-permute-start | bytes 393224 | tf_op jit(solution)/shard_map/ppermute | solution.py:322
  21.5 2.1 %collective-permute-start.8 = (bf16[128,1024]{1,0:T(8,128)(2,1)S(1)}, bf16[128,1024]{1,0:T(8,128)(2,1)S(1)}, u32[]{:S(2)}, u32[]{:S(2)}) collective-permute-start(bf16[128,1024]{1,0:T(8,128)(2,1)S(1)} %get-tuple-element.34), channel_id=1, source_target_pairs={{0,1},{1,0},{2,3},{3,2},{4,5},{5,4},{6,7},{7,6},{8,9},{9,8},{10,11... | collective-permute-start | bytes 786440 | tf_op jit(solution)/shard_map/ppermute | solution.py:322
  23.6 0.0 collective-permute-done.10
  23.6 1.2 %collective-permute-start.11 = (bf16[128,512]{1,0:T(8,128)(2,1)S(1)}, bf16[128,512]{1,0:T(8,128)(2,1)S(1)}, u32[]{:S(2)}, u32[]{:S(2)}) collective-permute-start(bf16[128,512]{1,0:T(8,128)(2,1)S(1)} %add_convert_fusion.1), channel_id=1, source_target_pairs={{0,2},{1,3},{2,0},{3,1},{4,6},{5,7},{6,4},{7,5},{8,10},{9,11},{10,... | collective-permute-start | bytes 393224 | tf_op jit(solution)/shard_map/ppermute | solution.py:322
  24.8 2.9 %collective-permute-done.9 = bf16[128,512]{1,0:T(8,128)(2,1)S(1)} collective-permute-done((bf16[128,512]{1,0:T(8,128)(2,1)S(1)}, bf16[128,512]{1,0:T(8,128)(2,1)S(1)}, u32[]{:S(2)}, u32[]{:S(2)}) %collective-permute-start.9) | collective-permute-done | bytes 131104 | tf_op jit(solution)/shard_map/ppermute | solution.py:322
  27.8 4.1 %collective-permute-done.11 = bf16[128,512]{1,0:T(8,128)(2,1)S(1)} collective-permute-done((bf16[128,512]{1,0:T(8,128)(2,1)S(1)}, bf16[128,512]{1,0:T(8,128)(2,1)S(1)}, u32[]{:S(2)}, u32[]{:S(2)}) %collective-permute-start.11) | collective-permute-done | bytes 131104 | tf_op jit(solution)/shard_map/ppermute | solution.py:322
  31.9 0.9 %collective-permute-done.8 = bf16[128,1024]{1,0:T(8,128)(2,1)S(1)} collective-permute-done((bf16[128,1024]{1,0:T(8,128)(2,1)S(1)}, bf16[128,1024]{1,0:T(8,128)(2,1)S(1)}, u32[]{:S(2)}, u32[]{:S(2)}) %collective-permute-start.8) | collective-permute-done | bytes 262176 | tf_op jit(solution)/shard_map/ppermute | solution.py:322
  32.8 0.8 %add_convert_fusion = bf16[128,1024]{1,0:T(8,128)(2,1)} fusion(f32[128,1024]{1,0:T(8,128)S(1)} %get-tuple-element.31, bf16[128,1024]{1,0:T(8,128)(2,1)S(1)} %collective-permute-done.8, bf16[128,512]{1,0:T(8,128)(2,1)S(1)} %collective-permute-done.11, bf16[128,512]{1,0:T(8,128)(2,1)S(1)} %collective-permute-done.9), kind=kLoop, calls=%fused_computation | loop fusion | flops 1048576 | bytes 1310720 | tf_op jit(solution)/shard_map/convert_element_type | solution.py:413
  (3 shorter events, 0.1 us)
Async XLA Ops:
  0.0 11.0 %copy-start.3 = (bf16[128,128]{1,0:T(8,128)(2,1)S(1)}, bf16[128,128]{1,0:T(8,128)(2,1)}, u32[]{:S(2)}) copy-start(bf16[128,128]{1,0:T(8,128)(2,1)} %refs_0_.3) | copy-start | bytes 98308
  0.0 11.0 %copy-start.4 = (bf16[128,128]{1,0:T(8,128)(2,1)S(1)}, bf16[128,128]{1,0:T(8,128)(2,1)}, u32[]{:S(2)}) copy-start(bf16[128,128]{1,0:T(8,128)(2,1)} %refs_1_.3) | copy-start | bytes 98308
  0.0 11.0 %copy-start.5 = (bf16[128,128]{1,0:T(8,128)(2,1)S(1)}, bf16[128,128]{1,0:T(8,128)(2,1)}, u32[]{:S(2)}) copy-start(bf16[128,128]{1,0:T(8,128)(2,1)} %refs_2_.3) | copy-start | bytes 98308
  0.0 11.0 %copy-start.6 = (bf16[128,128]{1,0:T(8,128)(2,1)S(1)}, bf16[128,128]{1,0:T(8,128)(2,1)}, u32[]{:S(2)}) copy-start(bf16[128,128]{1,0:T(8,128)(2,1)} %refs_3_.3) | copy-start | bytes 98308
  0.0 11.0 %copy-start.7 = (bf16[128,128]{1,0:T(8,128)(2,1)S(1)}, bf16[128,128]{1,0:T(8,128)(2,1)}, u32[]{:S(2)}) copy-start(bf16[128,128]{1,0:T(8,128)(2,1)} %refs_4_.2) | copy-start | bytes 98308
  0.0 12.2 %copy-start = (bf16[4096,128]{1,0:T(8,128)(2,1)S(1)}, bf16[4096,128]{1,0:T(8,128)(2,1)}, u32[]{:S(2)}) copy-start(bf16[4096,128]{1,0:T(8,128)(2,1)} %wq_ref.3) | copy-start | bytes 3145732
  0.0 12.2 %copy-start.1 = (bf16[4096,128]{1,0:T(8,128)(2,1)S(1)}, bf16[4096,128]{1,0:T(8,128)(2,1)}, u32[]{:S(2)}) copy-start(bf16[4096,128]{1,0:T(8,128)(2,1)} %wk_ref.3) | copy-start | bytes 3145732
  0.0 12.2 %copy-start.2 = (bf16[4096,128]{1,0:T(8,128)(2,1)S(1)}, bf16[4096,128]{1,0:T(8,128)(2,1)}, u32[]{:S(2)}) copy-start(bf16[4096,128]{1,0:T(8,128)(2,1)} %wv_ref.3) | copy-start | bytes 3145732
  1.9 6.6 %collective-permute-start.1 = (bf16[144,256]{1,0:T(8,128)(2,1)}, bf16[144,256]{1,0:T(8,128)(2,1)S(1)}, u32[]{:S(2)}, u32[]{:S(2)}) collective-permute-start(bf16[144,256]{1,0:T(8,128)(2,1)} %get-tuple-element.22), channel_id=1, source_target_pairs={{0,24},{4,28},{8,16},{12,20},{16,8},{20,12},{24,0},{28,4},{1,25},{... | collective-permute-start | bytes 221192 | tf_op jit(solution)/shard_map/ppermute | solution.py:322
  5.8 4.6 %collective-permute-start = (bf16[144,256]{1,0:T(8,128)(2,1)}, bf16[144,256]{1,0:T(8,128)(2,1)S(1)}, u32[]{:S(2)}, u32[]{:S(2)}) collective-permute-start(bf16[144,256]{1,0:T(8,128)(2,1)} %get-tuple-element.22), channel_id=1, source_target_pairs={{0,16},{4,20},{8,24},{12,28},{16,0},{20,4},{24,8},{28,12},{1,17},{... | collective-permute-start | bytes 221192 | tf_op jit(solution)/shard_map/ppermute | solution.py:322
  6.4 4.6 %copy-start.8 = (f32[128,1]{0,1:T(1,128)S(1)}, f32[128,1]{0,1:T(1,128)}, u32[]{:S(2)}) copy-start(f32[128,1]{0,1:T(1,128)} %param.14) | copy-start | bytes 1540
  6.4 4.6 %collective-permute-start.3 = (bf16[144,256]{1,0:T(8,128)(2,1)}, bf16[144,256]{1,0:T(8,128)(2,1)S(1)}, u32[]{:S(2)}, u32[]{:S(2)}) collective-permute-start(bf16[144,256]{1,0:T(8,128)(2,1)} %get-tuple-element.25), channel_id=1, source_target_pairs={{0,8},{4,12},{8,0},{12,4},{16,24},{20,28},{24,16},{28,20},{1,9},{5... | collective-permute-start | bytes 221192 | tf_op jit(solution)/shard_map/ppermute | solution.py:322
  6.5 4.5 %collective-permute-start.2 = (bf16[144,256]{1,0:T(8,128)(2,1)}, bf16[144,256]{1,0:T(8,128)(2,1)S(1)}, u32[]{:S(2)}, u32[]{:S(2)}) collective-permute-start(bf16[144,256]{1,0:T(8,128)(2,1)} %get-tuple-element.24), channel_id=1, source_target_pairs={{0,4},{4,0},{8,12},{12,8},{16,20},{20,16},{24,28},{28,24},{1,5},{5... | collective-permute-start | bytes 221192 | tf_op jit(solution)/shard_map/ppermute | solution.py:322
  10.4 1.8 %collective-permute-start.5 = (bf16[144,256]{1,0:T(8,128)(2,1)S(1)}, bf16[144,256]{1,0:T(8,128)(2,1)S(1)}, u32[]{:S(2)}, u32[]{:S(2)}) collective-permute-start(bf16[144,256]{1,0:T(8,128)(2,1)S(1)} %collective-permute-done.refs_8_), channel_id=1, source_target_pairs={{0,4},{4,0},{8,12},{12,8},{16,20},{20,16},{24,28},{28,24},{1,5},{5... | collective-permute-start | bytes 221192 | tf_op jit(solution)/shard_map/ppermute | solution.py:322
  10.4 1.8 %collective-permute-start.6 = (bf16[144,256]{1,0:T(8,128)(2,1)S(1)}, bf16[144,256]{1,0:T(8,128)(2,1)S(1)}, u32[]{:S(2)}, u32[]{:S(2)}) collective-permute-start(bf16[144,256]{1,0:T(8,128)(2,1)S(1)} %collective-permute-done.1.refs_9_), channel_id=1, source_target_pairs={{0,4},{4,0},{8,12},{12,8},{16,20},{20,16},{24,28},{28,24},{1,5},{5... | collective-permute-start | bytes 221192 | tf_op jit(solution)/shard_map/ppermute | solution.py:322
  10.9 1.3 %collective-permute-start.4 = (bf16[144,256]{1,0:T(8,128)(2,1)S(1)}, bf16[144,256]{1,0:T(8,128)(2,1)S(1)}, u32[]{:S(2)}, u32[]{:S(2)}) collective-permute-start(bf16[144,256]{1,0:T(8,128)(2,1)S(1)} %collective-permute-done.3.refs_7_), channel_id=1, source_target_pairs={{0,4},{4,0},{8,12},{12,8},{16,20},{20,16},{24,28},{28,24},{1,5},{5... | collective-permute-start | bytes 221192 | tf_op jit(solution)/shard_map/ppermute | solution.py:322
  12.9 5.8 %collective-permute-start.7 = (bf16[128,512]{1,0:T(8,128)(2,1)S(1)}, bf16[128,512]{1,0:T(8,128)(2,1)S(1)}, u32[]{:S(2)}, u32[]{:S(2)}) collective-permute-start(bf16[128,512]{1,0:T(8,128)(2,1)S(1)} %get-tuple-element.33), channel_id=1, source_target_pairs={{0,1},{1,0},{2,3},{3,2},{4,5},{5,4},{6,7},{7,6},{8,9},{9,8},{10,11... | collective-permute-start | bytes 393224 | tf_op jit(solution)/shard_map/ppermute | solution.py:322
  15.7 7.9 %collective-permute-start.10 = (bf16[128,512]{1,0:T(8,128)(2,1)S(1)}, bf16[128,512]{1,0:T(8,128)(2,1)S(1)}, u32[]{:S(2)}, u32[]{:S(2)}) collective-permute-start(bf16[128,512]{1,0:T(8,128)(2,1)S(1)} %get-tuple-element.38), channel_id=1, source_target_pairs={{0,1},{1,0},{2,3},{3,2},{4,5},{5,4},{6,7},{7,6},{8,9},{9,8},{10,11... | collective-permute-start | bytes 393224 | tf_op jit(solution)/shard_map/ppermute | solution.py:322
  18.7 9.0 %collective-permute-start.9 = (bf16[128,512]{1,0:T(8,128)(2,1)S(1)}, bf16[128,512]{1,0:T(8,128)(2,1)S(1)}, u32[]{:S(2)}, u32[]{:S(2)}) collective-permute-start(bf16[128,512]{1,0:T(8,128)(2,1)S(1)} %add_convert_fusion.2), channel_id=1, source_target_pairs={{0,2},{1,3},{2,0},{3,1},{4,6},{5,7},{6,4},{7,5},{8,10},{9,11},{10,... | collective-permute-start | bytes 393224 | tf_op jit(solution)/shard_map/ppermute | solution.py:322
  21.5 11.3 %collective-permute-start.8 = (bf16[128,1024]{1,0:T(8,128)(2,1)S(1)}, bf16[128,1024]{1,0:T(8,128)(2,1)S(1)}, u32[]{:S(2)}, u32[]{:S(2)}) collective-permute-start(bf16[128,1024]{1,0:T(8,128)(2,1)S(1)} %get-tuple-element.34), channel_id=1, source_target_pairs={{0,1},{1,0},{2,3},{3,2},{4,5},{5,4},{6,7},{7,6},{8,9},{9,8},{10,11... | collective-permute-start | bytes 786440 | tf_op jit(solution)/shard_map/ppermute | solution.py:322
  23.6 8.3 %collective-permute-start.11 = (bf16[128,512]{1,0:T(8,128)(2,1)S(1)}, bf16[128,512]{1,0:T(8,128)(2,1)S(1)}, u32[]{:S(2)}, u32[]{:S(2)}) collective-permute-start(bf16[128,512]{1,0:T(8,128)(2,1)S(1)} %add_convert_fusion.1), channel_id=1, source_target_pairs={{0,2},{1,3},{2,0},{3,1},{4,6},{5,7},{6,4},{7,5},{8,10},{9,11},{10,... | collective-permute-start | bytes 393224 | tf_op jit(solution)/shard_map/ppermute | solution.py:322
